TPU v7x, 32 devices: a whole 2x2x4 slice. The times are simulated.
32 devices in a mesh: pipe: 4 (over y, core), expert: 8 (over z, x).
Axes of the slice: x: 2, y: 2, z: 4, core: 2. Of those that a mesh axis runs over, the one named last changes fastest.
Arguments:
- tokens_down: bfloat16 [4, 512, 3072], P('pipe', 'expert'), may hold values from -6 to 6
- cotan_down: bfloat16 [4, 512, 3072], P('pipe', 'expert'), may hold values from -0.59765625 to 0.59765625
- gates_down: bfloat16 [4, 512, 2], P('pipe', 'expert'), may hold values from 0.099609375 to 1
- experts_down: int32 [4, 512, 2], P('pipe', 'expert'), may hold values from 0 to 7, as said below
- tokens_up: bfloat16 [4, 512, 3072], P('pipe', 'expert'), may hold values from -6 to 6
- cotan_up: bfloat16 [4, 512, 3072], P('pipe', 'expert'), may hold values from -0.59765625 to 0.59765625
- gates_up: bfloat16 [4, 512, 2], P('pipe', 'expert'), may hold values from 0.099609375 to 1
- experts_up: int32 [4, 512, 2], P('pipe', 'expert'), may hold values from 0 to 7, as said below
- w_in: bfloat16 [4, 3072, 2048], P('pipe', None, 'expert'), may hold values from -0.109375 to 0.109375
Outputs:
- grad_out: bfloat16 [4, 2048, 3072], P('pipe', 'expert')
Inputs may be any that keep to these rules, and one draw needn't show every extreme that they name: `experts_down`: each row names two different experts. In each aligned block of 64 rows (the rows of one device) expert 0 is named by 1 to 17 rows, and by exactly 17 rows in one block of every section. `experts_up`: as for experts_down.
All inputs are finite; a program needn't handle non-finite values.
Results may differ from a plain program's by a relative error of at most 0.0058.
Values may be sent and summed in bfloat16 or wider, within the bound.
No kernel may reach another device: no remote copies, remote signals or barrier semaphores. Data moves between devices by JAX's collectives and lax.ppermute only.
A program may use at most 128 MiB of HBM per device.

v0:
```python
import jax
import jax.numpy as jnp
from jax import lax
from jax.sharding import PartitionSpec as P

CAP = 17


def from_partner(x, axis, bit):
    return lax.ppermute(x, axis, [(i, i ^ 1 << bit) for i in range(lax.axis_size(axis))])


def chosen_gates(gates, ids):
    picked = jnp.where(ids == 0, gates.astype(jnp.float32), jnp.float32(0.0))
    return jnp.sum(picked, axis=1).astype(jnp.bfloat16)


def pack_slots(tokens, cotangent, gate_chosen):
    chosen = gate_chosen != 0
    ranking = jnp.cumsum(chosen.astype(jnp.int32)) - 1
    placing = (
        (jnp.arange(CAP, dtype=jnp.int32)[:, None] == ranking[None, :]) & chosen[None, :]
    ).astype(jnp.bfloat16)
    scaled = (gate_chosen.astype(jnp.float32)[:, None] * cotangent.astype(jnp.float32)).astype(
        jnp.bfloat16
    )
    slot_tokens = jnp.dot(placing, tokens, preferred_element_type=jnp.float32).astype(jnp.bfloat16)
    slot_scaled = jnp.dot(placing, scaled, preferred_element_type=jnp.float32).astype(jnp.bfloat16)
    return (slot_tokens, slot_scaled)


def grad_rows(rows_x, rows_y, weight_in):
    hidden = jnp.dot(rows_x, weight_in, preferred_element_type=jnp.float32)
    active = (hidden * jax.nn.sigmoid(hidden)).astype(jnp.bfloat16)
    return lax.dot_general(
        active, rows_y, (((0,), (0,)), ((), ())), preferred_element_type=jnp.float32
    )


def body(
    tokens_down,
    cotan_down,
    gates_down,
    experts_down,
    tokens_up,
    cotan_up,
    gates_up,
    experts_up,
    w_in,
):
    weight_in = w_in[0]
    down_x, down_y = pack_slots(
        tokens_down[0], cotan_down[0], chosen_gates(gates_down[0], experts_down[0])
    )
    gate_upward = chosen_gates(gates_up[0], experts_up[0])
    digits = lax.axis_size("pipe").bit_length() - 1
    bit_order = list(range(digits))
    mirrored = (tokens_up[0], cotan_up[0], gate_upward)
    for bit_index in bit_order:
        mirrored = from_partner((mirrored[0], mirrored[1], mirrored[2]), "pipe", bit_index)
    up_x, up_y = pack_slots(mirrored[0], mirrored[1], mirrored[2])
    got_dx, got_dy = (
        lax.all_gather(down_x, "expert", axis=0, tiled=True),
        lax.all_gather(down_y, "expert", axis=0, tiled=True),
    )
    part_down = grad_rows(got_dx, got_dy, weight_in)
    got_ux, got_uy = (
        lax.all_gather(up_x, "expert", axis=0, tiled=True),
        lax.all_gather(up_y, "expert", axis=0, tiled=True),
    )
    summed = part_down + grad_rows(got_ux, got_uy, weight_in)
    return summed.astype(jnp.bfloat16)[None]


def solution(mesh):
    in_specs = (
        P("pipe", "expert", None),
        P("pipe", "expert", None),
        P("pipe", "expert", None),
        P("pipe", "expert", None),
        P("pipe", "expert", None),
        P("pipe", "expert", None),
        P("pipe", "expert", None),
        P("pipe", "expert", None),
        P("pipe", None, "expert"),
    )
    out_specs = P("pipe", "expert", None)
    return jax.shard_map(body, mesh=mesh, in_specs=in_specs, out_specs=out_specs, check_vma=False)
```

profile of v0, /device:TPU:0, one launch (start us, length us, event | category | flops | bytes accessed | tf_op | source)
XLA Modules:
  0.0 164.2 jit_solution(8645601030181546460)
XLA Ops:
  0.0 0.0 copy-start
  0.0 0.0 copy-start.2
  0.0 0.8 fusion.42
  0.8 0.5 collective-permute-start
  1.4 0.1 collective-permute-start.4
  1.4 0.4 collective-permute-start.2
  1.9 0.7 fusion.41
  2.6 0.1 copy.14
  2.7 0.1 reduce-window.16
  2.8 0.1 add_reduce_fusion.1
  2.9 1.3 fusion.3
  4.2 35.2 %all-gather.1 = bf16[8,17,3072]{2,1,0:T(8,128)(2,1)S(1)} all-gather(bf16[1,17,3072]{2,1,0:T(8,128)(2,1)S(1)} %fusion.3), channel_id=1, replica_groups=mesh['pipe'=4,'expert'=8] {'expert'}, dimensions={0}, use_global_device_ids=true | all-gather | bytes 940032 | tf_op jit(solution)/shard_map/all_gather | solution.py:64
  39.4 0.0 copy-done.2
  39.4 0.2 fusion.2
  39.6 35.6 %all-gather = bf16[8,17,3072]{2,1,0:T(8,128)(2,1)} all-gather(bf16[1,17,3072]{2,1,0:T(8,128)(2,1)S(1)} %fusion.2), channel_id=1, replica_groups=mesh['pipe'=4,'expert'=8] {'expert'}, dimensions={0}, use_global_device_ids=true | all-gather | bytes 940032 | tf_op jit(solution)/shard_map/all_gather | solution.py:63
  75.2 1.2 reshape.97
  76.4 0.0 copy-start.1
  76.4 1.7 %reshape.95 = bf16[136,3072]{1,0:T(8,128)(2,1)S(1)} reshape(bf16[8,17,3072]{2,1,0:T(8,128)(2,1)} %all-gather) | data formatting | bytes 1671168
  78.1 0.0 collective-permute-done
  78.1 1.6 collective-permute-start.1
  79.7 0.0 collective-permute-done.4
  79.7 0.5 collective-permute-start.5
  80.2 0.0 copy-done
  80.2 0.0 copy-done.1
  80.2 3.1 %fusion.23 = f32[256,3072]{1,0:T(8,128)} fusion(bf16[136,3072]{1,0:T(8,128)(2,1)S(1)} %copy-done.1, bf16[136,3072]{1,0:T(8,128)(2,1)S(1)} %reshape.95, bf16[1,3072,256]{2,1,0:T(8,128)(2,1)S(1)} %copy-done), kind=kOutput, calls=%fused_computation.24 | convolution fusion | flops 427993088 | bytes 6389760 | tf_op jit(solution)/shard_map/dot_general | solution.py:35
  83.3 0.0 collective-permute-done.1
  83.3 0.1 copy.15
  83.4 0.1 reduce-window.17
  83.5 0.1 add_reduce_fusion
  83.6 0.0 collective-permute-done.2
  83.6 1.6 collective-permute-start.3
  85.2 2.6 %collective-permute-done.5 = bf16[64,3072]{1,0:T(8,128)(2,1)} collective-permute-done((bf16[64,3072]{1,0:T(8,128)(2,1)}, bf16[64,3072]{1,0:T(8,128)(2,1)}, u32[]{:S(2)}, u32[]{:S(2)}) %collective-permute-start.5) | collective-permute-done | bytes 393248 | tf_op jit(solution)/shard_map/ppermute | solution.py:10
  87.8 1.3 fusion.5
  89.0 34.8 %all-gather.3 = bf16[8,17,3072]{2,1,0:T(8,128)(2,1)S(1)} all-gather(bf16[1,17,3072]{2,1,0:T(8,128)(2,1)S(1)} %fusion.5), channel_id=1, replica_groups=mesh['pipe'=4,'expert'=8] {'expert'}, dimensions={0}, use_global_device_ids=true | all-gather | bytes 940032 | tf_op jit(solution)/shard_map/all_gather | solution.py:69
  123.8 1.2 reshape.101
  125.0 0.0 collective-permute-done.3
  125.0 0.2 fusion.4
  125.2 32.8 %all-gather.2 = bf16[8,17,3072]{2,1,0:T(8,128)(2,1)S(1)} all-gather(bf16[1,17,3072]{2,1,0:T(8,128)(2,1)S(1)} %fusion.4), channel_id=1, replica_groups=mesh['pipe'=4,'expert'=8] {'expert'}, dimensions={0}, use_global_device_ids=true | all-gather | bytes 940032 | tf_op jit(solution)/shard_map/all_gather | solution.py:68
  158.0 1.2 reshape.99
  159.2 5.0 %fusion.1 = bf16[1,256,3072]{2,1,0:T(8,128)(2,1)} fusion(f32[256,3072]{1,0:T(8,128)} %fusion.23, bf16[136,3072]{1,0:T(8,128)(2,1)} %reshape.101, bf16[136,3072]{1,0:T(8,128)(2,1)} %reshape.99, bf16[1,3072,256]{2,1,0:T(8,128)(2,1)S(1)} %copy-done), kind=kOutput, calls=%fused_computation.2 | convolution fusion | flops 429565952 | bytes 7962624 | tf_op jit(solution)/shard_map/dot_general | solution.py:35
  (4 shorter events, 0.0 us)
Async XLA Ops:
  0.0 80.2 %copy-start = (bf16[1,3072,256]{2,1,0:T(8,128)(2,1)S(1)}, bf16[1,3072,256]{2,1,0:T(8,128)(2,1)}, u32[]{:S(2)}) copy-start(bf16[1,3072,256]{2,1,0:T(8,128)(2,1)} %param.17) | copy-start | bytes 4718596
  0.0 39.4 %copy-start.2 = (bf16[1,64,3072]{2,1,0:T(8,128)(2,1)S(1)}, bf16[1,64,3072]{2,1,0:T(8,128)(2,1)}, u32[]{:S(2)}) copy-start(bf16[1,64,3072]{2,1,0:T(8,128)(2,1)} %param.9) | copy-start | bytes 1179652
  0.8 77.2 %collective-permute-start = (bf16[64]{0:T(256)(128)(2,1)S(1)}, bf16[64]{0:T(256)(128)(2,1)S(1)}, u32[]{:S(2)}, u32[]{:S(2)}) collective-permute-start(bf16[64]{0:T(256)(128)(2,1)S(1)} %fusion.42), channel_id=1, source_target_pairs={{0,8},{8,0},{16,24},{24,16},{1,9},{9,1},{17,25},{25,17},{2,10},{10... | collective-permute-start | bytes 392 | tf_op jit(solution)/shard_map/ppermute | solution.py:10
  1.4 78.3 %collective-permute-start.4 = (bf16[64,3072]{1,0:T(8,128)(2,1)}, bf16[64,3072]{1,0:T(8,128)(2,1)}, u32[]{:S(2)}, u32[]{:S(2)}) collective-permute-start(bf16[64,3072]{1,0:T(8,128)(2,1)} %bitcast.43), channel_id=1, source_target_pairs={{0,8},{8,0},{16,24},{24,16},{1,9},{9,1},{17,25},{25,17},{2,10},{10... | collective-permute-start | bytes 1179656 | tf_op jit(solution)/shard_map/ppermute | solution.py:10
  1.4 82.2 %collective-permute-start.2 = (bf16[64,3072]{1,0:T(8,128)(2,1)}, bf16[64,3072]{1,0:T(8,128)(2,1)}, u32[]{:S(2)}, u32[]{:S(2)}) collective-permute-start(bf16[64,3072]{1,0:T(8,128)(2,1)} %bitcast.44), channel_id=1, source_target_pairs={{0,8},{8,0},{16,24},{24,16},{1,9},{9,1},{17,25},{25,17},{2,10},{10... | collective-permute-start | bytes 1179656 | tf_op jit(solution)/shard_map/ppermute | solution.py:10
  76.4 3.8 %copy-start.1 = (bf16[136,3072]{1,0:T(8,128)(2,1)S(1)}, bf16[136,3072]{1,0:T(8,128)(2,1)}, u32[]{:S(2)}) copy-start(bf16[136,3072]{1,0:T(8,128)(2,1)} %reshape.97) | copy-start | bytes 2506756
  78.1 5.2 %collective-permute-start.1 = (bf16[64]{0:T(256)(128)(2,1)S(1)}, bf16[64]{0:T(256)(128)(2,1)S(1)}, u32[]{:S(2)}, u32[]{:S(2)}) collective-permute-start(bf16[64]{0:T(256)(128)(2,1)S(1)} %collective-permute-done), channel_id=1, source_target_pairs={{0,16},{8,24},{16,0},{24,8},{1,17},{9,25},{17,1},{25,9},{2,18},{10... | collective-permute-start | bytes 392 | tf_op jit(solution)/shard_map/ppermute | solution.py:10
  79.7 8.1 %collective-permute-start.5 = (bf16[64,3072]{1,0:T(8,128)(2,1)}, bf16[64,3072]{1,0:T(8,128)(2,1)}, u32[]{:S(2)}, u32[]{:S(2)}) collective-permute-start(bf16[64,3072]{1,0:T(8,128)(2,1)} %collective-permute-done.4), channel_id=1, source_target_pairs={{0,16},{8,24},{16,0},{24,8},{1,17},{9,25},{17,1},{25,9},{2,18},{10... | collective-permute-start | bytes 1179656 | tf_op jit(solution)/shard_map/ppermute | solution.py:10
  83.6 41.4 %collective-permute-start.3 = (bf16[64,3072]{1,0:T(8,128)(2,1)}, bf16[64,3072]{1,0:T(8,128)(2,1)S(1)}, u32[]{:S(2)}, u32[]{:S(2)}) collective-permute-start(bf16[64,3072]{1,0:T(8,128)(2,1)} %collective-permute-done.2), channel_id=1, source_target_pairs={{0,16},{8,24},{16,0},{24,8},{1,17},{9,25},{17,1},{25,9},{2,18},{10... | collective-permute-start | bytes 1179656 | tf_op jit(solution)/shard_map/ppermute | solution.py:10
where the time goes:
time: 165 us; the launch traced here: 164 us
  blocking collectives  138 us (84%)
  matrix products  11 us (7%)
  local copies, waits for them, and re-layouts  5.48 us (3%)
  starting transfers between devices  4.7 us (3%)
  waiting for transfers between devices  2.58 us (2%)
  other arithmetic  1.96 us (1%)
    all_gather x1, blocking collectives, body(): lax.all_gather(down_x, 'expert', axis=0, tiled=True)  35.6 us
    all_gather x1, blocking collectives, body(): lax.all_gather(down_y, 'expert', axis=0, tiled=True)  35.2 us
    all_gather x1, blocking collectives, body(): lax.all_gather(up_y, 'expert', axis=0, tiled=True)  34.8 us
    all_gather x1, blocking collectives, body(): lax.all_gather(up_x, 'expert', axis=0, tiled=True)  32.8 us
    dot_general x2, matrix products, grad_rows(): lax.dot_general(active, rows_y, (((0,), (0,)), ((), ())), preferred_eleme...  8.09 us
    unnamed x10, local copies, waits for them, and re-layouts  5.29 us
    ppermute x6, starting transfers between devices, from_partner(): lax.ppermute(x, axis, [(i, i ^ 1 << bit) for i in range(lax.axis_size(axi...  4.7 us
  transfers between devices with their start and end apart: 6, of which 1 were waited for; matrix products, arithmetic and copies ran while one was open for 7% of the time, Pallas kernels for 0%

commit v1 on v0

v1 whole, which is shorter than its diff:
```python
import functools

import jax
import jax.numpy as jnp
from jax import lax
from jax.experimental import pallas as pl
from jax.experimental.pallas import tpu as pltpu
from jax.sharding import PartitionSpec as P

CAP = 17
MAIN = 16
SEGS = 8


def grid_cycle(n):
    fast = 1
    while 4 * fast * fast <= n:
        fast *= 2
    slow = n // fast
    order = [s * fast for s in range(slow)]
    for s in reversed(range(slow)):
        columns = range(1, fast)
        if (slow - 1 - s) % 2 == 1:
            columns = reversed(columns)
        order += [s * fast + c for c in columns]
    return order


def pack_kernel(tokens_ref, cotan_ref, gates_ref, ids_ref, out_ref):
    rows, width = tokens_ref.shape
    named = ids_ref[...] == 0
    picked = jnp.where(named, gates_ref[...].astype(jnp.float32), 0.0)
    gate = jnp.sum(picked, axis=0, keepdims=True)
    chosen = jnp.sum(named.astype(jnp.float32), axis=0, keepdims=True)
    earlier = (
        lax.broadcasted_iota(jnp.int32, (rows, rows), 0)
        < lax.broadcasted_iota(jnp.int32, (rows, rows), 1)
    ).astype(jnp.float32)
    slot = jnp.dot(
        jnp.broadcast_to(chosen, (8, rows)), earlier, preferred_element_type=jnp.float32
    )[:1]
    slot = slot.astype(jnp.int32)
    want = lax.broadcasted_iota(jnp.int32, (2 * MAIN, rows), 0)
    hit = (want == slot) & (chosen > 0.0) & (want < CAP)
    placing = hit.astype(jnp.bfloat16)
    slot_gate = jnp.sum(jnp.where(hit, gate, 0.0), axis=1, keepdims=True)
    x = jnp.dot(placing, tokens_ref[...], preferred_element_type=jnp.float32)
    y = jnp.dot(placing, cotan_ref[...], preferred_element_type=jnp.float32) * slot_gate
    seg = width // SEGS
    out_ref[:, :width] = x[:MAIN].astype(jnp.bfloat16)
    out_ref[:, width : 2 * width] = y[:MAIN].astype(jnp.bfloat16)
    tail = [x[MAIN : MAIN + 1, s * seg : (s + 1) * seg] for s in range(SEGS)]
    tail += [y[MAIN : MAIN + 1, s * seg : (s + 1) * seg] for s in range(SEGS)]
    out_ref[:, 2 * width :] = jnp.concatenate(tail, axis=0).astype(jnp.bfloat16)


def pack(tokens, cotan, gates, ids):
    rows, width = tokens.shape
    seg = width // SEGS
    return pl.pallas_call(
        pack_kernel,
        out_shape=jax.ShapeDtypeStruct((MAIN, 2 * width + seg), jnp.bfloat16),
        in_specs=[pl.BlockSpec(memory_space=pltpu.VMEM)] * 4,
        out_specs=pl.BlockSpec(memory_space=pltpu.VMEM),
        compiler_params=pltpu.CompilerParams(vmem_limit_bytes=16 * 2**20),
        cost_estimate=pl.CostEstimate(
            flops=4 * 2 * MAIN * rows * width, bytes_accessed=6 * rows * width, transcendentals=0
        ),
        name="pack_slots",
    )(tokens, cotan, gates.T, ids.T)


def grad_kernel(count, *refs):
    payloads, w_ref, out_ref = refs[:count], refs[count], refs[count + 1]
    width = w_ref.shape[0]
    seg = width // SEGS
    size = count * 2 * SEGS
    tails = jnp.concatenate([p[:, 2 * width :] for p in payloads], axis=0)
    row = lax.broadcasted_iota(jnp.int32, (size, size), 0)
    col = lax.broadcasted_iota(jnp.int32, (size, size), 1)
    order = ((row % count) * (2 * SEGS) + row // count == col).astype(jnp.bfloat16)
    tails = jnp.dot(order, tails, preferred_element_type=jnp.float32).astype(jnp.bfloat16)
    x_tail = jnp.concatenate(
        [tails[s * count : (s + 1) * count] for s in range(SEGS)], axis=1
    )
    y_tail = jnp.concatenate(
        [tails[(SEGS + s) * count : (SEGS + s + 1) * count] for s in range(SEGS)], axis=1
    )
    rows_x = jnp.concatenate([p[:, :width] for p in payloads] + [x_tail], axis=0)
    hidden = jnp.dot(rows_x, w_ref[...], preferred_element_type=jnp.float32)
    active = (hidden * jax.nn.sigmoid(hidden)).astype(jnp.bfloat16)
    for s in range(SEGS):
        cut = slice(width + s * seg, width + (s + 1) * seg)
        rows_y = jnp.concatenate(
            [p[:, cut] for p in payloads] + [y_tail[:, s * seg : (s + 1) * seg]], axis=0
        )
        out_ref[:, s * seg : (s + 1) * seg] = lax.dot_general(
            active, rows_y, (((0,), (0,)), ((), ())), preferred_element_type=jnp.float32
        ).astype(jnp.bfloat16)


def grad(payloads, weight_in):
    width, hidden = weight_in.shape
    count = len(payloads)
    return pl.pallas_call(
        functools.partial(grad_kernel, count),
        out_shape=jax.ShapeDtypeStruct((hidden, width), jnp.bfloat16),
        in_specs=[pl.BlockSpec(memory_space=pltpu.VMEM)] * (count + 1),
        out_specs=pl.BlockSpec(memory_space=pltpu.VMEM),
        compiler_params=pltpu.CompilerParams(vmem_limit_bytes=48 * 2**20),
        cost_estimate=pl.CostEstimate(
            flops=4 * CAP * count * width * hidden,
            bytes_accessed=4 * width * hidden,
            transcendentals=CAP * count * hidden,
        ),
        name="grad_of_slots",
    )(*payloads, weight_in)


def ring(block, right_steps, left_steps, cycle):
    n = len(cycle)
    right = [(cycle[i], cycle[(i + 1) % n]) for i in range(n)]
    left = [(b, a) for a, b in right]
    got, going_right, going_left = [block], block, block
    for step in range(max(right_steps, left_steps)):
        if step < right_steps:
            going_right = lax.ppermute(going_right, "expert", right)
            got.append(going_right)
        if step < left_steps:
            going_left = lax.ppermute(going_left, "expert", left)
            got.append(going_left)
    return got


def body(
    tokens_down,
    cotan_down,
    gates_down,
    experts_down,
    tokens_up,
    cotan_up,
    gates_up,
    experts_up,
    w_in,
):
    n_pipe, n_expert = lax.axis_size("pipe"), lax.axis_size("expert")
    up = pack(tokens_up[0], cotan_up[0], gates_up[0], experts_up[0])
    down = pack(tokens_down[0], cotan_down[0], gates_down[0], experts_down[0])
    up = lax.ppermute(up, "pipe", [(i, n_pipe - 1 - i) for i in range(n_pipe)])
    cycle = grid_cycle(n_expert)
    short = (n_expert - 1) // 2
    long = n_expert - 1 - short
    got = ring(down, long, short, cycle) + ring(up, short, long, cycle)
    return grad(got, w_in[0])[None]


def solution(mesh):
    rows = P("pipe", "expert", None)
    in_specs = (rows,) * 8 + (P("pipe", None, "expert"),)
    return jax.shard_map(body, mesh=mesh, in_specs=in_specs, out_specs=rows, check_vma=False)
```

time: 165 us -> 50.7 us (0.31)
  blocking collectives: 138 us -> 0 us
  starting transfers between devices: 4.7 us -> 23.7 us
  waiting for transfers between devices: 2.58 us -> 15.4 us
  matrix products: 11 us -> 0 us
  Pallas kernels: 0 us -> 4.54 us
  other arithmetic: 1.96 us -> 0 us
    all_gather x4 -> x0, blocking collectives: 138 us -> none  [the longest x1 35.6 us: body(): lax.all_gather(down_x, 'expert', axis=0, tiled=True)]
    ppermute x6 -> x15, starting transfers between devices: 4.7 us -> 23.7 us  [the longest x7 13.8 us: ring(): going_left = lax.ppermute(going_left, 'expert', left)]
    ppermute x6 -> x15, waiting for transfers between devices: 2.58 us -> 15.4 us  [the longest x7 10 us: ring(): going_left = lax.ppermute(going_left, 'expert', left)]
    dot_general x6 -> x0, matrix products: 11 us -> none  [the longest x2 8.09 us: grad_rows(): lax.dot_general(active, rows_y, (((0,), (0,)), ((), ())), preferred_eleme...]
    pallas_call x0 -> x3, Pallas kernels: none -> 4.54 us  [the longest x1 3.79 us: grad(): pl.pallas_call(functools.partial(grad_kernel, count), out_shape=jax.Shape...]
    unnamed x10 -> x18, local copies, waits for them, and re-layouts: 5.29 us -> 6.77 us
  transfers between devices with their start and end apart: 6 -> 15, of which waited for: 1 -> 13; matrix products, arithmetic and copies ran while one was open for 7% -> 0% of each run, Pallas kernels for 0% -> 1%
where the time goes in v1:
time: 50.7 us; the launch traced here: 50.4 us
  starting transfers between devices  23.7 us (47%)
  waiting for transfers between devices  15.4 us (30%)
  local copies, waits for them, and re-layouts  6.77 us (13%)
  Pallas kernels  4.54 us (9%)
    ppermute x7, starting transfers between devices, ring(): going_left = lax.ppermute(going_left, 'expert', left)  13.8 us
    ppermute x7, waiting for transfers between devices, ring(): going_left = lax.ppermute(going_left, 'expert', left)  10 us
    ppermute x7, starting transfers between devices, ring(): going_right = lax.ppermute(going_right, 'expert', right)  7.39 us
    unnamed x18, local copies, waits for them, and re-layouts  6.77 us
    ppermute x7, waiting for transfers between devices, ring(): going_right = lax.ppermute(going_right, 'expert', right)  5.09 us
    pallas_call x1, Pallas kernels, grad(): pl.pallas_call(functools.partial(grad_kernel, count), out_shape=jax.Shape...  3.79 us
    ppermute x1, starting transfers between devices, body(): up = lax.ppermute(up, 'pipe', [(i, n_pipe - 1 - i) for i in range(n_pipe)])  2.47 us
  transfers between devices with their start and end apart: 15, of which 13 were waited for; matrix products, arithmetic and copies ran while one was open for 0% of the time, Pallas kernels for 1%

profile of v1, /device:TPU:0, one launch (start us, length us, event | category | flops | bytes accessed | tf_op | source)
XLA Modules:
  0.0 50.4 jit_solution(6607349662338098636)
XLA Ops:
  0.0 0.0 copy-start
  0.0 0.0 copy-start.1
  0.0 1.1 %copy-done.1 = bf16[1,64,3072]{2,1,0:T(8,128)(2,1)S(1)} copy-done((bf16[1,64,3072]{2,1,0:T(8,128)(2,1)S(1)}, bf16[1,64,3072]{2,1,0:T(8,128)(2,1)}, u32[]{:S(2)}) %copy-start.1) | copy-done | bytes 393240
  1.1 0.0 copy-start.2
  1.1 1.0 %copy-done.2 = bf16[1,64,3072]{2,1,0:T(8,128)(2,1)S(1)} copy-done((bf16[1,64,3072]{2,1,0:T(8,128)(2,1)S(1)}, bf16[1,64,3072]{2,1,0:T(8,128)(2,1)}, u32[]{:S(2)}) %copy-start.2) | copy-done | bytes 393240
  2.1 0.0 copy-start.5
  2.1 0.7 %copy-done.5 = s32[1,64,2]{1,2,0:T(2,128)S(1)} copy-done((s32[1,64,2]{1,2,0:T(2,128)S(1)}, s32[1,64,2]{1,2,0:T(2,128)}, u32[]{:S(2)}) %copy-start.5) | copy-done | bytes 536
  2.8 0.7 %copy-done.7 = bf16[1,64,2]{1,2,0:T(2,128)(2,1)S(1)} copy-done((bf16[1,64,2]{1,2,0:T(2,128)(2,1)S(1)}, bf16[1,64,2]{1,2,0:T(2,128)(2,1)}, u32[]{:S(2)}) %copy-start.7) | copy-done | bytes 280
  3.5 0.4 pack_slots.3
  3.8 2.5 %collective-permute-start.7 = (bf16[16,6528]{1,0:T(8,128)(2,1)S(1)}, bf16[16,6528]{1,0:T(8,128)(2,1)S(1)}, u32[]{:S(2)}, u32[]{:S(2)}) collective-permute-start(bf16[16,6528]{1,0:T(8,128)(2,1)S(1)} %pack_slots.3), channel_id=1, source_target_pairs={{0,24},{8,16},{16,8},{24,0},{1,25},{9,17},{17,9},{25,1},{2,26},{10... | collective-permute-start | bytes 626696 | tf_op jit(solution)/shard_map/ppermute | solution.py:149
  6.3 0.0 copy-start.3
  6.3 1.0 %copy-done.3 = bf16[1,64,3072]{2,1,0:T(8,128)(2,1)S(1)} copy-done((bf16[1,64,3072]{2,1,0:T(8,128)(2,1)S(1)}, bf16[1,64,3072]{2,1,0:T(8,128)(2,1)}, u32[]{:S(2)}) %copy-start.3) | copy-done | bytes 393240
  7.3 0.0 copy-start.4
  7.3 1.0 %copy-done.4 = bf16[1,64,3072]{2,1,0:T(8,128)(2,1)S(1)} copy-done((bf16[1,64,3072]{2,1,0:T(8,128)(2,1)S(1)}, bf16[1,64,3072]{2,1,0:T(8,128)(2,1)}, u32[]{:S(2)}) %copy-start.4) | copy-done | bytes 393240
  8.3 0.7 %copy-done.6 = s32[1,64,2]{1,2,0:T(2,128)S(1)} copy-done((s32[1,64,2]{1,2,0:T(2,128)S(1)}, s32[1,64,2]{1,2,0:T(2,128)}, u32[]{:S(2)}) %copy-start.6) | copy-done | bytes 536
  9.0 0.7 %copy-done.8 = bf16[1,64,2]{1,2,0:T(2,128)(2,1)S(1)} copy-done((bf16[1,64,2]{1,2,0:T(2,128)(2,1)S(1)}, bf16[1,64,2]{1,2,0:T(2,128)(2,1)}, u32[]{:S(2)}) %copy-start.8) | copy-done | bytes 280
  9.6 0.4 pack_slots.2.refs_0_
  10.0 1.6 %collective-permute-start = (bf16[16,6528]{1,0:T(8,128)(2,1)S(1)}, bf16[16,6528]{1,0:T(8,128)(2,1)S(1)}, u32[]{:S(2)}, u32[]{:S(2)}) collective-permute-start(bf16[16,6528]{1,0:T(8,128)(2,1)S(1)} %pack_slots.2.refs_0_), channel_id=1, source_target_pairs={{0,2},{2,4},{4,6},{6,7},{7,5},{5,3},{3,1},{1,0},{8,10},{10,12},{12... | collective-permute-start | bytes 626696 | tf_op jit(solution)/shard_map/ppermute | solution.py:127
  11.6 0.2 collective-permute-done.7.refs_8_
  11.9 2.4 %collective-permute-start.9 = (bf16[16,6528]{1,0:T(8,128)(2,1)S(1)}, bf16[16,6528]{1,0:T(8,128)(2,1)S(1)}, u32[]{:S(2)}, u32[]{:S(2)}) collective-permute-start(bf16[16,6528]{1,0:T(8,128)(2,1)S(1)} %collective-permute-done.7.refs_8_), channel_id=1, source_target_pairs={{2,0},{4,2},{6,4},{7,6},{5,7},{3,5},{1,3},{0,1},{10,8},{12,10},{14... | collective-permute-start | bytes 626696 | tf_op jit(solution)/shard_map/ppermute | solution.py:130
  14.2 1.6 %collective-permute-start.1 = (bf16[16,6528]{1,0:T(8,128)(2,1)S(1)}, bf16[16,6528]{1,0:T(8,128)(2,1)S(1)}, u32[]{:S(2)}, u32[]{:S(2)}) collective-permute-start(bf16[16,6528]{1,0:T(8,128)(2,1)S(1)} %pack_slots.2.refs_0_), channel_id=1, source_target_pairs={{2,0},{4,2},{6,4},{7,6},{5,7},{3,5},{1,3},{0,1},{10,8},{12,10},{14... | collective-permute-start | bytes 626696 | tf_op jit(solution)/shard_map/ppermute | solution.py:130
  15.8 0.5 collective-permute-start.8
  16.3 1.6 %collective-permute-done.refs_1_ = bf16[16,6528]{1,0:T(8,128)(2,1)S(1)} collective-permute-done((bf16[16,6528]{1,0:T(8,128)(2,1)S(1)}, bf16[16,6528]{1,0:T(8,128)(2,1)S(1)}, u32[]{:S(2)}, u32[]{:S(2)}) %collective-permute-start) | collective-permute-done | bytes 208928 | tf_op jit(solution)/shard_map/ppermute | solution.py:127
  17.8 1.9 %collective-permute-start.2 = (bf16[16,6528]{1,0:T(8,128)(2,1)S(1)}, bf16[16,6528]{1,0:T(8,128)(2,1)S(1)}, u32[]{:S(2)}, u32[]{:S(2)}) collective-permute-start(bf16[16,6528]{1,0:T(8,128)(2,1)S(1)} %collective-permute-done.refs_1_), channel_id=1, source_target_pairs={{0,2},{2,4},{4,6},{6,7},{7,5},{5,3},{3,1},{1,0},{8,10},{10,12},{12... | collective-permute-start | bytes 626696 | tf_op jit(solution)/shard_map/ppermute | solution.py:127
  19.7 0.6 %collective-permute-done.9.refs_10_ = bf16[16,6528]{1,0:T(8,128)(2,1)S(1)} collective-permute-done((bf16[16,6528]{1,0:T(8,128)(2,1)S(1)}, bf16[16,6528]{1,0:T(8,128)(2,1)S(1)}, u32[]{:S(2)}, u32[]{:S(2)}) %collective-permute-start.9) | collective-permute-done | bytes 208928 | tf_op jit(solution)/shard_map/ppermute | solution.py:130
  20.3 2.0 %collective-permute-start.11 = (bf16[16,6528]{1,0:T(8,128)(2,1)S(1)}, bf16[16,6528]{1,0:T(8,128)(2,1)S(1)}, u32[]{:S(2)}, u32[]{:S(2)}) collective-permute-start(bf16[16,6528]{1,0:T(8,128)(2,1)S(1)} %collective-permute-done.9.refs_10_), channel_id=1, source_target_pairs={{2,0},{4,2},{6,4},{7,6},{5,7},{3,5},{1,3},{0,1},{10,8},{12,10},{14... | collective-permute-start | bytes 626696 | tf_op jit(solution)/shard_map/ppermute | solution.py:130
  22.2 2.5 %collective-permute-done.1.refs_2_ = bf16[16,6528]{1,0:T(8,128)(2,1)S(1)} collective-permute-done((bf16[16,6528]{1,0:T(8,128)(2,1)S(1)}, bf16[16,6528]{1,0:T(8,128)(2,1)S(1)}, u32[]{:S(2)}, u32[]{:S(2)}) %collective-permute-start.1) | collective-permute-done | bytes 208928 | tf_op jit(solution)/shard_map/ppermute | solution.py:130
  24.7 2.0 %collective-permute-start.3 = (bf16[16,6528]{1,0:T(8,128)(2,1)S(1)}, bf16[16,6528]{1,0:T(8,128)(2,1)S(1)}, u32[]{:S(2)}, u32[]{:S(2)}) collective-permute-start(bf16[16,6528]{1,0:T(8,128)(2,1)S(1)} %collective-permute-done.1.refs_2_), channel_id=1, source_target_pairs={{2,0},{4,2},{6,4},{7,6},{5,7},{3,5},{1,3},{0,1},{10,8},{12,10},{14... | collective-permute-start | bytes 626696 | tf_op jit(solution)/shard_map/ppermute | solution.py:130
  26.7 0.0 collective-permute-done.8.refs_9_
  26.7 0.1 collective-permute-start.10
  26.8 0.1 collective-permute-done.2.refs_3_
  26.9 1.9 %collective-permute-start.4 = (bf16[16,6528]{1,0:T(8,128)(2,1)S(1)}, bf16[16,6528]{1,0:T(8,128)(2,1)S(1)}, u32[]{:S(2)}, u32[]{:S(2)}) collective-permute-start(bf16[16,6528]{1,0:T(8,128)(2,1)S(1)} %collective-permute-done.2.refs_3_), channel_id=1, source_target_pairs={{0,2},{2,4},{4,6},{6,7},{7,5},{5,3},{3,1},{1,0},{8,10},{10,12},{12... | collective-permute-start | bytes 626696 | tf_op jit(solution)/shard_map/ppermute | solution.py:127
  28.8 0.4 collective-permute-done.11.refs_12_
  29.2 2.0 %collective-permute-start.13 = (bf16[16,6528]{1,0:T(8,128)(2,1)S(1)}, bf16[16,6528]{1,0:T(8,128)(2,1)S(1)}, u32[]{:S(2)}, u32[]{:S(2)}) collective-permute-start(bf16[16,6528]{1,0:T(8,128)(2,1)S(1)} %collective-permute-done.11.refs_12_), channel_id=1, source_target_pairs={{2,0},{4,2},{6,4},{7,6},{5,7},{3,5},{1,3},{0,1},{10,8},{12,10},{14... | collective-permute-start | bytes 626696 | tf_op jit(solution)/shard_map/ppermute | solution.py:130
  31.2 2.5 %collective-permute-done.3.refs_4_ = bf16[16,6528]{1,0:T(8,128)(2,1)S(1)} collective-permute-done((bf16[16,6528]{1,0:T(8,128)(2,1)S(1)}, bf16[16,6528]{1,0:T(8,128)(2,1)S(1)}, u32[]{:S(2)}, u32[]{:S(2)}) %collective-permute-start.3) | collective-permute-done | bytes 208928 | tf_op jit(solution)/shard_map/ppermute | solution.py:130
  33.7 2.0 %collective-permute-start.5 = (bf16[16,6528]{1,0:T(8,128)(2,1)S(1)}, bf16[16,6528]{1,0:T(8,128)(2,1)S(1)}, u32[]{:S(2)}, u32[]{:S(2)}) collective-permute-start(bf16[16,6528]{1,0:T(8,128)(2,1)S(1)} %collective-permute-done.3.refs_4_), channel_id=1, source_target_pairs={{2,0},{4,2},{6,4},{7,6},{5,7},{3,5},{1,3},{0,1},{10,8},{12,10},{14... | collective-permute-start | bytes 626696 | tf_op jit(solution)/shard_map/ppermute | solution.py:130
  35.7 0.0 collective-permute-done.10.refs_11_
  35.7 0.1 collective-permute-start.12
  35.8 0.7 %collective-permute-done.4.refs_5_ = bf16[16,6528]{1,0:T(8,128)(2,1)S(1)} collective-permute-done((bf16[16,6528]{1,0:T(8,128)(2,1)S(1)}, bf16[16,6528]{1,0:T(8,128)(2,1)S(1)}, u32[]{:S(2)}, u32[]{:S(2)}) %collective-permute-start.4) | collective-permute-done | bytes 208928 | tf_op jit(solution)/shard_map/ppermute | solution.py:127
  36.4 1.3 %collective-permute-start.6 = (bf16[16,6528]{1,0:T(8,128)(2,1)S(1)}, bf16[16,6528]{1,0:T(8,128)(2,1)S(1)}, u32[]{:S(2)}, u32[]{:S(2)}) collective-permute-start(bf16[16,6528]{1,0:T(8,128)(2,1)S(1)} %collective-permute-done.4.refs_5_), channel_id=1, source_target_pairs={{0,2},{2,4},{4,6},{6,7},{7,5},{5,3},{3,1},{1,0},{8,10},{10,12},{12... | collective-permute-start | bytes 626696 | tf_op jit(solution)/shard_map/ppermute | solution.py:127
  37.8 0.4 collective-permute-done.13.refs_14_
  38.2 2.0 %collective-permute-start.14 = (bf16[16,6528]{1,0:T(8,128)(2,1)S(1)}, bf16[16,6528]{1,0:T(8,128)(2,1)S(1)}, u32[]{:S(2)}, u32[]{:S(2)}) collective-permute-start(bf16[16,6528]{1,0:T(8,128)(2,1)S(1)} %collective-permute-done.13.refs_14_), channel_id=1, source_target_pairs={{2,0},{4,2},{6,4},{7,6},{5,7},{3,5},{1,3},{0,1},{10,8},{12,10},{14... | collective-permute-start | bytes 626696 | tf_op jit(solution)/shard_map/ppermute | solution.py:130
  40.1 2.5 %collective-permute-done.5.refs_6_ = bf16[16,6528]{1,0:T(8,128)(2,1)S(1)} collective-permute-done((bf16[16,6528]{1,0:T(8,128)(2,1)S(1)}, bf16[16,6528]{1,0:T(8,128)(2,1)S(1)}, u32[]{:S(2)}, u32[]{:S(2)}) %collective-permute-start.5) | collective-permute-done | bytes 208928 | tf_op jit(solution)/shard_map/ppermute | solution.py:130
  42.6 0.5 %collective-permute-done.12.refs_13_ = bf16[16,6528]{1,0:T(8,128)(2,1)S(1)} collective-permute-done((bf16[16,6528]{1,0:T(8,128)(2,1)S(1)}, bf16[16,6528]{1,0:T(8,128)(2,1)S(1)}, u32[]{:S(2)}, u32[]{:S(2)}) %collective-permute-start.12) | collective-permute-done | bytes 208928 | tf_op jit(solution)/shard_map/ppermute | solution.py:127
  43.2 2.2 %collective-permute-done.6.refs_7_ = bf16[16,6528]{1,0:T(8,128)(2,1)S(1)} collective-permute-done((bf16[16,6528]{1,0:T(8,128)(2,1)S(1)}, bf16[16,6528]{1,0:T(8,128)(2,1)S(1)}, u32[]{:S(2)}, u32[]{:S(2)}) %collective-permute-start.6) | collective-permute-done | bytes 208928 | tf_op jit(solution)/shard_map/ppermute | solution.py:127
  45.4 1.2 %collective-permute-done.14.refs_15_ = bf16[16,6528]{1,0:T(8,128)(2,1)S(1)} collective-permute-done((bf16[16,6528]{1,0:T(8,128)(2,1)S(1)}, bf16[16,6528]{1,0:T(8,128)(2,1)S(1)}, u32[]{:S(2)}, u32[]{:S(2)}) %collective-permute-start.14) | collective-permute-done | bytes 208928 | tf_op jit(solution)/shard_map/ppermute | solution.py:130
  46.6 0.0 copy-done
  46.6 3.8 %grad_of_slots.1 = bf16[256,3072]{1,0:T(8,128)(2,1)} custom-call(bf16[16,6528]{1,0:T(8,128)(2,1)S(1)} %pack_slots.2.refs_0_, bf16[16,6528]{1,0:T(8,128)(2,1)S(1)} %collective-permute-done.refs_1_, bf16[16,6528]{1,0:T(8,128)(2,1)S(1)} %collective-permute-done.1.refs_2_, bf16[16,6528]{1,0:T(8,128)(2,1)S(1)} %collective-permute-done.2.refs_3_, ...), custom_call_target="tpu_custom_call" | custom-call | flops 855638016 | bytes 3145728 | tf_op jit(solution)/shard_map/grad_of_slots/pallas_call | solution.py:105
  (3 shorter events, 0.0 us)
Async XLA Ops:
  0.0 46.6 %copy-start = (bf16[1,3072,256]{2,1,0:T(8,128)(2,1)S(1)}, bf16[1,3072,256]{2,1,0:T(8,128)(2,1)}, u32[]{:S(2)}) copy-start(bf16[1,3072,256]{2,1,0:T(8,128)(2,1)} %param.17) | copy-start | bytes 4718596
  0.0 1.1 %copy-start.1 = (bf16[1,64,3072]{2,1,0:T(8,128)(2,1)S(1)}, bf16[1,64,3072]{2,1,0:T(8,128)(2,1)}, u32[]{:S(2)}) copy-start(bf16[1,64,3072]{2,1,0:T(8,128)(2,1)} %param.13) | copy-start | bytes 1179652
  1.1 1.0 %copy-start.2 = (bf16[1,64,3072]{2,1,0:T(8,128)(2,1)S(1)}, bf16[1,64,3072]{2,1,0:T(8,128)(2,1)}, u32[]{:S(2)}) copy-start(bf16[1,64,3072]{2,1,0:T(8,128)(2,1)} %param.14) | copy-start | bytes 1179652
  2.1 0.7 %copy-start.5 = (s32[1,64,2]{1,2,0:T(2,128)S(1)}, s32[1,64,2]{1,2,0:T(2,128)}, u32[]{:S(2)}) copy-start(s32[1,64,2]{1,2,0:T(2,128)} %param.16) | copy-start | bytes 1540
  2.8 0.7 %copy-start.7 = (bf16[1,64,2]{1,2,0:T(2,128)(2,1)S(1)}, bf16[1,64,2]{1,2,0:T(2,128)(2,1)}, u32[]{:S(2)}) copy-start(bf16[1,64,2]{1,2,0:T(2,128)(2,1)} %param.15) | copy-start | bytes 772
  3.8 8.0 %collective-permute-start.7 = (bf16[16,6528]{1,0:T(8,128)(2,1)S(1)}, bf16[16,6528]{1,0:T(8,128)(2,1)S(1)}, u32[]{:S(2)}, u32[]{:S(2)}) collective-permute-start(bf16[16,6528]{1,0:T(8,128)(2,1)S(1)} %pack_slots.3), channel_id=1, source_target_pairs={{0,24},{8,16},{16,8},{24,0},{1,25},{9,17},{17,9},{25,1},{2,26},{10... | collective-permute-start | bytes 626696 | tf_op jit(solution)/shard_map/ppermute | solution.py:149
  6.3 1.0 %copy-start.3 = (bf16[1,64,3072]{2,1,0:T(8,128)(2,1)S(1)}, bf16[1,64,3072]{2,1,0:T(8,128)(2,1)}, u32[]{:S(2)}) copy-start(bf16[1,64,3072]{2,1,0:T(8,128)(2,1)} %param.9) | copy-start | bytes 1179652
  7.3 1.0 %copy-start.4 = (bf16[1,64,3072]{2,1,0:T(8,128)(2,1)S(1)}, bf16[1,64,3072]{2,1,0:T(8,128)(2,1)}, u32[]{:S(2)}) copy-start(bf16[1,64,3072]{2,1,0:T(8,128)(2,1)} %param.10) | copy-start | bytes 1179652
  8.3 0.7 %copy-start.6 = (s32[1,64,2]{1,2,0:T(2,128)S(1)}, s32[1,64,2]{1,2,0:T(2,128)}, u32[]{:S(2)}) copy-start(s32[1,64,2]{1,2,0:T(2,128)} %param.12) | copy-start | bytes 1540
  9.0 0.7 %copy-start.8 = (bf16[1,64,2]{1,2,0:T(2,128)(2,1)S(1)}, bf16[1,64,2]{1,2,0:T(2,128)(2,1)}, u32[]{:S(2)}) copy-start(bf16[1,64,2]{1,2,0:T(2,128)(2,1)} %param.11) | copy-start | bytes 772
  10.0 7.8 %collective-permute-start = (bf16[16,6528]{1,0:T(8,128)(2,1)S(1)}, bf16[16,6528]{1,0:T(8,128)(2,1)S(1)}, u32[]{:S(2)}, u32[]{:S(2)}) collective-permute-start(bf16[16,6528]{1,0:T(8,128)(2,1)S(1)} %pack_slots.2.refs_0_), channel_id=1, source_target_pairs={{0,2},{2,4},{4,6},{6,7},{7,5},{5,3},{3,1},{1,0},{8,10},{10,12},{12... | collective-permute-start | bytes 626696 | tf_op jit(solution)/shard_map/ppermute | solution.py:127
  11.9 8.4 %collective-permute-start.9 = (bf16[16,6528]{1,0:T(8,128)(2,1)S(1)}, bf16[16,6528]{1,0:T(8,128)(2,1)S(1)}, u32[]{:S(2)}, u32[]{:S(2)}) collective-permute-start(bf16[16,6528]{1,0:T(8,128)(2,1)S(1)} %collective-permute-done.7.refs_8_), channel_id=1, source_target_pairs={{2,0},{4,2},{6,4},{7,6},{5,7},{3,5},{1,3},{0,1},{10,8},{12,10},{14... | collective-permute-start | bytes 626696 | tf_op jit(solution)/shard_map/ppermute | solution.py:130
  14.2 10.5 %collective-permute-start.1 = (bf16[16,6528]{1,0:T(8,128)(2,1)S(1)}, bf16[16,6528]{1,0:T(8,128)(2,1)S(1)}, u32[]{:S(2)}, u32[]{:S(2)}) collective-permute-start(bf16[16,6528]{1,0:T(8,128)(2,1)S(1)} %pack_slots.2.refs_0_), channel_id=1, source_target_pairs={{2,0},{4,2},{6,4},{7,6},{5,7},{3,5},{1,3},{0,1},{10,8},{12,10},{14... | collective-permute-start | bytes 626696 | tf_op jit(solution)/shard_map/ppermute | solution.py:130
  15.8 10.9 %collective-permute-start.8 = (bf16[16,6528]{1,0:T(8,128)(2,1)S(1)}, bf16[16,6528]{1,0:T(8,128)(2,1)S(1)}, u32[]{:S(2)}, u32[]{:S(2)}) collective-permute-start(bf16[16,6528]{1,0:T(8,128)(2,1)S(1)} %collective-permute-done.7.refs_8_), channel_id=1, source_target_pairs={{0,2},{2,4},{4,6},{6,7},{7,5},{5,3},{3,1},{1,0},{8,10},{10,12},{12... | collective-permute-start | bytes 626696 | tf_op jit(solution)/shard_map/ppermute | solution.py:127
  17.8 9.1 %collective-permute-start.2 = (bf16[16,6528]{1,0:T(8,128)(2,1)S(1)}, bf16[16,6528]{1,0:T(8,128)(2,1)S(1)}, u32[]{:S(2)}, u32[]{:S(2)}) collective-permute-start(bf16[16,6528]{1,0:T(8,128)(2,1)S(1)} %collective-permute-done.refs_1_), channel_id=1, source_target_pairs={{0,2},{2,4},{4,6},{6,7},{7,5},{5,3},{3,1},{1,0},{8,10},{10,12},{12... | collective-permute-start | bytes 626696 | tf_op jit(solution)/shard_map/ppermute | solution.py:127
  20.3 9.0 %collective-permute-start.11 = (bf16[16,6528]{1,0:T(8,128)(2,1)S(1)}, bf16[16,6528]{1,0:T(8,128)(2,1)S(1)}, u32[]{:S(2)}, u32[]{:S(2)}) collective-permute-start(bf16[16,6528]{1,0:T(8,128)(2,1)S(1)} %collective-permute-done.9.refs_10_), channel_id=1, source_target_pairs={{2,0},{4,2},{6,4},{7,6},{5,7},{3,5},{1,3},{0,1},{10,8},{12,10},{14... | collective-permute-start | bytes 626696 | tf_op jit(solution)/shard_map/ppermute | solution.py:130
  24.7 9.0 %collective-permute-start.3 = (bf16[16,6528]{1,0:T(8,128)(2,1)S(1)}, bf16[16,6528]{1,0:T(8,128)(2,1)S(1)}, u32[]{:S(2)}, u32[]{:S(2)}) collective-permute-start(bf16[16,6528]{1,0:T(8,128)(2,1)S(1)} %collective-permute-done.1.refs_2_), channel_id=1, source_target_pairs={{2,0},{4,2},{6,4},{7,6},{5,7},{3,5},{1,3},{0,1},{10,8},{12,10},{14... | collective-permute-start | bytes 626696 | tf_op jit(solution)/shard_map/ppermute | solution.py:130
  26.7 9.0 %collective-permute-start.10 = (bf16[16,6528]{1,0:T(8,128)(2,1)S(1)}, bf16[16,6528]{1,0:T(8,128)(2,1)S(1)}, u32[]{:S(2)}, u32[]{:S(2)}) collective-permute-start(bf16[16,6528]{1,0:T(8,128)(2,1)S(1)} %collective-permute-done.8.refs_9_), channel_id=1, source_target_pairs={{0,2},{2,4},{4,6},{6,7},{7,5},{5,3},{3,1},{1,0},{8,10},{10,12},{12... | collective-permute-start | bytes 626696 | tf_op jit(solution)/shard_map/ppermute | solution.py:127
  26.9 9.5 %collective-permute-start.4 = (bf16[16,6528]{1,0:T(8,128)(2,1)S(1)}, bf16[16,6528]{1,0:T(8,128)(2,1)S(1)}, u32[]{:S(2)}, u32[]{:S(2)}) collective-permute-start(bf16[16,6528]{1,0:T(8,128)(2,1)S(1)} %collective-permute-done.2.refs_3_), channel_id=1, source_target_pairs={{0,2},{2,4},{4,6},{6,7},{7,5},{5,3},{3,1},{1,0},{8,10},{10,12},{12... | collective-permute-start | bytes 626696 | tf_op jit(solution)/shard_map/ppermute | solution.py:127
  29.2 9.0 %collective-permute-start.13 = (bf16[16,6528]{1,0:T(8,128)(2,1)S(1)}, bf16[16,6528]{1,0:T(8,128)(2,1)S(1)}, u32[]{:S(2)}, u32[]{:S(2)}) collective-permute-start(bf16[16,6528]{1,0:T(8,128)(2,1)S(1)} %collective-permute-done.11.refs_12_), channel_id=1, source_target_pairs={{2,0},{4,2},{6,4},{7,6},{5,7},{3,5},{1,3},{0,1},{10,8},{12,10},{14... | collective-permute-start | bytes 626696 | tf_op jit(solution)/shard_map/ppermute | solution.py:130
  33.7 9.0 %collective-permute-start.5 = (bf16[16,6528]{1,0:T(8,128)(2,1)S(1)}, bf16[16,6528]{1,0:T(8,128)(2,1)S(1)}, u32[]{:S(2)}, u32[]{:S(2)}) collective-permute-start(bf16[16,6528]{1,0:T(8,128)(2,1)S(1)} %collective-permute-done.3.refs_4_), channel_id=1, source_target_pairs={{2,0},{4,2},{6,4},{7,6},{5,7},{3,5},{1,3},{0,1},{10,8},{12,10},{14... | collective-permute-start | bytes 626696 | tf_op jit(solution)/shard_map/ppermute | solution.py:130
  35.7 7.5 %collective-permute-start.12 = (bf16[16,6528]{1,0:T(8,128)(2,1)S(1)}, bf16[16,6528]{1,0:T(8,128)(2,1)S(1)}, u32[]{:S(2)}, u32[]{:S(2)}) collective-permute-start(bf16[16,6528]{1,0:T(8,128)(2,1)S(1)} %collective-permute-done.10.refs_11_), channel_id=1, source_target_pairs={{0,2},{2,4},{4,6},{6,7},{7,5},{5,3},{3,1},{1,0},{8,10},{10,12},{12... | collective-permute-start | bytes 626696 | tf_op jit(solution)/shard_map/ppermute | solution.py:127
  36.4 9.0 %collective-permute-start.6 = (bf16[16,6528]{1,0:T(8,128)(2,1)S(1)}, bf16[16,6528]{1,0:T(8,128)(2,1)S(1)}, u32[]{:S(2)}, u32[]{:S(2)}) collective-permute-start(bf16[16,6528]{1,0:T(8,128)(2,1)S(1)} %collective-permute-done.4.refs_5_), channel_id=1, source_target_pairs={{0,2},{2,4},{4,6},{6,7},{7,5},{5,3},{3,1},{1,0},{8,10},{10,12},{12... | collective-permute-start | bytes 626696 | tf_op jit(solution)/shard_map/ppermute | solution.py:127
  38.2 8.4 %collective-permute-start.14 = (bf16[16,6528]{1,0:T(8,128)(2,1)S(1)}, bf16[16,6528]{1,0:T(8,128)(2,1)S(1)}, u32[]{:S(2)}, u32[]{:S(2)}) collective-permute-start(bf16[16,6528]{1,0:T(8,128)(2,1)S(1)} %collective-permute-done.13.refs_14_), channel_id=1, source_target_pairs={{2,0},{4,2},{6,4},{7,6},{5,7},{3,5},{1,3},{0,1},{10,8},{12,10},{14... | collective-permute-start | bytes 626696 | tf_op jit(solution)/shard_map/ppermute | solution.py:130

commit v2 on v1

v2 whole, which is shorter than its diff:
```python
import functools

import jax
import jax.numpy as jnp
from jax import lax
from jax.experimental import pallas as pl
from jax.experimental.pallas import tpu as pltpu
from jax.sharding import PartitionSpec as P

CAP = 17
MAIN = 16
SEGS = 8


def grid_cycle(n):
    fast = 1
    while 4 * fast * fast <= n:
        fast *= 2
    slow = n // fast
    order = [s * fast for s in range(slow)]
    for s in reversed(range(slow)):
        columns = range(1, fast)
        if (slow - 1 - s) % 2 == 1:
            columns = reversed(columns)
        order += [s * fast + c for c in columns]
    return order


def place(gates, ids):
    rows = ids.shape[1]
    named = ids == 0
    gate = jnp.sum(jnp.where(named, gates.astype(jnp.float32), 0.0), axis=0, keepdims=True)
    chosen = jnp.sum(named.astype(jnp.float32), axis=0, keepdims=True)
    earlier = (
        lax.broadcasted_iota(jnp.int32, (rows, rows), 0)
        < lax.broadcasted_iota(jnp.int32, (rows, rows), 1)
    ).astype(jnp.float32)
    slot = jnp.dot(
        jnp.broadcast_to(chosen, (8, rows)), earlier, preferred_element_type=jnp.float32
    )[:1].astype(jnp.int32)
    want = lax.broadcasted_iota(jnp.int32, (2 * MAIN, rows), 0)
    hit = (want == slot) & (chosen > 0.0) & (want < CAP)
    slot_gate = jnp.sum(jnp.where(hit, gate, 0.0), axis=1, keepdims=True)
    return hit.astype(jnp.bfloat16), slot_gate


def pack_kernel(*refs):
    hbm, outs, held, sems = refs[:8], refs[8:10], refs[10:18], refs[18]
    order = [2, 3, 6, 7, 4, 5, 0, 1]
    copies = {i: pltpu.make_async_copy(hbm[i], held[i], sems.at[i]) for i in order}
    for i in order:
        copies[i].start()
    for i in order[:4]:
        copies[i].wait()
    places = [place(held[d + 2][...], held[d + 3][...]) for d in (0, 4)]
    for d, (placing, slot_gate), out_ref in ((4, places[1], outs[1]), (0, places[0], outs[0])):
        copies[d].wait()
        copies[d + 1].wait()
        width = held[d].shape[1]
        seg = width // SEGS
        x = jnp.dot(placing, held[d][...], preferred_element_type=jnp.float32)
        y = jnp.dot(placing, held[d + 1][...], preferred_element_type=jnp.float32) * slot_gate
        out_ref[:, :width] = x[:MAIN].astype(jnp.bfloat16)
        out_ref[:, width : 2 * width] = y[:MAIN].astype(jnp.bfloat16)
        tail = [x[MAIN : MAIN + 1, s * seg : (s + 1) * seg] for s in range(SEGS)]
        tail += [y[MAIN : MAIN + 1, s * seg : (s + 1) * seg] for s in range(SEGS)]
        out_ref[:, 2 * width :] = jnp.concatenate(tail, axis=0).astype(jnp.bfloat16)


def pack(arrays):
    rows, width = arrays[0].shape
    seg = width // SEGS
    payload = jax.ShapeDtypeStruct((MAIN, 2 * width + seg), jnp.bfloat16)
    return pl.pallas_call(
        pack_kernel,
        out_shape=(payload, payload),
        in_specs=[pl.BlockSpec(memory_space=pltpu.HBM)] * 8,
        out_specs=(pl.BlockSpec(memory_space=pltpu.VMEM),) * 2,
        scratch_shapes=[pltpu.VMEM(a.shape, a.dtype) for a in arrays]
        + [pltpu.SemaphoreType.DMA((8,))],
        compiler_params=pltpu.CompilerParams(vmem_limit_bytes=60 * 2**20),
        cost_estimate=pl.CostEstimate(
            flops=8 * 2 * MAIN * rows * width, bytes_accessed=12 * rows * width, transcendentals=0
        ),
        name="pack_slots",
    )(*arrays)


class Block:
    def __init__(self, width, first, second=None):
        self.width, self.first, self.second = width, first, second

    def __getitem__(self, where):
        rows, lanes = where
        if self.second is None:
            return self.first[rows, lanes]
        if lanes.stop is not None and lanes.stop <= self.width:
            return self.first[rows, lanes]
        stop = lanes.stop if lanes.stop is None else lanes.stop - self.width
        return self.second[rows, lanes.start - self.width : stop]


def grad_kernel(count, last, *refs):
    blocks, refs = refs[: count + 1], refs[count + 1 :]
    w_ref, refs = refs[0], refs[1:]
    width = w_ref.shape[0]
    payloads = [Block(width, b) for b in blocks[: count - 1]] + [Block(width, *blocks[count - 1 :])]
    seg = width // SEGS
    size = count * 2 * SEGS
    tails = jnp.concatenate([p[:, 2 * width :] for p in payloads], axis=0)
    row = lax.broadcasted_iota(jnp.int32, (size, size), 0)
    col = lax.broadcasted_iota(jnp.int32, (size, size), 1)
    order = ((row % count) * (2 * SEGS) + row // count == col).astype(jnp.bfloat16)
    tails = jnp.dot(order, tails, preferred_element_type=jnp.float32)
    x_tail = jnp.concatenate(
        [tails[s * count : (s + 1) * count] for s in range(SEGS)], axis=1
    ).astype(jnp.bfloat16)
    y_tail = jnp.concatenate(
        [tails[(SEGS + s) * count : (SEGS + s + 1) * count] for s in range(SEGS)], axis=1
    ).astype(jnp.bfloat16)
    rows_x = jnp.concatenate([p[:, :width] for p in payloads] + [x_tail], axis=0)
    hidden = jnp.dot(rows_x, w_ref[...], preferred_element_type=jnp.float32)
    active = (hidden * jax.nn.sigmoid(hidden)).astype(jnp.bfloat16)
    if last:
        before, out_ref, made, sems = refs
    else:
        (out_ref,) = refs
    copies = []
    for s in range(SEGS):
        cut = slice(width + s * seg, width + (s + 1) * seg)
        here = slice(s * seg, (s + 1) * seg)
        rows_y = jnp.concatenate([p[:, cut] for p in payloads] + [y_tail[:, here]], axis=0)
        part = lax.dot_general(
            active, rows_y, (((0,), (0,)), ((), ())), preferred_element_type=jnp.float32
        )
        if not last:
            out_ref[:, here] = part
            continue
        made[:, here] = (before[:, here] + part).astype(jnp.bfloat16)
        copies.append(
            pltpu.make_async_copy(made.at[:, here], out_ref.at[:, here], sems.at[s])
        )
        copies[-1].start()
    for copy in copies:
        copy.wait()


def grad(payloads, weight_in, before=None, flops=0):
    width, hidden = weight_in.shape
    count = len(payloads) - 1
    last = before is not None
    operands = (*payloads, weight_in) + ((before,) if last else ())
    return pl.pallas_call(
        functools.partial(grad_kernel, count, last),
        out_shape=jax.ShapeDtypeStruct((hidden, width), jnp.bfloat16 if last else jnp.float32),
        in_specs=[pl.BlockSpec(memory_space=pltpu.VMEM)] * len(operands),
        out_specs=pl.BlockSpec(memory_space=pltpu.HBM if last else pltpu.VMEM),
        scratch_shapes=[
            pltpu.VMEM((hidden, width), jnp.bfloat16),
            pltpu.SemaphoreType.DMA((SEGS,)),
        ]
        if last
        else [],
        compiler_params=pltpu.CompilerParams(vmem_limit_bytes=40 * 2**20),
        cost_estimate=pl.CostEstimate(
            flops=flops or 4 * CAP * count * width * hidden,
            bytes_accessed=4 * width * hidden,
            transcendentals=CAP * count * hidden,
        ),
        name="grad_sum" if last else "grad_part",
    )(*operands)


def gather_both(down, up, n_pipe, cycle, width):
    n = len(cycle)
    right = [(cycle[i], cycle[(i + 1) % n]) for i in range(n)]
    left = [(b, a) for a, b in right]
    full = (n - 1) // 2

    def step(pair):
        return (
            lax.ppermute(pair[0], "expert", right),
            lax.ppermute(pair[1], "expert", left),
        )

    def mirrored(block, moves):
        pairs = [(p * n + a, (n_pipe - 1 - p) * n + b) for p in range(n_pipe) for a, b in moves]
        return lax.ppermute(block, ("pipe", "expert"), pairs)

    down_pair = step((down, down))
    up_pair = (mirrored(up, right), mirrored(up, left))
    got_down = [down, *down_pair]
    got_up = [mirrored(up, [(e, e) for e in range(n)]), *up_pair]
    for _ in range(1, full):
        down_pair = step(down_pair)
        got_down += down_pair
        up_pair = step(up_pair)
        got_up += up_pair
    down_pair = step((down_pair[0][:, :width], down_pair[1][:, width:]))
    up_pair = step((up_pair[0][:, :width], up_pair[1][:, width:]))
    return got_down + list(down_pair), got_up + list(up_pair)


def body(
    tokens_down,
    cotan_down,
    gates_down,
    experts_down,
    tokens_up,
    cotan_up,
    gates_up,
    experts_up,
    w_in,
):
    n_pipe, n_expert = lax.axis_size("pipe"), lax.axis_size("expert")
    down, up = pack(
        (
            *(tokens_down[0], cotan_down[0], gates_down[0].T, experts_down[0].T),
            *(tokens_up[0], cotan_up[0], gates_up[0].T, experts_up[0].T),
        )
    )
    got_down, got_up = gather_both(down, up, n_pipe, grid_cycle(n_expert), w_in.shape[1])
    part = grad(got_down, w_in[0])
    return grad(got_up, w_in[0], part)[None]


def solution(mesh):
    rows = P("pipe", "expert", None)
    in_specs = (rows,) * 8 + (P("pipe", None, "expert"),)
    return jax.shard_map(body, mesh=mesh, in_specs=in_specs, out_specs=rows, check_vma=False)
```

time: 50.7 us -> 44.4 us (0.88)
  starting transfers between devices: 23.7 us -> 16.3 us
  local copies, waits for them, and re-layouts: 6.77 us -> 0.97 us
  waiting for transfers between devices: 15.4 us -> 20.3 us
  Pallas kernels: 4.54 us -> 6.68 us
    ppermute x15 -> x17, starting transfers between devices: 23.7 us -> 16.3 us  [the longest x7 12 us: step(): lax.ppermute(pair[1], 'expert', left)]
    unnamed x18 -> x4, local copies, waits for them, and re-layouts: 6.77 us -> 0.93 us
    ppermute x15 -> x17, waiting for transfers between devices: 15.4 us -> 20.3 us  [the longest x7 10.8 us: step(): lax.ppermute(pair[1], 'expert', left)]
    pallas_call x3, Pallas kernels: 4.54 us -> 6.68 us  [the longest x2 4.11 us: grad(): pl.pallas_call(functools.partial(grad_kernel, count, last), out_shape=jax...]
  transfers between devices with their start and end apart: 15 -> 17, of which waited for: 13 -> 12; matrix products, arithmetic and copies ran while one was open for 0% -> 0% of each run, Pallas kernels for 1% -> 4%
where the time goes in v2:
time: 44.4 us; the launch traced here: 44.3 us
  waiting for transfers between devices  20.3 us (46%)
  starting transfers between devices  16.3 us (37%)
  Pallas kernels  6.68 us (15%)
  local copies, waits for them, and re-layouts  0.97 us (2%)
    ppermute x7, starting transfers between devices, step(): lax.ppermute(pair[1], 'expert', left)  12 us
    ppermute x7, waiting for transfers between devices, step(): lax.ppermute(pair[1], 'expert', left)  10.8 us
    ppermute x7, waiting for transfers between devices, step(): lax.ppermute(pair[0], 'expert', right)  6.11 us
    pallas_call x2, Pallas kernels, grad(): pl.pallas_call(functools.partial(grad_kernel, count, last), out_shape=jax...  4.11 us
    ppermute x3, waiting for transfers between devices, mirrored(): return lax.ppermute(block, ('pipe', 'expert'), pairs)  3.32 us
    ppermute x3, starting transfers between devices, mirrored(): return lax.ppermute(block, ('pipe', 'expert'), pairs)  3.13 us
    pallas_call x1, Pallas kernels, pack(): pl.pallas_call(pack_kernel, out_shape=(payload, payload), in_specs=[pl.Bl...  2.57 us
    ppermute x7, starting transfers between devices, step(): lax.ppermute(pair[0], 'expert', right)  1.12 us
  transfers between devices with their start and end apart: 17, of which 12 were waited for; matrix products, arithmetic and copies ran while one was open for 0% of the time, Pallas kernels for 4%

profile of v2, /device:TPU:0, one launch (start us, length us, event | category | flops | bytes accessed | tf_op | source)
XLA Modules:
  0.0 44.3 jit_solution(14858882077274881424)
XLA Ops:
  0.0 0.0 copy-start
  0.0 2.6 %pack_slots.1 = (bf16[16,6528]{1,0:T(8,128)(2,1)}, bf16[16,6528]{1,0:T(8,128)(2,1)}) custom-call(bf16[64,3072]{1,0:T(8,128)(2,1)} %bitcast.20, bf16[64,3072]{1,0:T(8,128)(2,1)} %bitcast.21, bf16[2,64]{1,0:T(2,128)(2,1)} %bitcast.26, s32[2,64]{1,0:T(2,128)} %bitcast.24, bf16[64,3072]{1,0:T(8,128)(2,1)} %bitcast.22, bf16[64,3072]{1,0:T(8,128)(2,1)} %bitcast.23, ...), custom_call_target="tpu_custom_call" | custom-call | flops 50331648 | bytes 2359296 | tf_op jit(solution)/shard_map/pack_slots/pallas_call | solution.py:74
  2.6 3.0 %collective-permute-start.10 = (bf16[16,6528]{1,0:T(8,128)(2,1)}, bf16[16,6528]{1,0:T(8,128)(2,1)S(1)}, u32[]{:S(2)}, u32[]{:S(2)}) collective-permute-start(bf16[16,6528]{1,0:T(8,128)(2,1)} %get-tuple-element.8.refs_0_), channel_id=1, source_target_pairs={{2,0},{4,2},{6,4},{7,6},{5,7},{3,5},{1,3},{0,1},{10,8},{12,10},{14... | collective-permute-start | bytes 626696 | tf_op jit(solution)/shard_map/ppermute | solution.py:183
  5.6 0.2 collective-permute-start.9
  5.7 1.7 %collective-permute-start.2 = (bf16[16,6528]{1,0:T(8,128)(2,1)}, bf16[16,6528]{1,0:T(8,128)(2,1)S(1)}, u32[]{:S(2)}, u32[]{:S(2)}) collective-permute-start(bf16[16,6528]{1,0:T(8,128)(2,1)} %get-tuple-element.7), channel_id=1, source_target_pairs={{2,24},{4,26},{6,28},{7,30},{5,31},{3,29},{1,27},{0,25},{10,16},{1... | collective-permute-start | bytes 626696 | tf_op jit(solution)/shard_map/ppermute | solution.py:188
  7.4 0.9 %collective-permute-start.1 = (bf16[16,6528]{1,0:T(8,128)(2,1)}, bf16[16,6528]{1,0:T(8,128)(2,1)S(1)}, u32[]{:S(2)}, u32[]{:S(2)}) collective-permute-start(bf16[16,6528]{1,0:T(8,128)(2,1)} %get-tuple-element.7), channel_id=1, source_target_pairs={{0,26},{2,28},{4,30},{6,31},{7,29},{5,27},{3,25},{1,24},{8,18},{10... | collective-permute-start | bytes 626696 | tf_op jit(solution)/shard_map/ppermute | solution.py:188
  8.4 3.4 %collective-permute-done.10.refs_2_ = bf16[16,6528]{1,0:T(8,128)(2,1)S(1)} collective-permute-done((bf16[16,6528]{1,0:T(8,128)(2,1)}, bf16[16,6528]{1,0:T(8,128)(2,1)S(1)}, u32[]{:S(2)}, u32[]{:S(2)}) %collective-permute-start.10) | collective-permute-done | bytes 208928 | tf_op jit(solution)/shard_map/ppermute | solution.py:183
  11.7 1.8 %collective-permute-start.12 = (bf16[16,6528]{1,0:T(8,128)(2,1)S(1)}, bf16[16,6528]{1,0:T(8,128)(2,1)S(1)}, u32[]{:S(2)}, u32[]{:S(2)}) collective-permute-start(bf16[16,6528]{1,0:T(8,128)(2,1)S(1)} %collective-permute-done.10.refs_2_), channel_id=1, source_target_pairs={{2,0},{4,2},{6,4},{7,6},{5,7},{3,5},{1,3},{0,1},{10,8},{12,10},{14... | collective-permute-start | bytes 626696 | tf_op jit(solution)/shard_map/ppermute | solution.py:183
  13.6 0.0 collective-permute-done.9.refs_1_
  13.6 0.2 collective-permute-start.11
  13.8 3.3 %collective-permute-done.2.refs_2_ = bf16[16,6528]{1,0:T(8,128)(2,1)S(1)} collective-permute-done((bf16[16,6528]{1,0:T(8,128)(2,1)}, bf16[16,6528]{1,0:T(8,128)(2,1)S(1)}, u32[]{:S(2)}, u32[]{:S(2)}) %collective-permute-start.2) | collective-permute-done | bytes 208928 | tf_op jit(solution)/shard_map/ppermute | solution.py:188
  17.1 1.5 %collective-permute-start.4 = (bf16[16,6528]{1,0:T(8,128)(2,1)S(1)}, bf16[16,6528]{1,0:T(8,128)(2,1)S(1)}, u32[]{:S(2)}, u32[]{:S(2)}) collective-permute-start(bf16[16,6528]{1,0:T(8,128)(2,1)S(1)} %collective-permute-done.2.refs_2_), channel_id=1, source_target_pairs={{2,0},{4,2},{6,4},{7,6},{5,7},{3,5},{1,3},{0,1},{10,8},{12,10},{14... | collective-permute-start | bytes 626696 | tf_op jit(solution)/shard_map/ppermute | solution.py:183
  18.6 0.0 collective-permute-done.1.refs_1_
  18.6 0.6 %collective-permute-start.3 = (bf16[16,6528]{1,0:T(8,128)(2,1)S(1)}, bf16[16,6528]{1,0:T(8,128)(2,1)S(1)}, u32[]{:S(2)}, u32[]{:S(2)}) collective-permute-start(bf16[16,6528]{1,0:T(8,128)(2,1)S(1)} %collective-permute-done.1.refs_1_), channel_id=1, source_target_pairs={{0,2},{2,4},{4,6},{6,7},{7,5},{5,3},{3,1},{1,0},{8,10},{10,12},{12... | collective-permute-start | bytes 626696 | tf_op jit(solution)/shard_map/ppermute | solution.py:182
  19.2 2.4 %collective-permute-done.12.refs_4_ = bf16[16,6528]{1,0:T(8,128)(2,1)S(1)} collective-permute-done((bf16[16,6528]{1,0:T(8,128)(2,1)S(1)}, bf16[16,6528]{1,0:T(8,128)(2,1)S(1)}, u32[]{:S(2)}, u32[]{:S(2)}) %collective-permute-start.12) | collective-permute-done | bytes 208928 | tf_op jit(solution)/shard_map/ppermute | solution.py:183
  21.6 1.4 %collective-permute-start.14 = (bf16[16,6528]{1,0:T(8,128)(2,1)S(1)}, bf16[16,6528]{1,0:T(8,128)(2,1)S(1)}, u32[]{:S(2)}, u32[]{:S(2)}) collective-permute-start(bf16[16,6528]{1,0:T(8,128)(2,1)S(1)} %collective-permute-done.12.refs_4_), channel_id=1, source_target_pairs={{2,0},{4,2},{6,4},{7,6},{5,7},{3,5},{1,3},{0,1},{10,8},{12,10},{14... | collective-permute-start | bytes 626696 | tf_op jit(solution)/shard_map/ppermute | solution.py:183
  23.0 0.7 %collective-permute-done.11.refs_3_ = bf16[16,6528]{1,0:T(8,128)(2,1)S(1)} collective-permute-done((bf16[16,6528]{1,0:T(8,128)(2,1)S(1)}, bf16[16,6528]{1,0:T(8,128)(2,1)S(1)}, u32[]{:S(2)}, u32[]{:S(2)}) %collective-permute-start.11) | collective-permute-done | bytes 208928 | tf_op jit(solution)/shard_map/ppermute | solution.py:182
  23.7 0.0 collective-permute-start.13
  23.7 1.9 %collective-permute-done.4.refs_4_ = bf16[16,6528]{1,0:T(8,128)(2,1)S(1)} collective-permute-done((bf16[16,6528]{1,0:T(8,128)(2,1)S(1)}, bf16[16,6528]{1,0:T(8,128)(2,1)S(1)}, u32[]{:S(2)}, u32[]{:S(2)}) %collective-permute-start.4) | collective-permute-done | bytes 208928 | tf_op jit(solution)/shard_map/ppermute | solution.py:183
  25.6 1.4 %collective-permute-start.6 = (bf16[16,6528]{1,0:T(8,128)(2,1)S(1)}, bf16[16,6528]{1,0:T(8,128)(2,1)S(1)}, u32[]{:S(2)}, u32[]{:S(2)}) collective-permute-start(bf16[16,6528]{1,0:T(8,128)(2,1)S(1)} %collective-permute-done.4.refs_4_), channel_id=1, source_target_pairs={{2,0},{4,2},{6,4},{7,6},{5,7},{3,5},{1,3},{0,1},{10,8},{12,10},{14... | collective-permute-start | bytes 626696 | tf_op jit(solution)/shard_map/ppermute | solution.py:183
  27.0 1.2 %collective-permute-done.3.refs_3_ = bf16[16,6528]{1,0:T(8,128)(2,1)S(1)} collective-permute-done((bf16[16,6528]{1,0:T(8,128)(2,1)S(1)}, bf16[16,6528]{1,0:T(8,128)(2,1)S(1)}, u32[]{:S(2)}, u32[]{:S(2)}) %collective-permute-start.3) | collective-permute-done | bytes 208928 | tf_op jit(solution)/shard_map/ppermute | solution.py:182
  28.2 0.0 collective-permute-start.5
  28.2 0.5 %collective-permute-start = (bf16[16,6528]{1,0:T(8,128)(2,1)}, bf16[16,6528]{1,0:T(8,128)(2,1)S(1)}, u32[]{:S(2)}, u32[]{:S(2)}) collective-permute-start(bf16[16,6528]{1,0:T(8,128)(2,1)} %get-tuple-element.7), channel_id=1, source_target_pairs={{0,24},{1,25},{2,26},{3,27},{4,28},{5,29},{6,30},{7,31},{8,16},{9,... | collective-permute-start | bytes 626696 | tf_op jit(solution)/shard_map/ppermute | solution.py:188
  28.7 1.4 %collective-permute-done.14.refs_6_ = bf16[16,6528]{1,0:T(8,128)(2,1)S(1)} collective-permute-done((bf16[16,6528]{1,0:T(8,128)(2,1)S(1)}, bf16[16,6528]{1,0:T(8,128)(2,1)S(1)}, u32[]{:S(2)}, u32[]{:S(2)}) %collective-permute-start.14) | collective-permute-done | bytes 208928 | tf_op jit(solution)/shard_map/ppermute | solution.py:183
  30.1 1.5 %collective-permute-start.16 = (bf16[16,3456]{1,0:T(8,128)(2,1)S(1)}, bf16[16,3456]{1,0:T(8,128)(2,1)S(1)}, u32[]{:S(2)}, u32[]{:S(2)}) collective-permute-start(bf16[16,3456]{1,0:T(8,128)(2,1)S(1)} %slice.19), channel_id=1, source_target_pairs={{2,0},{4,2},{6,4},{7,6},{5,7},{3,5},{1,3},{0,1},{10,8},{12,10},{14... | collective-permute-start | bytes 331784 | tf_op jit(solution)/shard_map/ppermute | solution.py:183
  31.5 1.1 %collective-permute-done.13.refs_5_ = bf16[16,6528]{1,0:T(8,128)(2,1)S(1)} collective-permute-done((bf16[16,6528]{1,0:T(8,128)(2,1)S(1)}, bf16[16,6528]{1,0:T(8,128)(2,1)S(1)}, u32[]{:S(2)}, u32[]{:S(2)}) %collective-permute-start.13) | collective-permute-done | bytes 208928 | tf_op jit(solution)/shard_map/ppermute | solution.py:182
  32.7 0.1 collective-permute-start.15
  32.7 1.8 %collective-permute-done.6.refs_6_ = bf16[16,6528]{1,0:T(8,128)(2,1)S(1)} collective-permute-done((bf16[16,6528]{1,0:T(8,128)(2,1)S(1)}, bf16[16,6528]{1,0:T(8,128)(2,1)S(1)}, u32[]{:S(2)}, u32[]{:S(2)}) %collective-permute-start.6) | collective-permute-done | bytes 208928 | tf_op jit(solution)/shard_map/ppermute | solution.py:183
  34.6 1.5 %collective-permute-start.8 = (bf16[16,3456]{1,0:T(8,128)(2,1)S(1)}, bf16[16,3456]{1,0:T(8,128)(2,1)S(1)}, u32[]{:S(2)}, u32[]{:S(2)}) collective-permute-start(bf16[16,3456]{1,0:T(8,128)(2,1)S(1)} %slice.17), channel_id=1, source_target_pairs={{2,0},{4,2},{6,4},{7,6},{5,7},{3,5},{1,3},{0,1},{10,8},{12,10},{14... | collective-permute-start | bytes 331784 | tf_op jit(solution)/shard_map/ppermute | solution.py:183
  36.0 1.1 %collective-permute-done.5.refs_5_ = bf16[16,6528]{1,0:T(8,128)(2,1)S(1)} collective-permute-done((bf16[16,6528]{1,0:T(8,128)(2,1)S(1)}, bf16[16,6528]{1,0:T(8,128)(2,1)S(1)}, u32[]{:S(2)}, u32[]{:S(2)}) %collective-permute-start.5) | collective-permute-done | bytes 208928 | tf_op jit(solution)/shard_map/ppermute | solution.py:182
  37.1 0.1 collective-permute-start.7
  37.2 1.8 %collective-permute-done.15.refs_7_ = bf16[16,3072]{1,0:T(8,128)(2,1)S(1)} collective-permute-done((bf16[16,3072]{1,0:T(8,128)(2,1)S(1)}, bf16[16,3072]{1,0:T(8,128)(2,1)S(1)}, u32[]{:S(2)}, u32[]{:S(2)}) %collective-permute-start.15) | collective-permute-done | bytes 98336 | tf_op jit(solution)/shard_map/ppermute | solution.py:182
  39.0 0.0 collective-permute-done.16.refs_8_
  39.0 0.0 copy-done
  39.0 0.0 copy-start.1
  39.0 0.9 %copy-done.1 = bf16[16,6528]{1,0:T(8,128)(2,1)S(1)} copy-done((bf16[16,6528]{1,0:T(8,128)(2,1)S(1)}, bf16[16,6528]{1,0:T(8,128)(2,1)}, u32[]{:S(2)}) %copy-start.1) | copy-done | bytes 208920
  39.9 1.7 %grad_part.1.refs_10_ = f32[256,3072]{1,0:T(8,128)S(1)} custom-call(bf16[16,6528]{1,0:T(8,128)(2,1)S(1)} %copy-done.1, bf16[16,6528]{1,0:T(8,128)(2,1)S(1)} %collective-permute-done.9.refs_1_, bf16[16,6528]{1,0:T(8,128)(2,1)S(1)} %collective-permute-done.10.refs_2_, bf16[16,6528]{1,0:T(8,128)(2,1)S(1)} %collective-permute-done.11.refs_3_, ...), custom_call_target="tpu_custom_call" | custom-call | flops 427819008 | bytes 3145728 | tf_op jit(solution)/shard_map/grad_part/pallas_call | solution.py:153
  41.6 0.0 collective-permute-done.refs_0_
  41.6 0.2 collective-permute-done.7.refs_7_
  41.8 0.0 collective-permute-done.8.refs_8_
  41.8 2.5 %grad_sum.1 = bf16[256,3072]{1,0:T(8,128)(2,1)} custom-call(bf16[16,6528]{1,0:T(8,128)(2,1)S(1)} %collective-permute-done.refs_0_, bf16[16,6528]{1,0:T(8,128)(2,1)S(1)} %collective-permute-done.1.refs_1_, bf16[16,6528]{1,0:T(8,128)(2,1)S(1)} %collective-permute-done.2.refs_2_, bf16[16,6528]{1,0:T(8,128)(2,1)S(1)} %collective-permute-done.3.refs_3_, ...), custom_call_target="tpu_custom_call" | custom-call | flops 427819008 | bytes 3145728 | tf_op jit(solution)/shard_map/grad_sum/pallas_call | solution.py:153
  (4 shorter events, 0.0 us)
Async XLA Ops:
  0.0 39.0 %copy-start = (bf16[1,3072,256]{2,1,0:T(8,128)(2,1)S(1)}, bf16[1,3072,256]{2,1,0:T(8,128)(2,1)}, u32[]{:S(2)}) copy-start(bf16[1,3072,256]{2,1,0:T(8,128)(2,1)} %param.17) | copy-start | bytes 4718596
  2.6 9.2 %collective-permute-start.10 = (bf16[16,6528]{1,0:T(8,128)(2,1)}, bf16[16,6528]{1,0:T(8,128)(2,1)S(1)}, u32[]{:S(2)}, u32[]{:S(2)}) collective-permute-start(bf16[16,6528]{1,0:T(8,128)(2,1)} %get-tuple-element.8.refs_0_), channel_id=1, source_target_pairs={{2,0},{4,2},{6,4},{7,6},{5,7},{3,5},{1,3},{0,1},{10,8},{12,10},{14... | collective-permute-start | bytes 626696 | tf_op jit(solution)/shard_map/ppermute | solution.py:183
  5.6 8.0 %collective-permute-start.9 = (bf16[16,6528]{1,0:T(8,128)(2,1)}, bf16[16,6528]{1,0:T(8,128)(2,1)S(1)}, u32[]{:S(2)}, u32[]{:S(2)}) collective-permute-start(bf16[16,6528]{1,0:T(8,128)(2,1)} %get-tuple-element.8.refs_0_), channel_id=1, source_target_pairs={{0,2},{2,4},{4,6},{6,7},{7,5},{5,3},{3,1},{1,0},{8,10},{10,12},{12... | collective-permute-start | bytes 626696 | tf_op jit(solution)/shard_map/ppermute | solution.py:182
  5.7 11.4 %collective-permute-start.2 = (bf16[16,6528]{1,0:T(8,128)(2,1)}, bf16[16,6528]{1,0:T(8,128)(2,1)S(1)}, u32[]{:S(2)}, u32[]{:S(2)}) collective-permute-start(bf16[16,6528]{1,0:T(8,128)(2,1)} %get-tuple-element.7), channel_id=1, source_target_pairs={{2,24},{4,26},{6,28},{7,30},{5,31},{3,29},{1,27},{0,25},{10,16},{1... | collective-permute-start | bytes 626696 | tf_op jit(solution)/shard_map/ppermute | solution.py:188
  7.4 11.1 %collective-permute-start.1 = (bf16[16,6528]{1,0:T(8,128)(2,1)}, bf16[16,6528]{1,0:T(8,128)(2,1)S(1)}, u32[]{:S(2)}, u32[]{:S(2)}) collective-permute-start(bf16[16,6528]{1,0:T(8,128)(2,1)} %get-tuple-element.7), channel_id=1, source_target_pairs={{0,26},{2,28},{4,30},{6,31},{7,29},{5,27},{3,25},{1,24},{8,18},{10... | collective-permute-start | bytes 626696 | tf_op jit(solution)/shard_map/ppermute | solution.py:188
  11.7 9.9 %collective-permute-start.12 = (bf16[16,6528]{1,0:T(8,128)(2,1)S(1)}, bf16[16,6528]{1,0:T(8,128)(2,1)S(1)}, u32[]{:S(2)}, u32[]{:S(2)}) collective-permute-start(bf16[16,6528]{1,0:T(8,128)(2,1)S(1)} %collective-permute-done.10.refs_2_), channel_id=1, source_target_pairs={{2,0},{4,2},{6,4},{7,6},{5,7},{3,5},{1,3},{0,1},{10,8},{12,10},{14... | collective-permute-start | bytes 626696 | tf_op jit(solution)/shard_map/ppermute | solution.py:183
  13.6 10.1 %collective-permute-start.11 = (bf16[16,6528]{1,0:T(8,128)(2,1)S(1)}, bf16[16,6528]{1,0:T(8,128)(2,1)S(1)}, u32[]{:S(2)}, u32[]{:S(2)}) collective-permute-start(bf16[16,6528]{1,0:T(8,128)(2,1)S(1)} %collective-permute-done.9.refs_1_), channel_id=1, source_target_pairs={{0,2},{2,4},{4,6},{6,7},{7,5},{5,3},{3,1},{1,0},{8,10},{10,12},{12... | collective-permute-start | bytes 626696 | tf_op jit(solution)/shard_map/ppermute | solution.py:182
  17.1 8.5 %collective-permute-start.4 = (bf16[16,6528]{1,0:T(8,128)(2,1)S(1)}, bf16[16,6528]{1,0:T(8,128)(2,1)S(1)}, u32[]{:S(2)}, u32[]{:S(2)}) collective-permute-start(bf16[16,6528]{1,0:T(8,128)(2,1)S(1)} %collective-permute-done.2.refs_2_), channel_id=1, source_target_pairs={{2,0},{4,2},{6,4},{7,6},{5,7},{3,5},{1,3},{0,1},{10,8},{12,10},{14... | collective-permute-start | bytes 626696 | tf_op jit(solution)/shard_map/ppermute | solution.py:183
  18.6 9.6 %collective-permute-start.3 = (bf16[16,6528]{1,0:T(8,128)(2,1)S(1)}, bf16[16,6528]{1,0:T(8,128)(2,1)S(1)}, u32[]{:S(2)}, u32[]{:S(2)}) collective-permute-start(bf16[16,6528]{1,0:T(8,128)(2,1)S(1)} %collective-permute-done.1.refs_1_), channel_id=1, source_target_pairs={{0,2},{2,4},{4,6},{6,7},{7,5},{5,3},{3,1},{1,0},{8,10},{10,12},{12... | collective-permute-start | bytes 626696 | tf_op jit(solution)/shard_map/ppermute | solution.py:182
  21.6 8.5 %collective-permute-start.14 = (bf16[16,6528]{1,0:T(8,128)(2,1)S(1)}, bf16[16,6528]{1,0:T(8,128)(2,1)S(1)}, u32[]{:S(2)}, u32[]{:S(2)}) collective-permute-start(bf16[16,6528]{1,0:T(8,128)(2,1)S(1)} %collective-permute-done.12.refs_4_), channel_id=1, source_target_pairs={{2,0},{4,2},{6,4},{7,6},{5,7},{3,5},{1,3},{0,1},{10,8},{12,10},{14... | collective-permute-start | bytes 626696 | tf_op jit(solution)/shard_map/ppermute | solution.py:183
  23.7 9.0 %collective-permute-start.13 = (bf16[16,6528]{1,0:T(8,128)(2,1)S(1)}, bf16[16,6528]{1,0:T(8,128)(2,1)S(1)}, u32[]{:S(2)}, u32[]{:S(2)}) collective-permute-start(bf16[16,6528]{1,0:T(8,128)(2,1)S(1)} %collective-permute-done.11.refs_3_), channel_id=1, source_target_pairs={{0,2},{2,4},{4,6},{6,7},{7,5},{5,3},{3,1},{1,0},{8,10},{10,12},{12... | collective-permute-start | bytes 626696 | tf_op jit(solution)/shard_map/ppermute | solution.py:182
  25.6 9.0 %collective-permute-start.6 = (bf16[16,6528]{1,0:T(8,128)(2,1)S(1)}, bf16[16,6528]{1,0:T(8,128)(2,1)S(1)}, u32[]{:S(2)}, u32[]{:S(2)}) collective-permute-start(bf16[16,6528]{1,0:T(8,128)(2,1)S(1)} %collective-permute-done.4.refs_4_), channel_id=1, source_target_pairs={{2,0},{4,2},{6,4},{7,6},{5,7},{3,5},{1,3},{0,1},{10,8},{12,10},{14... | collective-permute-start | bytes 626696 | tf_op jit(solution)/shard_map/ppermute | solution.py:183
  28.2 9.0 %collective-permute-start.5 = (bf16[16,6528]{1,0:T(8,128)(2,1)S(1)}, bf16[16,6528]{1,0:T(8,128)(2,1)S(1)}, u32[]{:S(2)}, u32[]{:S(2)}) collective-permute-start(bf16[16,6528]{1,0:T(8,128)(2,1)S(1)} %collective-permute-done.3.refs_3_), channel_id=1, source_target_pairs={{0,2},{2,4},{4,6},{6,7},{7,5},{5,3},{3,1},{1,0},{8,10},{10,12},{12... | collective-permute-start | bytes 626696 | tf_op jit(solution)/shard_map/ppermute | solution.py:182
  28.2 13.4 %collective-permute-start = (bf16[16,6528]{1,0:T(8,128)(2,1)}, bf16[16,6528]{1,0:T(8,128)(2,1)S(1)}, u32[]{:S(2)}, u32[]{:S(2)}) collective-permute-start(bf16[16,6528]{1,0:T(8,128)(2,1)} %get-tuple-element.7), channel_id=1, source_target_pairs={{0,24},{1,25},{2,26},{3,27},{4,28},{5,29},{6,30},{7,31},{8,16},{9,... | collective-permute-start | bytes 626696 | tf_op jit(solution)/shard_map/ppermute | solution.py:188
  30.1 8.9 %collective-permute-start.16 = (bf16[16,3456]{1,0:T(8,128)(2,1)S(1)}, bf16[16,3456]{1,0:T(8,128)(2,1)S(1)}, u32[]{:S(2)}, u32[]{:S(2)}) collective-permute-start(bf16[16,3456]{1,0:T(8,128)(2,1)S(1)} %slice.19), channel_id=1, source_target_pairs={{2,0},{4,2},{6,4},{7,6},{5,7},{3,5},{1,3},{0,1},{10,8},{12,10},{14... | collective-permute-start | bytes 331784 | tf_op jit(solution)/shard_map/ppermute | solution.py:183
  32.7 6.3 %collective-permute-start.15 = (bf16[16,3072]{1,0:T(8,128)(2,1)S(1)}, bf16[16,3072]{1,0:T(8,128)(2,1)S(1)}, u32[]{:S(2)}, u32[]{:S(2)}) collective-permute-start(bf16[16,3072]{1,0:T(8,128)(2,1)S(1)} %slice.18), channel_id=1, source_target_pairs={{0,2},{2,4},{4,6},{6,7},{7,5},{5,3},{3,1},{1,0},{8,10},{10,12},{12... | collective-permute-start | bytes 294920 | tf_op jit(solution)/shard_map/ppermute | solution.py:182
  34.6 7.3 %collective-permute-start.8 = (bf16[16,3456]{1,0:T(8,128)(2,1)S(1)}, bf16[16,3456]{1,0:T(8,128)(2,1)S(1)}, u32[]{:S(2)}, u32[]{:S(2)}) collective-permute-start(bf16[16,3456]{1,0:T(8,128)(2,1)S(1)} %slice.17), channel_id=1, source_target_pairs={{2,0},{4,2},{6,4},{7,6},{5,7},{3,5},{1,3},{0,1},{10,8},{12,10},{14... | collective-permute-start | bytes 331784 | tf_op jit(solution)/shard_map/ppermute | solution.py:183
  37.1 4.7 %collective-permute-start.7 = (bf16[16,3072]{1,0:T(8,128)(2,1)S(1)}, bf16[16,3072]{1,0:T(8,128)(2,1)S(1)}, u32[]{:S(2)}, u32[]{:S(2)}) collective-permute-start(bf16[16,3072]{1,0:T(8,128)(2,1)S(1)} %slice.16), channel_id=1, source_target_pairs={{0,2},{2,4},{4,6},{6,7},{7,5},{5,3},{3,1},{1,0},{8,10},{10,12},{12... | collective-permute-start | bytes 294920 | tf_op jit(solution)/shard_map/ppermute | solution.py:182
  39.0 0.9 %copy-start.1 = (bf16[16,6528]{1,0:T(8,128)(2,1)S(1)}, bf16[16,6528]{1,0:T(8,128)(2,1)}, u32[]{:S(2)}) copy-start(bf16[16,6528]{1,0:T(8,128)(2,1)} %get-tuple-element.8.refs_0_) | copy-start | bytes 626692

commit v3 on v2

--- a/solution.py
+++ b/solution.py
@@ -70,7 +70,8 @@
 def pack(arrays):
     rows, width = arrays[0].shape
     seg = width // SEGS
-    payload = jax.ShapeDtypeStruct((MAIN, 2 * width + seg), jnp.bfloat16)
+    payload = pltpu.VMEM((MAIN, 2 * width + seg), jnp.bfloat16)
+    arrays = [pltpu.with_memory_space_constraint(a, pltpu.HBM) for a in arrays]
     return pl.pallas_call(
         pack_kernel,
         out_shape=(payload, payload),
@@ -78,7 +79,7 @@
         out_specs=(pl.BlockSpec(memory_space=pltpu.VMEM),) * 2,
         scratch_shapes=[pltpu.VMEM(a.shape, a.dtype) for a in arrays]
         + [pltpu.SemaphoreType.DMA((8,))],
-        compiler_params=pltpu.CompilerParams(vmem_limit_bytes=60 * 2**20),
+        compiler_params=pltpu.CompilerParams(vmem_limit_bytes=16 * 2**20),
         cost_estimate=pl.CostEstimate(
             flops=8 * 2 * MAIN * rows * width, bytes_accessed=12 * rows * width, transcendentals=0
         ),
@@ -86,25 +87,9 @@
     )(*arrays)
 
 
-class Block:
-    def __init__(self, width, first, second=None):
-        self.width, self.first, self.second = width, first, second
-
-    def __getitem__(self, where):
-        rows, lanes = where
-        if self.second is None:
-            return self.first[rows, lanes]
-        if lanes.stop is not None and lanes.stop <= self.width:
-            return self.first[rows, lanes]
-        stop = lanes.stop if lanes.stop is None else lanes.stop - self.width
-        return self.second[rows, lanes.start - self.width : stop]
-
-
 def grad_kernel(count, last, *refs):
-    blocks, refs = refs[: count + 1], refs[count + 1 :]
-    w_ref, refs = refs[0], refs[1:]
+    payloads, w_ref, refs = refs[:count], refs[count], refs[count + 1 :]
     width = w_ref.shape[0]
-    payloads = [Block(width, b) for b in blocks[: count - 1]] + [Block(width, *blocks[count - 1 :])]
     seg = width // SEGS
     size = count * 2 * SEGS
     tails = jnp.concatenate([p[:, 2 * width :] for p in payloads], axis=0)
@@ -145,9 +130,9 @@
         copy.wait()
 
 
-def grad(payloads, weight_in, before=None, flops=0):
+def grad(payloads, weight_in, before=None):
     width, hidden = weight_in.shape
-    count = len(payloads) - 1
+    count = len(payloads)
     last = before is not None
     operands = (*payloads, weight_in) + ((before,) if last else ())
     return pl.pallas_call(
@@ -163,7 +148,7 @@
         else [],
         compiler_params=pltpu.CompilerParams(vmem_limit_bytes=40 * 2**20),
         cost_estimate=pl.CostEstimate(
-            flops=flops or 4 * CAP * count * width * hidden,
+            flops=4 * CAP * count * width * hidden,
             bytes_accessed=4 * width * hidden,
             transcendentals=CAP * count * hidden,
         ),
@@ -171,34 +156,37 @@
     )(*operands)
 
 
-def gather_both(down, up, n_pipe, cycle, width):
+def gather_both(down, up, n_pipe, cycle):
     n = len(cycle)
     right = [(cycle[i], cycle[(i + 1) % n]) for i in range(n)]
     left = [(b, a) for a, b in right]
-    full = (n - 1) // 2
-
-    def step(pair):
-        return (
-            lax.ppermute(pair[0], "expert", right),
-            lax.ppermute(pair[1], "expert", left),
-        )
 
     def mirrored(block, moves):
         pairs = [(p * n + a, (n_pipe - 1 - p) * n + b) for p in range(n_pipe) for a, b in moves]
         return lax.ppermute(block, ("pipe", "expert"), pairs)
 
-    down_pair = step((down, down))
-    up_pair = (mirrored(up, right), mirrored(up, left))
-    got_down = [down, *down_pair]
-    got_up = [mirrored(up, [(e, e) for e in range(n)]), *up_pair]
-    for _ in range(1, full):
-        down_pair = step(down_pair)
-        got_down += down_pair
-        up_pair = step(up_pair)
-        got_up += up_pair
-    down_pair = step((down_pair[0][:, :width], down_pair[1][:, width:]))
-    up_pair = step((up_pair[0][:, :width], up_pair[1][:, width:]))
-    return got_down + list(down_pair), got_up + list(up_pair)
+    def turn(at):
+        up_left, down_right, up_right, down_left = at
+        return (
+            lax.ppermute(up_left, "expert", left),
+            lax.ppermute(down_right, "expert", right),
+            lax.ppermute(up_right, "expert", right),
+            lax.ppermute(down_left, "expert", left),
+        )
+
+    at = (
+        mirrored(up, left),
+        lax.ppermute(down, "expert", right),
+        mirrored(up, right),
+        lax.ppermute(down, "expert", left),
+    )
+    got = [*at]
+    for _ in range(1, (n - 1) // 2):
+        at = turn(at)
+        got += at
+    last = (lax.ppermute(at[0], "expert", left), lax.ppermute(at[1], "expert", right))
+    own = mirrored(up, [(e, e) for e in range(n)])
+    return [*reversed(got), own, down], last
 
 
 def body(
@@ -219,9 +207,9 @@
             *(tokens_up[0], cotan_up[0], gates_up[0].T, experts_up[0].T),
         )
     )
-    got_down, got_up = gather_both(down, up, n_pipe, grid_cycle(n_expert), w_in.shape[1])
-    part = grad(got_down, w_in[0])
-    return grad(got_up, w_in[0], part)[None]
+    got, last = gather_both(down, up, n_pipe, grid_cycle(n_expert))
+    part = grad(got, w_in[0])
+    return grad(last, w_in[0], part)[None]
 
 
 def solution(mesh):

time: 44.4 us -> 42.2 us (0.950)
  local copies, waits for them, and re-layouts: 0.97 us -> 0.01 us
  waiting for transfers between devices: 20.3 us -> 19.4 us
  Pallas kernels: 6.68 us -> 6.18 us
    ppermute x14 -> x12, waiting for transfers between devices: 17 us -> 15.9 us  [the longest x2 4.89 us: turn(): lax.ppermute(up_left, 'expert', left)]
    unnamed x4 -> x2, local copies, waits for them, and re-layouts: 0.93 us -> 0.01 us
    pallas_call x1, Pallas kernels: 2.57 us -> 1.89 us  [pack(): pl.pallas_call(pack_kernel, out_shape=(payload, payload), in_specs=[pl.Bl...]
    ppermute x14 -> x12, starting transfers between devices: 13.2 us -> 13.1 us  [the longest x2 3.89 us: turn(): lax.ppermute(up_left, 'expert', left)]
  transfers between devices with their start and end apart: 17 -> 15, of which waited for: 12 -> 10; matrix products, arithmetic and copies ran while one was open for 0% -> 0% of each run, Pallas kernels for 4% -> 5%
where the time goes in v3:
time: 42.2 us; the launch traced here: 42.1 us
  waiting for transfers between devices  19.4 us (46%)
  starting transfers between devices  16.5 us (39%)
  Pallas kernels  6.18 us (15%)
    ppermute x2, waiting for transfers between devices, turn(): lax.ppermute(up_left, 'expert', left)  4.89 us
    ppermute x2, waiting for transfers between devices, turn(): lax.ppermute(down_left, 'expert', left)  4.88 us
    pallas_call x2, Pallas kernels, grad(): pl.pallas_call(functools.partial(grad_kernel, count, last), out_shape=jax...  4.3 us
    ppermute x2, starting transfers between devices, turn(): lax.ppermute(up_left, 'expert', left)  3.89 us
    ppermute x3, waiting for transfers between devices, mirrored(): return lax.ppermute(block, ('pipe', 'expert'), pairs)  3.5 us
    ppermute x3, starting transfers between devices, mirrored(): return lax.ppermute(block, ('pipe', 'expert'), pairs)  3.39 us
    ppermute x2, starting transfers between devices, turn(): lax.ppermute(down_left, 'expert', left)  2.98 us
    ppermute x1, waiting for transfers between devices, gather_both(): lax.ppermute(down, 'expert', left)  2.45 us
  transfers between devices with their start and end apart: 15, of which 10 were waited for; matrix products, arithmetic and copies ran while one was open for 0% of the time, Pallas kernels for 5%

profile of v3, /device:TPU:0, one launch (start us, length us, event | category | flops | bytes accessed | tf_op | source)
XLA Modules:
  0.0 42.1 jit_solution(15373325120813666671)
XLA Ops:
  0.0 0.0 copy-start
  0.0 1.9 %pack_slots.1 = (bf16[16,6528]{1,0:T(8,128)(2,1)S(1)}, bf16[16,6528]{1,0:T(8,128)(2,1)S(1)}) custom-call(bf16[64,3072]{1,0:T(8,128)(2,1)} %bitcast.20, bf16[64,3072]{1,0:T(8,128)(2,1)} %bitcast.21, bf16[2,64]{1,0:T(2,128)(2,1)} %bitcast.26, s32[2,64]{1,0:T(2,128)} %bitcast.24, bf16[64,3072]{1,0:T(8,128)(2,1)} %bitcast.22, bf16[64,3072]{1,0:T(8,128)(2,1)} %bitcast.23, ...), custom_call_target="tpu_custom_call" | custom-call | flops 50331648 | bytes 2359296 | tf_op jit(solution)/shard_map/pack_slots/pallas_call | solution.py:75
  1.9 3.4 %collective-permute-start = (bf16[16,6528]{1,0:T(8,128)(2,1)S(1)}, bf16[16,6528]{1,0:T(8,128)(2,1)S(1)}, u32[]{:S(2)}, u32[]{:S(2)}) collective-permute-start(bf16[16,6528]{1,0:T(8,128)(2,1)S(1)} %get-tuple-element.7), channel_id=1, source_target_pairs={{2,24},{4,26},{6,28},{7,30},{5,31},{3,29},{1,27},{0,25},{10,16},{1... | collective-permute-start | bytes 626696 | tf_op jit(solution)/shard_map/ppermute | solution.py:166
  5.3 0.5 %collective-permute-start.4 = (bf16[16,6528]{1,0:T(8,128)(2,1)S(1)}, bf16[16,6528]{1,0:T(8,128)(2,1)S(1)}, u32[]{:S(2)}, u32[]{:S(2)}) collective-permute-start(bf16[16,6528]{1,0:T(8,128)(2,1)S(1)} %get-tuple-element.8.refs_13_), channel_id=1, source_target_pairs={{0,2},{2,4},{4,6},{6,7},{7,5},{5,3},{3,1},{1,0},{8,10},{10,12},{12... | collective-permute-start | bytes 626696 | tf_op jit(solution)/shard_map/ppermute | solution.py:179
  5.8 1.5 %collective-permute-start.8 = (bf16[16,6528]{1,0:T(8,128)(2,1)S(1)}, bf16[16,6528]{1,0:T(8,128)(2,1)S(1)}, u32[]{:S(2)}, u32[]{:S(2)}) collective-permute-start(bf16[16,6528]{1,0:T(8,128)(2,1)S(1)} %get-tuple-element.8.refs_13_), channel_id=1, source_target_pairs={{2,0},{4,2},{6,4},{7,6},{5,7},{3,5},{1,3},{0,1},{10,8},{12,10},{14... | collective-permute-start | bytes 626696 | tf_op jit(solution)/shard_map/ppermute | solution.py:181
  7.3 0.0 collective-permute-start.11
  7.3 3.5 %collective-permute-done.refs_11_ = bf16[16,6528]{1,0:T(8,128)(2,1)S(1)} collective-permute-done((bf16[16,6528]{1,0:T(8,128)(2,1)S(1)}, bf16[16,6528]{1,0:T(8,128)(2,1)S(1)}, u32[]{:S(2)}, u32[]{:S(2)}) %collective-permute-start) | collective-permute-done | bytes 208928 | tf_op jit(solution)/shard_map/ppermute | solution.py:166
  10.8 2.4 %collective-permute-start.1 = (bf16[16,6528]{1,0:T(8,128)(2,1)S(1)}, bf16[16,6528]{1,0:T(8,128)(2,1)S(1)}, u32[]{:S(2)}, u32[]{:S(2)}) collective-permute-start(bf16[16,6528]{1,0:T(8,128)(2,1)S(1)} %collective-permute-done.refs_11_), channel_id=1, source_target_pairs={{2,0},{4,2},{6,4},{7,6},{5,7},{3,5},{1,3},{0,1},{10,8},{12,10},{14... | collective-permute-start | bytes 626696 | tf_op jit(solution)/shard_map/ppermute | solution.py:171
  13.2 0.1 collective-permute-done.4.refs_10_
  13.3 0.5 %collective-permute-start.5 = (bf16[16,6528]{1,0:T(8,128)(2,1)S(1)}, bf16[16,6528]{1,0:T(8,128)(2,1)S(1)}, u32[]{:S(2)}, u32[]{:S(2)}) collective-permute-start(bf16[16,6528]{1,0:T(8,128)(2,1)S(1)} %collective-permute-done.4.refs_10_), channel_id=1, source_target_pairs={{0,2},{2,4},{4,6},{6,7},{7,5},{5,3},{3,1},{1,0},{8,10},{10,12},{12... | collective-permute-start | bytes 626696 | tf_op jit(solution)/shard_map/ppermute | solution.py:172
  13.9 2.4 %collective-permute-done.8.refs_8_ = bf16[16,6528]{1,0:T(8,128)(2,1)S(1)} collective-permute-done((bf16[16,6528]{1,0:T(8,128)(2,1)S(1)}, bf16[16,6528]{1,0:T(8,128)(2,1)S(1)}, u32[]{:S(2)}, u32[]{:S(2)}) %collective-permute-start.8) | collective-permute-done | bytes 208928 | tf_op jit(solution)/shard_map/ppermute | solution.py:181
  16.3 1.5 %collective-permute-start.9 = (bf16[16,6528]{1,0:T(8,128)(2,1)S(1)}, bf16[16,6528]{1,0:T(8,128)(2,1)S(1)}, u32[]{:S(2)}, u32[]{:S(2)}) collective-permute-start(bf16[16,6528]{1,0:T(8,128)(2,1)S(1)} %collective-permute-done.8.refs_8_), channel_id=1, source_target_pairs={{2,0},{4,2},{6,4},{7,6},{5,7},{3,5},{1,3},{0,1},{10,8},{12,10},{14... | collective-permute-start | bytes 626696 | tf_op jit(solution)/shard_map/ppermute | solution.py:174
  17.8 0.0 collective-permute-done.11.refs_9_
  17.8 0.5 %collective-permute-start.12 = (bf16[16,6528]{1,0:T(8,128)(2,1)S(1)}, bf16[16,6528]{1,0:T(8,128)(2,1)S(1)}, u32[]{:S(2)}, u32[]{:S(2)}) collective-permute-start(bf16[16,6528]{1,0:T(8,128)(2,1)S(1)} %collective-permute-done.11.refs_9_), channel_id=1, source_target_pairs={{0,2},{2,4},{4,6},{6,7},{7,5},{5,3},{3,1},{1,0},{8,10},{10,12},{12... | collective-permute-start | bytes 626696 | tf_op jit(solution)/shard_map/ppermute | solution.py:173
  18.3 2.4 %collective-permute-done.1.refs_7_ = bf16[16,6528]{1,0:T(8,128)(2,1)S(1)} collective-permute-done((bf16[16,6528]{1,0:T(8,128)(2,1)S(1)}, bf16[16,6528]{1,0:T(8,128)(2,1)S(1)}, u32[]{:S(2)}, u32[]{:S(2)}) %collective-permute-start.1) | collective-permute-done | bytes 208928 | tf_op jit(solution)/shard_map/ppermute | solution.py:171
  20.8 1.5 %collective-permute-start.2 = (bf16[16,6528]{1,0:T(8,128)(2,1)S(1)}, bf16[16,6528]{1,0:T(8,128)(2,1)S(1)}, u32[]{:S(2)}, u32[]{:S(2)}) collective-permute-start(bf16[16,6528]{1,0:T(8,128)(2,1)S(1)} %collective-permute-done.1.refs_7_), channel_id=1, source_target_pairs={{2,0},{4,2},{6,4},{7,6},{5,7},{3,5},{1,3},{0,1},{10,8},{12,10},{14... | collective-permute-start | bytes 626696 | tf_op jit(solution)/shard_map/ppermute | solution.py:171
  22.3 0.0 collective-permute-done.5.refs_6_
  22.3 0.5 %collective-permute-start.6 = (bf16[16,6528]{1,0:T(8,128)(2,1)S(1)}, bf16[16,6528]{1,0:T(8,128)(2,1)S(1)}, u32[]{:S(2)}, u32[]{:S(2)}) collective-permute-start(bf16[16,6528]{1,0:T(8,128)(2,1)S(1)} %collective-permute-done.5.refs_6_), channel_id=1, source_target_pairs={{0,2},{2,4},{4,6},{6,7},{7,5},{5,3},{3,1},{1,0},{8,10},{10,12},{12... | collective-permute-start | bytes 626696 | tf_op jit(solution)/shard_map/ppermute | solution.py:172
  22.8 0.0 collective-permute-start.14
  22.8 2.4 %collective-permute-done.9.refs_4_ = bf16[16,6528]{1,0:T(8,128)(2,1)S(1)} collective-permute-done((bf16[16,6528]{1,0:T(8,128)(2,1)S(1)}, bf16[16,6528]{1,0:T(8,128)(2,1)S(1)}, u32[]{:S(2)}, u32[]{:S(2)}) %collective-permute-start.9) | collective-permute-done | bytes 208928 | tf_op jit(solution)/shard_map/ppermute | solution.py:174
  25.3 1.5 %collective-permute-start.10 = (bf16[16,6528]{1,0:T(8,128)(2,1)S(1)}, bf16[16,6528]{1,0:T(8,128)(2,1)S(1)}, u32[]{:S(2)}, u32[]{:S(2)}) collective-permute-start(bf16[16,6528]{1,0:T(8,128)(2,1)S(1)} %collective-permute-done.9.refs_4_), channel_id=1, source_target_pairs={{2,0},{4,2},{6,4},{7,6},{5,7},{3,5},{1,3},{0,1},{10,8},{12,10},{14... | collective-permute-start | bytes 626696 | tf_op jit(solution)/shard_map/ppermute | solution.py:174
  26.7 0.0 collective-permute-done.12.refs_5_
  26.8 0.5 %collective-permute-start.13 = (bf16[16,6528]{1,0:T(8,128)(2,1)S(1)}, bf16[16,6528]{1,0:T(8,128)(2,1)S(1)}, u32[]{:S(2)}, u32[]{:S(2)}) collective-permute-start(bf16[16,6528]{1,0:T(8,128)(2,1)S(1)} %collective-permute-done.12.refs_5_), channel_id=1, source_target_pairs={{0,2},{2,4},{4,6},{6,7},{7,5},{5,3},{3,1},{1,0},{8,10},{10,12},{12... | collective-permute-start | bytes 626696 | tf_op jit(solution)/shard_map/ppermute | solution.py:173
  27.3 2.4 %collective-permute-done.2.refs_3_ = bf16[16,6528]{1,0:T(8,128)(2,1)S(1)} collective-permute-done((bf16[16,6528]{1,0:T(8,128)(2,1)S(1)}, bf16[16,6528]{1,0:T(8,128)(2,1)S(1)}, u32[]{:S(2)}, u32[]{:S(2)}) %collective-permute-start.2) | collective-permute-done | bytes 208928 | tf_op jit(solution)/shard_map/ppermute | solution.py:171
  29.7 1.5 %collective-permute-start.3 = (bf16[16,6528]{1,0:T(8,128)(2,1)S(1)}, bf16[16,6528]{1,0:T(8,128)(2,1)S(1)}, u32[]{:S(2)}, u32[]{:S(2)}) collective-permute-start(bf16[16,6528]{1,0:T(8,128)(2,1)S(1)} %collective-permute-done.2.refs_3_), channel_id=1, source_target_pairs={{2,0},{4,2},{6,4},{7,6},{5,7},{3,5},{1,3},{0,1},{10,8},{12,10},{14... | collective-permute-start | bytes 626696 | tf_op jit(solution)/shard_map/ppermute | solution.py:187
  31.2 0.0 collective-permute-done.6.refs_2_
  31.2 0.5 %collective-permute-start.7 = (bf16[16,6528]{1,0:T(8,128)(2,1)S(1)}, bf16[16,6528]{1,0:T(8,128)(2,1)S(1)}, u32[]{:S(2)}, u32[]{:S(2)}) collective-permute-start(bf16[16,6528]{1,0:T(8,128)(2,1)S(1)} %collective-permute-done.6.refs_2_), channel_id=1, source_target_pairs={{0,2},{2,4},{4,6},{6,7},{7,5},{5,3},{3,1},{1,0},{8,10},{10,12},{12... | collective-permute-start | bytes 626696 | tf_op jit(solution)/shard_map/ppermute | solution.py:187
  31.8 0.0 collective-permute-done.14.refs_12_
  31.8 2.4 %collective-permute-done.10.refs_0_ = bf16[16,6528]{1,0:T(8,128)(2,1)S(1)} collective-permute-done((bf16[16,6528]{1,0:T(8,128)(2,1)S(1)}, bf16[16,6528]{1,0:T(8,128)(2,1)S(1)}, u32[]{:S(2)}, u32[]{:S(2)}) %collective-permute-start.10) | collective-permute-done | bytes 208928 | tf_op jit(solution)/shard_map/ppermute | solution.py:174
  34.2 1.5 %collective-permute-done.13.refs_1_ = bf16[16,6528]{1,0:T(8,128)(2,1)S(1)} collective-permute-done((bf16[16,6528]{1,0:T(8,128)(2,1)S(1)}, bf16[16,6528]{1,0:T(8,128)(2,1)S(1)}, u32[]{:S(2)}, u32[]{:S(2)}) %collective-permute-start.13) | collective-permute-done | bytes 208928 | tf_op jit(solution)/shard_map/ppermute | solution.py:173
  35.7 0.0 copy-done
  35.7 2.1 %grad_part.1.refs_3_ = f32[256,3072]{1,0:T(8,128)S(1)} custom-call(bf16[16,6528]{1,0:T(8,128)(2,1)S(1)} %collective-permute-done.10.refs_0_, bf16[16,6528]{1,0:T(8,128)(2,1)S(1)} %collective-permute-done.13.refs_1_, bf16[16,6528]{1,0:T(8,128)(2,1)S(1)} %collective-permute-done.6.refs_2_, bf16[16,6528]{1,0:T(8,128)(2,1)S(1)} %collective-permute-done.2.refs_3_, ...), custom_call_target="tpu_custom_call" | custom-call | flops 748683264 | bytes 3145728 | tf_op jit(solution)/shard_map/grad_part/pallas_call | solution.py:138
  37.8 0.9 %collective-permute-done.3.refs_0_ = bf16[16,6528]{1,0:T(8,128)(2,1)S(1)} collective-permute-done((bf16[16,6528]{1,0:T(8,128)(2,1)S(1)}, bf16[16,6528]{1,0:T(8,128)(2,1)S(1)}, u32[]{:S(2)}, u32[]{:S(2)}) %collective-permute-start.3) | collective-permute-done | bytes 208928 | tf_op jit(solution)/shard_map/ppermute | solution.py:187
  38.7 1.2 %collective-permute-done.7.refs_1_ = bf16[16,6528]{1,0:T(8,128)(2,1)S(1)} collective-permute-done((bf16[16,6528]{1,0:T(8,128)(2,1)S(1)}, bf16[16,6528]{1,0:T(8,128)(2,1)S(1)}, u32[]{:S(2)}, u32[]{:S(2)}) %collective-permute-start.7) | collective-permute-done | bytes 208928 | tf_op jit(solution)/shard_map/ppermute | solution.py:187
  39.9 2.2 %grad_sum.1 = bf16[256,3072]{1,0:T(8,128)(2,1)} custom-call(bf16[16,6528]{1,0:T(8,128)(2,1)S(1)} %collective-permute-done.3.refs_0_, bf16[16,6528]{1,0:T(8,128)(2,1)S(1)} %collective-permute-done.7.refs_1_, bf16[3072,256]{1,0:T(8,128)(2,1)S(1)} %bitcast.19, f32[256,3072]{1,0:T(8,128)S(1)} %grad_part.1.refs_3_), custom_call_target="tpu_custom_call" | custom-call | flops 106954752 | bytes 3145728 | tf_op jit(solution)/shard_map/grad_sum/pallas_call | solution.py:138
Async XLA Ops:
  0.0 35.7 %copy-start = (bf16[1,3072,256]{2,1,0:T(8,128)(2,1)S(1)}, bf16[1,3072,256]{2,1,0:T(8,128)(2,1)}, u32[]{:S(2)}) copy-start(bf16[1,3072,256]{2,1,0:T(8,128)(2,1)} %param.17) | copy-start | bytes 4718596
  1.9 8.9 %collective-permute-start = (bf16[16,6528]{1,0:T(8,128)(2,1)S(1)}, bf16[16,6528]{1,0:T(8,128)(2,1)S(1)}, u32[]{:S(2)}, u32[]{:S(2)}) collective-permute-start(bf16[16,6528]{1,0:T(8,128)(2,1)S(1)} %get-tuple-element.7), channel_id=1, source_target_pairs={{2,24},{4,26},{6,28},{7,30},{5,31},{3,29},{1,27},{0,25},{10,16},{1... | collective-permute-start | bytes 626696 | tf_op jit(solution)/shard_map/ppermute | solution.py:166
  5.3 8.0 %collective-permute-start.4 = (bf16[16,6528]{1,0:T(8,128)(2,1)S(1)}, bf16[16,6528]{1,0:T(8,128)(2,1)S(1)}, u32[]{:S(2)}, u32[]{:S(2)}) collective-permute-start(bf16[16,6528]{1,0:T(8,128)(2,1)S(1)} %get-tuple-element.8.refs_13_), channel_id=1, source_target_pairs={{0,2},{2,4},{4,6},{6,7},{7,5},{5,3},{3,1},{1,0},{8,10},{10,12},{12... | collective-permute-start | bytes 626696 | tf_op jit(solution)/shard_map/ppermute | solution.py:179
  5.8 10.5 %collective-permute-start.8 = (bf16[16,6528]{1,0:T(8,128)(2,1)S(1)}, bf16[16,6528]{1,0:T(8,128)(2,1)S(1)}, u32[]{:S(2)}, u32[]{:S(2)}) collective-permute-start(bf16[16,6528]{1,0:T(8,128)(2,1)S(1)} %get-tuple-element.8.refs_13_), channel_id=1, source_target_pairs={{2,0},{4,2},{6,4},{7,6},{5,7},{3,5},{1,3},{0,1},{10,8},{12,10},{14... | collective-permute-start | bytes 626696 | tf_op jit(solution)/shard_map/ppermute | solution.py:181
  7.3 10.5 %collective-permute-start.11 = (bf16[16,6528]{1,0:T(8,128)(2,1)S(1)}, bf16[16,6528]{1,0:T(8,128)(2,1)S(1)}, u32[]{:S(2)}, u32[]{:S(2)}) collective-permute-start(bf16[16,6528]{1,0:T(8,128)(2,1)S(1)} %get-tuple-element.7), channel_id=1, source_target_pairs={{0,26},{2,28},{4,30},{6,31},{7,29},{5,27},{3,25},{1,24},{8,18},{10... | collective-permute-start | bytes 626696 | tf_op jit(solution)/shard_map/ppermute | solution.py:166
  10.8 9.9 %collective-permute-start.1 = (bf16[16,6528]{1,0:T(8,128)(2,1)S(1)}, bf16[16,6528]{1,0:T(8,128)(2,1)S(1)}, u32[]{:S(2)}, u32[]{:S(2)}) collective-permute-start(bf16[16,6528]{1,0:T(8,128)(2,1)S(1)} %collective-permute-done.refs_11_), channel_id=1, source_target_pairs={{2,0},{4,2},{6,4},{7,6},{5,7},{3,5},{1,3},{0,1},{10,8},{12,10},{14... | collective-permute-start | bytes 626696 | tf_op jit(solution)/shard_map/ppermute | solution.py:171
  13.3 9.0 %collective-permute-start.5 = (bf16[16,6528]{1,0:T(8,128)(2,1)S(1)}, bf16[16,6528]{1,0:T(8,128)(2,1)S(1)}, u32[]{:S(2)}, u32[]{:S(2)}) collective-permute-start(bf16[16,6528]{1,0:T(8,128)(2,1)S(1)} %collective-permute-done.4.refs_10_), channel_id=1, source_target_pairs={{0,2},{2,4},{4,6},{6,7},{7,5},{5,3},{3,1},{1,0},{8,10},{10,12},{12... | collective-permute-start | bytes 626696 | tf_op jit(solution)/shard_map/ppermute | solution.py:172
  16.3 9.0 %collective-permute-start.9 = (bf16[16,6528]{1,0:T(8,128)(2,1)S(1)}, bf16[16,6528]{1,0:T(8,128)(2,1)S(1)}, u32[]{:S(2)}, u32[]{:S(2)}) collective-permute-start(bf16[16,6528]{1,0:T(8,128)(2,1)S(1)} %collective-permute-done.8.refs_8_), channel_id=1, source_target_pairs={{2,0},{4,2},{6,4},{7,6},{5,7},{3,5},{1,3},{0,1},{10,8},{12,10},{14... | collective-permute-start | bytes 626696 | tf_op jit(solution)/shard_map/ppermute | solution.py:174
  17.8 9.0 %collective-permute-start.12 = (bf16[16,6528]{1,0:T(8,128)(2,1)S(1)}, bf16[16,6528]{1,0:T(8,128)(2,1)S(1)}, u32[]{:S(2)}, u32[]{:S(2)}) collective-permute-start(bf16[16,6528]{1,0:T(8,128)(2,1)S(1)} %collective-permute-done.11.refs_9_), channel_id=1, source_target_pairs={{0,2},{2,4},{4,6},{6,7},{7,5},{5,3},{3,1},{1,0},{8,10},{10,12},{12... | collective-permute-start | bytes 626696 | tf_op jit(solution)/shard_map/ppermute | solution.py:173
  20.8 9.0 %collective-permute-start.2 = (bf16[16,6528]{1,0:T(8,128)(2,1)S(1)}, bf16[16,6528]{1,0:T(8,128)(2,1)S(1)}, u32[]{:S(2)}, u32[]{:S(2)}) collective-permute-start(bf16[16,6528]{1,0:T(8,128)(2,1)S(1)} %collective-permute-done.1.refs_7_), channel_id=1, source_target_pairs={{2,0},{4,2},{6,4},{7,6},{5,7},{3,5},{1,3},{0,1},{10,8},{12,10},{14... | collective-permute-start | bytes 626696 | tf_op jit(solution)/shard_map/ppermute | solution.py:171
  22.3 9.0 %collective-permute-start.6 = (bf16[16,6528]{1,0:T(8,128)(2,1)S(1)}, bf16[16,6528]{1,0:T(8,128)(2,1)S(1)}, u32[]{:S(2)}, u32[]{:S(2)}) collective-permute-start(bf16[16,6528]{1,0:T(8,128)(2,1)S(1)} %collective-permute-done.5.refs_6_), channel_id=1, source_target_pairs={{0,2},{2,4},{4,6},{6,7},{7,5},{5,3},{3,1},{1,0},{8,10},{10,12},{12... | collective-permute-start | bytes 626696 | tf_op jit(solution)/shard_map/ppermute | solution.py:172
  22.8 9.0 %collective-permute-start.14 = (bf16[16,6528]{1,0:T(8,128)(2,1)S(1)}, bf16[16,6528]{1,0:T(8,128)(2,1)S(1)}, u32[]{:S(2)}, u32[]{:S(2)}) collective-permute-start(bf16[16,6528]{1,0:T(8,128)(2,1)S(1)} %get-tuple-element.7), channel_id=1, source_target_pairs={{0,24},{1,25},{2,26},{3,27},{4,28},{5,29},{6,30},{7,31},{8,16},{9,... | collective-permute-start | bytes 626696 | tf_op jit(solution)/shard_map/ppermute | solution.py:166
  25.3 9.0 %collective-permute-start.10 = (bf16[16,6528]{1,0:T(8,128)(2,1)S(1)}, bf16[16,6528]{1,0:T(8,128)(2,1)S(1)}, u32[]{:S(2)}, u32[]{:S(2)}) collective-permute-start(bf16[16,6528]{1,0:T(8,128)(2,1)S(1)} %collective-permute-done.9.refs_4_), channel_id=1, source_target_pairs={{2,0},{4,2},{6,4},{7,6},{5,7},{3,5},{1,3},{0,1},{10,8},{12,10},{14... | collective-permute-start | bytes 626696 | tf_op jit(solution)/shard_map/ppermute | solution.py:174
  26.8 8.9 %collective-permute-start.13 = (bf16[16,6528]{1,0:T(8,128)(2,1)S(1)}, bf16[16,6528]{1,0:T(8,128)(2,1)S(1)}, u32[]{:S(2)}, u32[]{:S(2)}) collective-permute-start(bf16[16,6528]{1,0:T(8,128)(2,1)S(1)} %collective-permute-done.12.refs_5_), channel_id=1, source_target_pairs={{0,2},{2,4},{4,6},{6,7},{7,5},{5,3},{3,1},{1,0},{8,10},{10,12},{12... | collective-permute-start | bytes 626696 | tf_op jit(solution)/shard_map/ppermute | solution.py:173
  29.7 8.9 %collective-permute-start.3 = (bf16[16,6528]{1,0:T(8,128)(2,1)S(1)}, bf16[16,6528]{1,0:T(8,128)(2,1)S(1)}, u32[]{:S(2)}, u32[]{:S(2)}) collective-permute-start(bf16[16,6528]{1,0:T(8,128)(2,1)S(1)} %collective-permute-done.2.refs_3_), channel_id=1, source_target_pairs={{2,0},{4,2},{6,4},{7,6},{5,7},{3,5},{1,3},{0,1},{10,8},{12,10},{14... | collective-permute-start | bytes 626696 | tf_op jit(solution)/shard_map/ppermute | solution.py:187
  31.2 8.7 %collective-permute-start.7 = (bf16[16,6528]{1,0:T(8,128)(2,1)S(1)}, bf16[16,6528]{1,0:T(8,128)(2,1)S(1)}, u32[]{:S(2)}, u32[]{:S(2)}) collective-permute-start(bf16[16,6528]{1,0:T(8,128)(2,1)S(1)} %collective-permute-done.6.refs_2_), channel_id=1, source_target_pairs={{0,2},{2,4},{4,6},{6,7},{7,5},{5,3},{3,1},{1,0},{8,10},{10,12},{12... | collective-permute-start | bytes 626696 | tf_op jit(solution)/shard_map/ppermute | solution.py:187

commit v4 on v3

--- a/solution.py
+++ b/solution.py
@@ -61,10 +61,10 @@
         x = jnp.dot(placing, held[d][...], preferred_element_type=jnp.float32)
         y = jnp.dot(placing, held[d + 1][...], preferred_element_type=jnp.float32) * slot_gate
         out_ref[:, :width] = x[:MAIN].astype(jnp.bfloat16)
-        out_ref[:, width : 2 * width] = y[:MAIN].astype(jnp.bfloat16)
+        out_ref[:, width + seg :] = y[:MAIN].astype(jnp.bfloat16)
         tail = [x[MAIN : MAIN + 1, s * seg : (s + 1) * seg] for s in range(SEGS)]
         tail += [y[MAIN : MAIN + 1, s * seg : (s + 1) * seg] for s in range(SEGS)]
-        out_ref[:, 2 * width :] = jnp.concatenate(tail, axis=0).astype(jnp.bfloat16)
+        out_ref[:, width : width + seg] = jnp.concatenate(tail, axis=0).astype(jnp.bfloat16)
 
 
 def pack(arrays):
@@ -87,41 +87,58 @@
     )(*arrays)
 
 
-def grad_kernel(count, last, *refs):
-    payloads, w_ref, refs = refs[:count], refs[count], refs[count + 1 :]
-    width = w_ref.shape[0]
+def activate(payloads, w_ref):
+    count, width = len(payloads), w_ref.shape[0]
     seg = width // SEGS
     size = count * 2 * SEGS
-    tails = jnp.concatenate([p[:, 2 * width :] for p in payloads], axis=0)
+    tails = jnp.concatenate([p[:, width : width + seg] for p in payloads], axis=0)
     row = lax.broadcasted_iota(jnp.int32, (size, size), 0)
     col = lax.broadcasted_iota(jnp.int32, (size, size), 1)
     order = ((row % count) * (2 * SEGS) + row // count == col).astype(jnp.bfloat16)
     tails = jnp.dot(order, tails, preferred_element_type=jnp.float32)
-    x_tail = jnp.concatenate(
-        [tails[s * count : (s + 1) * count] for s in range(SEGS)], axis=1
-    ).astype(jnp.bfloat16)
-    y_tail = jnp.concatenate(
-        [tails[(SEGS + s) * count : (SEGS + s + 1) * count] for s in range(SEGS)], axis=1
-    ).astype(jnp.bfloat16)
+    x_tail, y_tail = (
+        jnp.concatenate(
+            [tails[s * count : (s + 1) * count] for s in range(first, first + SEGS)], axis=1
+        ).astype(jnp.bfloat16)
+        for first in (0, SEGS)
+    )
     rows_x = jnp.concatenate([p[:, :width] for p in payloads] + [x_tail], axis=0)
     hidden = jnp.dot(rows_x, w_ref[...], preferred_element_type=jnp.float32)
-    active = (hidden * jax.nn.sigmoid(hidden)).astype(jnp.bfloat16)
-    if last:
-        before, out_ref, made, sems = refs
-    else:
-        (out_ref,) = refs
+    return (hidden * jax.nn.sigmoid(hidden)).astype(jnp.bfloat16), y_tail
+
+
+def times(active, rows_y):
+    return lax.dot_general(
+        active, rows_y, (((0,), (0,)), ((), ())), preferred_element_type=jnp.float32
+    )
+
+
+def part_kernel(count, *refs):
+    payloads, (w_ref, out_ref) = refs[:count], refs[count:]
+    width = w_ref.shape[0]
+    seg = width // SEGS
+    active, y_tail = activate(payloads, w_ref)
+    for s in range(SEGS):
+        here = slice(s * seg, (s + 1) * seg)
+        there = slice(width + (s + 1) * seg, width + (s + 2) * seg)
+        rows_y = jnp.concatenate([p[:, there] for p in payloads] + [y_tail[:, here]], axis=0)
+        out_ref[:, here] = times(active, rows_y)
+
+
+def active_kernel(count, *refs):
+    payloads, (w_ref, active_ref, tail_ref) = refs[:count], refs[count:]
+    active_ref[...], tail_ref[...] = activate(payloads, w_ref)
+
+
+def sum_kernel(count, *refs):
+    blocks, (active_ref, tail_ref, before, out_ref, made, sems) = refs[:count], refs[count:]
+    seg = tail_ref.shape[1] // SEGS
+    active = active_ref[...]
     copies = []
     for s in range(SEGS):
-        cut = slice(width + s * seg, width + (s + 1) * seg)
         here = slice(s * seg, (s + 1) * seg)
-        rows_y = jnp.concatenate([p[:, cut] for p in payloads] + [y_tail[:, here]], axis=0)
-        part = lax.dot_general(
-            active, rows_y, (((0,), (0,)), ((), ())), preferred_element_type=jnp.float32
-        )
-        if not last:
-            out_ref[:, here] = part
-            continue
-        made[:, here] = (before[:, here] + part).astype(jnp.bfloat16)
+        rows_y = jnp.concatenate([b[:, here] for b in blocks] + [tail_ref[:, here]], axis=0)
+        made[:, here] = (before[:, here] + times(active, rows_y)).astype(jnp.bfloat16)
         copies.append(
             pltpu.make_async_copy(made.at[:, here], out_ref.at[:, here], sems.at[s])
         )
@@ -130,33 +147,60 @@
         copy.wait()
 
 
-def grad(payloads, weight_in, before=None):
-    width, hidden = weight_in.shape
-    count = len(payloads)
-    last = before is not None
-    operands = (*payloads, weight_in) + ((before,) if last else ())
+def local_call(kernel, name, operands, outs, scratch=(), flops=0):
+    specs = tuple(
+        pl.BlockSpec(
+            memory_space=pltpu.HBM if isinstance(out, jax.ShapeDtypeStruct) else pltpu.VMEM
+        )
+        for out in outs
+    )
     return pl.pallas_call(
-        functools.partial(grad_kernel, count, last),
-        out_shape=jax.ShapeDtypeStruct((hidden, width), jnp.bfloat16 if last else jnp.float32),
+        kernel,
+        out_shape=outs,
         in_specs=[pl.BlockSpec(memory_space=pltpu.VMEM)] * len(operands),
-        out_specs=pl.BlockSpec(memory_space=pltpu.HBM if last else pltpu.VMEM),
-        scratch_shapes=[
-            pltpu.VMEM((hidden, width), jnp.bfloat16),
-            pltpu.SemaphoreType.DMA((SEGS,)),
-        ]
-        if last
-        else [],
+        out_specs=specs,
+        scratch_shapes=scratch,
         compiler_params=pltpu.CompilerParams(vmem_limit_bytes=40 * 2**20),
         cost_estimate=pl.CostEstimate(
-            flops=4 * CAP * count * width * hidden,
-            bytes_accessed=4 * width * hidden,
-            transcendentals=CAP * count * hidden,
+            flops=flops, bytes_accessed=sum(o.size * o.dtype.itemsize for o in operands),
+            transcendentals=0,
         ),
-        name="grad_sum" if last else "grad_part",
+        name=name,
     )(*operands)
 
 
-def gather_both(down, up, n_pipe, cycle):
+def grad(got, firsts, seconds, weight_in):
+    width, hidden = weight_in.shape
+    count, late = len(got), len(firsts)
+    (before,) = local_call(
+        functools.partial(part_kernel, count),
+        "grad_part",
+        (*got, weight_in),
+        (pltpu.VMEM((hidden, width), jnp.float32),),
+        flops=4 * CAP * count * width * hidden,
+    )
+    active, tail = local_call(
+        functools.partial(active_kernel, late),
+        "active_late",
+        (*firsts, weight_in),
+        (
+            pltpu.VMEM((late * CAP, hidden), jnp.bfloat16),
+            pltpu.VMEM((late, width), jnp.bfloat16),
+        ),
+        flops=2 * CAP * late * width * hidden,
+    )
+    (total,) = local_call(
+        functools.partial(sum_kernel, late),
+        "grad_sum",
+        (*seconds, active, tail, before),
+        (jax.ShapeDtypeStruct((hidden, width), jnp.bfloat16),),
+        scratch=[pltpu.VMEM((hidden, width), jnp.bfloat16), pltpu.SemaphoreType.DMA((SEGS,))],
+        flops=2 * CAP * late * width * hidden,
+    )
+    return total
+
+
+def gather_both(down, up, n_pipe, cycle, cut):
     n = len(cycle)
     right = [(cycle[i], cycle[(i + 1) % n]) for i in range(n)]
     left = [(b, a) for a, b in right]
@@ -184,9 +228,12 @@
     for _ in range(1, (n - 1) // 2):
         at = turn(at)
         got += at
-    last = (lax.ppermute(at[0], "expert", left), lax.ppermute(at[1], "expert", right))
+    firsts, seconds = (
+        (lax.ppermute(l, "expert", left), lax.ppermute(r, "expert", right))
+        for l, r in ((at[0][:, :cut], at[1][:, :cut]), (at[0][:, cut:], at[1][:, cut:]))
+    )
     own = mirrored(up, [(e, e) for e in range(n)])
-    return [*reversed(got), own, down], last
+    return [*reversed(got), own, down], firsts, seconds
 
 
 def body(
@@ -207,9 +254,10 @@
             *(tokens_up[0], cotan_up[0], gates_up[0].T, experts_up[0].T),
         )
     )
-    got, last = gather_both(down, up, n_pipe, grid_cycle(n_expert))
-    part = grad(got, w_in[0])
-    return grad(last, w_in[0], part)[None]
+    width = w_in.shape[1]
+    cut = width + width // SEGS
+    gathered = gather_both(down, up, n_pipe, grid_cycle(n_expert), cut)
+    return grad(*gathered, w_in[0])[None]
 
 
 def solution(mesh):

time: 42.2 us -> 41.5 us (0.983)
  waiting for transfers between devices: 19.4 us -> 15.7 us
  starting transfers between devices: 16.5 us -> 19.7 us
    ppermute x2 -> x4, starting transfers between devices: 2.03 us -> 5.25 us  [the longest x2 3.08 us: gather_both(): lax.ppermute(l, 'expert', left)]
    ppermute x2, waiting for transfers between devices: 4.88 us -> 3.19 us  [turn(): lax.ppermute(down_left, 'expert', left)]
    ppermute x2, waiting for transfers between devices: 1.49 us -> 0.01 us  [turn(): lax.ppermute(up_right, 'expert', right)]
    ppermute x2 -> x4, waiting for transfers between devices: 2.09 us -> 1.55 us  [the longest x2 1.38 us: gather_both(): lax.ppermute(r, 'expert', right)]
    pallas_call x2 -> x3, Pallas kernels: 4.3 us -> 3.97 us  [local_call(): pl.pallas_call(kernel, out_shape=outs, in_specs=[pl.BlockSpec(memory_spac...]
  transfers between devices with their start and end apart: 15 -> 17, of which waited for: 10 -> 10; matrix products, arithmetic and copies ran while one was open for 0% -> 0% of each run, Pallas kernels for 5% -> 6%
where the time goes in v4:
time: 41.5 us; the launch traced here: 41.3 us
  starting transfers between devices  19.7 us (47%)
  waiting for transfers between devices  15.7 us (38%)
  Pallas kernels  5.86 us (14%)
    ppermute x2, waiting for transfers between devices, turn(): lax.ppermute(up_left, 'expert', left)  4.89 us
    pallas_call x3, Pallas kernels, local_call(): pl.pallas_call(kernel, out_shape=outs, in_specs=[pl.BlockSpec(memory_spac...  3.97 us
    ppermute x2, starting transfers between devices, turn(): lax.ppermute(up_left, 'expert', left)  3.89 us
    ppermute x3, waiting for transfers between devices, mirrored(): return lax.ppermute(block, ('pipe', 'expert'), pairs)  3.5 us
    ppermute x3, starting transfers between devices, mirrored(): return lax.ppermute(block, ('pipe', 'expert'), pairs)  3.39 us
    ppermute x2, waiting for transfers between devices, turn(): lax.ppermute(down_left, 'expert', left)  3.19 us
    ppermute x2, starting transfers between devices, gather_both(): lax.ppermute(l, 'expert', left)  3.08 us
    ppermute x2, starting transfers between devices, turn(): lax.ppermute(down_left, 'expert', left)  2.98 us
  transfers between devices with their start and end apart: 17, of which 10 were waited for; matrix products, arithmetic and copies ran while one was open for 0% of the time, Pallas kernels for 6%

profile of v4, /device:TPU:0, one launch (start us, length us, event | category | flops | bytes accessed | tf_op | source)
XLA Modules:
  0.0 41.3 jit_solution(16193215904054778921)
XLA Ops:
  0.0 0.0 copy-start
  0.0 1.9 %pack_slots.1 = (bf16[16,6528]{1,0:T(8,128)(2,1)S(1)}, bf16[16,6528]{1,0:T(8,128)(2,1)S(1)}) custom-call(bf16[64,3072]{1,0:T(8,128)(2,1)} %bitcast.20, bf16[64,3072]{1,0:T(8,128)(2,1)} %bitcast.21, bf16[2,64]{1,0:T(2,128)(2,1)} %bitcast.26, s32[2,64]{1,0:T(2,128)} %bitcast.24, bf16[64,3072]{1,0:T(8,128)(2,1)} %bitcast.22, bf16[64,3072]{1,0:T(8,128)(2,1)} %bitcast.23, ...), custom_call_target="tpu_custom_call" | custom-call | flops 50331648 | bytes 2359296 | tf_op jit(solution)/shard_map/pack_slots/pallas_call | solution.py:75
  1.9 3.4 %collective-permute-start = (bf16[16,6528]{1,0:T(8,128)(2,1)S(1)}, bf16[16,6528]{1,0:T(8,128)(2,1)S(1)}, u32[]{:S(2)}, u32[]{:S(2)}) collective-permute-start(bf16[16,6528]{1,0:T(8,128)(2,1)S(1)} %get-tuple-element.9), channel_id=1, source_target_pairs={{2,24},{4,26},{6,28},{7,30},{5,31},{3,29},{1,27},{0,25},{10,16},{1... | collective-permute-start | bytes 626696 | tf_op jit(solution)/shard_map/ppermute | solution.py:210
  5.3 0.5 %collective-permute-start.4 = (bf16[16,6528]{1,0:T(8,128)(2,1)S(1)}, bf16[16,6528]{1,0:T(8,128)(2,1)S(1)}, u32[]{:S(2)}, u32[]{:S(2)}) collective-permute-start(bf16[16,6528]{1,0:T(8,128)(2,1)S(1)} %get-tuple-element.10.refs_13_), channel_id=1, source_target_pairs={{0,2},{2,4},{4,6},{6,7},{7,5},{5,3},{3,1},{1,0},{8,10},{10,12},{12... | collective-permute-start | bytes 626696 | tf_op jit(solution)/shard_map/ppermute | solution.py:223
  5.8 1.5 %collective-permute-start.10 = (bf16[16,6528]{1,0:T(8,128)(2,1)S(1)}, bf16[16,6528]{1,0:T(8,128)(2,1)S(1)}, u32[]{:S(2)}, u32[]{:S(2)}) collective-permute-start(bf16[16,6528]{1,0:T(8,128)(2,1)S(1)} %get-tuple-element.10.refs_13_), channel_id=1, source_target_pairs={{2,0},{4,2},{6,4},{7,6},{5,7},{3,5},{1,3},{0,1},{10,8},{12,10},{14... | collective-permute-start | bytes 626696 | tf_op jit(solution)/shard_map/ppermute | solution.py:225
  7.3 0.0 collective-permute-start.13
  7.3 3.5 %collective-permute-done.refs_11_ = bf16[16,6528]{1,0:T(8,128)(2,1)S(1)} collective-permute-done((bf16[16,6528]{1,0:T(8,128)(2,1)S(1)}, bf16[16,6528]{1,0:T(8,128)(2,1)S(1)}, u32[]{:S(2)}, u32[]{:S(2)}) %collective-permute-start) | collective-permute-done | bytes 208928 | tf_op jit(solution)/shard_map/ppermute | solution.py:210
  10.8 2.4 %collective-permute-start.1 = (bf16[16,6528]{1,0:T(8,128)(2,1)S(1)}, bf16[16,6528]{1,0:T(8,128)(2,1)S(1)}, u32[]{:S(2)}, u32[]{:S(2)}) collective-permute-start(bf16[16,6528]{1,0:T(8,128)(2,1)S(1)} %collective-permute-done.refs_11_), channel_id=1, source_target_pairs={{2,0},{4,2},{6,4},{7,6},{5,7},{3,5},{1,3},{0,1},{10,8},{12,10},{14... | collective-permute-start | bytes 626696 | tf_op jit(solution)/shard_map/ppermute | solution.py:215
  13.2 0.1 collective-permute-done.4.refs_10_
  13.3 0.5 %collective-permute-start.5 = (bf16[16,6528]{1,0:T(8,128)(2,1)S(1)}, bf16[16,6528]{1,0:T(8,128)(2,1)S(1)}, u32[]{:S(2)}, u32[]{:S(2)}) collective-permute-start(bf16[16,6528]{1,0:T(8,128)(2,1)S(1)} %collective-permute-done.4.refs_10_), channel_id=1, source_target_pairs={{0,2},{2,4},{4,6},{6,7},{7,5},{5,3},{3,1},{1,0},{8,10},{10,12},{12... | collective-permute-start | bytes 626696 | tf_op jit(solution)/shard_map/ppermute | solution.py:216
  13.9 2.4 %collective-permute-done.10.refs_8_ = bf16[16,6528]{1,0:T(8,128)(2,1)S(1)} collective-permute-done((bf16[16,6528]{1,0:T(8,128)(2,1)S(1)}, bf16[16,6528]{1,0:T(8,128)(2,1)S(1)}, u32[]{:S(2)}, u32[]{:S(2)}) %collective-permute-start.10) | collective-permute-done | bytes 208928 | tf_op jit(solution)/shard_map/ppermute | solution.py:225
  16.3 1.5 %collective-permute-start.11 = (bf16[16,6528]{1,0:T(8,128)(2,1)S(1)}, bf16[16,6528]{1,0:T(8,128)(2,1)S(1)}, u32[]{:S(2)}, u32[]{:S(2)}) collective-permute-start(bf16[16,6528]{1,0:T(8,128)(2,1)S(1)} %collective-permute-done.10.refs_8_), channel_id=1, source_target_pairs={{2,0},{4,2},{6,4},{7,6},{5,7},{3,5},{1,3},{0,1},{10,8},{12,10},{14... | collective-permute-start | bytes 626696 | tf_op jit(solution)/shard_map/ppermute | solution.py:218
  17.8 0.0 collective-permute-done.13.refs_9_
  17.8 0.5 %collective-permute-start.14 = (bf16[16,6528]{1,0:T(8,128)(2,1)S(1)}, bf16[16,6528]{1,0:T(8,128)(2,1)S(1)}, u32[]{:S(2)}, u32[]{:S(2)}) collective-permute-start(bf16[16,6528]{1,0:T(8,128)(2,1)S(1)} %collective-permute-done.13.refs_9_), channel_id=1, source_target_pairs={{0,2},{2,4},{4,6},{6,7},{7,5},{5,3},{3,1},{1,0},{8,10},{10,12},{12... | collective-permute-start | bytes 626696 | tf_op jit(solution)/shard_map/ppermute | solution.py:217
  18.3 2.4 %collective-permute-done.1.refs_7_ = bf16[16,6528]{1,0:T(8,128)(2,1)S(1)} collective-permute-done((bf16[16,6528]{1,0:T(8,128)(2,1)S(1)}, bf16[16,6528]{1,0:T(8,128)(2,1)S(1)}, u32[]{:S(2)}, u32[]{:S(2)}) %collective-permute-start.1) | collective-permute-done | bytes 208928 | tf_op jit(solution)/shard_map/ppermute | solution.py:215
  20.8 1.5 %collective-permute-start.2 = (bf16[16,6528]{1,0:T(8,128)(2,1)S(1)}, bf16[16,6528]{1,0:T(8,128)(2,1)S(1)}, u32[]{:S(2)}, u32[]{:S(2)}) collective-permute-start(bf16[16,6528]{1,0:T(8,128)(2,1)S(1)} %collective-permute-done.1.refs_7_), channel_id=1, source_target_pairs={{2,0},{4,2},{6,4},{7,6},{5,7},{3,5},{1,3},{0,1},{10,8},{12,10},{14... | collective-permute-start | bytes 626696 | tf_op jit(solution)/shard_map/ppermute | solution.py:215
  22.3 0.0 collective-permute-done.5.refs_6_
  22.3 0.5 %collective-permute-start.6 = (bf16[16,6528]{1,0:T(8,128)(2,1)S(1)}, bf16[16,6528]{1,0:T(8,128)(2,1)S(1)}, u32[]{:S(2)}, u32[]{:S(2)}) collective-permute-start(bf16[16,6528]{1,0:T(8,128)(2,1)S(1)} %collective-permute-done.5.refs_6_), channel_id=1, source_target_pairs={{0,2},{2,4},{4,6},{6,7},{7,5},{5,3},{3,1},{1,0},{8,10},{10,12},{12... | collective-permute-start | bytes 626696 | tf_op jit(solution)/shard_map/ppermute | solution.py:216
  22.8 0.0 collective-permute-start.16
  22.8 2.4 %collective-permute-done.11.refs_4_ = bf16[16,6528]{1,0:T(8,128)(2,1)S(1)} collective-permute-done((bf16[16,6528]{1,0:T(8,128)(2,1)S(1)}, bf16[16,6528]{1,0:T(8,128)(2,1)S(1)}, u32[]{:S(2)}, u32[]{:S(2)}) %collective-permute-start.11) | collective-permute-done | bytes 208928 | tf_op jit(solution)/shard_map/ppermute | solution.py:218
  25.3 1.5 %collective-permute-start.12 = (bf16[16,6528]{1,0:T(8,128)(2,1)S(1)}, bf16[16,6528]{1,0:T(8,128)(2,1)S(1)}, u32[]{:S(2)}, u32[]{:S(2)}) collective-permute-start(bf16[16,6528]{1,0:T(8,128)(2,1)S(1)} %collective-permute-done.11.refs_4_), channel_id=1, source_target_pairs={{2,0},{4,2},{6,4},{7,6},{5,7},{3,5},{1,3},{0,1},{10,8},{12,10},{14... | collective-permute-start | bytes 626696 | tf_op jit(solution)/shard_map/ppermute | solution.py:218
  26.7 0.0 collective-permute-done.14.refs_5_
  26.8 0.5 %collective-permute-start.15 = (bf16[16,6528]{1,0:T(8,128)(2,1)S(1)}, bf16[16,6528]{1,0:T(8,128)(2,1)S(1)}, u32[]{:S(2)}, u32[]{:S(2)}) collective-permute-start(bf16[16,6528]{1,0:T(8,128)(2,1)S(1)} %collective-permute-done.14.refs_5_), channel_id=1, source_target_pairs={{0,2},{2,4},{4,6},{6,7},{7,5},{5,3},{3,1},{1,0},{8,10},{10,12},{12... | collective-permute-start | bytes 626696 | tf_op jit(solution)/shard_map/ppermute | solution.py:217
  27.3 2.4 %collective-permute-done.2.refs_3_ = bf16[16,6528]{1,0:T(8,128)(2,1)S(1)} collective-permute-done((bf16[16,6528]{1,0:T(8,128)(2,1)S(1)}, bf16[16,6528]{1,0:T(8,128)(2,1)S(1)}, u32[]{:S(2)}, u32[]{:S(2)}) %collective-permute-start.2) | collective-permute-done | bytes 208928 | tf_op jit(solution)/shard_map/ppermute | solution.py:215
  29.7 1.5 %collective-permute-start.8 = (bf16[16,3456]{1,0:T(8,128)(2,1)S(1)}, bf16[16,3456]{1,0:T(8,128)(2,1)S(1)}, u32[]{:S(2)}, u32[]{:S(2)}) collective-permute-start(bf16[16,3456]{1,0:T(8,128)(2,1)S(1)} %slice.18), channel_id=1, source_target_pairs={{2,0},{4,2},{6,4},{7,6},{5,7},{3,5},{1,3},{0,1},{10,8},{12,10},{14... | collective-permute-start | bytes 331784 | tf_op jit(solution)/shard_map/ppermute | solution.py:232
  31.3 0.0 collective-permute-done.6.refs_2_
  31.3 0.6 %collective-permute-start.9 = (bf16[16,3456]{1,0:T(8,128)(2,1)S(1)}, bf16[16,3456]{1,0:T(8,128)(2,1)S(1)}, u32[]{:S(2)}, u32[]{:S(2)}) collective-permute-start(bf16[16,3456]{1,0:T(8,128)(2,1)S(1)} %slice.19), channel_id=1, source_target_pairs={{0,2},{2,4},{4,6},{6,7},{7,5},{5,3},{3,1},{1,0},{8,10},{10,12},{12... | collective-permute-start | bytes 331784 | tf_op jit(solution)/shard_map/ppermute | solution.py:232
  31.9 0.0 collective-permute-done.16.refs_12_
  31.9 1.5 %collective-permute-start.3 = (bf16[16,3072]{1,0:T(8,128)(2,1)S(1)}, bf16[16,3072]{1,0:T(8,128)(2,1)S(1)}, u32[]{:S(2)}, u32[]{:S(2)}) collective-permute-start(bf16[16,3072]{1,0:T(8,128)(2,1)S(1)} %slice.16), channel_id=1, source_target_pairs={{2,0},{4,2},{6,4},{7,6},{5,7},{3,5},{1,3},{0,1},{10,8},{12,10},{14... | collective-permute-start | bytes 294920 | tf_op jit(solution)/shard_map/ppermute | solution.py:232
  33.5 0.7 %collective-permute-done.12.refs_0_ = bf16[16,6528]{1,0:T(8,128)(2,1)S(1)} collective-permute-done((bf16[16,6528]{1,0:T(8,128)(2,1)S(1)}, bf16[16,6528]{1,0:T(8,128)(2,1)S(1)}, u32[]{:S(2)}, u32[]{:S(2)}) %collective-permute-start.12) | collective-permute-done | bytes 208928 | tf_op jit(solution)/shard_map/ppermute | solution.py:218
  34.2 1.6 %collective-permute-start.7 = (bf16[16,3072]{1,0:T(8,128)(2,1)S(1)}, bf16[16,3072]{1,0:T(8,128)(2,1)S(1)}, u32[]{:S(2)}, u32[]{:S(2)}) collective-permute-start(bf16[16,3072]{1,0:T(8,128)(2,1)S(1)} %slice.17), channel_id=1, source_target_pairs={{0,2},{2,4},{4,6},{6,7},{7,5},{5,3},{3,1},{1,0},{8,10},{10,12},{12... | collective-permute-start | bytes 294920 | tf_op jit(solution)/shard_map/ppermute | solution.py:232
  35.8 0.0 collective-permute-done.15.refs_1_
  35.8 0.0 copy-done
  35.8 2.1 %grad_part.1.refs_4_ = f32[256,3072]{1,0:T(8,128)S(1)} custom-call(bf16[16,6528]{1,0:T(8,128)(2,1)S(1)} %collective-permute-done.12.refs_0_, bf16[16,6528]{1,0:T(8,128)(2,1)S(1)} %collective-permute-done.15.refs_1_, bf16[16,6528]{1,0:T(8,128)(2,1)S(1)} %collective-permute-done.6.refs_2_, bf16[16,6528]{1,0:T(8,128)(2,1)S(1)} %collective-permute-done.2.refs_3_, ...), custom_call_target="tpu_custom_call" | custom-call | flops 748683264 | bytes 4497408 | tf_op jit(solution)/shard_map/grad_part/pallas_call | solution.py:157
  37.9 0.0 collective-permute-done.8.refs_0_
  37.9 0.2 collective-permute-done.9.refs_1_
  38.1 0.4 %active_late.1 = (bf16[34,256]{1,0:T(8,128)(2,1)S(1)}, bf16[2,3072]{1,0:T(2,128)(2,1)S(1)}) custom-call(bf16[16,3456]{1,0:T(8,128)(2,1)S(1)} %collective-permute-done.8.refs_0_, bf16[16,3456]{1,0:T(8,128)(2,1)S(1)} %collective-permute-done.9.refs_1_, bf16[3072,256]{1,0:T(8,128)(2,1)S(1)} %bitcast.19), custom_call_target="tpu_custom_call" | custom-call | flops 53477376 | bytes 1794048 | tf_op jit(solution)/shard_map/active_late/pallas_call | solution.py:157
  38.5 0.2 collective-permute-done.3.refs_0_
  38.7 1.2 %collective-permute-done.7.refs_1_ = bf16[16,3072]{1,0:T(8,128)(2,1)S(1)} collective-permute-done((bf16[16,3072]{1,0:T(8,128)(2,1)S(1)}, bf16[16,3072]{1,0:T(8,128)(2,1)S(1)}, u32[]{:S(2)}, u32[]{:S(2)}) %collective-permute-start.7) | collective-permute-done | bytes 98336 | tf_op jit(solution)/shard_map/ppermute | solution.py:232
  39.9 1.5 %grad_sum.1 = bf16[256,3072]{1,0:T(8,128)(2,1)} custom-call(bf16[16,3072]{1,0:T(8,128)(2,1)S(1)} %collective-permute-done.3.refs_0_, bf16[16,3072]{1,0:T(8,128)(2,1)S(1)} %collective-permute-done.7.refs_1_, bf16[34,256]{1,0:T(8,128)(2,1)S(1)} %get-tuple-element.11.refs_2_, bf16[2,3072]{1,0:T(2,128)(2,1)S(1)} %get-tuple-element.12.refs_3_, ...), custom_call_target="tpu_custom_call" | custom-call | flops 53477376 | bytes 3372032 | tf_op jit(solution)/shard_map/grad_sum/pallas_call | solution.py:157
  (4 shorter events, 0.0 us)
Async XLA Ops:
  0.0 35.8 %copy-start = (bf16[1,3072,256]{2,1,0:T(8,128)(2,1)S(1)}, bf16[1,3072,256]{2,1,0:T(8,128)(2,1)}, u32[]{:S(2)}) copy-start(bf16[1,3072,256]{2,1,0:T(8,128)(2,1)} %param.17) | copy-start | bytes 4718596
  1.9 8.9 %collective-permute-start = (bf16[16,6528]{1,0:T(8,128)(2,1)S(1)}, bf16[16,6528]{1,0:T(8,128)(2,1)S(1)}, u32[]{:S(2)}, u32[]{:S(2)}) collective-permute-start(bf16[16,6528]{1,0:T(8,128)(2,1)S(1)} %get-tuple-element.9), channel_id=1, source_target_pairs={{2,24},{4,26},{6,28},{7,30},{5,31},{3,29},{1,27},{0,25},{10,16},{1... | collective-permute-start | bytes 626696 | tf_op jit(solution)/shard_map/ppermute | solution.py:210
  5.3 8.0 %collective-permute-start.4 = (bf16[16,6528]{1,0:T(8,128)(2,1)S(1)}, bf16[16,6528]{1,0:T(8,128)(2,1)S(1)}, u32[]{:S(2)}, u32[]{:S(2)}) collective-permute-start(bf16[16,6528]{1,0:T(8,128)(2,1)S(1)} %get-tuple-element.10.refs_13_), channel_id=1, source_target_pairs={{0,2},{2,4},{4,6},{6,7},{7,5},{5,3},{3,1},{1,0},{8,10},{10,12},{12... | collective-permute-start | bytes 626696 | tf_op jit(solution)/shard_map/ppermute | solution.py:223
  5.8 10.5 %collective-permute-start.10 = (bf16[16,6528]{1,0:T(8,128)(2,1)S(1)}, bf16[16,6528]{1,0:T(8,128)(2,1)S(1)}, u32[]{:S(2)}, u32[]{:S(2)}) collective-permute-start(bf16[16,6528]{1,0:T(8,128)(2,1)S(1)} %get-tuple-element.10.refs_13_), channel_id=1, source_target_pairs={{2,0},{4,2},{6,4},{7,6},{5,7},{3,5},{1,3},{0,1},{10,8},{12,10},{14... | collective-permute-start | bytes 626696 | tf_op jit(solution)/shard_map/ppermute | solution.py:225
  7.3 10.5 %collective-permute-start.13 = (bf16[16,6528]{1,0:T(8,128)(2,1)S(1)}, bf16[16,6528]{1,0:T(8,128)(2,1)S(1)}, u32[]{:S(2)}, u32[]{:S(2)}) collective-permute-start(bf16[16,6528]{1,0:T(8,128)(2,1)S(1)} %get-tuple-element.9), channel_id=1, source_target_pairs={{0,26},{2,28},{4,30},{6,31},{7,29},{5,27},{3,25},{1,24},{8,18},{10... | collective-permute-start | bytes 626696 | tf_op jit(solution)/shard_map/ppermute | solution.py:210
  10.8 9.9 %collective-permute-start.1 = (bf16[16,6528]{1,0:T(8,128)(2,1)S(1)}, bf16[16,6528]{1,0:T(8,128)(2,1)S(1)}, u32[]{:S(2)}, u32[]{:S(2)}) collective-permute-start(bf16[16,6528]{1,0:T(8,128)(2,1)S(1)} %collective-permute-done.refs_11_), channel_id=1, source_target_pairs={{2,0},{4,2},{6,4},{7,6},{5,7},{3,5},{1,3},{0,1},{10,8},{12,10},{14... | collective-permute-start | bytes 626696 | tf_op jit(solution)/shard_map/ppermute | solution.py:215
  13.3 9.0 %collective-permute-start.5 = (bf16[16,6528]{1,0:T(8,128)(2,1)S(1)}, bf16[16,6528]{1,0:T(8,128)(2,1)S(1)}, u32[]{:S(2)}, u32[]{:S(2)}) collective-permute-start(bf16[16,6528]{1,0:T(8,128)(2,1)S(1)} %collective-permute-done.4.refs_10_), channel_id=1, source_target_pairs={{0,2},{2,4},{4,6},{6,7},{7,5},{5,3},{3,1},{1,0},{8,10},{10,12},{12... | collective-permute-start | bytes 626696 | tf_op jit(solution)/shard_map/ppermute | solution.py:216
  16.3 9.0 %collective-permute-start.11 = (bf16[16,6528]{1,0:T(8,128)(2,1)S(1)}, bf16[16,6528]{1,0:T(8,128)(2,1)S(1)}, u32[]{:S(2)}, u32[]{:S(2)}) collective-permute-start(bf16[16,6528]{1,0:T(8,128)(2,1)S(1)} %collective-permute-done.10.refs_8_), channel_id=1, source_target_pairs={{2,0},{4,2},{6,4},{7,6},{5,7},{3,5},{1,3},{0,1},{10,8},{12,10},{14... | collective-permute-start | bytes 626696 | tf_op jit(solution)/shard_map/ppermute | solution.py:218
  17.8 9.0 %collective-permute-start.14 = (bf16[16,6528]{1,0:T(8,128)(2,1)S(1)}, bf16[16,6528]{1,0:T(8,128)(2,1)S(1)}, u32[]{:S(2)}, u32[]{:S(2)}) collective-permute-start(bf16[16,6528]{1,0:T(8,128)(2,1)S(1)} %collective-permute-done.13.refs_9_), channel_id=1, source_target_pairs={{0,2},{2,4},{4,6},{6,7},{7,5},{5,3},{3,1},{1,0},{8,10},{10,12},{12... | collective-permute-start | bytes 626696 | tf_op jit(solution)/shard_map/ppermute | solution.py:217
  20.8 9.0 %collective-permute-start.2 = (bf16[16,6528]{1,0:T(8,128)(2,1)S(1)}, bf16[16,6528]{1,0:T(8,128)(2,1)S(1)}, u32[]{:S(2)}, u32[]{:S(2)}) collective-permute-start(bf16[16,6528]{1,0:T(8,128)(2,1)S(1)} %collective-permute-done.1.refs_7_), channel_id=1, source_target_pairs={{2,0},{4,2},{6,4},{7,6},{5,7},{3,5},{1,3},{0,1},{10,8},{12,10},{14... | collective-permute-start | bytes 626696 | tf_op jit(solution)/shard_map/ppermute | solution.py:215
  22.3 9.0 %collective-permute-start.6 = (bf16[16,6528]{1,0:T(8,128)(2,1)S(1)}, bf16[16,6528]{1,0:T(8,128)(2,1)S(1)}, u32[]{:S(2)}, u32[]{:S(2)}) collective-permute-start(bf16[16,6528]{1,0:T(8,128)(2,1)S(1)} %collective-permute-done.5.refs_6_), channel_id=1, source_target_pairs={{0,2},{2,4},{4,6},{6,7},{7,5},{5,3},{3,1},{1,0},{8,10},{10,12},{12... | collective-permute-start | bytes 626696 | tf_op jit(solution)/shard_map/ppermute | solution.py:216
  22.8 9.1 %collective-permute-start.16 = (bf16[16,6528]{1,0:T(8,128)(2,1)S(1)}, bf16[16,6528]{1,0:T(8,128)(2,1)S(1)}, u32[]{:S(2)}, u32[]{:S(2)}) collective-permute-start(bf16[16,6528]{1,0:T(8,128)(2,1)S(1)} %get-tuple-element.9), channel_id=1, source_target_pairs={{0,24},{1,25},{2,26},{3,27},{4,28},{5,29},{6,30},{7,31},{8,16},{9,... | collective-permute-start | bytes 626696 | tf_op jit(solution)/shard_map/ppermute | solution.py:210
  25.3 9.0 %collective-permute-start.12 = (bf16[16,6528]{1,0:T(8,128)(2,1)S(1)}, bf16[16,6528]{1,0:T(8,128)(2,1)S(1)}, u32[]{:S(2)}, u32[]{:S(2)}) collective-permute-start(bf16[16,6528]{1,0:T(8,128)(2,1)S(1)} %collective-permute-done.11.refs_4_), channel_id=1, source_target_pairs={{2,0},{4,2},{6,4},{7,6},{5,7},{3,5},{1,3},{0,1},{10,8},{12,10},{14... | collective-permute-start | bytes 626696 | tf_op jit(solution)/shard_map/ppermute | solution.py:218
  26.8 9.0 %collective-permute-start.15 = (bf16[16,6528]{1,0:T(8,128)(2,1)S(1)}, bf16[16,6528]{1,0:T(8,128)(2,1)S(1)}, u32[]{:S(2)}, u32[]{:S(2)}) collective-permute-start(bf16[16,6528]{1,0:T(8,128)(2,1)S(1)} %collective-permute-done.14.refs_5_), channel_id=1, source_target_pairs={{0,2},{2,4},{4,6},{6,7},{7,5},{5,3},{3,1},{1,0},{8,10},{10,12},{12... | collective-permute-start | bytes 626696 | tf_op jit(solution)/shard_map/ppermute | solution.py:217
  29.7 8.1 %collective-permute-start.8 = (bf16[16,3456]{1,0:T(8,128)(2,1)S(1)}, bf16[16,3456]{1,0:T(8,128)(2,1)S(1)}, u32[]{:S(2)}, u32[]{:S(2)}) collective-permute-start(bf16[16,3456]{1,0:T(8,128)(2,1)S(1)} %slice.18), channel_id=1, source_target_pairs={{2,0},{4,2},{6,4},{7,6},{5,7},{3,5},{1,3},{0,1},{10,8},{12,10},{14... | collective-permute-start | bytes 331784 | tf_op jit(solution)/shard_map/ppermute | solution.py:232
  31.3 6.8 %collective-permute-start.9 = (bf16[16,3456]{1,0:T(8,128)(2,1)S(1)}, bf16[16,3456]{1,0:T(8,128)(2,1)S(1)}, u32[]{:S(2)}, u32[]{:S(2)}) collective-permute-start(bf16[16,3456]{1,0:T(8,128)(2,1)S(1)} %slice.19), channel_id=1, source_target_pairs={{0,2},{2,4},{4,6},{6,7},{7,5},{5,3},{3,1},{1,0},{8,10},{10,12},{12... | collective-permute-start | bytes 331784 | tf_op jit(solution)/shard_map/ppermute | solution.py:232
  31.9 6.8 %collective-permute-start.3 = (bf16[16,3072]{1,0:T(8,128)(2,1)S(1)}, bf16[16,3072]{1,0:T(8,128)(2,1)S(1)}, u32[]{:S(2)}, u32[]{:S(2)}) collective-permute-start(bf16[16,3072]{1,0:T(8,128)(2,1)S(1)} %slice.16), channel_id=1, source_target_pairs={{2,0},{4,2},{6,4},{7,6},{5,7},{3,5},{1,3},{0,1},{10,8},{12,10},{14... | collective-permute-start | bytes 294920 | tf_op jit(solution)/shard_map/ppermute | solution.py:232
  34.2 5.7 %collective-permute-start.7 = (bf16[16,3072]{1,0:T(8,128)(2,1)S(1)}, bf16[16,3072]{1,0:T(8,128)(2,1)S(1)}, u32[]{:S(2)}, u32[]{:S(2)}) collective-permute-start(bf16[16,3072]{1,0:T(8,128)(2,1)S(1)} %slice.17), channel_id=1, source_target_pairs={{0,2},{2,4},{4,6},{6,7},{7,5},{5,3},{3,1},{1,0},{8,10},{10,12},{12... | collective-permute-start | bytes 294920 | tf_op jit(solution)/shard_map/ppermute | solution.py:232

commit v5 on v4

--- a/solution.py
+++ b/solution.py
@@ -10,6 +10,7 @@
 CAP = 17
 MAIN = 16
 SEGS = 8
+SHIFT = 2
 
 
 def grid_cycle(n):
@@ -130,14 +131,20 @@
     active_ref[...], tail_ref[...] = activate(payloads, w_ref)
 
 
-def sum_kernel(count, *refs):
-    blocks, (active_ref, tail_ref, before, out_ref, made, sems) = refs[:count], refs[count:]
-    seg = tail_ref.shape[1] // SEGS
+def sum_kernel(count, starts, *refs):
+    pieces, (active_ref, tail_ref, before, out_ref, made, sems) = refs[:count], refs[count:]
+    width = tail_ref.shape[1]
+    seg = width // SEGS
     active = active_ref[...]
     copies = []
     for s in range(SEGS):
         here = slice(s * seg, (s + 1) * seg)
-        rows_y = jnp.concatenate([b[:, here] for b in blocks] + [tail_ref[:, here]], axis=0)
+        rows_y = []
+        for ends in starts:
+            index, first, lanes = [e for e in ends if e[1] <= here.start][-1]
+            at = lanes + here.start - first
+            rows_y.append(pieces[index][:, at : at + seg])
+        rows_y = jnp.concatenate(rows_y + [tail_ref[:, here]], axis=0)
         made[:, here] = (before[:, here] + times(active, rows_y)).astype(jnp.bfloat16)
         copies.append(
             pltpu.make_async_copy(made.at[:, here], out_ref.at[:, here], sems.at[s])
@@ -169,38 +176,43 @@
     )(*operands)
 
 
-def grad(got, firsts, seconds, weight_in):
+def grad_part(blocks, weight_in):
     width, hidden = weight_in.shape
-    count, late = len(got), len(firsts)
-    (before,) = local_call(
-        functools.partial(part_kernel, count),
+    (part,) = local_call(
+        functools.partial(part_kernel, len(blocks)),
         "grad_part",
-        (*got, weight_in),
+        (*blocks, weight_in),
         (pltpu.VMEM((hidden, width), jnp.float32),),
-        flops=4 * CAP * count * width * hidden,
-    )
+        flops=4 * CAP * len(blocks) * width * hidden,
+    )
+    return part
+
+
+def grad_sum(late, pieces, starts, weight_in, before):
+    width, hidden = weight_in.shape
+    count = len(late)
     active, tail = local_call(
-        functools.partial(active_kernel, late),
+        functools.partial(active_kernel, count),
         "active_late",
-        (*firsts, weight_in),
+        (*late, weight_in),
         (
-            pltpu.VMEM((late * CAP, hidden), jnp.bfloat16),
-            pltpu.VMEM((late, width), jnp.bfloat16),
+            pltpu.VMEM((count * CAP, hidden), jnp.bfloat16),
+            pltpu.VMEM((count, width), jnp.bfloat16),
         ),
-        flops=2 * CAP * late * width * hidden,
+        flops=2 * CAP * count * width * hidden,
     )
     (total,) = local_call(
-        functools.partial(sum_kernel, late),
+        functools.partial(sum_kernel, len(pieces), starts),
         "grad_sum",
-        (*seconds, active, tail, before),
+        (*pieces, active, tail, before),
         (jax.ShapeDtypeStruct((hidden, width), jnp.bfloat16),),
         scratch=[pltpu.VMEM((hidden, width), jnp.bfloat16), pltpu.SemaphoreType.DMA((SEGS,))],
-        flops=2 * CAP * late * width * hidden,
+        flops=2 * CAP * count * width * hidden,
     )
     return total
 
 
-def gather_both(down, up, n_pipe, cycle, cut):
+def gather_and_multiply(down, up, weight_in, n_pipe, cycle):
     n = len(cycle)
     right = [(cycle[i], cycle[(i + 1) % n]) for i in range(n)]
     left = [(b, a) for a, b in right]
@@ -224,16 +236,31 @@
         mirrored(up, right),
         lax.ppermute(down, "expert", left),
     )
-    got = [*at]
-    for _ in range(1, (n - 1) // 2):
+    early = [*at]
+    for _ in range(2, (n - 1) // 2):
         at = turn(at)
-        got += at
-    firsts, seconds = (
-        (lax.ppermute(l, "expert", left), lax.ppermute(r, "expert", right))
-        for l, r in ((at[0][:, :cut], at[1][:, :cut]), (at[0][:, cut:], at[1][:, cut:]))
-    )
+        early += at
     own = mirrored(up, [(e, e) for e in range(n)])
-    return [*reversed(got), own, down], firsts, seconds
+    part = grad_part([*reversed(early), own, down], weight_in)
+    at = turn(at)
+    at0, _ = lax.optimization_barrier((at[0], part))
+    at = (at0, *at[1:])
+    up_left, down_right, up_right, down_left = at
+    width = weight_in.shape[0]
+    cut = width + width // SEGS
+    up_last = lax.ppermute(up_left, "expert", left)
+    down_first = lax.ppermute(down_right[:, :cut], "expert", right)
+    shift = width - SHIFT * (width // SEGS)
+    late = (down_left, up_right, down_right, up_left, up_last, down_first)
+    pieces = (
+        *late[:-1],
+        lax.ppermute(down_left[:, cut + shift :], "expert", left),
+        lax.ppermute(down_right[:, cut : cut + shift], "expert", right),
+    )
+    last = len(late) - 1
+    starts = [((i, 0, cut),) for i in range(last)]
+    starts += [((last + 1, 0, 0), (last, shift, 0))]
+    return grad_sum(late, pieces, starts, weight_in, part)
 
 
 def body(
@@ -254,10 +281,7 @@
             *(tokens_up[0], cotan_up[0], gates_up[0].T, experts_up[0].T),
         )
     )
-    width = w_in.shape[1]
-    cut = width + width // SEGS
-    gathered = gather_both(down, up, n_pipe, grid_cycle(n_expert), cut)
-    return grad(*gathered, w_in[0])[None]
+    return gather_and_multiply(down, up, w_in[0], n_pipe, grid_cycle(n_expert))[None]
 
 
 def solution(mesh):

time: 41.5 us -> 41 us (0.988)
  waiting for transfers between devices: 15.7 us -> 14.9 us
  starting transfers between devices: 19.7 us -> 20.2 us
    ppermute x2, waiting for transfers between devices: 4.89 us -> 2.46 us  [turn(): lax.ppermute(up_left, 'expert', left)]
    ppermute x6, waiting for transfers between devices: 4.08 us -> 5.71 us  [the longest x1 2.45 us: gather_and_multiply(): lax.ppermute(down, 'expert', left)]
    ppermute x3, starting transfers between devices: 3.39 us -> 4.01 us  [mirrored(): return lax.ppermute(block, ('pipe', 'expert'), pairs)]
where the time goes in v5:
time: 41 us; the launch traced here: 40.8 us
  starting transfers between devices  20.2 us (49%)
  waiting for transfers between devices  14.9 us (36%)
  Pallas kernels  5.61 us (14%)
    ppermute x3, starting transfers between devices, mirrored(): return lax.ppermute(block, ('pipe', 'expert'), pairs)  4.01 us
    ppermute x2, starting transfers between devices, turn(): lax.ppermute(up_left, 'expert', left)  3.89 us
    pallas_call x3, Pallas kernels, local_call(): pl.pallas_call(kernel, out_shape=outs, in_specs=[pl.BlockSpec(memory_spac...  3.73 us
    ppermute x3, waiting for transfers between devices, mirrored(): return lax.ppermute(block, ('pipe', 'expert'), pairs)  3.5 us
    ppermute x2, waiting for transfers between devices, turn(): lax.ppermute(down_left, 'expert', left)  3.24 us
    ppermute x2, starting transfers between devices, turn(): lax.ppermute(down_left, 'expert', left)  2.98 us
    ppermute x2, waiting for transfers between devices, turn(): lax.ppermute(up_left, 'expert', left)  2.46 us
    ppermute x1, waiting for transfers between devices, gather_and_multiply(): lax.ppermute(down, 'expert', left)  2.45 us
  transfers between devices with their start and end apart: 17, of which 10 were waited for; matrix products, arithmetic and copies ran while one was open for 0% of the time, Pallas kernels for 6%

profile of v5, /device:TPU:0, one launch (start us, length us, event | category | flops | bytes accessed | tf_op | source)
XLA Modules:
  0.0 40.8 jit_solution(5733467572477965523)
XLA Ops:
  0.0 0.0 copy-start
  0.0 1.9 %pack_slots.1 = (bf16[16,6528]{1,0:T(8,128)(2,1)S(1)}, bf16[16,6528]{1,0:T(8,128)(2,1)S(1)}) custom-call(bf16[64,3072]{1,0:T(8,128)(2,1)} %bitcast.20, bf16[64,3072]{1,0:T(8,128)(2,1)} %bitcast.21, bf16[2,64]{1,0:T(2,128)(2,1)} %bitcast.26, s32[2,64]{1,0:T(2,128)} %bitcast.24, bf16[64,3072]{1,0:T(8,128)(2,1)} %bitcast.22, bf16[64,3072]{1,0:T(8,128)(2,1)} %bitcast.23, ...), custom_call_target="tpu_custom_call" | custom-call | flops 50331648 | bytes 2359296 | tf_op jit(solution)/shard_map/pack_slots/pallas_call | solution.py:76
  1.9 3.4 %collective-permute-start.9 = (bf16[16,6528]{1,0:T(8,128)(2,1)S(1)}, bf16[16,6528]{1,0:T(8,128)(2,1)S(1)}, u32[]{:S(2)}, u32[]{:S(2)}) collective-permute-start(bf16[16,6528]{1,0:T(8,128)(2,1)S(1)} %get-tuple-element.11), channel_id=1, source_target_pairs={{2,24},{4,26},{6,28},{7,30},{5,31},{3,29},{1,27},{0,25},{10,16},{1... | collective-permute-start | bytes 626696 | tf_op jit(solution)/shard_map/ppermute | solution.py:222
  5.3 0.5 %collective-permute-start.6 = (bf16[16,6528]{1,0:T(8,128)(2,1)S(1)}, bf16[16,6528]{1,0:T(8,128)(2,1)S(1)}, u32[]{:S(2)}, u32[]{:S(2)}) collective-permute-start(bf16[16,6528]{1,0:T(8,128)(2,1)S(1)} %get-tuple-element.10.refs_9_), channel_id=1, source_target_pairs={{0,2},{2,4},{4,6},{6,7},{7,5},{5,3},{3,1},{1,0},{8,10},{10,12},{12... | collective-permute-start | bytes 626696 | tf_op jit(solution)/shard_map/ppermute | solution.py:235
  5.8 1.5 %collective-permute-start = (bf16[16,6528]{1,0:T(8,128)(2,1)S(1)}, bf16[16,6528]{1,0:T(8,128)(2,1)S(1)}, u32[]{:S(2)}, u32[]{:S(2)}) collective-permute-start(bf16[16,6528]{1,0:T(8,128)(2,1)S(1)} %get-tuple-element.10.refs_9_), channel_id=1, source_target_pairs={{2,0},{4,2},{6,4},{7,6},{5,7},{3,5},{1,3},{0,1},{10,8},{12,10},{14... | collective-permute-start | bytes 626696 | tf_op jit(solution)/shard_map/ppermute | solution.py:237
  7.3 0.0 collective-permute-start.3
  7.3 3.5 %collective-permute-done.9.refs_7_ = bf16[16,6528]{1,0:T(8,128)(2,1)S(1)} collective-permute-done((bf16[16,6528]{1,0:T(8,128)(2,1)S(1)}, bf16[16,6528]{1,0:T(8,128)(2,1)S(1)}, u32[]{:S(2)}, u32[]{:S(2)}) %collective-permute-start.9) | collective-permute-done | bytes 208928 | tf_op jit(solution)/shard_map/ppermute | solution.py:222
  10.8 2.4 %collective-permute-start.10 = (bf16[16,6528]{1,0:T(8,128)(2,1)S(1)}, bf16[16,6528]{1,0:T(8,128)(2,1)S(1)}, u32[]{:S(2)}, u32[]{:S(2)}) collective-permute-start(bf16[16,6528]{1,0:T(8,128)(2,1)S(1)} %collective-permute-done.9.refs_7_), channel_id=1, source_target_pairs={{2,0},{4,2},{6,4},{7,6},{5,7},{3,5},{1,3},{0,1},{10,8},{12,10},{14... | collective-permute-start | bytes 626696 | tf_op jit(solution)/shard_map/ppermute | solution.py:227
  13.2 0.1 collective-permute-done.6.refs_6_
  13.3 0.5 %collective-permute-start.7 = (bf16[16,6528]{1,0:T(8,128)(2,1)S(1)}, bf16[16,6528]{1,0:T(8,128)(2,1)S(1)}, u32[]{:S(2)}, u32[]{:S(2)}) collective-permute-start(bf16[16,6528]{1,0:T(8,128)(2,1)S(1)} %collective-permute-done.6.refs_6_), channel_id=1, source_target_pairs={{0,2},{2,4},{4,6},{6,7},{7,5},{5,3},{3,1},{1,0},{8,10},{10,12},{12... | collective-permute-start | bytes 626696 | tf_op jit(solution)/shard_map/ppermute | solution.py:228
  13.9 2.4 %collective-permute-done.refs_4_ = bf16[16,6528]{1,0:T(8,128)(2,1)S(1)} collective-permute-done((bf16[16,6528]{1,0:T(8,128)(2,1)S(1)}, bf16[16,6528]{1,0:T(8,128)(2,1)S(1)}, u32[]{:S(2)}, u32[]{:S(2)}) %collective-permute-start) | collective-permute-done | bytes 208928 | tf_op jit(solution)/shard_map/ppermute | solution.py:237
  16.3 1.5 %collective-permute-start.1 = (bf16[16,6528]{1,0:T(8,128)(2,1)S(1)}, bf16[16,6528]{1,0:T(8,128)(2,1)S(1)}, u32[]{:S(2)}, u32[]{:S(2)}) collective-permute-start(bf16[16,6528]{1,0:T(8,128)(2,1)S(1)} %collective-permute-done.refs_4_), channel_id=1, source_target_pairs={{2,0},{4,2},{6,4},{7,6},{5,7},{3,5},{1,3},{0,1},{10,8},{12,10},{14... | collective-permute-start | bytes 626696 | tf_op jit(solution)/shard_map/ppermute | solution.py:230
  17.8 0.0 collective-permute-done.3.refs_5_
  17.8 0.5 %collective-permute-start.4 = (bf16[16,6528]{1,0:T(8,128)(2,1)S(1)}, bf16[16,6528]{1,0:T(8,128)(2,1)S(1)}, u32[]{:S(2)}, u32[]{:S(2)}) collective-permute-start(bf16[16,6528]{1,0:T(8,128)(2,1)S(1)} %collective-permute-done.3.refs_5_), channel_id=1, source_target_pairs={{0,2},{2,4},{4,6},{6,7},{7,5},{5,3},{3,1},{1,0},{8,10},{10,12},{12... | collective-permute-start | bytes 626696 | tf_op jit(solution)/shard_map/ppermute | solution.py:229
  18.3 0.6 %collective-permute-start.12 = (bf16[16,6528]{1,0:T(8,128)(2,1)S(1)}, bf16[16,6528]{1,0:T(8,128)(2,1)S(1)}, u32[]{:S(2)}, u32[]{:S(2)}) collective-permute-start(bf16[16,6528]{1,0:T(8,128)(2,1)S(1)} %get-tuple-element.11), channel_id=1, source_target_pairs={{0,24},{1,25},{2,26},{3,27},{4,28},{5,29},{6,30},{7,31},{8,16},{9,... | collective-permute-start | bytes 626696 | tf_op jit(solution)/shard_map/ppermute | solution.py:222
  19.0 1.8 %collective-permute-done.10.refs_3_ = bf16[16,6528]{1,0:T(8,128)(2,1)S(1)} collective-permute-done((bf16[16,6528]{1,0:T(8,128)(2,1)S(1)}, bf16[16,6528]{1,0:T(8,128)(2,1)S(1)}, u32[]{:S(2)}, u32[]{:S(2)}) %collective-permute-start.10) | collective-permute-done | bytes 208928 | tf_op jit(solution)/shard_map/ppermute | solution.py:227
  20.8 1.5 %collective-permute-start.11 = (bf16[16,6528]{1,0:T(8,128)(2,1)S(1)}, bf16[16,6528]{1,0:T(8,128)(2,1)S(1)}, u32[]{:S(2)}, u32[]{:S(2)}) collective-permute-start(bf16[16,6528]{1,0:T(8,128)(2,1)S(1)} %collective-permute-done.10.refs_3_), channel_id=1, source_target_pairs={{2,0},{4,2},{6,4},{7,6},{5,7},{3,5},{1,3},{0,1},{10,8},{12,10},{14... | collective-permute-start | bytes 626696 | tf_op jit(solution)/shard_map/ppermute | solution.py:227
  22.3 0.0 collective-permute-done.7.refs_2_
  22.3 0.5 %collective-permute-start.8 = (bf16[16,6528]{1,0:T(8,128)(2,1)S(1)}, bf16[16,6528]{1,0:T(8,128)(2,1)S(1)}, u32[]{:S(2)}, u32[]{:S(2)}) collective-permute-start(bf16[16,6528]{1,0:T(8,128)(2,1)S(1)} %collective-permute-done.7.refs_2_), channel_id=1, source_target_pairs={{0,2},{2,4},{4,6},{6,7},{7,5},{5,3},{3,1},{1,0},{8,10},{10,12},{12... | collective-permute-start | bytes 626696 | tf_op jit(solution)/shard_map/ppermute | solution.py:228
  22.8 2.4 %collective-permute-done.1.refs_0_ = bf16[16,6528]{1,0:T(8,128)(2,1)S(1)} collective-permute-done((bf16[16,6528]{1,0:T(8,128)(2,1)S(1)}, bf16[16,6528]{1,0:T(8,128)(2,1)S(1)}, u32[]{:S(2)}, u32[]{:S(2)}) %collective-permute-start.1) | collective-permute-done | bytes 208928 | tf_op jit(solution)/shard_map/ppermute | solution.py:230
  25.3 1.5 %collective-permute-start.2 = (bf16[16,6528]{1,0:T(8,128)(2,1)S(1)}, bf16[16,6528]{1,0:T(8,128)(2,1)S(1)}, u32[]{:S(2)}, u32[]{:S(2)}) collective-permute-start(bf16[16,6528]{1,0:T(8,128)(2,1)S(1)} %collective-permute-done.1.refs_0_), channel_id=1, source_target_pairs={{2,0},{4,2},{6,4},{7,6},{5,7},{3,5},{1,3},{0,1},{10,8},{12,10},{14... | collective-permute-start | bytes 626696 | tf_op jit(solution)/shard_map/ppermute | solution.py:230
  26.7 0.0 collective-permute-done.4.refs_1_
  26.8 0.5 %collective-permute-start.5 = (bf16[16,6528]{1,0:T(8,128)(2,1)S(1)}, bf16[16,6528]{1,0:T(8,128)(2,1)S(1)}, u32[]{:S(2)}, u32[]{:S(2)}) collective-permute-start(bf16[16,6528]{1,0:T(8,128)(2,1)S(1)} %collective-permute-done.4.refs_1_), channel_id=1, source_target_pairs={{0,2},{2,4},{4,6},{6,7},{7,5},{5,3},{3,1},{1,0},{8,10},{10,12},{12... | collective-permute-start | bytes 626696 | tf_op jit(solution)/shard_map/ppermute | solution.py:229
  27.3 0.0 collective-permute-done.12.refs_8_
  27.3 0.0 copy-done
  27.3 1.8 %grad_part.1.refs_9_ = f32[256,3072]{1,0:T(8,128)S(1)} custom-call(bf16[16,6528]{1,0:T(8,128)(2,1)S(1)} %collective-permute-done.1.refs_0_, bf16[16,6528]{1,0:T(8,128)(2,1)S(1)} %collective-permute-done.4.refs_1_, bf16[16,6528]{1,0:T(8,128)(2,1)S(1)} %collective-permute-done.7.refs_2_, bf16[16,6528]{1,0:T(8,128)(2,1)S(1)} %collective-permute-done.10.refs_3_, ...), custom_call_target="tpu_custom_call" | custom-call | flops 534773760 | bytes 3661824 | tf_op jit(solution)/shard_map/grad_part/pallas_call | solution.py:164
  29.1 0.6 %collective-permute-done.11.refs_3_ = bf16[16,6528]{1,0:T(8,128)(2,1)S(1)} collective-permute-done((bf16[16,6528]{1,0:T(8,128)(2,1)S(1)}, bf16[16,6528]{1,0:T(8,128)(2,1)S(1)}, u32[]{:S(2)}, u32[]{:S(2)}) %collective-permute-start.11) | collective-permute-done | bytes 208928 | tf_op jit(solution)/shard_map/ppermute | solution.py:227
  29.7 1.5 %collective-permute-start.13 = (bf16[16,6528]{1,0:T(8,128)(2,1)S(1)}, bf16[16,6528]{1,0:T(8,128)(2,1)S(1)}, u32[]{:S(2)}, u32[]{:S(2)}) collective-permute-start(bf16[16,6528]{1,0:T(8,128)(2,1)S(1)} %collective-permute-done.11.refs_3_), channel_id=1, source_target_pairs={{2,0},{4,2},{6,4},{7,6},{5,7},{3,5},{1,3},{0,1},{10,8},{12,10},{14... | collective-permute-start | bytes 626696 | tf_op jit(solution)/shard_map/ppermute | solution.py:251
  31.2 0.0 collective-permute-done.8.refs_2_
  31.2 0.6 %collective-permute-start.16 = (bf16[16,3456]{1,0:T(8,128)(2,1)S(1)}, bf16[16,3456]{1,0:T(8,128)(2,1)S(1)}, u32[]{:S(2)}, u32[]{:S(2)}) collective-permute-start(bf16[16,3456]{1,0:T(8,128)(2,1)S(1)} %slice.14), channel_id=1, source_target_pairs={{0,2},{2,4},{4,6},{6,7},{7,5},{5,3},{3,1},{1,0},{8,10},{10,12},{12... | collective-permute-start | bytes 331784 | tf_op jit(solution)/shard_map/ppermute | solution.py:252
  31.8 1.6 %collective-permute-start.15 = (bf16[16,2304]{1,0:T(8,128)(2,1)S(1)}, bf16[16,2304]{1,0:T(8,128)(2,1)S(1)}, u32[]{:S(2)}, u32[]{:S(2)}) collective-permute-start(bf16[16,2304]{1,0:T(8,128)(2,1)S(1)} %slice.13), channel_id=1, source_target_pairs={{0,2},{2,4},{4,6},{6,7},{7,5},{5,3},{3,1},{1,0},{8,10},{10,12},{12... | collective-permute-start | bytes 221192 | tf_op jit(solution)/shard_map/ppermute | solution.py:258
  33.4 0.8 %collective-permute-done.2.refs_0_ = bf16[16,6528]{1,0:T(8,128)(2,1)S(1)} collective-permute-done((bf16[16,6528]{1,0:T(8,128)(2,1)S(1)}, bf16[16,6528]{1,0:T(8,128)(2,1)S(1)}, u32[]{:S(2)}, u32[]{:S(2)}) %collective-permute-start.2) | collective-permute-done | bytes 208928 | tf_op jit(solution)/shard_map/ppermute | solution.py:230
  34.2 1.5 %collective-permute-start.14 = (bf16[16,768]{1,0:T(8,128)(2,1)S(1)}, bf16[16,768]{1,0:T(8,128)(2,1)S(1)}, u32[]{:S(2)}, u32[]{:S(2)}) collective-permute-start(bf16[16,768]{1,0:T(8,128)(2,1)S(1)} %slice.12), channel_id=1, source_target_pairs={{2,0},{4,2},{6,4},{7,6},{5,7},{3,5},{1,3},{0,1},{10,8},{12,10},{14... | collective-permute-start | bytes 73736 | tf_op jit(solution)/shard_map/ppermute | solution.py:257
  35.7 0.0 collective-permute-done.5.refs_1_
  35.7 2.4 %collective-permute-done.16.refs_5_ = bf16[16,3456]{1,0:T(8,128)(2,1)S(1)} collective-permute-done((bf16[16,3456]{1,0:T(8,128)(2,1)S(1)}, bf16[16,3456]{1,0:T(8,128)(2,1)S(1)}, u32[]{:S(2)}, u32[]{:S(2)}) %collective-permute-start.16) | collective-permute-done | bytes 110624 | tf_op jit(solution)/shard_map/ppermute | solution.py:252
  38.1 0.6 %collective-permute-done.13.refs_4_ = bf16[16,6528]{1,0:T(8,128)(2,1)S(1)} collective-permute-done((bf16[16,6528]{1,0:T(8,128)(2,1)S(1)}, bf16[16,6528]{1,0:T(8,128)(2,1)S(1)}, u32[]{:S(2)}, u32[]{:S(2)}) %collective-permute-start.13) | collective-permute-done | bytes 208928 | tf_op jit(solution)/shard_map/ppermute | solution.py:251
  38.7 0.5 %active_late.1 = (bf16[102,256]{1,0:T(8,128)(2,1)S(1)}, bf16[6,3072]{1,0:T(8,128)(2,1)S(1)}) custom-call(bf16[16,6528]{1,0:T(8,128)(2,1)S(1)} %collective-permute-done.2.refs_0_, bf16[16,6528]{1,0:T(8,128)(2,1)S(1)} %collective-permute-done.5.refs_1_, bf16[16,6528]{1,0:T(8,128)(2,1)S(1)} %collective-permute-done.8.refs_2_, ...), custom_call_target="tpu_custom_call" | custom-call | flops 160432128 | bytes 2727936 | tf_op jit(solution)/shard_map/active_late/pallas_call | solution.py:164
  39.2 0.0 collective-permute-done.14.refs_5_
  39.2 0.2 collective-permute-done.15.refs_6_
  39.4 1.5 %grad_sum.1 = bf16[256,3072]{1,0:T(8,128)(2,1)} custom-call(bf16[16,6528]{1,0:T(8,128)(2,1)S(1)} %collective-permute-done.2.refs_0_, bf16[16,6528]{1,0:T(8,128)(2,1)S(1)} %collective-permute-done.5.refs_1_, bf16[16,6528]{1,0:T(8,128)(2,1)S(1)} %collective-permute-done.8.refs_2_, bf16[16,6528]{1,0:T(8,128)(2,1)S(1)} %collective-permute-done.11.refs_3_, ...), custom_call_target="tpu_custom_call" | custom-call | flops 160432128 | bytes 4377600 | tf_op jit(solution)/shard_map/grad_sum/pallas_call | solution.py:164
  (3 shorter events, 0.0 us)
Async XLA Ops:
  0.0 27.3 %copy-start = (bf16[1,3072,256]{2,1,0:T(8,128)(2,1)S(1)}, bf16[1,3072,256]{2,1,0:T(8,128)(2,1)}, u32[]{:S(2)}) copy-start(bf16[1,3072,256]{2,1,0:T(8,128)(2,1)} %param.17) | copy-start | bytes 4718596
  1.9 8.9 %collective-permute-start.9 = (bf16[16,6528]{1,0:T(8,128)(2,1)S(1)}, bf16[16,6528]{1,0:T(8,128)(2,1)S(1)}, u32[]{:S(2)}, u32[]{:S(2)}) collective-permute-start(bf16[16,6528]{1,0:T(8,128)(2,1)S(1)} %get-tuple-element.11), channel_id=1, source_target_pairs={{2,24},{4,26},{6,28},{7,30},{5,31},{3,29},{1,27},{0,25},{10,16},{1... | collective-permute-start | bytes 626696 | tf_op jit(solution)/shard_map/ppermute | solution.py:222
  5.3 8.0 %collective-permute-start.6 = (bf16[16,6528]{1,0:T(8,128)(2,1)S(1)}, bf16[16,6528]{1,0:T(8,128)(2,1)S(1)}, u32[]{:S(2)}, u32[]{:S(2)}) collective-permute-start(bf16[16,6528]{1,0:T(8,128)(2,1)S(1)} %get-tuple-element.10.refs_9_), channel_id=1, source_target_pairs={{0,2},{2,4},{4,6},{6,7},{7,5},{5,3},{3,1},{1,0},{8,10},{10,12},{12... | collective-permute-start | bytes 626696 | tf_op jit(solution)/shard_map/ppermute | solution.py:235
  5.8 10.5 %collective-permute-start = (bf16[16,6528]{1,0:T(8,128)(2,1)S(1)}, bf16[16,6528]{1,0:T(8,128)(2,1)S(1)}, u32[]{:S(2)}, u32[]{:S(2)}) collective-permute-start(bf16[16,6528]{1,0:T(8,128)(2,1)S(1)} %get-tuple-element.10.refs_9_), channel_id=1, source_target_pairs={{2,0},{4,2},{6,4},{7,6},{5,7},{3,5},{1,3},{0,1},{10,8},{12,10},{14... | collective-permute-start | bytes 626696 | tf_op jit(solution)/shard_map/ppermute | solution.py:237
  7.3 10.5 %collective-permute-start.3 = (bf16[16,6528]{1,0:T(8,128)(2,1)S(1)}, bf16[16,6528]{1,0:T(8,128)(2,1)S(1)}, u32[]{:S(2)}, u32[]{:S(2)}) collective-permute-start(bf16[16,6528]{1,0:T(8,128)(2,1)S(1)} %get-tuple-element.11), channel_id=1, source_target_pairs={{0,26},{2,28},{4,30},{6,31},{7,29},{5,27},{3,25},{1,24},{8,18},{10... | collective-permute-start | bytes 626696 | tf_op jit(solution)/shard_map/ppermute | solution.py:222
  10.8 9.9 %collective-permute-start.10 = (bf16[16,6528]{1,0:T(8,128)(2,1)S(1)}, bf16[16,6528]{1,0:T(8,128)(2,1)S(1)}, u32[]{:S(2)}, u32[]{:S(2)}) collective-permute-start(bf16[16,6528]{1,0:T(8,128)(2,1)S(1)} %collective-permute-done.9.refs_7_), channel_id=1, source_target_pairs={{2,0},{4,2},{6,4},{7,6},{5,7},{3,5},{1,3},{0,1},{10,8},{12,10},{14... | collective-permute-start | bytes 626696 | tf_op jit(solution)/shard_map/ppermute | solution.py:227
  13.3 9.0 %collective-permute-start.7 = (bf16[16,6528]{1,0:T(8,128)(2,1)S(1)}, bf16[16,6528]{1,0:T(8,128)(2,1)S(1)}, u32[]{:S(2)}, u32[]{:S(2)}) collective-permute-start(bf16[16,6528]{1,0:T(8,128)(2,1)S(1)} %collective-permute-done.6.refs_6_), channel_id=1, source_target_pairs={{0,2},{2,4},{4,6},{6,7},{7,5},{5,3},{3,1},{1,0},{8,10},{10,12},{12... | collective-permute-start | bytes 626696 | tf_op jit(solution)/shard_map/ppermute | solution.py:228
  16.3 9.0 %collective-permute-start.1 = (bf16[16,6528]{1,0:T(8,128)(2,1)S(1)}, bf16[16,6528]{1,0:T(8,128)(2,1)S(1)}, u32[]{:S(2)}, u32[]{:S(2)}) collective-permute-start(bf16[16,6528]{1,0:T(8,128)(2,1)S(1)} %collective-permute-done.refs_4_), channel_id=1, source_target_pairs={{2,0},{4,2},{6,4},{7,6},{5,7},{3,5},{1,3},{0,1},{10,8},{12,10},{14... | collective-permute-start | bytes 626696 | tf_op jit(solution)/shard_map/ppermute | solution.py:230
  17.8 9.0 %collective-permute-start.4 = (bf16[16,6528]{1,0:T(8,128)(2,1)S(1)}, bf16[16,6528]{1,0:T(8,128)(2,1)S(1)}, u32[]{:S(2)}, u32[]{:S(2)}) collective-permute-start(bf16[16,6528]{1,0:T(8,128)(2,1)S(1)} %collective-permute-done.3.refs_5_), channel_id=1, source_target_pairs={{0,2},{2,4},{4,6},{6,7},{7,5},{5,3},{3,1},{1,0},{8,10},{10,12},{12... | collective-permute-start | bytes 626696 | tf_op jit(solution)/shard_map/ppermute | solution.py:229
  18.3 9.0 %collective-permute-start.12 = (bf16[16,6528]{1,0:T(8,128)(2,1)S(1)}, bf16[16,6528]{1,0:T(8,128)(2,1)S(1)}, u32[]{:S(2)}, u32[]{:S(2)}) collective-permute-start(bf16[16,6528]{1,0:T(8,128)(2,1)S(1)} %get-tuple-element.11), channel_id=1, source_target_pairs={{0,24},{1,25},{2,26},{3,27},{4,28},{5,29},{6,30},{7,31},{8,16},{9,... | collective-permute-start | bytes 626696 | tf_op jit(solution)/shard_map/ppermute | solution.py:222
  20.8 9.0 %collective-permute-start.11 = (bf16[16,6528]{1,0:T(8,128)(2,1)S(1)}, bf16[16,6528]{1,0:T(8,128)(2,1)S(1)}, u32[]{:S(2)}, u32[]{:S(2)}) collective-permute-start(bf16[16,6528]{1,0:T(8,128)(2,1)S(1)} %collective-permute-done.10.refs_3_), channel_id=1, source_target_pairs={{2,0},{4,2},{6,4},{7,6},{5,7},{3,5},{1,3},{0,1},{10,8},{12,10},{14... | collective-permute-start | bytes 626696 | tf_op jit(solution)/shard_map/ppermute | solution.py:227
  22.3 9.0 %collective-permute-start.8 = (bf16[16,6528]{1,0:T(8,128)(2,1)S(1)}, bf16[16,6528]{1,0:T(8,128)(2,1)S(1)}, u32[]{:S(2)}, u32[]{:S(2)}) collective-permute-start(bf16[16,6528]{1,0:T(8,128)(2,1)S(1)} %collective-permute-done.7.refs_2_), channel_id=1, source_target_pairs={{0,2},{2,4},{4,6},{6,7},{7,5},{5,3},{3,1},{1,0},{8,10},{10,12},{12... | collective-permute-start | bytes 626696 | tf_op jit(solution)/shard_map/ppermute | solution.py:228
  25.3 9.0 %collective-permute-start.2 = (bf16[16,6528]{1,0:T(8,128)(2,1)S(1)}, bf16[16,6528]{1,0:T(8,128)(2,1)S(1)}, u32[]{:S(2)}, u32[]{:S(2)}) collective-permute-start(bf16[16,6528]{1,0:T(8,128)(2,1)S(1)} %collective-permute-done.1.refs_0_), channel_id=1, source_target_pairs={{2,0},{4,2},{6,4},{7,6},{5,7},{3,5},{1,3},{0,1},{10,8},{12,10},{14... | collective-permute-start | bytes 626696 | tf_op jit(solution)/shard_map/ppermute | solution.py:230
  26.8 9.0 %collective-permute-start.5 = (bf16[16,6528]{1,0:T(8,128)(2,1)S(1)}, bf16[16,6528]{1,0:T(8,128)(2,1)S(1)}, u32[]{:S(2)}, u32[]{:S(2)}) collective-permute-start(bf16[16,6528]{1,0:T(8,128)(2,1)S(1)} %collective-permute-done.4.refs_1_), channel_id=1, source_target_pairs={{0,2},{2,4},{4,6},{6,7},{7,5},{5,3},{3,1},{1,0},{8,10},{10,12},{12... | collective-permute-start | bytes 626696 | tf_op jit(solution)/shard_map/ppermute | solution.py:229
  29.7 9.0 %collective-permute-start.13 = (bf16[16,6528]{1,0:T(8,128)(2,1)S(1)}, bf16[16,6528]{1,0:T(8,128)(2,1)S(1)}, u32[]{:S(2)}, u32[]{:S(2)}) collective-permute-start(bf16[16,6528]{1,0:T(8,128)(2,1)S(1)} %collective-permute-done.11.refs_3_), channel_id=1, source_target_pairs={{2,0},{4,2},{6,4},{7,6},{5,7},{3,5},{1,3},{0,1},{10,8},{12,10},{14... | collective-permute-start | bytes 626696 | tf_op jit(solution)/shard_map/ppermute | solution.py:251
  31.2 6.8 %collective-permute-start.16 = (bf16[16,3456]{1,0:T(8,128)(2,1)S(1)}, bf16[16,3456]{1,0:T(8,128)(2,1)S(1)}, u32[]{:S(2)}, u32[]{:S(2)}) collective-permute-start(bf16[16,3456]{1,0:T(8,128)(2,1)S(1)} %slice.14), channel_id=1, source_target_pairs={{0,2},{2,4},{4,6},{6,7},{7,5},{5,3},{3,1},{1,0},{8,10},{10,12},{12... | collective-permute-start | bytes 331784 | tf_op jit(solution)/shard_map/ppermute | solution.py:252
  31.8 7.5 %collective-permute-start.15 = (bf16[16,2304]{1,0:T(8,128)(2,1)S(1)}, bf16[16,2304]{1,0:T(8,128)(2,1)S(1)}, u32[]{:S(2)}, u32[]{:S(2)}) collective-permute-start(bf16[16,2304]{1,0:T(8,128)(2,1)S(1)} %slice.13), channel_id=1, source_target_pairs={{0,2},{2,4},{4,6},{6,7},{7,5},{5,3},{3,1},{1,0},{8,10},{10,12},{12... | collective-permute-start | bytes 221192 | tf_op jit(solution)/shard_map/ppermute | solution.py:258
  34.2 5.0 %collective-permute-start.14 = (bf16[16,768]{1,0:T(8,128)(2,1)S(1)}, bf16[16,768]{1,0:T(8,128)(2,1)S(1)}, u32[]{:S(2)}, u32[]{:S(2)}) collective-permute-start(bf16[16,768]{1,0:T(8,128)(2,1)S(1)} %slice.12), channel_id=1, source_target_pairs={{2,0},{4,2},{6,4},{7,6},{5,7},{3,5},{1,3},{0,1},{10,8},{12,10},{14... | collective-permute-start | bytes 73736 | tf_op jit(solution)/shard_map/ppermute | solution.py:257

commit v6 on v4

--- a/solution.py
+++ b/solution.py
@@ -205,34 +205,38 @@
     right = [(cycle[i], cycle[(i + 1) % n]) for i in range(n)]
     left = [(b, a) for a, b in right]
 
-    def mirrored(block, moves):
-        pairs = [(p * n + a, (n_pipe - 1 - p) * n + b) for p in range(n_pipe) for a, b in moves]
+    def move(block, moves, mirrored=False):
+        pairs = []
+        for p in range(n_pipe):
+            turned = p % 2 != 2 * p // n_pipe
+            to = n_pipe - 1 - p if mirrored else p
+            pairs += [(p * n + (b if turned else a), to * n + (a if turned else b)) for a, b in moves]
         return lax.ppermute(block, ("pipe", "expert"), pairs)
 
     def turn(at):
         up_left, down_right, up_right, down_left = at
         return (
-            lax.ppermute(up_left, "expert", left),
-            lax.ppermute(down_right, "expert", right),
-            lax.ppermute(up_right, "expert", right),
-            lax.ppermute(down_left, "expert", left),
+            move(up_left, left),
+            move(down_right, right),
+            move(up_right, right),
+            move(down_left, left),
         )
 
     at = (
-        mirrored(up, left),
-        lax.ppermute(down, "expert", right),
-        mirrored(up, right),
-        lax.ppermute(down, "expert", left),
+        move(up, left, mirrored=True),
+        move(down, right),
+        move(up, right, mirrored=True),
+        move(down, left),
     )
     got = [*at]
     for _ in range(1, (n - 1) // 2):
         at = turn(at)
         got += at
     firsts, seconds = (
-        (lax.ppermute(l, "expert", left), lax.ppermute(r, "expert", right))
+        (move(l, left), move(r, right))
         for l, r in ((at[0][:, :cut], at[1][:, :cut]), (at[0][:, cut:], at[1][:, cut:]))
     )
-    own = mirrored(up, [(e, e) for e in range(n)])
+    own = move(up, [(e, e) for e in range(n)], mirrored=True)
     return [*reversed(got), own, down], firsts, seconds
 
 

time: 41.5 us -> 40.6 us (0.978)
  waiting for transfers between devices: 15.7 us -> 12.9 us
  starting transfers between devices: 19.7 us -> 21.5 us
    ppermute x17, waiting for transfers between devices: 15.7 us -> 12.9 us  [move(): return lax.ppermute(block, ('pipe', 'expert'), pairs)]
    ppermute x17, starting transfers between devices: 19.7 us -> 21.5 us  [move(): return lax.ppermute(block, ('pipe', 'expert'), pairs)]
  transfers between devices with their start and end apart: 17 -> 17, of which waited for: 10 -> 12; matrix products, arithmetic and copies ran while one was open for 0% -> 0% of each run, Pallas kernels for 6% -> 6%
where the time goes in v6:
time: 40.6 us; the launch traced here: 40.4 us
  starting transfers between devices  21.5 us (53%)
  waiting for transfers between devices  12.9 us (32%)
  Pallas kernels  5.86 us (14%)
    ppermute x17, starting transfers between devices, move(): return lax.ppermute(block, ('pipe', 'expert'), pairs)  21.5 us
    ppermute x17, waiting for transfers between devices, move(): return lax.ppermute(block, ('pipe', 'expert'), pairs)  12.9 us
    pallas_call x3, Pallas kernels, local_call(): pl.pallas_call(kernel, out_shape=outs, in_specs=[pl.BlockSpec(memory_spac...  3.97 us
    pallas_call x1, Pallas kernels, pack(): pl.pallas_call(pack_kernel, out_shape=(payload, payload), in_specs=[pl.Bl...  1.89 us
  transfers between devices with their start and end apart: 17, of which 12 were waited for; matrix products, arithmetic and copies ran while one was open for 0% of the time, Pallas kernels for 6%

profile of v6, /device:TPU:0, one launch (start us, length us, event | category | flops | bytes accessed | tf_op | source)
XLA Modules:
  0.0 40.4 jit_solution(4104097812661461887)
XLA Ops:
  0.0 0.0 copy-start
  0.0 1.9 %pack_slots.1 = (bf16[16,6528]{1,0:T(8,128)(2,1)S(1)}, bf16[16,6528]{1,0:T(8,128)(2,1)S(1)}) custom-call(bf16[64,3072]{1,0:T(8,128)(2,1)} %bitcast.20, bf16[64,3072]{1,0:T(8,128)(2,1)} %bitcast.21, bf16[2,64]{1,0:T(2,128)(2,1)} %bitcast.26, s32[2,64]{1,0:T(2,128)} %bitcast.24, bf16[64,3072]{1,0:T(8,128)(2,1)} %bitcast.22, bf16[64,3072]{1,0:T(8,128)(2,1)} %bitcast.23, ...), custom_call_target="tpu_custom_call" | custom-call | flops 50331648 | bytes 2359296 | tf_op jit(solution)/shard_map/pack_slots/pallas_call | solution.py:75
  1.9 3.4 %collective-permute-start = (bf16[16,6528]{1,0:T(8,128)(2,1)S(1)}, bf16[16,6528]{1,0:T(8,128)(2,1)S(1)}, u32[]{:S(2)}, u32[]{:S(2)}) collective-permute-start(bf16[16,6528]{1,0:T(8,128)(2,1)S(1)} %get-tuple-element.9), channel_id=1, source_target_pairs={{2,24},{4,26},{6,28},{7,30},{5,31},{3,29},{1,27},{0,25},{8,18},{10... | collective-permute-start | bytes 626696 | tf_op jit(solution)/shard_map/ppermute | solution.py:214
  5.3 0.5 %collective-permute-start.4 = (bf16[16,6528]{1,0:T(8,128)(2,1)S(1)}, bf16[16,6528]{1,0:T(8,128)(2,1)S(1)}, u32[]{:S(2)}, u32[]{:S(2)}) collective-permute-start(bf16[16,6528]{1,0:T(8,128)(2,1)S(1)} %get-tuple-element.10.refs_13_), channel_id=1, source_target_pairs={{0,2},{2,4},{4,6},{6,7},{7,5},{5,3},{3,1},{1,0},{10,8},{12,10},{14... | collective-permute-start | bytes 626696 | tf_op jit(solution)/shard_map/ppermute | solution.py:214
  5.8 1.5 %collective-permute-start.10 = (bf16[16,6528]{1,0:T(8,128)(2,1)S(1)}, bf16[16,6528]{1,0:T(8,128)(2,1)S(1)}, u32[]{:S(2)}, u32[]{:S(2)}) collective-permute-start(bf16[16,6528]{1,0:T(8,128)(2,1)S(1)} %get-tuple-element.10.refs_13_), channel_id=1, source_target_pairs={{2,0},{4,2},{6,4},{7,6},{5,7},{3,5},{1,3},{0,1},{8,10},{10,12},{12... | collective-permute-start | bytes 626696 | tf_op jit(solution)/shard_map/ppermute | solution.py:214
  7.3 0.0 collective-permute-start.13
  7.3 3.3 %collective-permute-done.refs_11_ = bf16[16,6528]{1,0:T(8,128)(2,1)S(1)} collective-permute-done((bf16[16,6528]{1,0:T(8,128)(2,1)S(1)}, bf16[16,6528]{1,0:T(8,128)(2,1)S(1)}, u32[]{:S(2)}, u32[]{:S(2)}) %collective-permute-start) | collective-permute-done | bytes 208928 | tf_op jit(solution)/shard_map/ppermute | solution.py:214
  10.6 2.7 %collective-permute-start.1 = (bf16[16,6528]{1,0:T(8,128)(2,1)S(1)}, bf16[16,6528]{1,0:T(8,128)(2,1)S(1)}, u32[]{:S(2)}, u32[]{:S(2)}) collective-permute-start(bf16[16,6528]{1,0:T(8,128)(2,1)S(1)} %collective-permute-done.refs_11_), channel_id=1, source_target_pairs={{2,0},{4,2},{6,4},{7,6},{5,7},{3,5},{1,3},{0,1},{8,10},{10,12},{12... | collective-permute-start | bytes 626696 | tf_op jit(solution)/shard_map/ppermute | solution.py:214
  13.3 0.2 collective-permute-done.4.refs_10_
  13.5 0.3 collective-permute-start.5
  13.8 1.5 %collective-permute-done.10.refs_8_ = bf16[16,6528]{1,0:T(8,128)(2,1)S(1)} collective-permute-done((bf16[16,6528]{1,0:T(8,128)(2,1)S(1)}, bf16[16,6528]{1,0:T(8,128)(2,1)S(1)}, u32[]{:S(2)}, u32[]{:S(2)}) %collective-permute-start.10) | collective-permute-done | bytes 208928 | tf_op jit(solution)/shard_map/ppermute | solution.py:214
  15.3 2.3 %collective-permute-start.11 = (bf16[16,6528]{1,0:T(8,128)(2,1)S(1)}, bf16[16,6528]{1,0:T(8,128)(2,1)S(1)}, u32[]{:S(2)}, u32[]{:S(2)}) collective-permute-start(bf16[16,6528]{1,0:T(8,128)(2,1)S(1)} %collective-permute-done.10.refs_8_), channel_id=1, source_target_pairs={{2,0},{4,2},{6,4},{7,6},{5,7},{3,5},{1,3},{0,1},{8,10},{10,12},{12... | collective-permute-start | bytes 626696 | tf_op jit(solution)/shard_map/ppermute | solution.py:214
  17.6 0.2 collective-permute-done.13.refs_9_
  17.7 0.0 collective-permute-start.14
  17.7 2.1 %collective-permute-done.1.refs_7_ = bf16[16,6528]{1,0:T(8,128)(2,1)S(1)} collective-permute-done((bf16[16,6528]{1,0:T(8,128)(2,1)S(1)}, bf16[16,6528]{1,0:T(8,128)(2,1)S(1)}, u32[]{:S(2)}, u32[]{:S(2)}) %collective-permute-start.1) | collective-permute-done | bytes 208928 | tf_op jit(solution)/shard_map/ppermute | solution.py:214
  19.8 2.3 %collective-permute-start.2 = (bf16[16,6528]{1,0:T(8,128)(2,1)S(1)}, bf16[16,6528]{1,0:T(8,128)(2,1)S(1)}, u32[]{:S(2)}, u32[]{:S(2)}) collective-permute-start(bf16[16,6528]{1,0:T(8,128)(2,1)S(1)} %collective-permute-done.1.refs_7_), channel_id=1, source_target_pairs={{2,0},{4,2},{6,4},{7,6},{5,7},{3,5},{1,3},{0,1},{8,10},{10,12},{12... | collective-permute-start | bytes 626696 | tf_op jit(solution)/shard_map/ppermute | solution.py:214
  22.0 0.4 collective-permute-done.5.refs_6_
  22.4 0.3 collective-permute-start.6
  22.7 0.0 collective-permute-start.16
  22.7 1.5 %collective-permute-done.11.refs_4_ = bf16[16,6528]{1,0:T(8,128)(2,1)S(1)} collective-permute-done((bf16[16,6528]{1,0:T(8,128)(2,1)S(1)}, bf16[16,6528]{1,0:T(8,128)(2,1)S(1)}, u32[]{:S(2)}, u32[]{:S(2)}) %collective-permute-start.11) | collective-permute-done | bytes 208928 | tf_op jit(solution)/shard_map/ppermute | solution.py:214
  24.2 2.3 %collective-permute-start.12 = (bf16[16,6528]{1,0:T(8,128)(2,1)S(1)}, bf16[16,6528]{1,0:T(8,128)(2,1)S(1)}, u32[]{:S(2)}, u32[]{:S(2)}) collective-permute-start(bf16[16,6528]{1,0:T(8,128)(2,1)S(1)} %collective-permute-done.11.refs_4_), channel_id=1, source_target_pairs={{2,0},{4,2},{6,4},{7,6},{5,7},{3,5},{1,3},{0,1},{8,10},{10,12},{12... | collective-permute-start | bytes 626696 | tf_op jit(solution)/shard_map/ppermute | solution.py:214
  26.5 0.4 collective-permute-done.14.refs_5_
  26.9 0.3 collective-permute-start.15
  27.2 1.5 %collective-permute-done.2.refs_3_ = bf16[16,6528]{1,0:T(8,128)(2,1)S(1)} collective-permute-done((bf16[16,6528]{1,0:T(8,128)(2,1)S(1)}, bf16[16,6528]{1,0:T(8,128)(2,1)S(1)}, u32[]{:S(2)}, u32[]{:S(2)}) %collective-permute-start.2) | collective-permute-done | bytes 208928 | tf_op jit(solution)/shard_map/ppermute | solution.py:214
  28.7 2.3 %collective-permute-start.8 = (bf16[16,3456]{1,0:T(8,128)(2,1)S(1)}, bf16[16,3456]{1,0:T(8,128)(2,1)S(1)}, u32[]{:S(2)}, u32[]{:S(2)}) collective-permute-start(bf16[16,3456]{1,0:T(8,128)(2,1)S(1)} %slice.18), channel_id=1, source_target_pairs={{2,0},{4,2},{6,4},{7,6},{5,7},{3,5},{1,3},{0,1},{8,10},{10,12},{12... | collective-permute-start | bytes 331784 | tf_op jit(solution)/shard_map/ppermute | solution.py:214
  31.0 0.3 collective-permute-done.6.refs_2_
  31.4 0.4 collective-permute-start.9
  31.8 0.0 collective-permute-done.16.refs_12_
  31.8 1.8 %collective-permute-start.3 = (bf16[16,3072]{1,0:T(8,128)(2,1)S(1)}, bf16[16,3072]{1,0:T(8,128)(2,1)S(1)}, u32[]{:S(2)}, u32[]{:S(2)}) collective-permute-start(bf16[16,3072]{1,0:T(8,128)(2,1)S(1)} %slice.16), channel_id=1, source_target_pairs={{2,0},{4,2},{6,4},{7,6},{5,7},{3,5},{1,3},{0,1},{8,10},{10,12},{12... | collective-permute-start | bytes 294920 | tf_op jit(solution)/shard_map/ppermute | solution.py:214
  33.5 0.0 collective-permute-done.12.refs_0_
  33.5 1.2 %collective-permute-start.7 = (bf16[16,3072]{1,0:T(8,128)(2,1)S(1)}, bf16[16,3072]{1,0:T(8,128)(2,1)S(1)}, u32[]{:S(2)}, u32[]{:S(2)}) collective-permute-start(bf16[16,3072]{1,0:T(8,128)(2,1)S(1)} %slice.17), channel_id=1, source_target_pairs={{0,2},{2,4},{4,6},{6,7},{7,5},{5,3},{3,1},{1,0},{10,8},{12,10},{14... | collective-permute-start | bytes 294920 | tf_op jit(solution)/shard_map/ppermute | solution.py:214
  34.8 1.1 %collective-permute-done.15.refs_1_ = bf16[16,6528]{1,0:T(8,128)(2,1)S(1)} collective-permute-done((bf16[16,6528]{1,0:T(8,128)(2,1)S(1)}, bf16[16,6528]{1,0:T(8,128)(2,1)S(1)}, u32[]{:S(2)}, u32[]{:S(2)}) %collective-permute-start.15) | collective-permute-done | bytes 208928 | tf_op jit(solution)/shard_map/ppermute | solution.py:214
  35.8 0.0 copy-done
  35.8 2.1 %grad_part.1.refs_4_ = f32[256,3072]{1,0:T(8,128)S(1)} custom-call(bf16[16,6528]{1,0:T(8,128)(2,1)S(1)} %collective-permute-done.12.refs_0_, bf16[16,6528]{1,0:T(8,128)(2,1)S(1)} %collective-permute-done.15.refs_1_, bf16[16,6528]{1,0:T(8,128)(2,1)S(1)} %collective-permute-done.6.refs_2_, bf16[16,6528]{1,0:T(8,128)(2,1)S(1)} %collective-permute-done.2.refs_3_, ...), custom_call_target="tpu_custom_call" | custom-call | flops 748683264 | bytes 4497408 | tf_op jit(solution)/shard_map/grad_part/pallas_call | solution.py:157
  37.9 0.0 collective-permute-done.8.refs_0_
  37.9 0.0 collective-permute-done.9.refs_1_
  37.9 0.4 %active_late.1 = (bf16[34,256]{1,0:T(8,128)(2,1)S(1)}, bf16[2,3072]{1,0:T(2,128)(2,1)S(1)}) custom-call(bf16[16,3456]{1,0:T(8,128)(2,1)S(1)} %collective-permute-done.8.refs_0_, bf16[16,3456]{1,0:T(8,128)(2,1)S(1)} %collective-permute-done.9.refs_1_, bf16[3072,256]{1,0:T(8,128)(2,1)S(1)} %bitcast.19), custom_call_target="tpu_custom_call" | custom-call | flops 53477376 | bytes 1794048 | tf_op jit(solution)/shard_map/active_late/pallas_call | solution.py:157
  38.4 0.0 collective-permute-done.3.refs_0_
  38.4 0.6 %collective-permute-done.7.refs_1_ = bf16[16,3072]{1,0:T(8,128)(2,1)S(1)} collective-permute-done((bf16[16,3072]{1,0:T(8,128)(2,1)S(1)}, bf16[16,3072]{1,0:T(8,128)(2,1)S(1)}, u32[]{:S(2)}, u32[]{:S(2)}) %collective-permute-start.7) | collective-permute-done | bytes 98336 | tf_op jit(solution)/shard_map/ppermute | solution.py:214
  39.0 1.5 %grad_sum.1 = bf16[256,3072]{1,0:T(8,128)(2,1)} custom-call(bf16[16,3072]{1,0:T(8,128)(2,1)S(1)} %collective-permute-done.3.refs_0_, bf16[16,3072]{1,0:T(8,128)(2,1)S(1)} %collective-permute-done.7.refs_1_, bf16[34,256]{1,0:T(8,128)(2,1)S(1)} %get-tuple-element.11.refs_2_, bf16[2,3072]{1,0:T(2,128)(2,1)S(1)} %get-tuple-element.12.refs_3_, ...), custom_call_target="tpu_custom_call" | custom-call | flops 53477376 | bytes 3372032 | tf_op jit(solution)/shard_map/grad_sum/pallas_call | solution.py:157
  (4 shorter events, 0.0 us)
Async XLA Ops:
  0.0 35.8 %copy-start = (bf16[1,3072,256]{2,1,0:T(8,128)(2,1)S(1)}, bf16[1,3072,256]{2,1,0:T(8,128)(2,1)}, u32[]{:S(2)}) copy-start(bf16[1,3072,256]{2,1,0:T(8,128)(2,1)} %param.17) | copy-start | bytes 4718596
  1.9 8.7 %collective-permute-start = (bf16[16,6528]{1,0:T(8,128)(2,1)S(1)}, bf16[16,6528]{1,0:T(8,128)(2,1)S(1)}, u32[]{:S(2)}, u32[]{:S(2)}) collective-permute-start(bf16[16,6528]{1,0:T(8,128)(2,1)S(1)} %get-tuple-element.9), channel_id=1, source_target_pairs={{2,24},{4,26},{6,28},{7,30},{5,31},{3,29},{1,27},{0,25},{8,18},{10... | collective-permute-start | bytes 626696 | tf_op jit(solution)/shard_map/ppermute | solution.py:214
  5.3 8.2 %collective-permute-start.4 = (bf16[16,6528]{1,0:T(8,128)(2,1)S(1)}, bf16[16,6528]{1,0:T(8,128)(2,1)S(1)}, u32[]{:S(2)}, u32[]{:S(2)}) collective-permute-start(bf16[16,6528]{1,0:T(8,128)(2,1)S(1)} %get-tuple-element.10.refs_13_), channel_id=1, source_target_pairs={{0,2},{2,4},{4,6},{6,7},{7,5},{5,3},{3,1},{1,0},{10,8},{12,10},{14... | collective-permute-start | bytes 626696 | tf_op jit(solution)/shard_map/ppermute | solution.py:214
  5.8 9.5 %collective-permute-start.10 = (bf16[16,6528]{1,0:T(8,128)(2,1)S(1)}, bf16[16,6528]{1,0:T(8,128)(2,1)S(1)}, u32[]{:S(2)}, u32[]{:S(2)}) collective-permute-start(bf16[16,6528]{1,0:T(8,128)(2,1)S(1)} %get-tuple-element.10.refs_13_), channel_id=1, source_target_pairs={{2,0},{4,2},{6,4},{7,6},{5,7},{3,5},{1,3},{0,1},{8,10},{10,12},{12... | collective-permute-start | bytes 626696 | tf_op jit(solution)/shard_map/ppermute | solution.py:214
  7.3 10.4 %collective-permute-start.13 = (bf16[16,6528]{1,0:T(8,128)(2,1)S(1)}, bf16[16,6528]{1,0:T(8,128)(2,1)S(1)}, u32[]{:S(2)}, u32[]{:S(2)}) collective-permute-start(bf16[16,6528]{1,0:T(8,128)(2,1)S(1)} %get-tuple-element.9), channel_id=1, source_target_pairs={{0,26},{2,28},{4,30},{6,31},{7,29},{5,27},{3,25},{1,24},{10,16},{1... | collective-permute-start | bytes 626696 | tf_op jit(solution)/shard_map/ppermute | solution.py:214
  10.6 9.2 %collective-permute-start.1 = (bf16[16,6528]{1,0:T(8,128)(2,1)S(1)}, bf16[16,6528]{1,0:T(8,128)(2,1)S(1)}, u32[]{:S(2)}, u32[]{:S(2)}) collective-permute-start(bf16[16,6528]{1,0:T(8,128)(2,1)S(1)} %collective-permute-done.refs_11_), channel_id=1, source_target_pairs={{2,0},{4,2},{6,4},{7,6},{5,7},{3,5},{1,3},{0,1},{8,10},{10,12},{12... | collective-permute-start | bytes 626696 | tf_op jit(solution)/shard_map/ppermute | solution.py:214
  13.5 9.0 %collective-permute-start.5 = (bf16[16,6528]{1,0:T(8,128)(2,1)S(1)}, bf16[16,6528]{1,0:T(8,128)(2,1)S(1)}, u32[]{:S(2)}, u32[]{:S(2)}) collective-permute-start(bf16[16,6528]{1,0:T(8,128)(2,1)S(1)} %collective-permute-done.4.refs_10_), channel_id=1, source_target_pairs={{0,2},{2,4},{4,6},{6,7},{7,5},{5,3},{3,1},{1,0},{10,8},{12,10},{14... | collective-permute-start | bytes 626696 | tf_op jit(solution)/shard_map/ppermute | solution.py:214
  15.3 9.0 %collective-permute-start.11 = (bf16[16,6528]{1,0:T(8,128)(2,1)S(1)}, bf16[16,6528]{1,0:T(8,128)(2,1)S(1)}, u32[]{:S(2)}, u32[]{:S(2)}) collective-permute-start(bf16[16,6528]{1,0:T(8,128)(2,1)S(1)} %collective-permute-done.10.refs_8_), channel_id=1, source_target_pairs={{2,0},{4,2},{6,4},{7,6},{5,7},{3,5},{1,3},{0,1},{8,10},{10,12},{12... | collective-permute-start | bytes 626696 | tf_op jit(solution)/shard_map/ppermute | solution.py:214
  17.7 9.2 %collective-permute-start.14 = (bf16[16,6528]{1,0:T(8,128)(2,1)S(1)}, bf16[16,6528]{1,0:T(8,128)(2,1)S(1)}, u32[]{:S(2)}, u32[]{:S(2)}) collective-permute-start(bf16[16,6528]{1,0:T(8,128)(2,1)S(1)} %collective-permute-done.13.refs_9_), channel_id=1, source_target_pairs={{0,2},{2,4},{4,6},{6,7},{7,5},{5,3},{3,1},{1,0},{10,8},{12,10},{14... | collective-permute-start | bytes 626696 | tf_op jit(solution)/shard_map/ppermute | solution.py:214
  19.8 9.0 %collective-permute-start.2 = (bf16[16,6528]{1,0:T(8,128)(2,1)S(1)}, bf16[16,6528]{1,0:T(8,128)(2,1)S(1)}, u32[]{:S(2)}, u32[]{:S(2)}) collective-permute-start(bf16[16,6528]{1,0:T(8,128)(2,1)S(1)} %collective-permute-done.1.refs_7_), channel_id=1, source_target_pairs={{2,0},{4,2},{6,4},{7,6},{5,7},{3,5},{1,3},{0,1},{8,10},{10,12},{12... | collective-permute-start | bytes 626696 | tf_op jit(solution)/shard_map/ppermute | solution.py:214
  22.4 9.0 %collective-permute-start.6 = (bf16[16,6528]{1,0:T(8,128)(2,1)S(1)}, bf16[16,6528]{1,0:T(8,128)(2,1)S(1)}, u32[]{:S(2)}, u32[]{:S(2)}) collective-permute-start(bf16[16,6528]{1,0:T(8,128)(2,1)S(1)} %collective-permute-done.5.refs_6_), channel_id=1, source_target_pairs={{0,2},{2,4},{4,6},{6,7},{7,5},{5,3},{3,1},{1,0},{10,8},{12,10},{14... | collective-permute-start | bytes 626696 | tf_op jit(solution)/shard_map/ppermute | solution.py:214
  22.7 9.0 %collective-permute-start.16 = (bf16[16,6528]{1,0:T(8,128)(2,1)S(1)}, bf16[16,6528]{1,0:T(8,128)(2,1)S(1)}, u32[]{:S(2)}, u32[]{:S(2)}) collective-permute-start(bf16[16,6528]{1,0:T(8,128)(2,1)S(1)} %get-tuple-element.9), channel_id=1, source_target_pairs={{0,24},{1,25},{2,26},{3,27},{4,28},{5,29},{6,30},{7,31},{8,16},{9,... | collective-permute-start | bytes 626696 | tf_op jit(solution)/shard_map/ppermute | solution.py:214
  24.2 9.3 %collective-permute-start.12 = (bf16[16,6528]{1,0:T(8,128)(2,1)S(1)}, bf16[16,6528]{1,0:T(8,128)(2,1)S(1)}, u32[]{:S(2)}, u32[]{:S(2)}) collective-permute-start(bf16[16,6528]{1,0:T(8,128)(2,1)S(1)} %collective-permute-done.11.refs_4_), channel_id=1, source_target_pairs={{2,0},{4,2},{6,4},{7,6},{5,7},{3,5},{1,3},{0,1},{8,10},{10,12},{12... | collective-permute-start | bytes 626696 | tf_op jit(solution)/shard_map/ppermute | solution.py:214
  26.9 9.0 %collective-permute-start.15 = (bf16[16,6528]{1,0:T(8,128)(2,1)S(1)}, bf16[16,6528]{1,0:T(8,128)(2,1)S(1)}, u32[]{:S(2)}, u32[]{:S(2)}) collective-permute-start(bf16[16,6528]{1,0:T(8,128)(2,1)S(1)} %collective-permute-done.14.refs_5_), channel_id=1, source_target_pairs={{0,2},{2,4},{4,6},{6,7},{7,5},{5,3},{3,1},{1,0},{10,8},{12,10},{14... | collective-permute-start | bytes 626696 | tf_op jit(solution)/shard_map/ppermute | solution.py:214
  28.7 9.2 %collective-permute-start.8 = (bf16[16,3456]{1,0:T(8,128)(2,1)S(1)}, bf16[16,3456]{1,0:T(8,128)(2,1)S(1)}, u32[]{:S(2)}, u32[]{:S(2)}) collective-permute-start(bf16[16,3456]{1,0:T(8,128)(2,1)S(1)} %slice.18), channel_id=1, source_target_pairs={{2,0},{4,2},{6,4},{7,6},{5,7},{3,5},{1,3},{0,1},{8,10},{10,12},{12... | collective-permute-start | bytes 331784 | tf_op jit(solution)/shard_map/ppermute | solution.py:214
  31.4 6.6 %collective-permute-start.9 = (bf16[16,3456]{1,0:T(8,128)(2,1)S(1)}, bf16[16,3456]{1,0:T(8,128)(2,1)S(1)}, u32[]{:S(2)}, u32[]{:S(2)}) collective-permute-start(bf16[16,3456]{1,0:T(8,128)(2,1)S(1)} %slice.19), channel_id=1, source_target_pairs={{0,2},{2,4},{4,6},{6,7},{7,5},{5,3},{3,1},{1,0},{10,8},{12,10},{14... | collective-permute-start | bytes 331784 | tf_op jit(solution)/shard_map/ppermute | solution.py:214
  31.8 6.6 %collective-permute-start.3 = (bf16[16,3072]{1,0:T(8,128)(2,1)S(1)}, bf16[16,3072]{1,0:T(8,128)(2,1)S(1)}, u32[]{:S(2)}, u32[]{:S(2)}) collective-permute-start(bf16[16,3072]{1,0:T(8,128)(2,1)S(1)} %slice.16), channel_id=1, source_target_pairs={{2,0},{4,2},{6,4},{7,6},{5,7},{3,5},{1,3},{0,1},{8,10},{10,12},{12... | collective-permute-start | bytes 294920 | tf_op jit(solution)/shard_map/ppermute | solution.py:214
  33.5 5.4 %collective-permute-start.7 = (bf16[16,3072]{1,0:T(8,128)(2,1)S(1)}, bf16[16,3072]{1,0:T(8,128)(2,1)S(1)}, u32[]{:S(2)}, u32[]{:S(2)}) collective-permute-start(bf16[16,3072]{1,0:T(8,128)(2,1)S(1)} %slice.17), channel_id=1, source_target_pairs={{0,2},{2,4},{4,6},{6,7},{7,5},{5,3},{3,1},{1,0},{10,8},{12,10},{14... | collective-permute-start | bytes 294920 | tf_op jit(solution)/shard_map/ppermute | solution.py:214

commit v7 on v6

--- a/solution.py
+++ b/solution.py
@@ -44,18 +44,33 @@
     return hit.astype(jnp.bfloat16), slot_gate
 
 
-def pack_kernel(*refs):
-    hbm, outs, held, sems = refs[:8], refs[8:10], refs[10:18], refs[18]
-    order = [2, 3, 6, 7, 4, 5, 0, 1]
-    copies = {i: pltpu.make_async_copy(hbm[i], held[i], sems.at[i]) for i in order}
-    for i in order:
-        copies[i].start()
+def is_turned(p, n_pipe):
+    return p % 2 != 2 * p // n_pipe
+
+
+def pack_kernel(n_pipe, *refs):
+    hbm, (lead, trail, up, down), held, sems = refs[:8], refs[8:12], refs[12:20], refs[20]
+    order = (2, 3, 6, 7, 0, 1, 4, 5)
+    turned = is_turned(lax.axis_index("pipe"), n_pipe)
+
+    def copies(swapped):
+        sources = hbm[:4] + hbm[4:] if swapped else hbm[4:] + hbm[:4]
+        return [pltpu.make_async_copy(sources[i], held[i], sems.at[i]) for i in order]
+
+    for swapped in (False, True):
+
+        @pl.when(turned == swapped)
+        def _():
+            for copy in copies(swapped):
+                copy.start()
+
+    waits = dict(zip(order, copies(False)))
     for i in order[:4]:
-        copies[i].wait()
+        waits[i].wait()
     places = [place(held[d + 2][...], held[d + 3][...]) for d in (0, 4)]
-    for d, (placing, slot_gate), out_ref in ((4, places[1], outs[1]), (0, places[0], outs[0])):
-        copies[d].wait()
-        copies[d + 1].wait()
+    for d, (placing, slot_gate), out_ref in ((0, places[0], lead), (4, places[1], trail)):
+        waits[d].wait()
+        waits[d + 1].wait()
         width = held[d].shape[1]
         seg = width // SEGS
         x = jnp.dot(placing, held[d][...], preferred_element_type=jnp.float32)
@@ -65,18 +80,24 @@
         tail = [x[MAIN : MAIN + 1, s * seg : (s + 1) * seg] for s in range(SEGS)]
         tail += [y[MAIN : MAIN + 1, s * seg : (s + 1) * seg] for s in range(SEGS)]
         out_ref[:, width : width + seg] = jnp.concatenate(tail, axis=0).astype(jnp.bfloat16)
-
-
-def pack(arrays):
+    for swapped, first, second in ((False, up, down), (True, down, up)):
+
+        @pl.when(turned == swapped)
+        def _():
+            first[...] = lead[...]
+            second[...] = trail[...]
+
+
+def pack(arrays, n_pipe):
     rows, width = arrays[0].shape
     seg = width // SEGS
     payload = pltpu.VMEM((MAIN, 2 * width + seg), jnp.bfloat16)
     arrays = [pltpu.with_memory_space_constraint(a, pltpu.HBM) for a in arrays]
     return pl.pallas_call(
-        pack_kernel,
-        out_shape=(payload, payload),
+        functools.partial(pack_kernel, n_pipe),
+        out_shape=(payload,) * 4,
         in_specs=[pl.BlockSpec(memory_space=pltpu.HBM)] * 8,
-        out_specs=(pl.BlockSpec(memory_space=pltpu.VMEM),) * 2,
+        out_specs=(pl.BlockSpec(memory_space=pltpu.VMEM),) * 4,
         scratch_shapes=[pltpu.VMEM(a.shape, a.dtype) for a in arrays]
         + [pltpu.SemaphoreType.DMA((8,))],
         compiler_params=pltpu.CompilerParams(vmem_limit_bytes=16 * 2**20),
@@ -140,11 +161,10 @@
         rows_y = jnp.concatenate([b[:, here] for b in blocks] + [tail_ref[:, here]], axis=0)
         made[:, here] = (before[:, here] + times(active, rows_y)).astype(jnp.bfloat16)
         copies.append(
-            pltpu.make_async_copy(made.at[:, here], out_ref.at[:, here], sems.at[s])
+            pltpu.make_async_copy(made.at[:, here], out_ref.at[:, here], sems.at[0])
         )
         copies[-1].start()
-    for copy in copies:
-        copy.wait()
+    pltpu.make_async_copy(made, out_ref, sems.at[0]).wait()
 
 
 def local_call(kernel, name, operands, outs, scratch=(), flops=0):
@@ -200,33 +220,27 @@
     return total
 
 
-def gather_both(down, up, n_pipe, cycle, cut):
+def gather_both(lead, trail, up, n_pipe, cycle, cut):
     n = len(cycle)
     right = [(cycle[i], cycle[(i + 1) % n]) for i in range(n)]
     left = [(b, a) for a, b in right]
 
-    def move(block, moves, mirrored=False):
+    def move(block, moves, mirrored=lambda turned: False):
         pairs = []
         for p in range(n_pipe):
-            turned = p % 2 != 2 * p // n_pipe
-            to = n_pipe - 1 - p if mirrored else p
+            turned = is_turned(p, n_pipe)
+            to = n_pipe - 1 - p if mirrored(turned) else p
             pairs += [(p * n + (b if turned else a), to * n + (a if turned else b)) for a, b in moves]
         return lax.ppermute(block, ("pipe", "expert"), pairs)
 
     def turn(at):
-        up_left, down_right, up_right, down_left = at
-        return (
-            move(up_left, left),
-            move(down_right, right),
-            move(up_right, right),
-            move(down_left, left),
-        )
+        return (move(at[0], left), move(at[1], right), move(at[2], right), move(at[3], left))
 
     at = (
-        move(up, left, mirrored=True),
-        move(down, right),
-        move(up, right, mirrored=True),
-        move(down, left),
+        move(lead, left, lambda turned: not turned),
+        move(trail, right, lambda turned: turned),
+        move(lead, right, lambda turned: not turned),
+        move(trail, left, lambda turned: turned),
     )
     got = [*at]
     for _ in range(1, (n - 1) // 2):
@@ -236,8 +250,8 @@
         (move(l, left), move(r, right))
         for l, r in ((at[0][:, :cut], at[1][:, :cut]), (at[0][:, cut:], at[1][:, cut:]))
     )
-    own = move(up, [(e, e) for e in range(n)], mirrored=True)
-    return [*reversed(got), own, down], firsts, seconds
+    own = move(up, [(e, e) for e in range(n)], lambda turned: True)
+    return [*reversed(got), own], firsts, seconds
 
 
 def body(
@@ -252,16 +266,17 @@
     w_in,
 ):
     n_pipe, n_expert = lax.axis_size("pipe"), lax.axis_size("expert")
-    down, up = pack(
+    lead, trail, up, down = pack(
         (
             *(tokens_down[0], cotan_down[0], gates_down[0].T, experts_down[0].T),
             *(tokens_up[0], cotan_up[0], gates_up[0].T, experts_up[0].T),
-        )
+        ),
+        n_pipe,
     )
     width = w_in.shape[1]
     cut = width + width // SEGS
-    gathered = gather_both(down, up, n_pipe, grid_cycle(n_expert), cut)
-    return grad(*gathered, w_in[0])[None]
+    got, firsts, seconds = gather_both(lead, trail, up, n_pipe, grid_cycle(n_expert), cut)
+    return grad([*got, down], firsts, seconds, w_in[0])[None]
 
 
 def solution(mesh):

time: 40.6 us -> 40.2 us (level)
  starting transfers between devices: 21.5 us -> 19.9 us
  waiting for transfers between devices: 12.9 us -> 14.2 us
    ppermute x17, starting transfers between devices: 21.5 us -> 19.9 us  [move(): return lax.ppermute(block, ('pipe', 'expert'), pairs)]
    ppermute x17, waiting for transfers between devices: 12.9 us -> 14.2 us  [move(): return lax.ppermute(block, ('pipe', 'expert'), pairs)]
  transfers between devices with their start and end apart: 17 -> 17, of which waited for: 12 -> 10; matrix products, arithmetic and copies ran while one was open for 0% -> 0% of each run, Pallas kernels for 6% -> 6%
where the time goes in v7:
time: 40.2 us; the launch traced here: 40.1 us
  starting transfers between devices  19.9 us (50%)
  waiting for transfers between devices  14.2 us (35%)
  Pallas kernels  5.87 us (15%)
    ppermute x17, starting transfers between devices, move(): return lax.ppermute(block, ('pipe', 'expert'), pairs)  19.9 us
    ppermute x17, waiting for transfers between devices, move(): return lax.ppermute(block, ('pipe', 'expert'), pairs)  14.2 us
    pallas_call x3, Pallas kernels, local_call(): pl.pallas_call(kernel, out_shape=outs, in_specs=[pl.BlockSpec(memory_spac...  3.97 us
    pallas_call x1, Pallas kernels, pack(): pl.pallas_call(functools.partial(pack_kernel, n_pipe), out_shape=(payload...  1.9 us
  transfers between devices with their start and end apart: 17, of which 10 were waited for; matrix products, arithmetic and copies ran while one was open for 0% of the time, Pallas kernels for 6%

profile of v7, /device:TPU:0, one launch (start us, length us, event | category | flops | bytes accessed | tf_op | source)
XLA Modules:
  0.0 40.1 jit_solution(3023084110971558527)
XLA Ops:
  0.0 0.0 copy-start
  0.0 1.9 %pack_slots.1 = (bf16[16,6528]{1,0:T(8,128)(2,1)S(1)}, bf16[16,6528]{1,0:T(8,128)(2,1)S(1)}, bf16[16,6528]{1,0:T(8,128)(2,1)S(1)}, bf16[16,6528]{1,0:T(8,128)(2,1)S(1)}) custom-call(bf16[64,3072]{1,0:T(8,128)(2,1)} %bitcast.20, bf16[64,3072]{1,0:T(8,128)(2,1)} %bitcast.21, bf16[2,64]{1,0:T(2,128)(2,1)} %bitcast.26, s32[2,64]{1,0:T(2,128)} %bitcast.24, ...), custom_call_target="tpu_custom_call" | custom-call | flops 50331648 | bytes 2359296 | tf_op jit(solution)/shard_map/pack_slots/pallas_call | solution.py:96
  1.9 3.4 %collective-permute-start = (bf16[16,6528]{1,0:T(8,128)(2,1)S(1)}, bf16[16,6528]{1,0:T(8,128)(2,1)S(1)}, u32[]{:S(2)}, u32[]{:S(2)}) collective-permute-start(bf16[16,6528]{1,0:T(8,128)(2,1)S(1)} %get-tuple-element.11), channel_id=1, source_target_pairs={{2,24},{4,26},{6,28},{7,30},{5,31},{3,29},{1,27},{0,25},{8,10},{10... | collective-permute-start | bytes 626696 | tf_op jit(solution)/shard_map/ppermute | solution.py:234
  5.3 0.5 %collective-permute-start.4 = (bf16[16,6528]{1,0:T(8,128)(2,1)S(1)}, bf16[16,6528]{1,0:T(8,128)(2,1)S(1)}, u32[]{:S(2)}, u32[]{:S(2)}) collective-permute-start(bf16[16,6528]{1,0:T(8,128)(2,1)S(1)} %get-tuple-element.12), channel_id=1, source_target_pairs={{0,2},{2,4},{4,6},{6,7},{7,5},{5,3},{3,1},{1,0},{10,16},{12,18},{1... | collective-permute-start | bytes 626696 | tf_op jit(solution)/shard_map/ppermute | solution.py:234
  5.8 1.5 %collective-permute-start.10 = (bf16[16,6528]{1,0:T(8,128)(2,1)S(1)}, bf16[16,6528]{1,0:T(8,128)(2,1)S(1)}, u32[]{:S(2)}, u32[]{:S(2)}) collective-permute-start(bf16[16,6528]{1,0:T(8,128)(2,1)S(1)} %get-tuple-element.12), channel_id=1, source_target_pairs={{2,0},{4,2},{6,4},{7,6},{5,7},{3,5},{1,3},{0,1},{8,18},{10,20},{12... | collective-permute-start | bytes 626696 | tf_op jit(solution)/shard_map/ppermute | solution.py:234
  7.3 0.0 collective-permute-start.13
  7.4 3.8 %collective-permute-done.refs_11_ = bf16[16,6528]{1,0:T(8,128)(2,1)S(1)} collective-permute-done((bf16[16,6528]{1,0:T(8,128)(2,1)S(1)}, bf16[16,6528]{1,0:T(8,128)(2,1)S(1)}, u32[]{:S(2)}, u32[]{:S(2)}) %collective-permute-start) | collective-permute-done | bytes 208928 | tf_op jit(solution)/shard_map/ppermute | solution.py:234
  11.2 1.8 %collective-permute-start.1 = (bf16[16,6528]{1,0:T(8,128)(2,1)S(1)}, bf16[16,6528]{1,0:T(8,128)(2,1)S(1)}, u32[]{:S(2)}, u32[]{:S(2)}) collective-permute-start(bf16[16,6528]{1,0:T(8,128)(2,1)S(1)} %collective-permute-done.refs_11_), channel_id=1, source_target_pairs={{2,0},{4,2},{6,4},{7,6},{5,7},{3,5},{1,3},{0,1},{8,10},{10,12},{12... | collective-permute-start | bytes 626696 | tf_op jit(solution)/shard_map/ppermute | solution.py:234
  12.9 0.3 collective-permute-done.4.refs_10_
  13.2 0.0 collective-permute-start.5
  13.3 2.4 %collective-permute-done.10.refs_8_ = bf16[16,6528]{1,0:T(8,128)(2,1)S(1)} collective-permute-done((bf16[16,6528]{1,0:T(8,128)(2,1)S(1)}, bf16[16,6528]{1,0:T(8,128)(2,1)S(1)}, u32[]{:S(2)}, u32[]{:S(2)}) %collective-permute-start.10) | collective-permute-done | bytes 208928 | tf_op jit(solution)/shard_map/ppermute | solution.py:234
  15.6 2.5 %collective-permute-start.11 = (bf16[16,6528]{1,0:T(8,128)(2,1)S(1)}, bf16[16,6528]{1,0:T(8,128)(2,1)S(1)}, u32[]{:S(2)}, u32[]{:S(2)}) collective-permute-start(bf16[16,6528]{1,0:T(8,128)(2,1)S(1)} %collective-permute-done.10.refs_8_), channel_id=1, source_target_pairs={{2,0},{4,2},{6,4},{7,6},{5,7},{3,5},{1,3},{0,1},{8,10},{10,12},{12... | collective-permute-start | bytes 626696 | tf_op jit(solution)/shard_map/ppermute | solution.py:234
  18.1 0.0 collective-permute-done.13.refs_9_
  18.1 0.0 collective-permute-start.14
  18.1 2.0 %collective-permute-done.1.refs_7_ = bf16[16,6528]{1,0:T(8,128)(2,1)S(1)} collective-permute-done((bf16[16,6528]{1,0:T(8,128)(2,1)S(1)}, bf16[16,6528]{1,0:T(8,128)(2,1)S(1)}, u32[]{:S(2)}, u32[]{:S(2)}) %collective-permute-start.1) | collective-permute-done | bytes 208928 | tf_op jit(solution)/shard_map/ppermute | solution.py:234
  20.1 2.5 %collective-permute-start.2 = (bf16[16,6528]{1,0:T(8,128)(2,1)S(1)}, bf16[16,6528]{1,0:T(8,128)(2,1)S(1)}, u32[]{:S(2)}, u32[]{:S(2)}) collective-permute-start(bf16[16,6528]{1,0:T(8,128)(2,1)S(1)} %collective-permute-done.1.refs_7_), channel_id=1, source_target_pairs={{2,0},{4,2},{6,4},{7,6},{5,7},{3,5},{1,3},{0,1},{8,10},{10,12},{12... | collective-permute-start | bytes 626696 | tf_op jit(solution)/shard_map/ppermute | solution.py:234
  22.6 0.0 collective-permute-done.5.refs_6_
  22.6 0.1 collective-permute-start.6
  22.7 0.0 collective-permute-start.16
  22.7 1.9 %collective-permute-done.11.refs_4_ = bf16[16,6528]{1,0:T(8,128)(2,1)S(1)} collective-permute-done((bf16[16,6528]{1,0:T(8,128)(2,1)S(1)}, bf16[16,6528]{1,0:T(8,128)(2,1)S(1)}, u32[]{:S(2)}, u32[]{:S(2)}) %collective-permute-start.11) | collective-permute-done | bytes 208928 | tf_op jit(solution)/shard_map/ppermute | solution.py:234
  24.6 2.5 %collective-permute-start.12 = (bf16[16,6528]{1,0:T(8,128)(2,1)S(1)}, bf16[16,6528]{1,0:T(8,128)(2,1)S(1)}, u32[]{:S(2)}, u32[]{:S(2)}) collective-permute-start(bf16[16,6528]{1,0:T(8,128)(2,1)S(1)} %collective-permute-done.11.refs_4_), channel_id=1, source_target_pairs={{2,0},{4,2},{6,4},{7,6},{5,7},{3,5},{1,3},{0,1},{8,10},{10,12},{12... | collective-permute-start | bytes 626696 | tf_op jit(solution)/shard_map/ppermute | solution.py:234
  27.1 0.0 collective-permute-done.14.refs_5_
  27.1 0.1 collective-permute-start.15
  27.1 1.9 %collective-permute-done.2.refs_3_ = bf16[16,6528]{1,0:T(8,128)(2,1)S(1)} collective-permute-done((bf16[16,6528]{1,0:T(8,128)(2,1)S(1)}, bf16[16,6528]{1,0:T(8,128)(2,1)S(1)}, u32[]{:S(2)}, u32[]{:S(2)}) %collective-permute-start.2) | collective-permute-done | bytes 208928 | tf_op jit(solution)/shard_map/ppermute | solution.py:234
  29.1 2.5 %collective-permute-start.8 = (bf16[16,3456]{1,0:T(8,128)(2,1)S(1)}, bf16[16,3456]{1,0:T(8,128)(2,1)S(1)}, u32[]{:S(2)}, u32[]{:S(2)}) collective-permute-start(bf16[16,3456]{1,0:T(8,128)(2,1)S(1)} %slice.18), channel_id=1, source_target_pairs={{2,0},{4,2},{6,4},{7,6},{5,7},{3,5},{1,3},{0,1},{8,10},{10,12},{12... | collective-permute-start | bytes 331784 | tf_op jit(solution)/shard_map/ppermute | solution.py:234
  31.6 0.0 collective-permute-done.6.refs_2_
  31.6 0.1 collective-permute-start.9
  31.7 0.0 collective-permute-done.16.refs_12_
  31.7 2.1 %collective-permute-start.3 = (bf16[16,3072]{1,0:T(8,128)(2,1)S(1)}, bf16[16,3072]{1,0:T(8,128)(2,1)S(1)}, u32[]{:S(2)}, u32[]{:S(2)}) collective-permute-start(bf16[16,3072]{1,0:T(8,128)(2,1)S(1)} %slice.16), channel_id=1, source_target_pairs={{2,0},{4,2},{6,4},{7,6},{5,7},{3,5},{1,3},{0,1},{8,10},{10,12},{12... | collective-permute-start | bytes 294920 | tf_op jit(solution)/shard_map/ppermute | solution.py:234
  33.8 0.0 collective-permute-done.12.refs_0_
  33.8 0.4 %collective-permute-start.7 = (bf16[16,3072]{1,0:T(8,128)(2,1)S(1)}, bf16[16,3072]{1,0:T(8,128)(2,1)S(1)}, u32[]{:S(2)}, u32[]{:S(2)}) collective-permute-start(bf16[16,3072]{1,0:T(8,128)(2,1)S(1)} %slice.17), channel_id=1, source_target_pairs={{0,2},{2,4},{4,6},{6,7},{7,5},{5,3},{3,1},{1,0},{10,8},{12,10},{14... | collective-permute-start | bytes 294920 | tf_op jit(solution)/shard_map/ppermute | solution.py:234
  34.2 0.4 %collective-permute-done.15.refs_1_ = bf16[16,6528]{1,0:T(8,128)(2,1)S(1)} collective-permute-done((bf16[16,6528]{1,0:T(8,128)(2,1)S(1)}, bf16[16,6528]{1,0:T(8,128)(2,1)S(1)}, u32[]{:S(2)}, u32[]{:S(2)}) %collective-permute-start.15) | collective-permute-done | bytes 208928 | tf_op jit(solution)/shard_map/ppermute | solution.py:234
  34.7 0.0 copy-done
  34.7 2.1 %grad_part.1.refs_4_ = f32[256,3072]{1,0:T(8,128)S(1)} custom-call(bf16[16,6528]{1,0:T(8,128)(2,1)S(1)} %collective-permute-done.12.refs_0_, bf16[16,6528]{1,0:T(8,128)(2,1)S(1)} %collective-permute-done.15.refs_1_, bf16[16,6528]{1,0:T(8,128)(2,1)S(1)} %collective-permute-done.6.refs_2_, bf16[16,6528]{1,0:T(8,128)(2,1)S(1)} %collective-permute-done.2.refs_3_, ...), custom_call_target="tpu_custom_call" | custom-call | flops 748683264 | bytes 4497408 | tf_op jit(solution)/shard_map/grad_part/pallas_call | solution.py:177
  36.8 0.0 collective-permute-done.8.refs_0_
  36.8 0.5 %collective-permute-done.9.refs_1_ = bf16[16,3456]{1,0:T(8,128)(2,1)S(1)} collective-permute-done((bf16[16,3456]{1,0:T(8,128)(2,1)S(1)}, bf16[16,3456]{1,0:T(8,128)(2,1)S(1)}, u32[]{:S(2)}, u32[]{:S(2)}) %collective-permute-start.9) | collective-permute-done | bytes 110624 | tf_op jit(solution)/shard_map/ppermute | solution.py:234
  37.3 0.4 %active_late.1 = (bf16[34,256]{1,0:T(8,128)(2,1)S(1)}, bf16[2,3072]{1,0:T(2,128)(2,1)S(1)}) custom-call(bf16[16,3456]{1,0:T(8,128)(2,1)S(1)} %collective-permute-done.8.refs_0_, bf16[16,3456]{1,0:T(8,128)(2,1)S(1)} %collective-permute-done.9.refs_1_, bf16[3072,256]{1,0:T(8,128)(2,1)S(1)} %bitcast.19), custom_call_target="tpu_custom_call" | custom-call | flops 53477376 | bytes 1794048 | tf_op jit(solution)/shard_map/active_late/pallas_call | solution.py:177
  37.8 0.3 collective-permute-done.3.refs_0_
  38.0 0.6 %collective-permute-done.7.refs_1_ = bf16[16,3072]{1,0:T(8,128)(2,1)S(1)} collective-permute-done((bf16[16,3072]{1,0:T(8,128)(2,1)S(1)}, bf16[16,3072]{1,0:T(8,128)(2,1)S(1)}, u32[]{:S(2)}, u32[]{:S(2)}) %collective-permute-start.7) | collective-permute-done | bytes 98336 | tf_op jit(solution)/shard_map/ppermute | solution.py:234
  38.6 1.5 %grad_sum.1 = bf16[256,3072]{1,0:T(8,128)(2,1)} custom-call(bf16[16,3072]{1,0:T(8,128)(2,1)S(1)} %collective-permute-done.3.refs_0_, bf16[16,3072]{1,0:T(8,128)(2,1)S(1)} %collective-permute-done.7.refs_1_, bf16[34,256]{1,0:T(8,128)(2,1)S(1)} %get-tuple-element.13.refs_2_, bf16[2,3072]{1,0:T(2,128)(2,1)S(1)} %get-tuple-element.14.refs_3_, ...), custom_call_target="tpu_custom_call" | custom-call | flops 53477376 | bytes 3372032 | tf_op jit(solution)/shard_map/grad_sum/pallas_call | solution.py:177
  (4 shorter events, 0.0 us)
Async XLA Ops:
  0.0 34.7 %copy-start = (bf16[1,3072,256]{2,1,0:T(8,128)(2,1)S(1)}, bf16[1,3072,256]{2,1,0:T(8,128)(2,1)}, u32[]{:S(2)}) copy-start(bf16[1,3072,256]{2,1,0:T(8,128)(2,1)} %param.17) | copy-start | bytes 4718596
  1.9 9.3 %collective-permute-start = (bf16[16,6528]{1,0:T(8,128)(2,1)S(1)}, bf16[16,6528]{1,0:T(8,128)(2,1)S(1)}, u32[]{:S(2)}, u32[]{:S(2)}) collective-permute-start(bf16[16,6528]{1,0:T(8,128)(2,1)S(1)} %get-tuple-element.11), channel_id=1, source_target_pairs={{2,24},{4,26},{6,28},{7,30},{5,31},{3,29},{1,27},{0,25},{8,10},{10... | collective-permute-start | bytes 626696 | tf_op jit(solution)/shard_map/ppermute | solution.py:234
  5.3 7.9 %collective-permute-start.4 = (bf16[16,6528]{1,0:T(8,128)(2,1)S(1)}, bf16[16,6528]{1,0:T(8,128)(2,1)S(1)}, u32[]{:S(2)}, u32[]{:S(2)}) collective-permute-start(bf16[16,6528]{1,0:T(8,128)(2,1)S(1)} %get-tuple-element.12), channel_id=1, source_target_pairs={{0,2},{2,4},{4,6},{6,7},{7,5},{5,3},{3,1},{1,0},{10,16},{12,18},{1... | collective-permute-start | bytes 626696 | tf_op jit(solution)/shard_map/ppermute | solution.py:234
  5.8 9.8 %collective-permute-start.10 = (bf16[16,6528]{1,0:T(8,128)(2,1)S(1)}, bf16[16,6528]{1,0:T(8,128)(2,1)S(1)}, u32[]{:S(2)}, u32[]{:S(2)}) collective-permute-start(bf16[16,6528]{1,0:T(8,128)(2,1)S(1)} %get-tuple-element.12), channel_id=1, source_target_pairs={{2,0},{4,2},{6,4},{7,6},{5,7},{3,5},{1,3},{0,1},{8,18},{10,20},{12... | collective-permute-start | bytes 626696 | tf_op jit(solution)/shard_map/ppermute | solution.py:234
  7.3 10.8 %collective-permute-start.13 = (bf16[16,6528]{1,0:T(8,128)(2,1)S(1)}, bf16[16,6528]{1,0:T(8,128)(2,1)S(1)}, u32[]{:S(2)}, u32[]{:S(2)}) collective-permute-start(bf16[16,6528]{1,0:T(8,128)(2,1)S(1)} %get-tuple-element.11), channel_id=1, source_target_pairs={{0,26},{2,28},{4,30},{6,31},{7,29},{5,27},{3,25},{1,24},{10,8},{12... | collective-permute-start | bytes 626696 | tf_op jit(solution)/shard_map/ppermute | solution.py:234
  11.2 9.0 %collective-permute-start.1 = (bf16[16,6528]{1,0:T(8,128)(2,1)S(1)}, bf16[16,6528]{1,0:T(8,128)(2,1)S(1)}, u32[]{:S(2)}, u32[]{:S(2)}) collective-permute-start(bf16[16,6528]{1,0:T(8,128)(2,1)S(1)} %collective-permute-done.refs_11_), channel_id=1, source_target_pairs={{2,0},{4,2},{6,4},{7,6},{5,7},{3,5},{1,3},{0,1},{8,10},{10,12},{12... | collective-permute-start | bytes 626696 | tf_op jit(solution)/shard_map/ppermute | solution.py:234
  13.2 9.4 %collective-permute-start.5 = (bf16[16,6528]{1,0:T(8,128)(2,1)S(1)}, bf16[16,6528]{1,0:T(8,128)(2,1)S(1)}, u32[]{:S(2)}, u32[]{:S(2)}) collective-permute-start(bf16[16,6528]{1,0:T(8,128)(2,1)S(1)} %collective-permute-done.4.refs_10_), channel_id=1, source_target_pairs={{0,2},{2,4},{4,6},{6,7},{7,5},{5,3},{3,1},{1,0},{10,8},{12,10},{14... | collective-permute-start | bytes 626696 | tf_op jit(solution)/shard_map/ppermute | solution.py:234
  15.6 9.0 %collective-permute-start.11 = (bf16[16,6528]{1,0:T(8,128)(2,1)S(1)}, bf16[16,6528]{1,0:T(8,128)(2,1)S(1)}, u32[]{:S(2)}, u32[]{:S(2)}) collective-permute-start(bf16[16,6528]{1,0:T(8,128)(2,1)S(1)} %collective-permute-done.10.refs_8_), channel_id=1, source_target_pairs={{2,0},{4,2},{6,4},{7,6},{5,7},{3,5},{1,3},{0,1},{8,10},{10,12},{12... | collective-permute-start | bytes 626696 | tf_op jit(solution)/shard_map/ppermute | solution.py:234
  18.1 9.0 %collective-permute-start.14 = (bf16[16,6528]{1,0:T(8,128)(2,1)S(1)}, bf16[16,6528]{1,0:T(8,128)(2,1)S(1)}, u32[]{:S(2)}, u32[]{:S(2)}) collective-permute-start(bf16[16,6528]{1,0:T(8,128)(2,1)S(1)} %collective-permute-done.13.refs_9_), channel_id=1, source_target_pairs={{0,2},{2,4},{4,6},{6,7},{7,5},{5,3},{3,1},{1,0},{10,8},{12,10},{14... | collective-permute-start | bytes 626696 | tf_op jit(solution)/shard_map/ppermute | solution.py:234
  20.1 9.0 %collective-permute-start.2 = (bf16[16,6528]{1,0:T(8,128)(2,1)S(1)}, bf16[16,6528]{1,0:T(8,128)(2,1)S(1)}, u32[]{:S(2)}, u32[]{:S(2)}) collective-permute-start(bf16[16,6528]{1,0:T(8,128)(2,1)S(1)} %collective-permute-done.1.refs_7_), channel_id=1, source_target_pairs={{2,0},{4,2},{6,4},{7,6},{5,7},{3,5},{1,3},{0,1},{8,10},{10,12},{12... | collective-permute-start | bytes 626696 | tf_op jit(solution)/shard_map/ppermute | solution.py:234
  22.6 9.0 %collective-permute-start.6 = (bf16[16,6528]{1,0:T(8,128)(2,1)S(1)}, bf16[16,6528]{1,0:T(8,128)(2,1)S(1)}, u32[]{:S(2)}, u32[]{:S(2)}) collective-permute-start(bf16[16,6528]{1,0:T(8,128)(2,1)S(1)} %collective-permute-done.5.refs_6_), channel_id=1, source_target_pairs={{0,2},{2,4},{4,6},{6,7},{7,5},{5,3},{3,1},{1,0},{10,8},{12,10},{14... | collective-permute-start | bytes 626696 | tf_op jit(solution)/shard_map/ppermute | solution.py:234
  22.7 9.1 %collective-permute-start.16 = (bf16[16,6528]{1,0:T(8,128)(2,1)S(1)}, bf16[16,6528]{1,0:T(8,128)(2,1)S(1)}, u32[]{:S(2)}, u32[]{:S(2)}) collective-permute-start(bf16[16,6528]{1,0:T(8,128)(2,1)S(1)} %get-tuple-element.15), channel_id=1, source_target_pairs={{0,24},{1,25},{2,26},{3,27},{4,28},{5,29},{6,30},{7,31},{8,16},{9,... | collective-permute-start | bytes 626696 | tf_op jit(solution)/shard_map/ppermute | solution.py:234
  24.6 9.2 %collective-permute-start.12 = (bf16[16,6528]{1,0:T(8,128)(2,1)S(1)}, bf16[16,6528]{1,0:T(8,128)(2,1)S(1)}, u32[]{:S(2)}, u32[]{:S(2)}) collective-permute-start(bf16[16,6528]{1,0:T(8,128)(2,1)S(1)} %collective-permute-done.11.refs_4_), channel_id=1, source_target_pairs={{2,0},{4,2},{6,4},{7,6},{5,7},{3,5},{1,3},{0,1},{8,10},{10,12},{12... | collective-permute-start | bytes 626696 | tf_op jit(solution)/shard_map/ppermute | solution.py:234
  27.1 7.6 %collective-permute-start.15 = (bf16[16,6528]{1,0:T(8,128)(2,1)S(1)}, bf16[16,6528]{1,0:T(8,128)(2,1)S(1)}, u32[]{:S(2)}, u32[]{:S(2)}) collective-permute-start(bf16[16,6528]{1,0:T(8,128)(2,1)S(1)} %collective-permute-done.14.refs_5_), channel_id=1, source_target_pairs={{0,2},{2,4},{4,6},{6,7},{7,5},{5,3},{3,1},{1,0},{10,8},{12,10},{14... | collective-permute-start | bytes 626696 | tf_op jit(solution)/shard_map/ppermute | solution.py:234
  29.1 7.7 %collective-permute-start.8 = (bf16[16,3456]{1,0:T(8,128)(2,1)S(1)}, bf16[16,3456]{1,0:T(8,128)(2,1)S(1)}, u32[]{:S(2)}, u32[]{:S(2)}) collective-permute-start(bf16[16,3456]{1,0:T(8,128)(2,1)S(1)} %slice.18), channel_id=1, source_target_pairs={{2,0},{4,2},{6,4},{7,6},{5,7},{3,5},{1,3},{0,1},{8,10},{10,12},{12... | collective-permute-start | bytes 331784 | tf_op jit(solution)/shard_map/ppermute | solution.py:234
  31.6 5.7 %collective-permute-start.9 = (bf16[16,3456]{1,0:T(8,128)(2,1)S(1)}, bf16[16,3456]{1,0:T(8,128)(2,1)S(1)}, u32[]{:S(2)}, u32[]{:S(2)}) collective-permute-start(bf16[16,3456]{1,0:T(8,128)(2,1)S(1)} %slice.19), channel_id=1, source_target_pairs={{0,2},{2,4},{4,6},{6,7},{7,5},{5,3},{3,1},{1,0},{10,8},{12,10},{14... | collective-permute-start | bytes 331784 | tf_op jit(solution)/shard_map/ppermute | solution.py:234
  31.7 6.3 %collective-permute-start.3 = (bf16[16,3072]{1,0:T(8,128)(2,1)S(1)}, bf16[16,3072]{1,0:T(8,128)(2,1)S(1)}, u32[]{:S(2)}, u32[]{:S(2)}) collective-permute-start(bf16[16,3072]{1,0:T(8,128)(2,1)S(1)} %slice.16), channel_id=1, source_target_pairs={{2,0},{4,2},{6,4},{7,6},{5,7},{3,5},{1,3},{0,1},{8,10},{10,12},{12... | collective-permute-start | bytes 294920 | tf_op jit(solution)/shard_map/ppermute | solution.py:234
  33.8 4.8 %collective-permute-start.7 = (bf16[16,3072]{1,0:T(8,128)(2,1)S(1)}, bf16[16,3072]{1,0:T(8,128)(2,1)S(1)}, u32[]{:S(2)}, u32[]{:S(2)}) collective-permute-start(bf16[16,3072]{1,0:T(8,128)(2,1)S(1)} %slice.17), channel_id=1, source_target_pairs={{0,2},{2,4},{4,6},{6,7},{7,5},{5,3},{3,1},{1,0},{10,8},{12,10},{14... | collective-permute-start | bytes 294920 | tf_op jit(solution)/shard_map/ppermute | solution.py:234

commit v8 on v7

--- a/solution.py
+++ b/solution.py
@@ -48,38 +48,54 @@
     return p % 2 != 2 * p // n_pipe
 
 
-def pack_kernel(n_pipe, *refs):
-    hbm, (lead, trail, up, down), held, sems = refs[:8], refs[8:12], refs[12:20], refs[20]
-    order = (2, 3, 6, 7, 0, 1, 4, 5)
+def write_payload(out_ref, tokens_ref, cotan_ref, placing, slot_gate):
+    width = tokens_ref.shape[1]
+    seg = width // SEGS
+    x = jnp.dot(placing, tokens_ref[...], preferred_element_type=jnp.float32)
+    y = jnp.dot(placing, cotan_ref[...], preferred_element_type=jnp.float32) * slot_gate
+    out_ref[:, :width] = x[:MAIN].astype(jnp.bfloat16)
+    out_ref[:, width + seg :] = y[:MAIN].astype(jnp.bfloat16)
+    tail = [x[MAIN : MAIN + 1, s * seg : (s + 1) * seg] for s in range(SEGS)]
+    tail += [y[MAIN : MAIN + 1, s * seg : (s + 1) * seg] for s in range(SEGS)]
+    out_ref[:, width : width + seg] = jnp.concatenate(tail, axis=0).astype(jnp.bfloat16)
+
+
+def lead_kernel(n_pipe, *refs):
+    hbm, lead, trail, (tokens_ref, cotan_ref, gates_ref, ids_ref, sems) = (
+        refs[:8],
+        refs[8],
+        refs[9:13],
+        refs[13:],
+    )
+    held = (tokens_ref, cotan_ref, gates_ref, ids_ref, *trail)
+    order = (2, 3, 0, 1, 6, 7, 4, 5)
     turned = is_turned(lax.axis_index("pipe"), n_pipe)
 
     def copies(swapped):
         sources = hbm[:4] + hbm[4:] if swapped else hbm[4:] + hbm[:4]
-        return [pltpu.make_async_copy(sources[i], held[i], sems.at[i]) for i in order]
+        return {i: pltpu.make_async_copy(sources[i], held[i], sems.at[i]) for i in order}
 
     for swapped in (False, True):
 
         @pl.when(turned == swapped)
         def _():
-            for copy in copies(swapped):
+            for copy in copies(swapped).values():
                 copy.start()
 
-    waits = dict(zip(order, copies(False)))
-    for i in order[:4]:
+    waits = copies(False)
+    waits[2].wait()
+    waits[3].wait()
+    placed = place(gates_ref[...], ids_ref[...])
+    waits[0].wait()
+    waits[1].wait()
+    write_payload(lead, tokens_ref, cotan_ref, *placed)
+    for i in range(4, 8):
         waits[i].wait()
-    places = [place(held[d + 2][...], held[d + 3][...]) for d in (0, 4)]
-    for d, (placing, slot_gate), out_ref in ((0, places[0], lead), (4, places[1], trail)):
-        waits[d].wait()
-        waits[d + 1].wait()
-        width = held[d].shape[1]
-        seg = width // SEGS
-        x = jnp.dot(placing, held[d][...], preferred_element_type=jnp.float32)
-        y = jnp.dot(placing, held[d + 1][...], preferred_element_type=jnp.float32) * slot_gate
-        out_ref[:, :width] = x[:MAIN].astype(jnp.bfloat16)
-        out_ref[:, width + seg :] = y[:MAIN].astype(jnp.bfloat16)
-        tail = [x[MAIN : MAIN + 1, s * seg : (s + 1) * seg] for s in range(SEGS)]
-        tail += [y[MAIN : MAIN + 1, s * seg : (s + 1) * seg] for s in range(SEGS)]
-        out_ref[:, width : width + seg] = jnp.concatenate(tail, axis=0).astype(jnp.bfloat16)
+
+
+def trail_kernel(n_pipe, lead, tokens_ref, cotan_ref, gates_ref, ids_ref, trail, up, down):
+    write_payload(trail, tokens_ref, cotan_ref, *place(gates_ref[...], ids_ref[...]))
+    turned = is_turned(lax.axis_index("pipe"), n_pipe)
     for swapped, first, second in ((False, up, down), (True, down, up)):
 
         @pl.when(turned == swapped)
@@ -93,19 +109,27 @@
     seg = width // SEGS
     payload = pltpu.VMEM((MAIN, 2 * width + seg), jnp.bfloat16)
     arrays = [pltpu.with_memory_space_constraint(a, pltpu.HBM) for a in arrays]
-    return pl.pallas_call(
-        functools.partial(pack_kernel, n_pipe),
-        out_shape=(payload,) * 4,
+    lead, *trail = pl.pallas_call(
+        functools.partial(lead_kernel, n_pipe),
+        out_shape=(payload, *(pltpu.VMEM(a.shape, a.dtype) for a in arrays[:4])),
         in_specs=[pl.BlockSpec(memory_space=pltpu.HBM)] * 8,
-        out_specs=(pl.BlockSpec(memory_space=pltpu.VMEM),) * 4,
-        scratch_shapes=[pltpu.VMEM(a.shape, a.dtype) for a in arrays]
+        out_specs=(pl.BlockSpec(memory_space=pltpu.VMEM),) * 5,
+        scratch_shapes=[pltpu.VMEM(a.shape, a.dtype) for a in arrays[:4]]
         + [pltpu.SemaphoreType.DMA((8,))],
         compiler_params=pltpu.CompilerParams(vmem_limit_bytes=16 * 2**20),
         cost_estimate=pl.CostEstimate(
-            flops=8 * 2 * MAIN * rows * width, bytes_accessed=12 * rows * width, transcendentals=0
+            flops=4 * 2 * MAIN * rows * width, bytes_accessed=12 * rows * width, transcendentals=0
         ),
-        name="pack_slots",
+        name="pack_lead",
     )(*arrays)
+    rest = local_call(
+        functools.partial(trail_kernel, n_pipe),
+        "pack_trail",
+        (lead, *trail),
+        (payload,) * 3,
+        flops=4 * 2 * MAIN * rows * width,
+    )
+    return (lead, *rest)
 
 
 def activate(payloads, w_ref):
@@ -147,18 +171,29 @@
 
 
 def active_kernel(count, *refs):
-    payloads, (w_ref, active_ref, tail_ref) = refs[:count], refs[count:]
-    active_ref[...], tail_ref[...] = activate(payloads, w_ref)
-
-
-def sum_kernel(count, *refs):
+    payloads, (w_ref, *before, active_ref, tail_ref) = refs[:count], refs[count:]
+    active, tail = activate(payloads, w_ref)
+    if before:
+        mains = before[0].shape[0] // CAP * MAIN
+        first, second = before[0][...].astype(jnp.float32), active.astype(jnp.float32)
+        active = jnp.concatenate(
+            [first[:mains], second[: count * MAIN], first[mains:], second[count * MAIN :]], axis=0
+        ).astype(jnp.bfloat16)
+        tail = jnp.concatenate(
+            [before[1][...].astype(jnp.float32), tail.astype(jnp.float32)], axis=0
+        ).astype(jnp.bfloat16)
+    active_ref[...], tail_ref[...] = active, tail
+
+
+def sum_kernel(count, offsets, *refs):
     blocks, (active_ref, tail_ref, before, out_ref, made, sems) = refs[:count], refs[count:]
     seg = tail_ref.shape[1] // SEGS
     active = active_ref[...]
     copies = []
     for s in range(SEGS):
         here = slice(s * seg, (s + 1) * seg)
-        rows_y = jnp.concatenate([b[:, here] for b in blocks] + [tail_ref[:, here]], axis=0)
+        rows_y = [b[:, o + s * seg : o + (s + 1) * seg] for b, o in zip(blocks, offsets)]
+        rows_y = jnp.concatenate(rows_y + [tail_ref[:, here]], axis=0)
         made[:, here] = (before[:, here] + times(active, rows_y)).astype(jnp.bfloat16)
         copies.append(
             pltpu.make_async_copy(made.at[:, here], out_ref.at[:, here], sems.at[0])
@@ -191,7 +226,7 @@
 
 def grad(got, firsts, seconds, weight_in):
     width, hidden = weight_in.shape
-    count, late = len(got), len(firsts)
+    count, late = len(got), len(seconds)
     (before,) = local_call(
         functools.partial(part_kernel, count),
         "grad_part",
@@ -199,18 +234,22 @@
         (pltpu.VMEM((hidden, width), jnp.float32),),
         flops=4 * CAP * count * width * hidden,
     )
-    active, tail = local_call(
-        functools.partial(active_kernel, late),
-        "active_late",
-        (*firsts, weight_in),
-        (
-            pltpu.VMEM((late * CAP, hidden), jnp.bfloat16),
-            pltpu.VMEM((late, width), jnp.bfloat16),
-        ),
-        flops=2 * CAP * late * width * hidden,
-    )
+    done, ready = (), 0
+    for group in firsts:
+        ready += len(group)
+        done = local_call(
+            functools.partial(active_kernel, len(group)),
+            "active_late",
+            (*group, weight_in, *done),
+            (
+                pltpu.VMEM((ready * CAP, hidden), jnp.bfloat16),
+                pltpu.VMEM((ready, width), jnp.bfloat16),
+            ),
+            flops=2 * CAP * len(group) * width * hidden,
+        )
+    active, tail = done
     (total,) = local_call(
-        functools.partial(sum_kernel, late),
+        functools.partial(sum_kernel, late, [b.shape[1] - width for b in seconds]),
         "grad_sum",
         (*seconds, active, tail, before),
         (jax.ShapeDtypeStruct((hidden, width), jnp.bfloat16),),
@@ -246,12 +285,11 @@
     for _ in range(1, (n - 1) // 2):
         at = turn(at)
         got += at
-    firsts, seconds = (
-        (move(l, left), move(r, right))
-        for l, r in ((at[0][:, :cut], at[1][:, :cut]), (at[0][:, cut:], at[1][:, cut:]))
-    )
+    whole = move(at[0], left)
+    firsts = ((at[2], whole), (move(at[1][:, :cut], right),))
+    seconds = (at[2], whole, move(at[1][:, cut:], right))
     own = move(up, [(e, e) for e in range(n)], lambda turned: True)
-    return [*reversed(got), own], firsts, seconds
+    return [*reversed(got[:-2]), got[-1], own], firsts, seconds
 
 
 def body(

time: 40.2 us -> 39.8 us (0.990)
  waiting for transfers between devices: 14.2 us -> 11.6 us
  starting transfers between devices: 19.9 us -> 21.6 us
  Pallas kernels: 5.87 us -> 6.31 us
    ppermute x17 -> x16, waiting for transfers between devices: 14.2 us -> 11.6 us  [move(): return lax.ppermute(block, ('pipe', 'expert'), pairs)]
    ppermute x17 -> x16, starting transfers between devices: 19.9 us -> 21.6 us  [move(): return lax.ppermute(block, ('pipe', 'expert'), pairs)]
    pallas_call x3 -> x5, Pallas kernels: 3.97 us -> 4.7 us  [local_call(): pl.pallas_call(kernel, out_shape=outs, in_specs=[pl.BlockSpec(memory_spac...]
  transfers between devices with their start and end apart: 17 -> 16, of which waited for: 10 -> 13; matrix products, arithmetic and copies ran while one was open for 0% -> 0% of each run, Pallas kernels for 6% -> 8%
where the time goes in v8:
time: 39.8 us; the launch traced here: 39.6 us
  starting transfers between devices  21.6 us (54%)
  waiting for transfers between devices  11.6 us (29%)
  Pallas kernels  6.31 us (16%)
    ppermute x16, starting transfers between devices, move(): return lax.ppermute(block, ('pipe', 'expert'), pairs)  21.6 us
    ppermute x16, waiting for transfers between devices, move(): return lax.ppermute(block, ('pipe', 'expert'), pairs)  11.6 us
    pallas_call x5, Pallas kernels, local_call(): pl.pallas_call(kernel, out_shape=outs, in_specs=[pl.BlockSpec(memory_spac...  4.7 us
    pallas_call x1, Pallas kernels, pack(): pl.pallas_call(functools.partial(lead_kernel, n_pipe), out_shape=(payload...  1.61 us
  transfers between devices with their start and end apart: 16, of which 13 were waited for; matrix products, arithmetic and copies ran while one was open for 0% of the time, Pallas kernels for 8%

profile of v8, /device:TPU:0, one launch (start us, length us, event | category | flops | bytes accessed | tf_op | source)
XLA Modules:
  0.0 39.6 jit_solution(13953251219022898666)
XLA Ops:
  0.0 0.0 copy-start
  0.0 1.6 %pack_lead.1 = (bf16[16,6528]{1,0:T(8,128)(2,1)S(1)}, bf16[64,3072]{1,0:T(8,128)(2,1)S(1)}, bf16[64,3072]{1,0:T(8,128)(2,1)S(1)}, bf16[2,64]{1,0:T(2,128)(2,1)S(1)}, s32[2,64]{1,0:T(2,128)S(1)}) custom-call(bf16[64,3072]{1,0:T(8,128)(2,1)} %bitcast.21, bf16[64,3072]{1,0:T(8,128)(2,1)} %bitcast.22, bf16[2,64]{1,0:T(2,128)(2,1)} %bitcast.27, ...), custom_call_target="tpu_custom_call" | custom-call | flops 25165824 | bytes 2359296 | tf_op jit(solution)/shard_map/pack_lead/pallas_call | solution.py:112
  1.6 3.4 %collective-permute-start.3 = (bf16[16,6528]{1,0:T(8,128)(2,1)S(1)}, bf16[16,6528]{1,0:T(8,128)(2,1)S(1)}, u32[]{:S(2)}, u32[]{:S(2)}) collective-permute-start(bf16[16,6528]{1,0:T(8,128)(2,1)S(1)} %get-tuple-element.17.lead), channel_id=1, source_target_pairs={{2,24},{4,26},{6,28},{7,30},{5,31},{3,29},{1,27},{0,25},{8,10},{10... | collective-permute-start | bytes 626696 | tf_op jit(solution)/shard_map/ppermute | solution.py:273
  5.0 0.4 pack_trail.1
  5.4 0.6 %collective-permute-start.7 = (bf16[16,6528]{1,0:T(8,128)(2,1)S(1)}, bf16[16,6528]{1,0:T(8,128)(2,1)S(1)}, u32[]{:S(2)}, u32[]{:S(2)}) collective-permute-start(bf16[16,6528]{1,0:T(8,128)(2,1)S(1)} %get-tuple-element.22), channel_id=1, source_target_pairs={{0,2},{2,4},{4,6},{6,7},{7,5},{5,3},{3,1},{1,0},{10,16},{12,18},{1... | collective-permute-start | bytes 626696 | tf_op jit(solution)/shard_map/ppermute | solution.py:273
  6.0 1.5 %collective-permute-start.12 = (bf16[16,6528]{1,0:T(8,128)(2,1)S(1)}, bf16[16,6528]{1,0:T(8,128)(2,1)S(1)}, u32[]{:S(2)}, u32[]{:S(2)}) collective-permute-start(bf16[16,6528]{1,0:T(8,128)(2,1)S(1)} %get-tuple-element.22), channel_id=1, source_target_pairs={{2,0},{4,2},{6,4},{7,6},{5,7},{3,5},{1,3},{0,1},{8,18},{10,20},{12... | collective-permute-start | bytes 626696 | tf_op jit(solution)/shard_map/ppermute | solution.py:273
  7.5 0.0 collective-permute-start
  7.5 2.3 %collective-permute-done.3.refs_9_ = bf16[16,6528]{1,0:T(8,128)(2,1)S(1)} collective-permute-done((bf16[16,6528]{1,0:T(8,128)(2,1)S(1)}, bf16[16,6528]{1,0:T(8,128)(2,1)S(1)}, u32[]{:S(2)}, u32[]{:S(2)}) %collective-permute-start.3) | collective-permute-done | bytes 208928 | tf_op jit(solution)/shard_map/ppermute | solution.py:273
  9.8 2.0 %collective-permute-start.4 = (bf16[16,6528]{1,0:T(8,128)(2,1)S(1)}, bf16[16,6528]{1,0:T(8,128)(2,1)S(1)}, u32[]{:S(2)}, u32[]{:S(2)}) collective-permute-start(bf16[16,6528]{1,0:T(8,128)(2,1)S(1)} %collective-permute-done.3.refs_9_), channel_id=1, source_target_pairs={{2,0},{4,2},{6,4},{7,6},{5,7},{3,5},{1,3},{0,1},{8,10},{10,12},{12... | collective-permute-start | bytes 626696 | tf_op jit(solution)/shard_map/ppermute | solution.py:273
  11.8 1.6 %collective-permute-done.7.refs_8_ = bf16[16,6528]{1,0:T(8,128)(2,1)S(1)} collective-permute-done((bf16[16,6528]{1,0:T(8,128)(2,1)S(1)}, bf16[16,6528]{1,0:T(8,128)(2,1)S(1)}, u32[]{:S(2)}, u32[]{:S(2)}) %collective-permute-start.7) | collective-permute-done | bytes 208928 | tf_op jit(solution)/shard_map/ppermute | solution.py:273
  13.3 0.0 collective-permute-start.8
  13.4 0.9 %collective-permute-done.12.refs_6_ = bf16[16,6528]{1,0:T(8,128)(2,1)S(1)} collective-permute-done((bf16[16,6528]{1,0:T(8,128)(2,1)S(1)}, bf16[16,6528]{1,0:T(8,128)(2,1)S(1)}, u32[]{:S(2)}, u32[]{:S(2)}) %collective-permute-start.12) | collective-permute-done | bytes 208928 | tf_op jit(solution)/shard_map/ppermute | solution.py:273
  14.3 2.5 %collective-permute-start.13 = (bf16[16,6528]{1,0:T(8,128)(2,1)S(1)}, bf16[16,6528]{1,0:T(8,128)(2,1)S(1)}, u32[]{:S(2)}, u32[]{:S(2)}) collective-permute-start(bf16[16,6528]{1,0:T(8,128)(2,1)S(1)} %collective-permute-done.12.refs_6_), channel_id=1, source_target_pairs={{2,0},{4,2},{6,4},{7,6},{5,7},{3,5},{1,3},{0,1},{8,10},{10,12},{12... | collective-permute-start | bytes 626696 | tf_op jit(solution)/shard_map/ppermute | solution.py:273
  16.7 1.1 %collective-permute-done.refs_7_ = bf16[16,6528]{1,0:T(8,128)(2,1)S(1)} collective-permute-done((bf16[16,6528]{1,0:T(8,128)(2,1)S(1)}, bf16[16,6528]{1,0:T(8,128)(2,1)S(1)}, u32[]{:S(2)}, u32[]{:S(2)}) %collective-permute-start) | collective-permute-done | bytes 208928 | tf_op jit(solution)/shard_map/ppermute | solution.py:273
  17.8 0.7 %collective-permute-start.1 = (bf16[16,6528]{1,0:T(8,128)(2,1)S(1)}, bf16[16,6528]{1,0:T(8,128)(2,1)S(1)}, u32[]{:S(2)}, u32[]{:S(2)}) collective-permute-start(bf16[16,6528]{1,0:T(8,128)(2,1)S(1)} %collective-permute-done.refs_7_), channel_id=1, source_target_pairs={{0,2},{2,4},{4,6},{6,7},{7,5},{5,3},{3,1},{1,0},{10,8},{12,10},{14... | collective-permute-start | bytes 626696 | tf_op jit(solution)/shard_map/ppermute | solution.py:273
  18.5 0.3 collective-permute-done.4.refs_5_
  18.7 2.5 %collective-permute-start.5 = (bf16[16,6528]{1,0:T(8,128)(2,1)S(1)}, bf16[16,6528]{1,0:T(8,128)(2,1)S(1)}, u32[]{:S(2)}, u32[]{:S(2)}) collective-permute-start(bf16[16,6528]{1,0:T(8,128)(2,1)S(1)} %collective-permute-done.4.refs_5_), channel_id=1, source_target_pairs={{2,0},{4,2},{6,4},{7,6},{5,7},{3,5},{1,3},{0,1},{8,10},{10,12},{12... | collective-permute-start | bytes 626696 | tf_op jit(solution)/shard_map/ppermute | solution.py:273
  21.2 0.7 %collective-permute-done.8.refs_4_ = bf16[16,6528]{1,0:T(8,128)(2,1)S(1)} collective-permute-done((bf16[16,6528]{1,0:T(8,128)(2,1)S(1)}, bf16[16,6528]{1,0:T(8,128)(2,1)S(1)}, u32[]{:S(2)}, u32[]{:S(2)}) %collective-permute-start.8) | collective-permute-done | bytes 208928 | tf_op jit(solution)/shard_map/ppermute | solution.py:273
  21.9 0.3 collective-permute-start.9
  22.2 0.7 %collective-permute-start.15 = (bf16[16,6528]{1,0:T(8,128)(2,1)S(1)}, bf16[16,6528]{1,0:T(8,128)(2,1)S(1)}, u32[]{:S(2)}, u32[]{:S(2)}) collective-permute-start(bf16[16,6528]{1,0:T(8,128)(2,1)S(1)} %get-tuple-element.27), channel_id=1, source_target_pairs={{0,24},{1,25},{2,26},{3,27},{4,28},{5,29},{6,30},{7,31},{8,16},{9,... | collective-permute-start | bytes 626696 | tf_op jit(solution)/shard_map/ppermute | solution.py:273
  22.9 0.3 collective-permute-done.13.refs_2_
  23.2 2.5 %collective-permute-start.14 = (bf16[16,6528]{1,0:T(8,128)(2,1)S(1)}, bf16[16,6528]{1,0:T(8,128)(2,1)S(1)}, u32[]{:S(2)}, u32[]{:S(2)}) collective-permute-start(bf16[16,6528]{1,0:T(8,128)(2,1)S(1)} %collective-permute-done.13.refs_2_), channel_id=1, source_target_pairs={{2,0},{4,2},{6,4},{7,6},{5,7},{3,5},{1,3},{0,1},{8,10},{10,12},{12... | collective-permute-start | bytes 626696 | tf_op jit(solution)/shard_map/ppermute | solution.py:273
  25.7 0.7 %collective-permute-done.1.refs_3_ = bf16[16,6528]{1,0:T(8,128)(2,1)S(1)} collective-permute-done((bf16[16,6528]{1,0:T(8,128)(2,1)S(1)}, bf16[16,6528]{1,0:T(8,128)(2,1)S(1)}, u32[]{:S(2)}, u32[]{:S(2)}) %collective-permute-start.1) | collective-permute-done | bytes 208928 | tf_op jit(solution)/shard_map/ppermute | solution.py:273
  26.4 0.3 collective-permute-start.2
  26.6 1.0 %collective-permute-done.5.refs_1_ = bf16[16,6528]{1,0:T(8,128)(2,1)S(1)} collective-permute-done((bf16[16,6528]{1,0:T(8,128)(2,1)S(1)}, bf16[16,6528]{1,0:T(8,128)(2,1)S(1)}, u32[]{:S(2)}, u32[]{:S(2)}) %collective-permute-start.5) | collective-permute-done | bytes 208928 | tf_op jit(solution)/shard_map/ppermute | solution.py:273
  27.7 2.5 %collective-permute-start.6 = (bf16[16,6528]{1,0:T(8,128)(2,1)S(1)}, bf16[16,6528]{1,0:T(8,128)(2,1)S(1)}, u32[]{:S(2)}, u32[]{:S(2)}) collective-permute-start(bf16[16,6528]{1,0:T(8,128)(2,1)S(1)} %collective-permute-done.5.refs_1_), channel_id=1, source_target_pairs={{2,0},{4,2},{6,4},{7,6},{5,7},{3,5},{1,3},{0,1},{8,10},{10,12},{12... | collective-permute-start | bytes 626696 | tf_op jit(solution)/shard_map/ppermute | solution.py:273
  30.2 0.7 %collective-permute-done.9.refs_0_ = bf16[16,6528]{1,0:T(8,128)(2,1)S(1)} collective-permute-done((bf16[16,6528]{1,0:T(8,128)(2,1)S(1)}, bf16[16,6528]{1,0:T(8,128)(2,1)S(1)}, u32[]{:S(2)}, u32[]{:S(2)}) %collective-permute-start.9) | collective-permute-done | bytes 208928 | tf_op jit(solution)/shard_map/ppermute | solution.py:273
  30.9 0.3 collective-permute-start.11
  31.2 0.0 collective-permute-done.15.refs_11_
  31.2 1.9 %collective-permute-start.10 = (bf16[16,3072]{1,0:T(8,128)(2,1)S(1)}, bf16[16,3072]{1,0:T(8,128)(2,1)S(1)}, u32[]{:S(2)}, u32[]{:S(2)}) collective-permute-start(bf16[16,3072]{1,0:T(8,128)(2,1)S(1)} %slice.8), channel_id=1, source_target_pairs={{0,2},{2,4},{4,6},{6,7},{7,5},{5,3},{3,1},{1,0},{10,8},{12,10},{14... | collective-permute-start | bytes 294920 | tf_op jit(solution)/shard_map/ppermute | solution.py:273
  33.1 0.0 collective-permute-done.14.refs_10_
  33.1 0.0 copy-done
  33.1 2.0 %grad_part.1.refs_5_ = f32[256,3072]{1,0:T(8,128)S(1)} custom-call(bf16[16,6528]{1,0:T(8,128)(2,1)S(1)} %collective-permute-done.9.refs_0_, bf16[16,6528]{1,0:T(8,128)(2,1)S(1)} %collective-permute-done.5.refs_1_, bf16[16,6528]{1,0:T(8,128)(2,1)S(1)} %collective-permute-done.13.refs_2_, bf16[16,6528]{1,0:T(8,128)(2,1)S(1)} %collective-permute-done.1.refs_3_, ...), custom_call_target="tpu_custom_call" | custom-call | flops 695205888 | bytes 4288512 | tf_op jit(solution)/shard_map/grad_part/pallas_call | solution.py:212
  35.2 0.2 collective-permute-done.2.refs_0_
  35.3 1.3 %collective-permute-done.6.refs_1_ = bf16[16,6528]{1,0:T(8,128)(2,1)S(1)} collective-permute-done((bf16[16,6528]{1,0:T(8,128)(2,1)S(1)}, bf16[16,6528]{1,0:T(8,128)(2,1)S(1)}, u32[]{:S(2)}, u32[]{:S(2)}) %collective-permute-start.6) | collective-permute-done | bytes 208928 | tf_op jit(solution)/shard_map/ppermute | solution.py:273
  36.6 0.4 %active_late.2 = (bf16[34,256]{1,0:T(8,128)(2,1)S(1)}, bf16[2,3072]{1,0:T(2,128)(2,1)S(1)}) custom-call(bf16[16,6528]{1,0:T(8,128)(2,1)S(1)} %collective-permute-done.2.refs_0_, bf16[16,6528]{1,0:T(8,128)(2,1)S(1)} %collective-permute-done.6.refs_1_, bf16[3072,256]{1,0:T(8,128)(2,1)S(1)} %bitcast.19), custom_call_target="tpu_custom_call" | custom-call | flops 53477376 | bytes 1990656 | tf_op jit(solution)/shard_map/active_late/pallas_call | solution.py:212
  37.1 0.0 collective-permute-done.11.refs_0_
  37.1 0.4 %active_late.3 = (bf16[51,256]{1,0:T(8,128)(2,1)S(1)}, bf16[3,3072]{1,0:T(4,128)(2,1)S(1)}) custom-call(bf16[16,3456]{1,0:T(8,128)(2,1)S(1)} %collective-permute-done.11.refs_0_, bf16[3072,256]{1,0:T(8,128)(2,1)S(1)} %bitcast.20, bf16[34,256]{1,0:T(8,128)(2,1)S(1)} %get-tuple-element.23.refs_2_, bf16[2,3072]{1,0:T(2,128)(2,1)S(1)} %get-tuple-element.24.refs_3_), custom_call_target="tpu_custom_call" | custom-call | flops 26738688 | bytes 1713152 | tf_op jit(solution)/shard_map/active_late/pallas_call | solution.py:212
  37.5 0.6 %collective-permute-done.10.refs_2_ = bf16[16,3072]{1,0:T(8,128)(2,1)S(1)} collective-permute-done((bf16[16,3072]{1,0:T(8,128)(2,1)S(1)}, bf16[16,3072]{1,0:T(8,128)(2,1)S(1)}, u32[]{:S(2)}, u32[]{:S(2)}) %collective-permute-start.10) | collective-permute-done | bytes 98336 | tf_op jit(solution)/shard_map/ppermute | solution.py:273
  38.1 1.5 %grad_sum.1 = bf16[256,3072]{1,0:T(8,128)(2,1)} custom-call(bf16[16,6528]{1,0:T(8,128)(2,1)S(1)} %collective-permute-done.2.refs_0_, bf16[16,6528]{1,0:T(8,128)(2,1)S(1)} %collective-permute-done.6.refs_1_, bf16[16,3072]{1,0:T(8,128)(2,1)S(1)} %collective-permute-done.10.refs_2_, bf16[51,256]{1,0:T(8,128)(2,1)S(1)} %get-tuple-element.25.refs_3_, ...), custom_call_target="tpu_custom_call" | custom-call | flops 80216064 | bytes 3706368 | tf_op jit(solution)/shard_map/grad_sum/pallas_call | solution.py:212
  (2 shorter events, 0.0 us)
Async XLA Ops:
  0.0 33.1 %copy-start = (bf16[1,3072,256]{2,1,0:T(8,128)(2,1)S(1)}, bf16[1,3072,256]{2,1,0:T(8,128)(2,1)}, u32[]{:S(2)}) copy-start(bf16[1,3072,256]{2,1,0:T(8,128)(2,1)} %param.17) | copy-start | bytes 4718596
  1.6 8.2 %collective-permute-start.3 = (bf16[16,6528]{1,0:T(8,128)(2,1)S(1)}, bf16[16,6528]{1,0:T(8,128)(2,1)S(1)}, u32[]{:S(2)}, u32[]{:S(2)}) collective-permute-start(bf16[16,6528]{1,0:T(8,128)(2,1)S(1)} %get-tuple-element.17.lead), channel_id=1, source_target_pairs={{2,24},{4,26},{6,28},{7,30},{5,31},{3,29},{1,27},{0,25},{8,10},{10... | collective-permute-start | bytes 626696 | tf_op jit(solution)/shard_map/ppermute | solution.py:273
  5.4 7.9 %collective-permute-start.7 = (bf16[16,6528]{1,0:T(8,128)(2,1)S(1)}, bf16[16,6528]{1,0:T(8,128)(2,1)S(1)}, u32[]{:S(2)}, u32[]{:S(2)}) collective-permute-start(bf16[16,6528]{1,0:T(8,128)(2,1)S(1)} %get-tuple-element.22), channel_id=1, source_target_pairs={{0,2},{2,4},{4,6},{6,7},{7,5},{5,3},{3,1},{1,0},{10,16},{12,18},{1... | collective-permute-start | bytes 626696 | tf_op jit(solution)/shard_map/ppermute | solution.py:273
  6.0 8.3 %collective-permute-start.12 = (bf16[16,6528]{1,0:T(8,128)(2,1)S(1)}, bf16[16,6528]{1,0:T(8,128)(2,1)S(1)}, u32[]{:S(2)}, u32[]{:S(2)}) collective-permute-start(bf16[16,6528]{1,0:T(8,128)(2,1)S(1)} %get-tuple-element.22), channel_id=1, source_target_pairs={{2,0},{4,2},{6,4},{7,6},{5,7},{3,5},{1,3},{0,1},{8,18},{10,20},{12... | collective-permute-start | bytes 626696 | tf_op jit(solution)/shard_map/ppermute | solution.py:273
  7.5 10.3 %collective-permute-start = (bf16[16,6528]{1,0:T(8,128)(2,1)S(1)}, bf16[16,6528]{1,0:T(8,128)(2,1)S(1)}, u32[]{:S(2)}, u32[]{:S(2)}) collective-permute-start(bf16[16,6528]{1,0:T(8,128)(2,1)S(1)} %get-tuple-element.17.lead), channel_id=1, source_target_pairs={{0,26},{2,28},{4,30},{6,31},{7,29},{5,27},{3,25},{1,24},{10,8},{12... | collective-permute-start | bytes 626696 | tf_op jit(solution)/shard_map/ppermute | solution.py:273
  9.8 9.0 %collective-permute-start.4 = (bf16[16,6528]{1,0:T(8,128)(2,1)S(1)}, bf16[16,6528]{1,0:T(8,128)(2,1)S(1)}, u32[]{:S(2)}, u32[]{:S(2)}) collective-permute-start(bf16[16,6528]{1,0:T(8,128)(2,1)S(1)} %collective-permute-done.3.refs_9_), channel_id=1, source_target_pairs={{2,0},{4,2},{6,4},{7,6},{5,7},{3,5},{1,3},{0,1},{8,10},{10,12},{12... | collective-permute-start | bytes 626696 | tf_op jit(solution)/shard_map/ppermute | solution.py:273
  13.3 8.6 %collective-permute-start.8 = (bf16[16,6528]{1,0:T(8,128)(2,1)S(1)}, bf16[16,6528]{1,0:T(8,128)(2,1)S(1)}, u32[]{:S(2)}, u32[]{:S(2)}) collective-permute-start(bf16[16,6528]{1,0:T(8,128)(2,1)S(1)} %collective-permute-done.7.refs_8_), channel_id=1, source_target_pairs={{0,2},{2,4},{4,6},{6,7},{7,5},{5,3},{3,1},{1,0},{10,8},{12,10},{14... | collective-permute-start | bytes 626696 | tf_op jit(solution)/shard_map/ppermute | solution.py:273
  14.3 9.0 %collective-permute-start.13 = (bf16[16,6528]{1,0:T(8,128)(2,1)S(1)}, bf16[16,6528]{1,0:T(8,128)(2,1)S(1)}, u32[]{:S(2)}, u32[]{:S(2)}) collective-permute-start(bf16[16,6528]{1,0:T(8,128)(2,1)S(1)} %collective-permute-done.12.refs_6_), channel_id=1, source_target_pairs={{2,0},{4,2},{6,4},{7,6},{5,7},{3,5},{1,3},{0,1},{8,10},{10,12},{12... | collective-permute-start | bytes 626696 | tf_op jit(solution)/shard_map/ppermute | solution.py:273
  17.8 8.6 %collective-permute-start.1 = (bf16[16,6528]{1,0:T(8,128)(2,1)S(1)}, bf16[16,6528]{1,0:T(8,128)(2,1)S(1)}, u32[]{:S(2)}, u32[]{:S(2)}) collective-permute-start(bf16[16,6528]{1,0:T(8,128)(2,1)S(1)} %collective-permute-done.refs_7_), channel_id=1, source_target_pairs={{0,2},{2,4},{4,6},{6,7},{7,5},{5,3},{3,1},{1,0},{10,8},{12,10},{14... | collective-permute-start | bytes 626696 | tf_op jit(solution)/shard_map/ppermute | solution.py:273
  18.7 9.0 %collective-permute-start.5 = (bf16[16,6528]{1,0:T(8,128)(2,1)S(1)}, bf16[16,6528]{1,0:T(8,128)(2,1)S(1)}, u32[]{:S(2)}, u32[]{:S(2)}) collective-permute-start(bf16[16,6528]{1,0:T(8,128)(2,1)S(1)} %collective-permute-done.4.refs_5_), channel_id=1, source_target_pairs={{2,0},{4,2},{6,4},{7,6},{5,7},{3,5},{1,3},{0,1},{8,10},{10,12},{12... | collective-permute-start | bytes 626696 | tf_op jit(solution)/shard_map/ppermute | solution.py:273
  21.9 9.0 %collective-permute-start.9 = (bf16[16,6528]{1,0:T(8,128)(2,1)S(1)}, bf16[16,6528]{1,0:T(8,128)(2,1)S(1)}, u32[]{:S(2)}, u32[]{:S(2)}) collective-permute-start(bf16[16,6528]{1,0:T(8,128)(2,1)S(1)} %collective-permute-done.8.refs_4_), channel_id=1, source_target_pairs={{0,2},{2,4},{4,6},{6,7},{7,5},{5,3},{3,1},{1,0},{10,8},{12,10},{14... | collective-permute-start | bytes 626696 | tf_op jit(solution)/shard_map/ppermute | solution.py:273
  22.2 9.0 %collective-permute-start.15 = (bf16[16,6528]{1,0:T(8,128)(2,1)S(1)}, bf16[16,6528]{1,0:T(8,128)(2,1)S(1)}, u32[]{:S(2)}, u32[]{:S(2)}) collective-permute-start(bf16[16,6528]{1,0:T(8,128)(2,1)S(1)} %get-tuple-element.27), channel_id=1, source_target_pairs={{0,24},{1,25},{2,26},{3,27},{4,28},{5,29},{6,30},{7,31},{8,16},{9,... | collective-permute-start | bytes 626696 | tf_op jit(solution)/shard_map/ppermute | solution.py:273
  23.2 9.9 %collective-permute-start.14 = (bf16[16,6528]{1,0:T(8,128)(2,1)S(1)}, bf16[16,6528]{1,0:T(8,128)(2,1)S(1)}, u32[]{:S(2)}, u32[]{:S(2)}) collective-permute-start(bf16[16,6528]{1,0:T(8,128)(2,1)S(1)} %collective-permute-done.13.refs_2_), channel_id=1, source_target_pairs={{2,0},{4,2},{6,4},{7,6},{5,7},{3,5},{1,3},{0,1},{8,10},{10,12},{12... | collective-permute-start | bytes 626696 | tf_op jit(solution)/shard_map/ppermute | solution.py:273
  26.4 9.0 %collective-permute-start.2 = (bf16[16,6528]{1,0:T(8,128)(2,1)S(1)}, bf16[16,6528]{1,0:T(8,128)(2,1)S(1)}, u32[]{:S(2)}, u32[]{:S(2)}) collective-permute-start(bf16[16,6528]{1,0:T(8,128)(2,1)S(1)} %collective-permute-done.1.refs_3_), channel_id=1, source_target_pairs={{0,2},{2,4},{4,6},{6,7},{7,5},{5,3},{3,1},{1,0},{10,8},{12,10},{14... | collective-permute-start | bytes 626696 | tf_op jit(solution)/shard_map/ppermute | solution.py:273
  27.7 9.0 %collective-permute-start.6 = (bf16[16,6528]{1,0:T(8,128)(2,1)S(1)}, bf16[16,6528]{1,0:T(8,128)(2,1)S(1)}, u32[]{:S(2)}, u32[]{:S(2)}) collective-permute-start(bf16[16,6528]{1,0:T(8,128)(2,1)S(1)} %collective-permute-done.5.refs_1_), channel_id=1, source_target_pairs={{2,0},{4,2},{6,4},{7,6},{5,7},{3,5},{1,3},{0,1},{8,10},{10,12},{12... | collective-permute-start | bytes 626696 | tf_op jit(solution)/shard_map/ppermute | solution.py:273
  30.9 6.2 %collective-permute-start.11 = (bf16[16,3456]{1,0:T(8,128)(2,1)S(1)}, bf16[16,3456]{1,0:T(8,128)(2,1)S(1)}, u32[]{:S(2)}, u32[]{:S(2)}) collective-permute-start(bf16[16,3456]{1,0:T(8,128)(2,1)S(1)} %slice.9), channel_id=1, source_target_pairs={{0,2},{2,4},{4,6},{6,7},{7,5},{5,3},{3,1},{1,0},{10,8},{12,10},{14... | collective-permute-start | bytes 331784 | tf_op jit(solution)/shard_map/ppermute | solution.py:273
  31.2 6.9 %collective-permute-start.10 = (bf16[16,3072]{1,0:T(8,128)(2,1)S(1)}, bf16[16,3072]{1,0:T(8,128)(2,1)S(1)}, u32[]{:S(2)}, u32[]{:S(2)}) collective-permute-start(bf16[16,3072]{1,0:T(8,128)(2,1)S(1)} %slice.8), channel_id=1, source_target_pairs={{0,2},{2,4},{4,6},{6,7},{7,5},{5,3},{3,1},{1,0},{10,8},{12,10},{14... | collective-permute-start | bytes 294920 | tf_op jit(solution)/shard_map/ppermute | solution.py:273

commit v9 on v8

--- a/solution.py
+++ b/solution.py
@@ -224,6 +224,24 @@
     )(*operands)
 
 
+def fetch_kernel(source, out_ref, sem):
+    copy = pltpu.make_async_copy(source, out_ref, sem)
+    copy.start()
+    copy.wait()
+
+
+def fetch(weight_in):
+    return pl.pallas_call(
+        fetch_kernel,
+        out_shape=pltpu.VMEM(weight_in.shape, weight_in.dtype),
+        in_specs=[pl.BlockSpec(memory_space=pltpu.HBM)],
+        out_specs=pl.BlockSpec(memory_space=pltpu.VMEM),
+        scratch_shapes=[pltpu.SemaphoreType.DMA],
+        compiler_params=pltpu.CompilerParams(vmem_limit_bytes=16 * 2**20),
+        name="fetch_weights",
+    )(pltpu.with_memory_space_constraint(weight_in, pltpu.HBM))
+
+
 def grad(got, firsts, seconds, weight_in):
     width, hidden = weight_in.shape
     count, late = len(got), len(seconds)
@@ -259,7 +277,7 @@
     return total
 
 
-def gather_both(lead, trail, up, n_pipe, cycle, cut):
+def gather_both(lead, trail, up, held, n_pipe, cycle, cut):
     n = len(cycle)
     right = [(cycle[i], cycle[(i + 1) % n]) for i in range(n)]
     left = [(b, a) for a, b in right]
@@ -282,6 +300,8 @@
         move(trail, left, lambda turned: turned),
     )
     got = [*at]
+    first, held = lax.optimization_barrier((at[0], held))
+    at = (first, *at[1:])
     for _ in range(1, (n - 1) // 2):
         at = turn(at)
         got += at
@@ -313,8 +333,9 @@
     )
     width = w_in.shape[1]
     cut = width + width // SEGS
-    got, firsts, seconds = gather_both(lead, trail, up, n_pipe, grid_cycle(n_expert), cut)
-    return grad([*got, down], firsts, seconds, w_in[0])[None]
+    weight_in = fetch(w_in[0])
+    got, firsts, seconds = gather_both(lead, trail, up, weight_in, n_pipe, grid_cycle(n_expert), cut)
+    return grad([*got, down], firsts, seconds, weight_in)[None]
 
 
 def solution(mesh):

time: 39.8 us -> 39.7 us (level)
  waiting for transfers between devices: 11.6 us -> 10.1 us
  Pallas kernels: 6.31 us -> 7.61 us
    ppermute x16, waiting for transfers between devices: 11.6 us -> 10.1 us  [move(): return lax.ppermute(block, ('pipe', 'expert'), pairs)]
    pallas_call x0 -> x1, Pallas kernels: none -> 1.42 us  [fetch(): pl.pallas_call(fetch_kernel, out_shape=pltpu.VMEM(weight_in.shape, weight...]
  transfers between devices with their start and end apart: 16 -> 16, of which waited for: 13 -> 13; matrix products, arithmetic and copies ran while one was open for 0% -> 0% of each run, Pallas kernels for 8% -> 12%
where the time goes in v9:
time: 39.7 us; the launch traced here: 39.5 us
  starting transfers between devices  21.6 us (54%)
  waiting for transfers between devices  10.1 us (25%)
  Pallas kernels  7.61 us (19%)
    ppermute x16, starting transfers between devices, move(): return lax.ppermute(block, ('pipe', 'expert'), pairs)  21.6 us
    ppermute x16, waiting for transfers between devices, move(): return lax.ppermute(block, ('pipe', 'expert'), pairs)  10.1 us
    pallas_call x5, Pallas kernels, local_call(): pl.pallas_call(kernel, out_shape=outs, in_specs=[pl.BlockSpec(memory_spac...  4.7 us
    pallas_call x1, Pallas kernels, pack(): pl.pallas_call(functools.partial(lead_kernel, n_pipe), out_shape=(payload...  1.49 us
    pallas_call x1, Pallas kernels, fetch(): pl.pallas_call(fetch_kernel, out_shape=pltpu.VMEM(weight_in.shape, weight...  1.42 us
  transfers between devices with their start and end apart: 16, of which 13 were waited for; matrix products, arithmetic and copies ran while one was open for 0% of the time, Pallas kernels for 12%

profile of v9, /device:TPU:0, one launch (start us, length us, event | category | flops | bytes accessed | tf_op | source)
XLA Modules:
  0.0 39.5 jit_solution(14238103548195284816)
XLA Ops:
  0.0 1.5 %pack_lead.1 = (bf16[16,6528]{1,0:T(8,128)(2,1)S(1)}, bf16[64,3072]{1,0:T(8,128)(2,1)S(1)}, bf16[64,3072]{1,0:T(8,128)(2,1)S(1)}, bf16[2,64]{1,0:T(2,128)(2,1)S(1)}, s32[2,64]{1,0:T(2,128)S(1)}) custom-call(bf16[64,3072]{1,0:T(8,128)(2,1)} %bitcast.19, bf16[64,3072]{1,0:T(8,128)(2,1)} %bitcast.20, bf16[2,64]{1,0:T(2,128)(2,1)} %bitcast.25, ...), custom_call_target="tpu_custom_call" | custom-call | flops 25165824 | bytes 2359296 | tf_op jit(solution)/shard_map/pack_lead/pallas_call | solution.py:112
  1.5 3.4 %collective-permute-start.3 = (bf16[16,6528]{1,0:T(8,128)(2,1)S(1)}, bf16[16,6528]{1,0:T(8,128)(2,1)S(1)}, u32[]{:S(2)}, u32[]{:S(2)}) collective-permute-start(bf16[16,6528]{1,0:T(8,128)(2,1)S(1)} %get-tuple-element.18.lead), channel_id=1, source_target_pairs={{2,24},{4,26},{6,28},{7,30},{5,31},{3,29},{1,27},{0,25},{8,10},{10... | collective-permute-start | bytes 626696 | tf_op jit(solution)/shard_map/ppermute | solution.py:291
  4.9 0.4 pack_trail.1
  5.3 0.6 %collective-permute-start.7 = (bf16[16,6528]{1,0:T(8,128)(2,1)S(1)}, bf16[16,6528]{1,0:T(8,128)(2,1)S(1)}, u32[]{:S(2)}, u32[]{:S(2)}) collective-permute-start(bf16[16,6528]{1,0:T(8,128)(2,1)S(1)} %get-tuple-element.24), channel_id=1, source_target_pairs={{0,2},{2,4},{4,6},{6,7},{7,5},{5,3},{3,1},{1,0},{10,16},{12,18},{1... | collective-permute-start | bytes 626696 | tf_op jit(solution)/shard_map/ppermute | solution.py:291
  5.9 1.5 %collective-permute-start.12 = (bf16[16,6528]{1,0:T(8,128)(2,1)S(1)}, bf16[16,6528]{1,0:T(8,128)(2,1)S(1)}, u32[]{:S(2)}, u32[]{:S(2)}) collective-permute-start(bf16[16,6528]{1,0:T(8,128)(2,1)S(1)} %get-tuple-element.24), channel_id=1, source_target_pairs={{2,0},{4,2},{6,4},{7,6},{5,7},{3,5},{1,3},{0,1},{8,18},{10,20},{12... | collective-permute-start | bytes 626696 | tf_op jit(solution)/shard_map/ppermute | solution.py:291
  7.4 0.0 collective-permute-start
  7.4 1.4 %fetch_weights.1.refs_2_.refs_1_.refs_13_ = bf16[3072,256]{1,0:T(8,128)(2,1)S(1)} custom-call(bf16[3072,256]{1,0:T(8,128)(2,1)} %bitcast.18), custom_call_target="tpu_custom_call" | custom-call | tf_op jit(solution)/shard_map/fetch_weights/pallas_call | solution.py:234
  8.8 0.8 %collective-permute-done.3.refs_9_ = bf16[16,6528]{1,0:T(8,128)(2,1)S(1)} collective-permute-done((bf16[16,6528]{1,0:T(8,128)(2,1)S(1)}, bf16[16,6528]{1,0:T(8,128)(2,1)S(1)}, u32[]{:S(2)}, u32[]{:S(2)}) %collective-permute-start.3) | collective-permute-done | bytes 208928 | tf_op jit(solution)/shard_map/ppermute | solution.py:291
  9.7 2.0 %collective-permute-start.4 = (bf16[16,6528]{1,0:T(8,128)(2,1)S(1)}, bf16[16,6528]{1,0:T(8,128)(2,1)S(1)}, u32[]{:S(2)}, u32[]{:S(2)}) collective-permute-start(bf16[16,6528]{1,0:T(8,128)(2,1)S(1)} %collective-permute-done.3.refs_9_), channel_id=1, source_target_pairs={{2,0},{4,2},{6,4},{7,6},{5,7},{3,5},{1,3},{0,1},{8,10},{10,12},{12... | collective-permute-start | bytes 626696 | tf_op jit(solution)/shard_map/ppermute | solution.py:291
  11.6 1.6 %collective-permute-done.7.refs_8_ = bf16[16,6528]{1,0:T(8,128)(2,1)S(1)} collective-permute-done((bf16[16,6528]{1,0:T(8,128)(2,1)S(1)}, bf16[16,6528]{1,0:T(8,128)(2,1)S(1)}, u32[]{:S(2)}, u32[]{:S(2)}) %collective-permute-start.7) | collective-permute-done | bytes 208928 | tf_op jit(solution)/shard_map/ppermute | solution.py:291
  13.2 0.0 collective-permute-start.8
  13.2 0.9 %collective-permute-done.12.refs_6_ = bf16[16,6528]{1,0:T(8,128)(2,1)S(1)} collective-permute-done((bf16[16,6528]{1,0:T(8,128)(2,1)S(1)}, bf16[16,6528]{1,0:T(8,128)(2,1)S(1)}, u32[]{:S(2)}, u32[]{:S(2)}) %collective-permute-start.12) | collective-permute-done | bytes 208928 | tf_op jit(solution)/shard_map/ppermute | solution.py:291
  14.1 2.5 %collective-permute-start.13 = (bf16[16,6528]{1,0:T(8,128)(2,1)S(1)}, bf16[16,6528]{1,0:T(8,128)(2,1)S(1)}, u32[]{:S(2)}, u32[]{:S(2)}) collective-permute-start(bf16[16,6528]{1,0:T(8,128)(2,1)S(1)} %collective-permute-done.12.refs_6_), channel_id=1, source_target_pairs={{2,0},{4,2},{6,4},{7,6},{5,7},{3,5},{1,3},{0,1},{8,10},{10,12},{12... | collective-permute-start | bytes 626696 | tf_op jit(solution)/shard_map/ppermute | solution.py:291
  16.6 1.1 %collective-permute-done.refs_7_ = bf16[16,6528]{1,0:T(8,128)(2,1)S(1)} collective-permute-done((bf16[16,6528]{1,0:T(8,128)(2,1)S(1)}, bf16[16,6528]{1,0:T(8,128)(2,1)S(1)}, u32[]{:S(2)}, u32[]{:S(2)}) %collective-permute-start) | collective-permute-done | bytes 208928 | tf_op jit(solution)/shard_map/ppermute | solution.py:291
  17.7 0.7 %collective-permute-start.1 = (bf16[16,6528]{1,0:T(8,128)(2,1)S(1)}, bf16[16,6528]{1,0:T(8,128)(2,1)S(1)}, u32[]{:S(2)}, u32[]{:S(2)}) collective-permute-start(bf16[16,6528]{1,0:T(8,128)(2,1)S(1)} %collective-permute-done.refs_7_), channel_id=1, source_target_pairs={{0,2},{2,4},{4,6},{6,7},{7,5},{5,3},{3,1},{1,0},{10,8},{12,10},{14... | collective-permute-start | bytes 626696 | tf_op jit(solution)/shard_map/ppermute | solution.py:291
  18.4 0.3 collective-permute-done.4.refs_5_
  18.6 2.5 %collective-permute-start.5 = (bf16[16,6528]{1,0:T(8,128)(2,1)S(1)}, bf16[16,6528]{1,0:T(8,128)(2,1)S(1)}, u32[]{:S(2)}, u32[]{:S(2)}) collective-permute-start(bf16[16,6528]{1,0:T(8,128)(2,1)S(1)} %collective-permute-done.4.refs_5_), channel_id=1, source_target_pairs={{2,0},{4,2},{6,4},{7,6},{5,7},{3,5},{1,3},{0,1},{8,10},{10,12},{12... | collective-permute-start | bytes 626696 | tf_op jit(solution)/shard_map/ppermute | solution.py:291
  21.1 0.7 %collective-permute-done.8.refs_4_ = bf16[16,6528]{1,0:T(8,128)(2,1)S(1)} collective-permute-done((bf16[16,6528]{1,0:T(8,128)(2,1)S(1)}, bf16[16,6528]{1,0:T(8,128)(2,1)S(1)}, u32[]{:S(2)}, u32[]{:S(2)}) %collective-permute-start.8) | collective-permute-done | bytes 208928 | tf_op jit(solution)/shard_map/ppermute | solution.py:291
  21.8 0.3 collective-permute-start.9
  22.1 0.7 %collective-permute-start.15 = (bf16[16,6528]{1,0:T(8,128)(2,1)S(1)}, bf16[16,6528]{1,0:T(8,128)(2,1)S(1)}, u32[]{:S(2)}, u32[]{:S(2)}) collective-permute-start(bf16[16,6528]{1,0:T(8,128)(2,1)S(1)} %get-tuple-element.29), channel_id=1, source_target_pairs={{0,24},{1,25},{2,26},{3,27},{4,28},{5,29},{6,30},{7,31},{8,16},{9,... | collective-permute-start | bytes 626696 | tf_op jit(solution)/shard_map/ppermute | solution.py:291
  22.8 0.3 collective-permute-done.13.refs_2_
  23.1 2.5 %collective-permute-start.14 = (bf16[16,6528]{1,0:T(8,128)(2,1)S(1)}, bf16[16,6528]{1,0:T(8,128)(2,1)S(1)}, u32[]{:S(2)}, u32[]{:S(2)}) collective-permute-start(bf16[16,6528]{1,0:T(8,128)(2,1)S(1)} %collective-permute-done.13.refs_2_), channel_id=1, source_target_pairs={{2,0},{4,2},{6,4},{7,6},{5,7},{3,5},{1,3},{0,1},{8,10},{10,12},{12... | collective-permute-start | bytes 626696 | tf_op jit(solution)/shard_map/ppermute | solution.py:291
  25.6 0.7 %collective-permute-done.1.refs_3_ = bf16[16,6528]{1,0:T(8,128)(2,1)S(1)} collective-permute-done((bf16[16,6528]{1,0:T(8,128)(2,1)S(1)}, bf16[16,6528]{1,0:T(8,128)(2,1)S(1)}, u32[]{:S(2)}, u32[]{:S(2)}) %collective-permute-start.1) | collective-permute-done | bytes 208928 | tf_op jit(solution)/shard_map/ppermute | solution.py:291
  26.2 0.3 collective-permute-start.2
  26.5 1.0 %collective-permute-done.5.refs_1_ = bf16[16,6528]{1,0:T(8,128)(2,1)S(1)} collective-permute-done((bf16[16,6528]{1,0:T(8,128)(2,1)S(1)}, bf16[16,6528]{1,0:T(8,128)(2,1)S(1)}, u32[]{:S(2)}, u32[]{:S(2)}) %collective-permute-start.5) | collective-permute-done | bytes 208928 | tf_op jit(solution)/shard_map/ppermute | solution.py:291
  27.6 2.5 %collective-permute-start.6 = (bf16[16,6528]{1,0:T(8,128)(2,1)S(1)}, bf16[16,6528]{1,0:T(8,128)(2,1)S(1)}, u32[]{:S(2)}, u32[]{:S(2)}) collective-permute-start(bf16[16,6528]{1,0:T(8,128)(2,1)S(1)} %collective-permute-done.5.refs_1_), channel_id=1, source_target_pairs={{2,0},{4,2},{6,4},{7,6},{5,7},{3,5},{1,3},{0,1},{8,10},{10,12},{12... | collective-permute-start | bytes 626696 | tf_op jit(solution)/shard_map/ppermute | solution.py:291
  30.0 0.7 %collective-permute-done.9.refs_0_ = bf16[16,6528]{1,0:T(8,128)(2,1)S(1)} collective-permute-done((bf16[16,6528]{1,0:T(8,128)(2,1)S(1)}, bf16[16,6528]{1,0:T(8,128)(2,1)S(1)}, u32[]{:S(2)}, u32[]{:S(2)}) %collective-permute-start.9) | collective-permute-done | bytes 208928 | tf_op jit(solution)/shard_map/ppermute | solution.py:291
  30.7 0.3 collective-permute-start.11
  31.1 0.0 collective-permute-done.15.refs_11_
  31.1 1.9 %collective-permute-start.10 = (bf16[16,3072]{1,0:T(8,128)(2,1)S(1)}, bf16[16,3072]{1,0:T(8,128)(2,1)S(1)}, u32[]{:S(2)}, u32[]{:S(2)}) collective-permute-start(bf16[16,3072]{1,0:T(8,128)(2,1)S(1)} %slice.8), channel_id=1, source_target_pairs={{0,2},{2,4},{4,6},{6,7},{7,5},{5,3},{3,1},{1,0},{10,8},{12,10},{14... | collective-permute-start | bytes 294920 | tf_op jit(solution)/shard_map/ppermute | solution.py:291
  33.0 0.0 collective-permute-done.14.refs_10_
  33.0 2.0 %grad_part.1.refs_5_ = f32[256,3072]{1,0:T(8,128)S(1)} custom-call(bf16[16,6528]{1,0:T(8,128)(2,1)S(1)} %collective-permute-done.9.refs_0_, bf16[16,6528]{1,0:T(8,128)(2,1)S(1)} %collective-permute-done.5.refs_1_, bf16[16,6528]{1,0:T(8,128)(2,1)S(1)} %collective-permute-done.13.refs_2_, bf16[16,6528]{1,0:T(8,128)(2,1)S(1)} %collective-permute-done.1.refs_3_, ...), custom_call_target="tpu_custom_call" | custom-call | flops 695205888 | bytes 4288512 | tf_op jit(solution)/shard_map/grad_part/pallas_call | solution.py:212
  35.0 0.2 collective-permute-done.2.refs_0_
  35.2 1.3 %collective-permute-done.6.refs_1_ = bf16[16,6528]{1,0:T(8,128)(2,1)S(1)} collective-permute-done((bf16[16,6528]{1,0:T(8,128)(2,1)S(1)}, bf16[16,6528]{1,0:T(8,128)(2,1)S(1)}, u32[]{:S(2)}, u32[]{:S(2)}) %collective-permute-start.6) | collective-permute-done | bytes 208928 | tf_op jit(solution)/shard_map/ppermute | solution.py:291
  36.5 0.4 %active_late.2 = (bf16[34,256]{1,0:T(8,128)(2,1)S(1)}, bf16[2,3072]{1,0:T(2,128)(2,1)S(1)}) custom-call(bf16[16,6528]{1,0:T(8,128)(2,1)S(1)} %collective-permute-done.2.refs_0_, bf16[16,6528]{1,0:T(8,128)(2,1)S(1)} %collective-permute-done.6.refs_1_, bf16[3072,256]{1,0:T(8,128)(2,1)S(1)} %fetch_weights.1.refs_2_.refs_1_.refs_13_), custom_call_target="tpu_custom_call" | custom-call | flops 53477376 | bytes 1990656 | tf_op jit(solution)/shard_map/active_late/pallas_call | solution.py:212
  37.0 0.0 collective-permute-done.11.refs_0_
  37.0 0.4 %active_late.3 = (bf16[51,256]{1,0:T(8,128)(2,1)S(1)}, bf16[3,3072]{1,0:T(4,128)(2,1)S(1)}) custom-call(bf16[16,3456]{1,0:T(8,128)(2,1)S(1)} %collective-permute-done.11.refs_0_, bf16[3072,256]{1,0:T(8,128)(2,1)S(1)} %fetch_weights.1.refs_2_.refs_1_.refs_13_, bf16[34,256]{1,0:T(8,128)(2,1)S(1)} %get-tuple-element.25.refs_2_, ...), custom_call_target="tpu_custom_call" | custom-call | flops 26738688 | bytes 1713152 | tf_op jit(solution)/shard_map/active_late/pallas_call | solution.py:212
  37.4 0.6 %collective-permute-done.10.refs_2_ = bf16[16,3072]{1,0:T(8,128)(2,1)S(1)} collective-permute-done((bf16[16,3072]{1,0:T(8,128)(2,1)S(1)}, bf16[16,3072]{1,0:T(8,128)(2,1)S(1)}, u32[]{:S(2)}, u32[]{:S(2)}) %collective-permute-start.10) | collective-permute-done | bytes 98336 | tf_op jit(solution)/shard_map/ppermute | solution.py:291
  38.0 1.5 %grad_sum.1 = bf16[256,3072]{1,0:T(8,128)(2,1)} custom-call(bf16[16,6528]{1,0:T(8,128)(2,1)S(1)} %collective-permute-done.2.refs_0_, bf16[16,6528]{1,0:T(8,128)(2,1)S(1)} %collective-permute-done.6.refs_1_, bf16[16,3072]{1,0:T(8,128)(2,1)S(1)} %collective-permute-done.10.refs_2_, bf16[51,256]{1,0:T(8,128)(2,1)S(1)} %get-tuple-element.27.refs_3_, ...), custom_call_target="tpu_custom_call" | custom-call | flops 80216064 | bytes 3706368 | tf_op jit(solution)/shard_map/grad_sum/pallas_call | solution.py:212
  (2 shorter events, 0.0 us)
Async XLA Ops:
  1.5 8.2 %collective-permute-start.3 = (bf16[16,6528]{1,0:T(8,128)(2,1)S(1)}, bf16[16,6528]{1,0:T(8,128)(2,1)S(1)}, u32[]{:S(2)}, u32[]{:S(2)}) collective-permute-start(bf16[16,6528]{1,0:T(8,128)(2,1)S(1)} %get-tuple-element.18.lead), channel_id=1, source_target_pairs={{2,24},{4,26},{6,28},{7,30},{5,31},{3,29},{1,27},{0,25},{8,10},{10... | collective-permute-start | bytes 626696 | tf_op jit(solution)/shard_map/ppermute | solution.py:291
  5.3 7.9 %collective-permute-start.7 = (bf16[16,6528]{1,0:T(8,128)(2,1)S(1)}, bf16[16,6528]{1,0:T(8,128)(2,1)S(1)}, u32[]{:S(2)}, u32[]{:S(2)}) collective-permute-start(bf16[16,6528]{1,0:T(8,128)(2,1)S(1)} %get-tuple-element.24), channel_id=1, source_target_pairs={{0,2},{2,4},{4,6},{6,7},{7,5},{5,3},{3,1},{1,0},{10,16},{12,18},{1... | collective-permute-start | bytes 626696 | tf_op jit(solution)/shard_map/ppermute | solution.py:291
  5.9 8.3 %collective-permute-start.12 = (bf16[16,6528]{1,0:T(8,128)(2,1)S(1)}, bf16[16,6528]{1,0:T(8,128)(2,1)S(1)}, u32[]{:S(2)}, u32[]{:S(2)}) collective-permute-start(bf16[16,6528]{1,0:T(8,128)(2,1)S(1)} %get-tuple-element.24), channel_id=1, source_target_pairs={{2,0},{4,2},{6,4},{7,6},{5,7},{3,5},{1,3},{0,1},{8,18},{10,20},{12... | collective-permute-start | bytes 626696 | tf_op jit(solution)/shard_map/ppermute | solution.py:291
  7.4 10.3 %collective-permute-start = (bf16[16,6528]{1,0:T(8,128)(2,1)S(1)}, bf16[16,6528]{1,0:T(8,128)(2,1)S(1)}, u32[]{:S(2)}, u32[]{:S(2)}) collective-permute-start(bf16[16,6528]{1,0:T(8,128)(2,1)S(1)} %get-tuple-element.18.lead), channel_id=1, source_target_pairs={{0,26},{2,28},{4,30},{6,31},{7,29},{5,27},{3,25},{1,24},{10,8},{12... | collective-permute-start | bytes 626696 | tf_op jit(solution)/shard_map/ppermute | solution.py:291
  9.7 9.0 %collective-permute-start.4 = (bf16[16,6528]{1,0:T(8,128)(2,1)S(1)}, bf16[16,6528]{1,0:T(8,128)(2,1)S(1)}, u32[]{:S(2)}, u32[]{:S(2)}) collective-permute-start(bf16[16,6528]{1,0:T(8,128)(2,1)S(1)} %collective-permute-done.3.refs_9_), channel_id=1, source_target_pairs={{2,0},{4,2},{6,4},{7,6},{5,7},{3,5},{1,3},{0,1},{8,10},{10,12},{12... | collective-permute-start | bytes 626696 | tf_op jit(solution)/shard_map/ppermute | solution.py:291
  13.2 8.6 %collective-permute-start.8 = (bf16[16,6528]{1,0:T(8,128)(2,1)S(1)}, bf16[16,6528]{1,0:T(8,128)(2,1)S(1)}, u32[]{:S(2)}, u32[]{:S(2)}) collective-permute-start(bf16[16,6528]{1,0:T(8,128)(2,1)S(1)} %collective-permute-done.7.refs_8_), channel_id=1, source_target_pairs={{0,2},{2,4},{4,6},{6,7},{7,5},{5,3},{3,1},{1,0},{10,8},{12,10},{14... | collective-permute-start | bytes 626696 | tf_op jit(solution)/shard_map/ppermute | solution.py:291
  14.1 9.0 %collective-permute-start.13 = (bf16[16,6528]{1,0:T(8,128)(2,1)S(1)}, bf16[16,6528]{1,0:T(8,128)(2,1)S(1)}, u32[]{:S(2)}, u32[]{:S(2)}) collective-permute-start(bf16[16,6528]{1,0:T(8,128)(2,1)S(1)} %collective-permute-done.12.refs_6_), channel_id=1, source_target_pairs={{2,0},{4,2},{6,4},{7,6},{5,7},{3,5},{1,3},{0,1},{8,10},{10,12},{12... | collective-permute-start | bytes 626696 | tf_op jit(solution)/shard_map/ppermute | solution.py:291
  17.7 8.6 %collective-permute-start.1 = (bf16[16,6528]{1,0:T(8,128)(2,1)S(1)}, bf16[16,6528]{1,0:T(8,128)(2,1)S(1)}, u32[]{:S(2)}, u32[]{:S(2)}) collective-permute-start(bf16[16,6528]{1,0:T(8,128)(2,1)S(1)} %collective-permute-done.refs_7_), channel_id=1, source_target_pairs={{0,2},{2,4},{4,6},{6,7},{7,5},{5,3},{3,1},{1,0},{10,8},{12,10},{14... | collective-permute-start | bytes 626696 | tf_op jit(solution)/shard_map/ppermute | solution.py:291
  18.6 9.0 %collective-permute-start.5 = (bf16[16,6528]{1,0:T(8,128)(2,1)S(1)}, bf16[16,6528]{1,0:T(8,128)(2,1)S(1)}, u32[]{:S(2)}, u32[]{:S(2)}) collective-permute-start(bf16[16,6528]{1,0:T(8,128)(2,1)S(1)} %collective-permute-done.4.refs_5_), channel_id=1, source_target_pairs={{2,0},{4,2},{6,4},{7,6},{5,7},{3,5},{1,3},{0,1},{8,10},{10,12},{12... | collective-permute-start | bytes 626696 | tf_op jit(solution)/shard_map/ppermute | solution.py:291
  21.8 9.0 %collective-permute-start.9 = (bf16[16,6528]{1,0:T(8,128)(2,1)S(1)}, bf16[16,6528]{1,0:T(8,128)(2,1)S(1)}, u32[]{:S(2)}, u32[]{:S(2)}) collective-permute-start(bf16[16,6528]{1,0:T(8,128)(2,1)S(1)} %collective-permute-done.8.refs_4_), channel_id=1, source_target_pairs={{0,2},{2,4},{4,6},{6,7},{7,5},{5,3},{3,1},{1,0},{10,8},{12,10},{14... | collective-permute-start | bytes 626696 | tf_op jit(solution)/shard_map/ppermute | solution.py:291
  22.1 9.0 %collective-permute-start.15 = (bf16[16,6528]{1,0:T(8,128)(2,1)S(1)}, bf16[16,6528]{1,0:T(8,128)(2,1)S(1)}, u32[]{:S(2)}, u32[]{:S(2)}) collective-permute-start(bf16[16,6528]{1,0:T(8,128)(2,1)S(1)} %get-tuple-element.29), channel_id=1, source_target_pairs={{0,24},{1,25},{2,26},{3,27},{4,28},{5,29},{6,30},{7,31},{8,16},{9,... | collective-permute-start | bytes 626696 | tf_op jit(solution)/shard_map/ppermute | solution.py:291
  23.1 9.9 %collective-permute-start.14 = (bf16[16,6528]{1,0:T(8,128)(2,1)S(1)}, bf16[16,6528]{1,0:T(8,128)(2,1)S(1)}, u32[]{:S(2)}, u32[]{:S(2)}) collective-permute-start(bf16[16,6528]{1,0:T(8,128)(2,1)S(1)} %collective-permute-done.13.refs_2_), channel_id=1, source_target_pairs={{2,0},{4,2},{6,4},{7,6},{5,7},{3,5},{1,3},{0,1},{8,10},{10,12},{12... | collective-permute-start | bytes 626696 | tf_op jit(solution)/shard_map/ppermute | solution.py:291
  26.2 9.0 %collective-permute-start.2 = (bf16[16,6528]{1,0:T(8,128)(2,1)S(1)}, bf16[16,6528]{1,0:T(8,128)(2,1)S(1)}, u32[]{:S(2)}, u32[]{:S(2)}) collective-permute-start(bf16[16,6528]{1,0:T(8,128)(2,1)S(1)} %collective-permute-done.1.refs_3_), channel_id=1, source_target_pairs={{0,2},{2,4},{4,6},{6,7},{7,5},{5,3},{3,1},{1,0},{10,8},{12,10},{14... | collective-permute-start | bytes 626696 | tf_op jit(solution)/shard_map/ppermute | solution.py:291
  27.6 9.0 %collective-permute-start.6 = (bf16[16,6528]{1,0:T(8,128)(2,1)S(1)}, bf16[16,6528]{1,0:T(8,128)(2,1)S(1)}, u32[]{:S(2)}, u32[]{:S(2)}) collective-permute-start(bf16[16,6528]{1,0:T(8,128)(2,1)S(1)} %collective-permute-done.5.refs_1_), channel_id=1, source_target_pairs={{2,0},{4,2},{6,4},{7,6},{5,7},{3,5},{1,3},{0,1},{8,10},{10,12},{12... | collective-permute-start | bytes 626696 | tf_op jit(solution)/shard_map/ppermute | solution.py:291
  30.7 6.2 %collective-permute-start.11 = (bf16[16,3456]{1,0:T(8,128)(2,1)S(1)}, bf16[16,3456]{1,0:T(8,128)(2,1)S(1)}, u32[]{:S(2)}, u32[]{:S(2)}) collective-permute-start(bf16[16,3456]{1,0:T(8,128)(2,1)S(1)} %slice.9), channel_id=1, source_target_pairs={{0,2},{2,4},{4,6},{6,7},{7,5},{5,3},{3,1},{1,0},{10,8},{12,10},{14... | collective-permute-start | bytes 331784 | tf_op jit(solution)/shard_map/ppermute | solution.py:291
  31.1 6.9 %collective-permute-start.10 = (bf16[16,3072]{1,0:T(8,128)(2,1)S(1)}, bf16[16,3072]{1,0:T(8,128)(2,1)S(1)}, u32[]{:S(2)}, u32[]{:S(2)}) collective-permute-start(bf16[16,3072]{1,0:T(8,128)(2,1)S(1)} %slice.8), channel_id=1, source_target_pairs={{0,2},{2,4},{4,6},{6,7},{7,5},{5,3},{3,1},{1,0},{10,8},{12,10},{14... | collective-permute-start | bytes 294920 | tf_op jit(solution)/shard_map/ppermute | solution.py:291

commit v10 on v9

--- a/solution.py
+++ b/solution.py
@@ -93,15 +93,8 @@
         waits[i].wait()
 
 
-def trail_kernel(n_pipe, lead, tokens_ref, cotan_ref, gates_ref, ids_ref, trail, up, down):
+def trail_kernel(tokens_ref, cotan_ref, gates_ref, ids_ref, trail):
     write_payload(trail, tokens_ref, cotan_ref, *place(gates_ref[...], ids_ref[...]))
-    turned = is_turned(lax.axis_index("pipe"), n_pipe)
-    for swapped, first, second in ((False, up, down), (True, down, up)):
-
-        @pl.when(turned == swapped)
-        def _():
-            first[...] = lead[...]
-            second[...] = trail[...]
 
 
 def pack(arrays, n_pipe):
@@ -122,14 +115,14 @@
         ),
         name="pack_lead",
     )(*arrays)
-    rest = local_call(
-        functools.partial(trail_kernel, n_pipe),
+    (rest,) = local_call(
+        trail_kernel,
         "pack_trail",
-        (lead, *trail),
-        (payload,) * 3,
+        tuple(trail),
+        (payload,),
         flops=4 * 2 * MAIN * rows * width,
     )
-    return (lead, *rest)
+    return lead, rest
 
 
 def activate(payloads, w_ref):
@@ -224,22 +217,31 @@
     )(*operands)
 
 
-def fetch_kernel(source, out_ref, sem):
-    copy = pltpu.make_async_copy(source, out_ref, sem)
+def fetch_kernel(n_pipe, source, lead, trail, weights, up, down, sem):
+    copy = pltpu.make_async_copy(source, weights, sem)
     copy.start()
+    turned = is_turned(lax.axis_index("pipe"), n_pipe)
+    for swapped, first, second in ((False, up, down), (True, down, up)):
+
+        @pl.when(turned == swapped)
+        def _():
+            first[...] = lead[...]
+            second[...] = trail[...]
     copy.wait()
 
 
-def fetch(weight_in):
+def fetch(weight_in, lead, trail, n_pipe):
+    payload = pltpu.VMEM(lead.shape, lead.dtype)
+    vmem = pl.BlockSpec(memory_space=pltpu.VMEM)
     return pl.pallas_call(
-        fetch_kernel,
-        out_shape=pltpu.VMEM(weight_in.shape, weight_in.dtype),
-        in_specs=[pl.BlockSpec(memory_space=pltpu.HBM)],
-        out_specs=pl.BlockSpec(memory_space=pltpu.VMEM),
+        functools.partial(fetch_kernel, n_pipe),
+        out_shape=(pltpu.VMEM(weight_in.shape, weight_in.dtype), payload, payload),
+        in_specs=[pl.BlockSpec(memory_space=pltpu.HBM), vmem, vmem],
+        out_specs=(vmem,) * 3,
         scratch_shapes=[pltpu.SemaphoreType.DMA],
         compiler_params=pltpu.CompilerParams(vmem_limit_bytes=16 * 2**20),
         name="fetch_weights",
-    )(pltpu.with_memory_space_constraint(weight_in, pltpu.HBM))
+    )(pltpu.with_memory_space_constraint(weight_in, pltpu.HBM), lead, trail)
 
 
 def grad(got, firsts, seconds, weight_in):
@@ -324,7 +326,7 @@
     w_in,
 ):
     n_pipe, n_expert = lax.axis_size("pipe"), lax.axis_size("expert")
-    lead, trail, up, down = pack(
+    lead, trail = pack(
         (
             *(tokens_down[0], cotan_down[0], gates_down[0].T, experts_down[0].T),
             *(tokens_up[0], cotan_up[0], gates_up[0].T, experts_up[0].T),
@@ -333,7 +335,7 @@
     )
     width = w_in.shape[1]
     cut = width + width // SEGS
-    weight_in = fetch(w_in[0])
+    weight_in, up, down = fetch(w_in[0], lead, trail, n_pipe)
     got, firsts, seconds = gather_both(lead, trail, up, weight_in, n_pipe, grid_cycle(n_expert), cut)
     return grad([*got, down], firsts, seconds, weight_in)[None]
 

time: 39.7 us -> 39.6 us (level)
  no operation moved by 1% of the time
where the time goes in v10:
time: 39.6 us; the launch traced here: 39.4 us
  starting transfers between devices  21.5 us (54%)
  waiting for transfers between devices  10.2 us (26%)
  Pallas kernels  7.59 us (19%)
    ppermute x16, starting transfers between devices, move(): return lax.ppermute(block, ('pipe', 'expert'), pairs)  21.5 us
    ppermute x16, waiting for transfers between devices, move(): return lax.ppermute(block, ('pipe', 'expert'), pairs)  10.2 us
    pallas_call x5, Pallas kernels, local_call(): pl.pallas_call(kernel, out_shape=outs, in_specs=[pl.BlockSpec(memory_spac...  4.69 us
    pallas_call x1, Pallas kernels, pack(): pl.pallas_call(functools.partial(lead_kernel, n_pipe), out_shape=(payload...  1.49 us
    pallas_call x1, Pallas kernels, fetch(): pl.pallas_call(functools.partial(fetch_kernel, n_pipe), out_shape=(pltpu....  1.42 us
  transfers between devices with their start and end apart: 16, of which 13 were waited for; matrix products, arithmetic and copies ran while one was open for 0% of the time, Pallas kernels for 12%

profile of v10, /device:TPU:0, one launch (start us, length us, event | category | flops | bytes accessed | tf_op | source)
XLA Modules:
  0.0 39.4 jit_solution(11473030776963013037)
XLA Ops:
  0.0 1.5 %pack_lead.1 = (bf16[16,6528]{1,0:T(8,128)(2,1)S(1)}, bf16[64,3072]{1,0:T(8,128)(2,1)S(1)}, bf16[64,3072]{1,0:T(8,128)(2,1)S(1)}, bf16[2,64]{1,0:T(2,128)(2,1)S(1)}, s32[2,64]{1,0:T(2,128)S(1)}) custom-call(bf16[64,3072]{1,0:T(8,128)(2,1)} %bitcast.19, bf16[64,3072]{1,0:T(8,128)(2,1)} %bitcast.20, bf16[2,64]{1,0:T(2,128)(2,1)} %bitcast.25, ...), custom_call_target="tpu_custom_call" | custom-call | flops 25165824 | bytes 2359296 | tf_op jit(solution)/shard_map/pack_lead/pallas_call | solution.py:105
  1.5 3.4 %collective-permute-start.3 = (bf16[16,6528]{1,0:T(8,128)(2,1)S(1)}, bf16[16,6528]{1,0:T(8,128)(2,1)S(1)}, u32[]{:S(2)}, u32[]{:S(2)}) collective-permute-start(bf16[16,6528]{1,0:T(8,128)(2,1)S(1)} %get-tuple-element.18.lead), channel_id=1, source_target_pairs={{2,24},{4,26},{6,28},{7,30},{5,31},{3,29},{1,27},{0,25},{8,10},{10... | collective-permute-start | bytes 626696 | tf_op jit(solution)/shard_map/ppermute | solution.py:293
  4.9 0.4 pack_trail.1.trail
  5.3 0.6 %collective-permute-start.7 = (bf16[16,6528]{1,0:T(8,128)(2,1)S(1)}, bf16[16,6528]{1,0:T(8,128)(2,1)S(1)}, u32[]{:S(2)}, u32[]{:S(2)}) collective-permute-start(bf16[16,6528]{1,0:T(8,128)(2,1)S(1)} %pack_trail.1.trail), channel_id=1, source_target_pairs={{0,2},{2,4},{4,6},{6,7},{7,5},{5,3},{3,1},{1,0},{10,16},{12,18},{1... | collective-permute-start | bytes 626696 | tf_op jit(solution)/shard_map/ppermute | solution.py:293
  5.9 1.5 %collective-permute-start.12 = (bf16[16,6528]{1,0:T(8,128)(2,1)S(1)}, bf16[16,6528]{1,0:T(8,128)(2,1)S(1)}, u32[]{:S(2)}, u32[]{:S(2)}) collective-permute-start(bf16[16,6528]{1,0:T(8,128)(2,1)S(1)} %pack_trail.1.trail), channel_id=1, source_target_pairs={{2,0},{4,2},{6,4},{7,6},{5,7},{3,5},{1,3},{0,1},{8,18},{10,20},{12... | collective-permute-start | bytes 626696 | tf_op jit(solution)/shard_map/ppermute | solution.py:293
  7.3 0.0 collective-permute-start
  7.4 1.4 %fetch_weights.1 = (bf16[3072,256]{1,0:T(8,128)(2,1)S(1)}, bf16[16,6528]{1,0:T(8,128)(2,1)S(1)}, bf16[16,6528]{1,0:T(8,128)(2,1)S(1)}) custom-call(bf16[3072,256]{1,0:T(8,128)(2,1)} %bitcast.18, bf16[16,6528]{1,0:T(8,128)(2,1)S(1)} %get-tuple-element.18.lead, bf16[16,6528]{1,0:T(8,128)(2,1)S(1)} %pack_trail.1.trail), custom_call_target="tpu_custom_call" | custom-call | tf_op jit(solution)/shard_map/fetch_weights/pallas_call | solution.py:236
  8.8 0.9 %collective-permute-done.3.refs_9_ = bf16[16,6528]{1,0:T(8,128)(2,1)S(1)} collective-permute-done((bf16[16,6528]{1,0:T(8,128)(2,1)S(1)}, bf16[16,6528]{1,0:T(8,128)(2,1)S(1)}, u32[]{:S(2)}, u32[]{:S(2)}) %collective-permute-start.3) | collective-permute-done | bytes 208928 | tf_op jit(solution)/shard_map/ppermute | solution.py:293
  9.7 1.9 %collective-permute-start.4 = (bf16[16,6528]{1,0:T(8,128)(2,1)S(1)}, bf16[16,6528]{1,0:T(8,128)(2,1)S(1)}, u32[]{:S(2)}, u32[]{:S(2)}) collective-permute-start(bf16[16,6528]{1,0:T(8,128)(2,1)S(1)} %collective-permute-done.3.refs_9_), channel_id=1, source_target_pairs={{2,0},{4,2},{6,4},{7,6},{5,7},{3,5},{1,3},{0,1},{8,10},{10,12},{12... | collective-permute-start | bytes 626696 | tf_op jit(solution)/shard_map/ppermute | solution.py:293
  11.7 1.5 %collective-permute-done.7.refs_8_ = bf16[16,6528]{1,0:T(8,128)(2,1)S(1)} collective-permute-done((bf16[16,6528]{1,0:T(8,128)(2,1)S(1)}, bf16[16,6528]{1,0:T(8,128)(2,1)S(1)}, u32[]{:S(2)}, u32[]{:S(2)}) %collective-permute-start.7) | collective-permute-done | bytes 208928 | tf_op jit(solution)/shard_map/ppermute | solution.py:293
  13.2 0.0 collective-permute-start.8
  13.2 1.0 %collective-permute-done.12.refs_6_ = bf16[16,6528]{1,0:T(8,128)(2,1)S(1)} collective-permute-done((bf16[16,6528]{1,0:T(8,128)(2,1)S(1)}, bf16[16,6528]{1,0:T(8,128)(2,1)S(1)}, u32[]{:S(2)}, u32[]{:S(2)}) %collective-permute-start.12) | collective-permute-done | bytes 208928 | tf_op jit(solution)/shard_map/ppermute | solution.py:293
  14.2 2.5 %collective-permute-start.13 = (bf16[16,6528]{1,0:T(8,128)(2,1)S(1)}, bf16[16,6528]{1,0:T(8,128)(2,1)S(1)}, u32[]{:S(2)}, u32[]{:S(2)}) collective-permute-start(bf16[16,6528]{1,0:T(8,128)(2,1)S(1)} %collective-permute-done.12.refs_6_), channel_id=1, source_target_pairs={{2,0},{4,2},{6,4},{7,6},{5,7},{3,5},{1,3},{0,1},{8,10},{10,12},{12... | collective-permute-start | bytes 626696 | tf_op jit(solution)/shard_map/ppermute | solution.py:293
  16.7 1.0 %collective-permute-done.refs_7_ = bf16[16,6528]{1,0:T(8,128)(2,1)S(1)} collective-permute-done((bf16[16,6528]{1,0:T(8,128)(2,1)S(1)}, bf16[16,6528]{1,0:T(8,128)(2,1)S(1)}, u32[]{:S(2)}, u32[]{:S(2)}) %collective-permute-start) | collective-permute-done | bytes 208928 | tf_op jit(solution)/shard_map/ppermute | solution.py:293
  17.7 0.6 %collective-permute-start.1 = (bf16[16,6528]{1,0:T(8,128)(2,1)S(1)}, bf16[16,6528]{1,0:T(8,128)(2,1)S(1)}, u32[]{:S(2)}, u32[]{:S(2)}) collective-permute-start(bf16[16,6528]{1,0:T(8,128)(2,1)S(1)} %collective-permute-done.refs_7_), channel_id=1, source_target_pairs={{0,2},{2,4},{4,6},{6,7},{7,5},{5,3},{3,1},{1,0},{10,8},{12,10},{14... | collective-permute-start | bytes 626696 | tf_op jit(solution)/shard_map/ppermute | solution.py:293
  18.3 0.4 collective-permute-done.4.refs_5_
  18.7 2.5 %collective-permute-start.5 = (bf16[16,6528]{1,0:T(8,128)(2,1)S(1)}, bf16[16,6528]{1,0:T(8,128)(2,1)S(1)}, u32[]{:S(2)}, u32[]{:S(2)}) collective-permute-start(bf16[16,6528]{1,0:T(8,128)(2,1)S(1)} %collective-permute-done.4.refs_5_), channel_id=1, source_target_pairs={{2,0},{4,2},{6,4},{7,6},{5,7},{3,5},{1,3},{0,1},{8,10},{10,12},{12... | collective-permute-start | bytes 626696 | tf_op jit(solution)/shard_map/ppermute | solution.py:293
  21.2 0.6 %collective-permute-done.8.refs_4_ = bf16[16,6528]{1,0:T(8,128)(2,1)S(1)} collective-permute-done((bf16[16,6528]{1,0:T(8,128)(2,1)S(1)}, bf16[16,6528]{1,0:T(8,128)(2,1)S(1)}, u32[]{:S(2)}, u32[]{:S(2)}) %collective-permute-start.8) | collective-permute-done | bytes 208928 | tf_op jit(solution)/shard_map/ppermute | solution.py:293
  21.7 0.3 collective-permute-start.9
  22.0 0.7 %collective-permute-start.15 = (bf16[16,6528]{1,0:T(8,128)(2,1)S(1)}, bf16[16,6528]{1,0:T(8,128)(2,1)S(1)}, u32[]{:S(2)}, u32[]{:S(2)}) collective-permute-start(bf16[16,6528]{1,0:T(8,128)(2,1)S(1)} %get-tuple-element.29), channel_id=1, source_target_pairs={{0,24},{1,25},{2,26},{3,27},{4,28},{5,29},{6,30},{7,31},{8,16},{9,... | collective-permute-start | bytes 626696 | tf_op jit(solution)/shard_map/ppermute | solution.py:293
  22.7 0.4 %collective-permute-done.13.refs_2_ = bf16[16,6528]{1,0:T(8,128)(2,1)S(1)} collective-permute-done((bf16[16,6528]{1,0:T(8,128)(2,1)S(1)}, bf16[16,6528]{1,0:T(8,128)(2,1)S(1)}, u32[]{:S(2)}, u32[]{:S(2)}) %collective-permute-start.13) | collective-permute-done | bytes 208928 | tf_op jit(solution)/shard_map/ppermute | solution.py:293
  23.2 2.5 %collective-permute-start.14 = (bf16[16,6528]{1,0:T(8,128)(2,1)S(1)}, bf16[16,6528]{1,0:T(8,128)(2,1)S(1)}, u32[]{:S(2)}, u32[]{:S(2)}) collective-permute-start(bf16[16,6528]{1,0:T(8,128)(2,1)S(1)} %collective-permute-done.13.refs_2_), channel_id=1, source_target_pairs={{2,0},{4,2},{6,4},{7,6},{5,7},{3,5},{1,3},{0,1},{8,10},{10,12},{12... | collective-permute-start | bytes 626696 | tf_op jit(solution)/shard_map/ppermute | solution.py:293
  25.6 0.6 %collective-permute-done.1.refs_3_ = bf16[16,6528]{1,0:T(8,128)(2,1)S(1)} collective-permute-done((bf16[16,6528]{1,0:T(8,128)(2,1)S(1)}, bf16[16,6528]{1,0:T(8,128)(2,1)S(1)}, u32[]{:S(2)}, u32[]{:S(2)}) %collective-permute-start.1) | collective-permute-done | bytes 208928 | tf_op jit(solution)/shard_map/ppermute | solution.py:293
  26.2 0.3 collective-permute-start.2
  26.5 1.1 %collective-permute-done.5.refs_1_ = bf16[16,6528]{1,0:T(8,128)(2,1)S(1)} collective-permute-done((bf16[16,6528]{1,0:T(8,128)(2,1)S(1)}, bf16[16,6528]{1,0:T(8,128)(2,1)S(1)}, u32[]{:S(2)}, u32[]{:S(2)}) %collective-permute-start.5) | collective-permute-done | bytes 208928 | tf_op jit(solution)/shard_map/ppermute | solution.py:293
  27.6 2.5 %collective-permute-start.6 = (bf16[16,6528]{1,0:T(8,128)(2,1)S(1)}, bf16[16,6528]{1,0:T(8,128)(2,1)S(1)}, u32[]{:S(2)}, u32[]{:S(2)}) collective-permute-start(bf16[16,6528]{1,0:T(8,128)(2,1)S(1)} %collective-permute-done.5.refs_1_), channel_id=1, source_target_pairs={{2,0},{4,2},{6,4},{7,6},{5,7},{3,5},{1,3},{0,1},{8,10},{10,12},{12... | collective-permute-start | bytes 626696 | tf_op jit(solution)/shard_map/ppermute | solution.py:293
  30.1 0.6 %collective-permute-done.9.refs_0_ = bf16[16,6528]{1,0:T(8,128)(2,1)S(1)} collective-permute-done((bf16[16,6528]{1,0:T(8,128)(2,1)S(1)}, bf16[16,6528]{1,0:T(8,128)(2,1)S(1)}, u32[]{:S(2)}, u32[]{:S(2)}) %collective-permute-start.9) | collective-permute-done | bytes 208928 | tf_op jit(solution)/shard_map/ppermute | solution.py:293
  30.7 0.3 collective-permute-start.11
  31.0 0.0 collective-permute-done.15.refs_11_
  31.0 1.9 %collective-permute-start.10 = (bf16[16,3072]{1,0:T(8,128)(2,1)S(1)}, bf16[16,3072]{1,0:T(8,128)(2,1)S(1)}, u32[]{:S(2)}, u32[]{:S(2)}) collective-permute-start(bf16[16,3072]{1,0:T(8,128)(2,1)S(1)} %slice.8), channel_id=1, source_target_pairs={{0,2},{2,4},{4,6},{6,7},{7,5},{5,3},{3,1},{1,0},{10,8},{12,10},{14... | collective-permute-start | bytes 294920 | tf_op jit(solution)/shard_map/ppermute | solution.py:293
  33.0 0.0 collective-permute-done.14.refs_10_
  33.0 2.0 %grad_part.1.refs_5_ = f32[256,3072]{1,0:T(8,128)S(1)} custom-call(bf16[16,6528]{1,0:T(8,128)(2,1)S(1)} %collective-permute-done.9.refs_0_, bf16[16,6528]{1,0:T(8,128)(2,1)S(1)} %collective-permute-done.5.refs_1_, bf16[16,6528]{1,0:T(8,128)(2,1)S(1)} %collective-permute-done.13.refs_2_, bf16[16,6528]{1,0:T(8,128)(2,1)S(1)} %collective-permute-done.1.refs_3_, ...), custom_call_target="tpu_custom_call" | custom-call | flops 695205888 | bytes 4288512 | tf_op jit(solution)/shard_map/grad_part/pallas_call | solution.py:205
  35.0 0.2 collective-permute-done.2.refs_0_
  35.2 1.4 %collective-permute-done.6.refs_1_ = bf16[16,6528]{1,0:T(8,128)(2,1)S(1)} collective-permute-done((bf16[16,6528]{1,0:T(8,128)(2,1)S(1)}, bf16[16,6528]{1,0:T(8,128)(2,1)S(1)}, u32[]{:S(2)}, u32[]{:S(2)}) %collective-permute-start.6) | collective-permute-done | bytes 208928 | tf_op jit(solution)/shard_map/ppermute | solution.py:293
  36.6 0.4 %active_late.2 = (bf16[34,256]{1,0:T(8,128)(2,1)S(1)}, bf16[2,3072]{1,0:T(2,128)(2,1)S(1)}) custom-call(bf16[16,6528]{1,0:T(8,128)(2,1)S(1)} %collective-permute-done.2.refs_0_, bf16[16,6528]{1,0:T(8,128)(2,1)S(1)} %collective-permute-done.6.refs_1_, bf16[3072,256]{1,0:T(8,128)(2,1)S(1)} %get-tuple-element.23.refs_2_.refs_1_.refs_13_), custom_call_target="tpu_custom_call" | custom-call | flops 53477376 | bytes 1990656 | tf_op jit(solution)/shard_map/active_late/pallas_call | solution.py:205
  37.0 0.0 collective-permute-done.11.refs_0_
  37.0 0.4 %active_late.3 = (bf16[51,256]{1,0:T(8,128)(2,1)S(1)}, bf16[3,3072]{1,0:T(4,128)(2,1)S(1)}) custom-call(bf16[16,3456]{1,0:T(8,128)(2,1)S(1)} %collective-permute-done.11.refs_0_, bf16[3072,256]{1,0:T(8,128)(2,1)S(1)} %get-tuple-element.23.refs_2_.refs_1_.refs_13_, bf16[34,256]{1,0:T(8,128)(2,1)S(1)} %get-tuple-element.25.refs_2_, ...), custom_call_target="tpu_custom_call" | custom-call | flops 26738688 | bytes 1713152 | tf_op jit(solution)/shard_map/active_late/pallas_call | solution.py:205
  37.5 0.5 %collective-permute-done.10.refs_2_ = bf16[16,3072]{1,0:T(8,128)(2,1)S(1)} collective-permute-done((bf16[16,3072]{1,0:T(8,128)(2,1)S(1)}, bf16[16,3072]{1,0:T(8,128)(2,1)S(1)}, u32[]{:S(2)}, u32[]{:S(2)}) %collective-permute-start.10) | collective-permute-done | bytes 98336 | tf_op jit(solution)/shard_map/ppermute | solution.py:293
  38.0 1.5 %grad_sum.1 = bf16[256,3072]{1,0:T(8,128)(2,1)} custom-call(bf16[16,6528]{1,0:T(8,128)(2,1)S(1)} %collective-permute-done.2.refs_0_, bf16[16,6528]{1,0:T(8,128)(2,1)S(1)} %collective-permute-done.6.refs_1_, bf16[16,3072]{1,0:T(8,128)(2,1)S(1)} %collective-permute-done.10.refs_2_, bf16[51,256]{1,0:T(8,128)(2,1)S(1)} %get-tuple-element.27.refs_3_, ...), custom_call_target="tpu_custom_call" | custom-call | flops 80216064 | bytes 3706368 | tf_op jit(solution)/shard_map/grad_sum/pallas_call | solution.py:205
  (2 shorter events, 0.0 us)
Async XLA Ops:
  1.5 8.2 %collective-permute-start.3 = (bf16[16,6528]{1,0:T(8,128)(2,1)S(1)}, bf16[16,6528]{1,0:T(8,128)(2,1)S(1)}, u32[]{:S(2)}, u32[]{:S(2)}) collective-permute-start(bf16[16,6528]{1,0:T(8,128)(2,1)S(1)} %get-tuple-element.18.lead), channel_id=1, source_target_pairs={{2,24},{4,26},{6,28},{7,30},{5,31},{3,29},{1,27},{0,25},{8,10},{10... | collective-permute-start | bytes 626696 | tf_op jit(solution)/shard_map/ppermute | solution.py:293
  5.3 7.9 %collective-permute-start.7 = (bf16[16,6528]{1,0:T(8,128)(2,1)S(1)}, bf16[16,6528]{1,0:T(8,128)(2,1)S(1)}, u32[]{:S(2)}, u32[]{:S(2)}) collective-permute-start(bf16[16,6528]{1,0:T(8,128)(2,1)S(1)} %pack_trail.1.trail), channel_id=1, source_target_pairs={{0,2},{2,4},{4,6},{6,7},{7,5},{5,3},{3,1},{1,0},{10,16},{12,18},{1... | collective-permute-start | bytes 626696 | tf_op jit(solution)/shard_map/ppermute | solution.py:293
  5.9 8.4 %collective-permute-start.12 = (bf16[16,6528]{1,0:T(8,128)(2,1)S(1)}, bf16[16,6528]{1,0:T(8,128)(2,1)S(1)}, u32[]{:S(2)}, u32[]{:S(2)}) collective-permute-start(bf16[16,6528]{1,0:T(8,128)(2,1)S(1)} %pack_trail.1.trail), channel_id=1, source_target_pairs={{2,0},{4,2},{6,4},{7,6},{5,7},{3,5},{1,3},{0,1},{8,18},{10,20},{12... | collective-permute-start | bytes 626696 | tf_op jit(solution)/shard_map/ppermute | solution.py:293
  7.3 10.3 %collective-permute-start = (bf16[16,6528]{1,0:T(8,128)(2,1)S(1)}, bf16[16,6528]{1,0:T(8,128)(2,1)S(1)}, u32[]{:S(2)}, u32[]{:S(2)}) collective-permute-start(bf16[16,6528]{1,0:T(8,128)(2,1)S(1)} %get-tuple-element.18.lead), channel_id=1, source_target_pairs={{0,26},{2,28},{4,30},{6,31},{7,29},{5,27},{3,25},{1,24},{10,8},{12... | collective-permute-start | bytes 626696 | tf_op jit(solution)/shard_map/ppermute | solution.py:293
  9.7 9.0 %collective-permute-start.4 = (bf16[16,6528]{1,0:T(8,128)(2,1)S(1)}, bf16[16,6528]{1,0:T(8,128)(2,1)S(1)}, u32[]{:S(2)}, u32[]{:S(2)}) collective-permute-start(bf16[16,6528]{1,0:T(8,128)(2,1)S(1)} %collective-permute-done.3.refs_9_), channel_id=1, source_target_pairs={{2,0},{4,2},{6,4},{7,6},{5,7},{3,5},{1,3},{0,1},{8,10},{10,12},{12... | collective-permute-start | bytes 626696 | tf_op jit(solution)/shard_map/ppermute | solution.py:293
  13.2 8.5 %collective-permute-start.8 = (bf16[16,6528]{1,0:T(8,128)(2,1)S(1)}, bf16[16,6528]{1,0:T(8,128)(2,1)S(1)}, u32[]{:S(2)}, u32[]{:S(2)}) collective-permute-start(bf16[16,6528]{1,0:T(8,128)(2,1)S(1)} %collective-permute-done.7.refs_8_), channel_id=1, source_target_pairs={{0,2},{2,4},{4,6},{6,7},{7,5},{5,3},{3,1},{1,0},{10,8},{12,10},{14... | collective-permute-start | bytes 626696 | tf_op jit(solution)/shard_map/ppermute | solution.py:293
  14.2 9.0 %collective-permute-start.13 = (bf16[16,6528]{1,0:T(8,128)(2,1)S(1)}, bf16[16,6528]{1,0:T(8,128)(2,1)S(1)}, u32[]{:S(2)}, u32[]{:S(2)}) collective-permute-start(bf16[16,6528]{1,0:T(8,128)(2,1)S(1)} %collective-permute-done.12.refs_6_), channel_id=1, source_target_pairs={{2,0},{4,2},{6,4},{7,6},{5,7},{3,5},{1,3},{0,1},{8,10},{10,12},{12... | collective-permute-start | bytes 626696 | tf_op jit(solution)/shard_map/ppermute | solution.py:293
  17.7 8.5 %collective-permute-start.1 = (bf16[16,6528]{1,0:T(8,128)(2,1)S(1)}, bf16[16,6528]{1,0:T(8,128)(2,1)S(1)}, u32[]{:S(2)}, u32[]{:S(2)}) collective-permute-start(bf16[16,6528]{1,0:T(8,128)(2,1)S(1)} %collective-permute-done.refs_7_), channel_id=1, source_target_pairs={{0,2},{2,4},{4,6},{6,7},{7,5},{5,3},{3,1},{1,0},{10,8},{12,10},{14... | collective-permute-start | bytes 626696 | tf_op jit(solution)/shard_map/ppermute | solution.py:293
  18.7 9.0 %collective-permute-start.5 = (bf16[16,6528]{1,0:T(8,128)(2,1)S(1)}, bf16[16,6528]{1,0:T(8,128)(2,1)S(1)}, u32[]{:S(2)}, u32[]{:S(2)}) collective-permute-start(bf16[16,6528]{1,0:T(8,128)(2,1)S(1)} %collective-permute-done.4.refs_5_), channel_id=1, source_target_pairs={{2,0},{4,2},{6,4},{7,6},{5,7},{3,5},{1,3},{0,1},{8,10},{10,12},{12... | collective-permute-start | bytes 626696 | tf_op jit(solution)/shard_map/ppermute | solution.py:293
  21.7 9.0 %collective-permute-start.9 = (bf16[16,6528]{1,0:T(8,128)(2,1)S(1)}, bf16[16,6528]{1,0:T(8,128)(2,1)S(1)}, u32[]{:S(2)}, u32[]{:S(2)}) collective-permute-start(bf16[16,6528]{1,0:T(8,128)(2,1)S(1)} %collective-permute-done.8.refs_4_), channel_id=1, source_target_pairs={{0,2},{2,4},{4,6},{6,7},{7,5},{5,3},{3,1},{1,0},{10,8},{12,10},{14... | collective-permute-start | bytes 626696 | tf_op jit(solution)/shard_map/ppermute | solution.py:293
  22.0 9.0 %collective-permute-start.15 = (bf16[16,6528]{1,0:T(8,128)(2,1)S(1)}, bf16[16,6528]{1,0:T(8,128)(2,1)S(1)}, u32[]{:S(2)}, u32[]{:S(2)}) collective-permute-start(bf16[16,6528]{1,0:T(8,128)(2,1)S(1)} %get-tuple-element.29), channel_id=1, source_target_pairs={{0,24},{1,25},{2,26},{3,27},{4,28},{5,29},{6,30},{7,31},{8,16},{9,... | collective-permute-start | bytes 626696 | tf_op jit(solution)/shard_map/ppermute | solution.py:293
  23.2 9.8 %collective-permute-start.14 = (bf16[16,6528]{1,0:T(8,128)(2,1)S(1)}, bf16[16,6528]{1,0:T(8,128)(2,1)S(1)}, u32[]{:S(2)}, u32[]{:S(2)}) collective-permute-start(bf16[16,6528]{1,0:T(8,128)(2,1)S(1)} %collective-permute-done.13.refs_2_), channel_id=1, source_target_pairs={{2,0},{4,2},{6,4},{7,6},{5,7},{3,5},{1,3},{0,1},{8,10},{10,12},{12... | collective-permute-start | bytes 626696 | tf_op jit(solution)/shard_map/ppermute | solution.py:293
  26.2 9.0 %collective-permute-start.2 = (bf16[16,6528]{1,0:T(8,128)(2,1)S(1)}, bf16[16,6528]{1,0:T(8,128)(2,1)S(1)}, u32[]{:S(2)}, u32[]{:S(2)}) collective-permute-start(bf16[16,6528]{1,0:T(8,128)(2,1)S(1)} %collective-permute-done.1.refs_3_), channel_id=1, source_target_pairs={{0,2},{2,4},{4,6},{6,7},{7,5},{5,3},{3,1},{1,0},{10,8},{12,10},{14... | collective-permute-start | bytes 626696 | tf_op jit(solution)/shard_map/ppermute | solution.py:293
  27.6 9.0 %collective-permute-start.6 = (bf16[16,6528]{1,0:T(8,128)(2,1)S(1)}, bf16[16,6528]{1,0:T(8,128)(2,1)S(1)}, u32[]{:S(2)}, u32[]{:S(2)}) collective-permute-start(bf16[16,6528]{1,0:T(8,128)(2,1)S(1)} %collective-permute-done.5.refs_1_), channel_id=1, source_target_pairs={{2,0},{4,2},{6,4},{7,6},{5,7},{3,5},{1,3},{0,1},{8,10},{10,12},{12... | collective-permute-start | bytes 626696 | tf_op jit(solution)/shard_map/ppermute | solution.py:293
  30.7 6.3 %collective-permute-start.11 = (bf16[16,3456]{1,0:T(8,128)(2,1)S(1)}, bf16[16,3456]{1,0:T(8,128)(2,1)S(1)}, u32[]{:S(2)}, u32[]{:S(2)}) collective-permute-start(bf16[16,3456]{1,0:T(8,128)(2,1)S(1)} %slice.9), channel_id=1, source_target_pairs={{0,2},{2,4},{4,6},{6,7},{7,5},{5,3},{3,1},{1,0},{10,8},{12,10},{14... | collective-permute-start | bytes 331784 | tf_op jit(solution)/shard_map/ppermute | solution.py:293
  31.0 6.9 %collective-permute-start.10 = (bf16[16,3072]{1,0:T(8,128)(2,1)S(1)}, bf16[16,3072]{1,0:T(8,128)(2,1)S(1)}, u32[]{:S(2)}, u32[]{:S(2)}) collective-permute-start(bf16[16,3072]{1,0:T(8,128)(2,1)S(1)} %slice.8), channel_id=1, source_target_pairs={{0,2},{2,4},{4,6},{6,7},{7,5},{5,3},{3,1},{1,0},{10,8},{12,10},{14... | collective-permute-start | bytes 294920 | tf_op jit(solution)/shard_map/ppermute | solution.py:293

commit v11 on v9

--- a/solution.py
+++ b/solution.py
@@ -10,6 +10,7 @@
 CAP = 17
 MAIN = 16
 SEGS = 8
+PIECES = 3
 
 
 def grid_cycle(n):
@@ -187,10 +188,10 @@
 
 def sum_kernel(count, offsets, *refs):
     blocks, (active_ref, tail_ref, before, out_ref, made, sems) = refs[:count], refs[count:]
-    seg = tail_ref.shape[1] // SEGS
+    seg = tail_ref.shape[1] // PIECES
     active = active_ref[...]
     copies = []
-    for s in range(SEGS):
+    for s in range(PIECES):
         here = slice(s * seg, (s + 1) * seg)
         rows_y = [b[:, o + s * seg : o + (s + 1) * seg] for b, o in zip(blocks, offsets)]
         rows_y = jnp.concatenate(rows_y + [tail_ref[:, here]], axis=0)

time: 39.7 us -> 39.8 us (level)
  no operation moved by 1% of the time
where the time goes in v11:
time: 39.8 us; the launch traced here: 39.5 us
  starting transfers between devices  21.6 us (54%)
  waiting for transfers between devices  10.1 us (25%)
  Pallas kernels  7.69 us (19%)
    ppermute x16, starting transfers between devices, move(): return lax.ppermute(block, ('pipe', 'expert'), pairs)  21.6 us
    ppermute x16, waiting for transfers between devices, move(): return lax.ppermute(block, ('pipe', 'expert'), pairs)  10.1 us
    pallas_call x5, Pallas kernels, local_call(): pl.pallas_call(kernel, out_shape=outs, in_specs=[pl.BlockSpec(memory_spac...  4.78 us
    pallas_call x1, Pallas kernels, pack(): pl.pallas_call(functools.partial(lead_kernel, n_pipe), out_shape=(payload...  1.49 us
    pallas_call x1, Pallas kernels, fetch(): pl.pallas_call(fetch_kernel, out_shape=pltpu.VMEM(weight_in.shape, weight...  1.42 us
  transfers between devices with their start and end apart: 16, of which 13 were waited for; matrix products, arithmetic and copies ran while one was open for 0% of the time, Pallas kernels for 12%

profile of v11, /device:TPU:0, one launch (start us, length us, event | category | flops | bytes accessed | tf_op | source)
XLA Modules:
  0.0 39.5 jit_solution(16680690304864579001)
XLA Ops:
  0.0 1.5 %pack_lead.1 = (bf16[16,6528]{1,0:T(8,128)(2,1)S(1)}, bf16[64,3072]{1,0:T(8,128)(2,1)S(1)}, bf16[64,3072]{1,0:T(8,128)(2,1)S(1)}, bf16[2,64]{1,0:T(2,128)(2,1)S(1)}, s32[2,64]{1,0:T(2,128)S(1)}) custom-call(bf16[64,3072]{1,0:T(8,128)(2,1)} %bitcast.19, bf16[64,3072]{1,0:T(8,128)(2,1)} %bitcast.20, bf16[2,64]{1,0:T(2,128)(2,1)} %bitcast.25, ...), custom_call_target="tpu_custom_call" | custom-call | flops 25165824 | bytes 2359296 | tf_op jit(solution)/shard_map/pack_lead/pallas_call | solution.py:113
  1.5 3.4 %collective-permute-start.3 = (bf16[16,6528]{1,0:T(8,128)(2,1)S(1)}, bf16[16,6528]{1,0:T(8,128)(2,1)S(1)}, u32[]{:S(2)}, u32[]{:S(2)}) collective-permute-start(bf16[16,6528]{1,0:T(8,128)(2,1)S(1)} %get-tuple-element.18.lead), channel_id=1, source_target_pairs={{2,24},{4,26},{6,28},{7,30},{5,31},{3,29},{1,27},{0,25},{8,10},{10... | collective-permute-start | bytes 626696 | tf_op jit(solution)/shard_map/ppermute | solution.py:292
  4.9 0.4 pack_trail.1
  5.3 0.6 %collective-permute-start.7 = (bf16[16,6528]{1,0:T(8,128)(2,1)S(1)}, bf16[16,6528]{1,0:T(8,128)(2,1)S(1)}, u32[]{:S(2)}, u32[]{:S(2)}) collective-permute-start(bf16[16,6528]{1,0:T(8,128)(2,1)S(1)} %get-tuple-element.24), channel_id=1, source_target_pairs={{0,2},{2,4},{4,6},{6,7},{7,5},{5,3},{3,1},{1,0},{10,16},{12,18},{1... | collective-permute-start | bytes 626696 | tf_op jit(solution)/shard_map/ppermute | solution.py:292
  5.9 1.5 %collective-permute-start.12 = (bf16[16,6528]{1,0:T(8,128)(2,1)S(1)}, bf16[16,6528]{1,0:T(8,128)(2,1)S(1)}, u32[]{:S(2)}, u32[]{:S(2)}) collective-permute-start(bf16[16,6528]{1,0:T(8,128)(2,1)S(1)} %get-tuple-element.24), channel_id=1, source_target_pairs={{2,0},{4,2},{6,4},{7,6},{5,7},{3,5},{1,3},{0,1},{8,18},{10,20},{12... | collective-permute-start | bytes 626696 | tf_op jit(solution)/shard_map/ppermute | solution.py:292
  7.4 0.0 collective-permute-start
  7.4 1.4 %fetch_weights.1.refs_2_.refs_1_.refs_13_ = bf16[3072,256]{1,0:T(8,128)(2,1)S(1)} custom-call(bf16[3072,256]{1,0:T(8,128)(2,1)} %bitcast.18), custom_call_target="tpu_custom_call" | custom-call | tf_op jit(solution)/shard_map/fetch_weights/pallas_call | solution.py:235
  8.8 0.8 %collective-permute-done.3.refs_9_ = bf16[16,6528]{1,0:T(8,128)(2,1)S(1)} collective-permute-done((bf16[16,6528]{1,0:T(8,128)(2,1)S(1)}, bf16[16,6528]{1,0:T(8,128)(2,1)S(1)}, u32[]{:S(2)}, u32[]{:S(2)}) %collective-permute-start.3) | collective-permute-done | bytes 208928 | tf_op jit(solution)/shard_map/ppermute | solution.py:292
  9.7 2.0 %collective-permute-start.4 = (bf16[16,6528]{1,0:T(8,128)(2,1)S(1)}, bf16[16,6528]{1,0:T(8,128)(2,1)S(1)}, u32[]{:S(2)}, u32[]{:S(2)}) collective-permute-start(bf16[16,6528]{1,0:T(8,128)(2,1)S(1)} %collective-permute-done.3.refs_9_), channel_id=1, source_target_pairs={{2,0},{4,2},{6,4},{7,6},{5,7},{3,5},{1,3},{0,1},{8,10},{10,12},{12... | collective-permute-start | bytes 626696 | tf_op jit(solution)/shard_map/ppermute | solution.py:292
  11.6 1.6 %collective-permute-done.7.refs_8_ = bf16[16,6528]{1,0:T(8,128)(2,1)S(1)} collective-permute-done((bf16[16,6528]{1,0:T(8,128)(2,1)S(1)}, bf16[16,6528]{1,0:T(8,128)(2,1)S(1)}, u32[]{:S(2)}, u32[]{:S(2)}) %collective-permute-start.7) | collective-permute-done | bytes 208928 | tf_op jit(solution)/shard_map/ppermute | solution.py:292
  13.2 0.0 collective-permute-start.8
  13.2 0.9 %collective-permute-done.12.refs_6_ = bf16[16,6528]{1,0:T(8,128)(2,1)S(1)} collective-permute-done((bf16[16,6528]{1,0:T(8,128)(2,1)S(1)}, bf16[16,6528]{1,0:T(8,128)(2,1)S(1)}, u32[]{:S(2)}, u32[]{:S(2)}) %collective-permute-start.12) | collective-permute-done | bytes 208928 | tf_op jit(solution)/shard_map/ppermute | solution.py:292
  14.1 2.5 %collective-permute-start.13 = (bf16[16,6528]{1,0:T(8,128)(2,1)S(1)}, bf16[16,6528]{1,0:T(8,128)(2,1)S(1)}, u32[]{:S(2)}, u32[]{:S(2)}) collective-permute-start(bf16[16,6528]{1,0:T(8,128)(2,1)S(1)} %collective-permute-done.12.refs_6_), channel_id=1, source_target_pairs={{2,0},{4,2},{6,4},{7,6},{5,7},{3,5},{1,3},{0,1},{8,10},{10,12},{12... | collective-permute-start | bytes 626696 | tf_op jit(solution)/shard_map/ppermute | solution.py:292
  16.6 1.1 %collective-permute-done.refs_7_ = bf16[16,6528]{1,0:T(8,128)(2,1)S(1)} collective-permute-done((bf16[16,6528]{1,0:T(8,128)(2,1)S(1)}, bf16[16,6528]{1,0:T(8,128)(2,1)S(1)}, u32[]{:S(2)}, u32[]{:S(2)}) %collective-permute-start) | collective-permute-done | bytes 208928 | tf_op jit(solution)/shard_map/ppermute | solution.py:292
  17.7 0.7 %collective-permute-start.1 = (bf16[16,6528]{1,0:T(8,128)(2,1)S(1)}, bf16[16,6528]{1,0:T(8,128)(2,1)S(1)}, u32[]{:S(2)}, u32[]{:S(2)}) collective-permute-start(bf16[16,6528]{1,0:T(8,128)(2,1)S(1)} %collective-permute-done.refs_7_), channel_id=1, source_target_pairs={{0,2},{2,4},{4,6},{6,7},{7,5},{5,3},{3,1},{1,0},{10,8},{12,10},{14... | collective-permute-start | bytes 626696 | tf_op jit(solution)/shard_map/ppermute | solution.py:292
  18.4 0.3 collective-permute-done.4.refs_5_
  18.6 2.5 %collective-permute-start.5 = (bf16[16,6528]{1,0:T(8,128)(2,1)S(1)}, bf16[16,6528]{1,0:T(8,128)(2,1)S(1)}, u32[]{:S(2)}, u32[]{:S(2)}) collective-permute-start(bf16[16,6528]{1,0:T(8,128)(2,1)S(1)} %collective-permute-done.4.refs_5_), channel_id=1, source_target_pairs={{2,0},{4,2},{6,4},{7,6},{5,7},{3,5},{1,3},{0,1},{8,10},{10,12},{12... | collective-permute-start | bytes 626696 | tf_op jit(solution)/shard_map/ppermute | solution.py:292
  21.1 0.7 %collective-permute-done.8.refs_4_ = bf16[16,6528]{1,0:T(8,128)(2,1)S(1)} collective-permute-done((bf16[16,6528]{1,0:T(8,128)(2,1)S(1)}, bf16[16,6528]{1,0:T(8,128)(2,1)S(1)}, u32[]{:S(2)}, u32[]{:S(2)}) %collective-permute-start.8) | collective-permute-done | bytes 208928 | tf_op jit(solution)/shard_map/ppermute | solution.py:292
  21.8 0.3 collective-permute-start.9
  22.1 0.7 %collective-permute-start.15 = (bf16[16,6528]{1,0:T(8,128)(2,1)S(1)}, bf16[16,6528]{1,0:T(8,128)(2,1)S(1)}, u32[]{:S(2)}, u32[]{:S(2)}) collective-permute-start(bf16[16,6528]{1,0:T(8,128)(2,1)S(1)} %get-tuple-element.29), channel_id=1, source_target_pairs={{0,24},{1,25},{2,26},{3,27},{4,28},{5,29},{6,30},{7,31},{8,16},{9,... | collective-permute-start | bytes 626696 | tf_op jit(solution)/shard_map/ppermute | solution.py:292
  22.8 0.3 collective-permute-done.13.refs_2_
  23.1 2.5 %collective-permute-start.14 = (bf16[16,6528]{1,0:T(8,128)(2,1)S(1)}, bf16[16,6528]{1,0:T(8,128)(2,1)S(1)}, u32[]{:S(2)}, u32[]{:S(2)}) collective-permute-start(bf16[16,6528]{1,0:T(8,128)(2,1)S(1)} %collective-permute-done.13.refs_2_), channel_id=1, source_target_pairs={{2,0},{4,2},{6,4},{7,6},{5,7},{3,5},{1,3},{0,1},{8,10},{10,12},{12... | collective-permute-start | bytes 626696 | tf_op jit(solution)/shard_map/ppermute | solution.py:292
  25.6 0.7 %collective-permute-done.1.refs_3_ = bf16[16,6528]{1,0:T(8,128)(2,1)S(1)} collective-permute-done((bf16[16,6528]{1,0:T(8,128)(2,1)S(1)}, bf16[16,6528]{1,0:T(8,128)(2,1)S(1)}, u32[]{:S(2)}, u32[]{:S(2)}) %collective-permute-start.1) | collective-permute-done | bytes 208928 | tf_op jit(solution)/shard_map/ppermute | solution.py:292
  26.2 0.3 collective-permute-start.2
  26.5 1.0 %collective-permute-done.5.refs_1_ = bf16[16,6528]{1,0:T(8,128)(2,1)S(1)} collective-permute-done((bf16[16,6528]{1,0:T(8,128)(2,1)S(1)}, bf16[16,6528]{1,0:T(8,128)(2,1)S(1)}, u32[]{:S(2)}, u32[]{:S(2)}) %collective-permute-start.5) | collective-permute-done | bytes 208928 | tf_op jit(solution)/shard_map/ppermute | solution.py:292
  27.6 2.5 %collective-permute-start.6 = (bf16[16,6528]{1,0:T(8,128)(2,1)S(1)}, bf16[16,6528]{1,0:T(8,128)(2,1)S(1)}, u32[]{:S(2)}, u32[]{:S(2)}) collective-permute-start(bf16[16,6528]{1,0:T(8,128)(2,1)S(1)} %collective-permute-done.5.refs_1_), channel_id=1, source_target_pairs={{2,0},{4,2},{6,4},{7,6},{5,7},{3,5},{1,3},{0,1},{8,10},{10,12},{12... | collective-permute-start | bytes 626696 | tf_op jit(solution)/shard_map/ppermute | solution.py:292
  30.0 0.7 %collective-permute-done.9.refs_0_ = bf16[16,6528]{1,0:T(8,128)(2,1)S(1)} collective-permute-done((bf16[16,6528]{1,0:T(8,128)(2,1)S(1)}, bf16[16,6528]{1,0:T(8,128)(2,1)S(1)}, u32[]{:S(2)}, u32[]{:S(2)}) %collective-permute-start.9) | collective-permute-done | bytes 208928 | tf_op jit(solution)/shard_map/ppermute | solution.py:292
  30.7 0.3 collective-permute-start.11
  31.1 0.0 collective-permute-done.15.refs_11_
  31.1 1.9 %collective-permute-start.10 = (bf16[16,3072]{1,0:T(8,128)(2,1)S(1)}, bf16[16,3072]{1,0:T(8,128)(2,1)S(1)}, u32[]{:S(2)}, u32[]{:S(2)}) collective-permute-start(bf16[16,3072]{1,0:T(8,128)(2,1)S(1)} %slice.8), channel_id=1, source_target_pairs={{0,2},{2,4},{4,6},{6,7},{7,5},{5,3},{3,1},{1,0},{10,8},{12,10},{14... | collective-permute-start | bytes 294920 | tf_op jit(solution)/shard_map/ppermute | solution.py:292
  33.0 0.0 collective-permute-done.14.refs_10_
  33.0 2.0 %grad_part.1.refs_5_ = f32[256,3072]{1,0:T(8,128)S(1)} custom-call(bf16[16,6528]{1,0:T(8,128)(2,1)S(1)} %collective-permute-done.9.refs_0_, bf16[16,6528]{1,0:T(8,128)(2,1)S(1)} %collective-permute-done.5.refs_1_, bf16[16,6528]{1,0:T(8,128)(2,1)S(1)} %collective-permute-done.13.refs_2_, bf16[16,6528]{1,0:T(8,128)(2,1)S(1)} %collective-permute-done.1.refs_3_, ...), custom_call_target="tpu_custom_call" | custom-call | flops 695205888 | bytes 4288512 | tf_op jit(solution)/shard_map/grad_part/pallas_call | solution.py:213
  35.0 0.2 collective-permute-done.2.refs_0_
  35.2 1.3 %collective-permute-done.6.refs_1_ = bf16[16,6528]{1,0:T(8,128)(2,1)S(1)} collective-permute-done((bf16[16,6528]{1,0:T(8,128)(2,1)S(1)}, bf16[16,6528]{1,0:T(8,128)(2,1)S(1)}, u32[]{:S(2)}, u32[]{:S(2)}) %collective-permute-start.6) | collective-permute-done | bytes 208928 | tf_op jit(solution)/shard_map/ppermute | solution.py:292
  36.5 0.4 %active_late.2 = (bf16[34,256]{1,0:T(8,128)(2,1)S(1)}, bf16[2,3072]{1,0:T(2,128)(2,1)S(1)}) custom-call(bf16[16,6528]{1,0:T(8,128)(2,1)S(1)} %collective-permute-done.2.refs_0_, bf16[16,6528]{1,0:T(8,128)(2,1)S(1)} %collective-permute-done.6.refs_1_, bf16[3072,256]{1,0:T(8,128)(2,1)S(1)} %fetch_weights.1.refs_2_.refs_1_.refs_13_), custom_call_target="tpu_custom_call" | custom-call | flops 53477376 | bytes 1990656 | tf_op jit(solution)/shard_map/active_late/pallas_call | solution.py:213
  37.0 0.0 collective-permute-done.11.refs_0_
  37.0 0.4 %active_late.3 = (bf16[51,256]{1,0:T(8,128)(2,1)S(1)}, bf16[3,3072]{1,0:T(4,128)(2,1)S(1)}) custom-call(bf16[16,3456]{1,0:T(8,128)(2,1)S(1)} %collective-permute-done.11.refs_0_, bf16[3072,256]{1,0:T(8,128)(2,1)S(1)} %fetch_weights.1.refs_2_.refs_1_.refs_13_, bf16[34,256]{1,0:T(8,128)(2,1)S(1)} %get-tuple-element.25.refs_2_, ...), custom_call_target="tpu_custom_call" | custom-call | flops 26738688 | bytes 1713152 | tf_op jit(solution)/shard_map/active_late/pallas_call | solution.py:213
  37.4 0.6 %collective-permute-done.10.refs_2_ = bf16[16,3072]{1,0:T(8,128)(2,1)S(1)} collective-permute-done((bf16[16,3072]{1,0:T(8,128)(2,1)S(1)}, bf16[16,3072]{1,0:T(8,128)(2,1)S(1)}, u32[]{:S(2)}, u32[]{:S(2)}) %collective-permute-start.10) | collective-permute-done | bytes 98336 | tf_op jit(solution)/shard_map/ppermute | solution.py:292
  38.0 1.5 %grad_sum.1 = bf16[256,3072]{1,0:T(8,128)(2,1)} custom-call(bf16[16,6528]{1,0:T(8,128)(2,1)S(1)} %collective-permute-done.2.refs_0_, bf16[16,6528]{1,0:T(8,128)(2,1)S(1)} %collective-permute-done.6.refs_1_, bf16[16,3072]{1,0:T(8,128)(2,1)S(1)} %collective-permute-done.10.refs_2_, bf16[51,256]{1,0:T(8,128)(2,1)S(1)} %get-tuple-element.27.refs_3_, ...), custom_call_target="tpu_custom_call" | custom-call | flops 80216064 | bytes 3706368 | tf_op jit(solution)/shard_map/grad_sum/pallas_call | solution.py:213
  (2 shorter events, 0.0 us)
Async XLA Ops:
  1.5 8.2 %collective-permute-start.3 = (bf16[16,6528]{1,0:T(8,128)(2,1)S(1)}, bf16[16,6528]{1,0:T(8,128)(2,1)S(1)}, u32[]{:S(2)}, u32[]{:S(2)}) collective-permute-start(bf16[16,6528]{1,0:T(8,128)(2,1)S(1)} %get-tuple-element.18.lead), channel_id=1, source_target_pairs={{2,24},{4,26},{6,28},{7,30},{5,31},{3,29},{1,27},{0,25},{8,10},{10... | collective-permute-start | bytes 626696 | tf_op jit(solution)/shard_map/ppermute | solution.py:292
  5.3 7.9 %collective-permute-start.7 = (bf16[16,6528]{1,0:T(8,128)(2,1)S(1)}, bf16[16,6528]{1,0:T(8,128)(2,1)S(1)}, u32[]{:S(2)}, u32[]{:S(2)}) collective-permute-start(bf16[16,6528]{1,0:T(8,128)(2,1)S(1)} %get-tuple-element.24), channel_id=1, source_target_pairs={{0,2},{2,4},{4,6},{6,7},{7,5},{5,3},{3,1},{1,0},{10,16},{12,18},{1... | collective-permute-start | bytes 626696 | tf_op jit(solution)/shard_map/ppermute | solution.py:292
  5.9 8.3 %collective-permute-start.12 = (bf16[16,6528]{1,0:T(8,128)(2,1)S(1)}, bf16[16,6528]{1,0:T(8,128)(2,1)S(1)}, u32[]{:S(2)}, u32[]{:S(2)}) collective-permute-start(bf16[16,6528]{1,0:T(8,128)(2,1)S(1)} %get-tuple-element.24), channel_id=1, source_target_pairs={{2,0},{4,2},{6,4},{7,6},{5,7},{3,5},{1,3},{0,1},{8,18},{10,20},{12... | collective-permute-start | bytes 626696 | tf_op jit(solution)/shard_map/ppermute | solution.py:292
  7.4 10.3 %collective-permute-start = (bf16[16,6528]{1,0:T(8,128)(2,1)S(1)}, bf16[16,6528]{1,0:T(8,128)(2,1)S(1)}, u32[]{:S(2)}, u32[]{:S(2)}) collective-permute-start(bf16[16,6528]{1,0:T(8,128)(2,1)S(1)} %get-tuple-element.18.lead), channel_id=1, source_target_pairs={{0,26},{2,28},{4,30},{6,31},{7,29},{5,27},{3,25},{1,24},{10,8},{12... | collective-permute-start | bytes 626696 | tf_op jit(solution)/shard_map/ppermute | solution.py:292
  9.7 9.0 %collective-permute-start.4 = (bf16[16,6528]{1,0:T(8,128)(2,1)S(1)}, bf16[16,6528]{1,0:T(8,128)(2,1)S(1)}, u32[]{:S(2)}, u32[]{:S(2)}) collective-permute-start(bf16[16,6528]{1,0:T(8,128)(2,1)S(1)} %collective-permute-done.3.refs_9_), channel_id=1, source_target_pairs={{2,0},{4,2},{6,4},{7,6},{5,7},{3,5},{1,3},{0,1},{8,10},{10,12},{12... | collective-permute-start | bytes 626696 | tf_op jit(solution)/shard_map/ppermute | solution.py:292
  13.2 8.6 %collective-permute-start.8 = (bf16[16,6528]{1,0:T(8,128)(2,1)S(1)}, bf16[16,6528]{1,0:T(8,128)(2,1)S(1)}, u32[]{:S(2)}, u32[]{:S(2)}) collective-permute-start(bf16[16,6528]{1,0:T(8,128)(2,1)S(1)} %collective-permute-done.7.refs_8_), channel_id=1, source_target_pairs={{0,2},{2,4},{4,6},{6,7},{7,5},{5,3},{3,1},{1,0},{10,8},{12,10},{14... | collective-permute-start | bytes 626696 | tf_op jit(solution)/shard_map/ppermute | solution.py:292
  14.1 9.0 %collective-permute-start.13 = (bf16[16,6528]{1,0:T(8,128)(2,1)S(1)}, bf16[16,6528]{1,0:T(8,128)(2,1)S(1)}, u32[]{:S(2)}, u32[]{:S(2)}) collective-permute-start(bf16[16,6528]{1,0:T(8,128)(2,1)S(1)} %collective-permute-done.12.refs_6_), channel_id=1, source_target_pairs={{2,0},{4,2},{6,4},{7,6},{5,7},{3,5},{1,3},{0,1},{8,10},{10,12},{12... | collective-permute-start | bytes 626696 | tf_op jit(solution)/shard_map/ppermute | solution.py:292
  17.7 8.6 %collective-permute-start.1 = (bf16[16,6528]{1,0:T(8,128)(2,1)S(1)}, bf16[16,6528]{1,0:T(8,128)(2,1)S(1)}, u32[]{:S(2)}, u32[]{:S(2)}) collective-permute-start(bf16[16,6528]{1,0:T(8,128)(2,1)S(1)} %collective-permute-done.refs_7_), channel_id=1, source_target_pairs={{0,2},{2,4},{4,6},{6,7},{7,5},{5,3},{3,1},{1,0},{10,8},{12,10},{14... | collective-permute-start | bytes 626696 | tf_op jit(solution)/shard_map/ppermute | solution.py:292
  18.6 9.0 %collective-permute-start.5 = (bf16[16,6528]{1,0:T(8,128)(2,1)S(1)}, bf16[16,6528]{1,0:T(8,128)(2,1)S(1)}, u32[]{:S(2)}, u32[]{:S(2)}) collective-permute-start(bf16[16,6528]{1,0:T(8,128)(2,1)S(1)} %collective-permute-done.4.refs_5_), channel_id=1, source_target_pairs={{2,0},{4,2},{6,4},{7,6},{5,7},{3,5},{1,3},{0,1},{8,10},{10,12},{12... | collective-permute-start | bytes 626696 | tf_op jit(solution)/shard_map/ppermute | solution.py:292
  21.8 9.0 %collective-permute-start.9 = (bf16[16,6528]{1,0:T(8,128)(2,1)S(1)}, bf16[16,6528]{1,0:T(8,128)(2,1)S(1)}, u32[]{:S(2)}, u32[]{:S(2)}) collective-permute-start(bf16[16,6528]{1,0:T(8,128)(2,1)S(1)} %collective-permute-done.8.refs_4_), channel_id=1, source_target_pairs={{0,2},{2,4},{4,6},{6,7},{7,5},{5,3},{3,1},{1,0},{10,8},{12,10},{14... | collective-permute-start | bytes 626696 | tf_op jit(solution)/shard_map/ppermute | solution.py:292
  22.1 9.0 %collective-permute-start.15 = (bf16[16,6528]{1,0:T(8,128)(2,1)S(1)}, bf16[16,6528]{1,0:T(8,128)(2,1)S(1)}, u32[]{:S(2)}, u32[]{:S(2)}) collective-permute-start(bf16[16,6528]{1,0:T(8,128)(2,1)S(1)} %get-tuple-element.29), channel_id=1, source_target_pairs={{0,24},{1,25},{2,26},{3,27},{4,28},{5,29},{6,30},{7,31},{8,16},{9,... | collective-permute-start | bytes 626696 | tf_op jit(solution)/shard_map/ppermute | solution.py:292
  23.1 9.9 %collective-permute-start.14 = (bf16[16,6528]{1,0:T(8,128)(2,1)S(1)}, bf16[16,6528]{1,0:T(8,128)(2,1)S(1)}, u32[]{:S(2)}, u32[]{:S(2)}) collective-permute-start(bf16[16,6528]{1,0:T(8,128)(2,1)S(1)} %collective-permute-done.13.refs_2_), channel_id=1, source_target_pairs={{2,0},{4,2},{6,4},{7,6},{5,7},{3,5},{1,3},{0,1},{8,10},{10,12},{12... | collective-permute-start | bytes 626696 | tf_op jit(solution)/shard_map/ppermute | solution.py:292
  26.2 9.0 %collective-permute-start.2 = (bf16[16,6528]{1,0:T(8,128)(2,1)S(1)}, bf16[16,6528]{1,0:T(8,128)(2,1)S(1)}, u32[]{:S(2)}, u32[]{:S(2)}) collective-permute-start(bf16[16,6528]{1,0:T(8,128)(2,1)S(1)} %collective-permute-done.1.refs_3_), channel_id=1, source_target_pairs={{0,2},{2,4},{4,6},{6,7},{7,5},{5,3},{3,1},{1,0},{10,8},{12,10},{14... | collective-permute-start | bytes 626696 | tf_op jit(solution)/shard_map/ppermute | solution.py:292
  27.6 9.0 %collective-permute-start.6 = (bf16[16,6528]{1,0:T(8,128)(2,1)S(1)}, bf16[16,6528]{1,0:T(8,128)(2,1)S(1)}, u32[]{:S(2)}, u32[]{:S(2)}) collective-permute-start(bf16[16,6528]{1,0:T(8,128)(2,1)S(1)} %collective-permute-done.5.refs_1_), channel_id=1, source_target_pairs={{2,0},{4,2},{6,4},{7,6},{5,7},{3,5},{1,3},{0,1},{8,10},{10,12},{12... | collective-permute-start | bytes 626696 | tf_op jit(solution)/shard_map/ppermute | solution.py:292
  30.7 6.2 %collective-permute-start.11 = (bf16[16,3456]{1,0:T(8,128)(2,1)S(1)}, bf16[16,3456]{1,0:T(8,128)(2,1)S(1)}, u32[]{:S(2)}, u32[]{:S(2)}) collective-permute-start(bf16[16,3456]{1,0:T(8,128)(2,1)S(1)} %slice.9), channel_id=1, source_target_pairs={{0,2},{2,4},{4,6},{6,7},{7,5},{5,3},{3,1},{1,0},{10,8},{12,10},{14... | collective-permute-start | bytes 331784 | tf_op jit(solution)/shard_map/ppermute | solution.py:292
  31.1 6.9 %collective-permute-start.10 = (bf16[16,3072]{1,0:T(8,128)(2,1)S(1)}, bf16[16,3072]{1,0:T(8,128)(2,1)S(1)}, u32[]{:S(2)}, u32[]{:S(2)}) collective-permute-start(bf16[16,3072]{1,0:T(8,128)(2,1)S(1)} %slice.8), channel_id=1, source_target_pairs={{0,2},{2,4},{4,6},{6,7},{7,5},{5,3},{3,1},{1,0},{10,8},{12,10},{14... | collective-permute-start | bytes 294920 | tf_op jit(solution)/shard_map/ppermute | solution.py:292
